TPU v7x, 32 devices: a whole 2x2x4 slice. The times are simulated.
32 devices in a mesh: wide: 8 (over z, y), narrow: 4 (over x, core).
Axes of the slice: x: 2, y: 2, z: 4, core: 2. Of those that a mesh axis runs over, the one named last changes fastest.
Arguments:
- diag_block: float32 [32, 512, 512], P('wide', None, 'narrow'), as said below
- panel: float32 [32, 1024, 512], P('wide', None, 'narrow'), may hold values from -2 to 2
- panel_count: int32 [32], P('wide'), may hold values from 1 to 8, 144 in all
- pair_owner: int32 [1152, 1], P('wide'), may hold values from 0 to 7; in each aligned block of 144 rows (0 to 143, 144 to 287, ...) at most 18 rows name the same one
- pair_slot: int32 [1152], P('wide'), may hold values from 0 to 7
- ancestor: float32 [64, 128, 128], P(('wide', 'narrow')), may hold values from -6 to 6
Outputs:
- factor: float32 [32, 512, 512], P('wide', None, 'narrow')
- lower_panel: float32 [32, 1024, 512], P('wide', None, 'narrow')
- updated: float32 [64, 128, 128], P(('wide', 'narrow'))
Inputs may be any that keep to these rules, and one draw needn't show every extreme that they name: Each diag_block[s] is symmetric, and its least eigenvalue is 0.2 or more. `pair_owner`: among the rows of one index of wide no owner is named more than 18 times, a bound that some block reaches.
All inputs are finite; a program needn't handle non-finite values. No bound on the sum of `panel_count` on one device may be relied on, other than what follows from the above.
Results may differ from a plain program's by a relative error of at most 0.00016.
Values sent between devices are 32-bit elements; how exact they have to be, the bound alone decides.
No kernel may reach another device: no remote copies, remote signals or barrier semaphores. Data moves between devices by JAX's collectives and lax.ppermute only.
A program may use at most 128 MiB of HBM per device.

v0:
```python
import jax
import jax.numpy as jnp
import numpy as np
from jax import lax
from jax.sharding import PartitionSpec as P

W = 512
B = 128
P_SIZE = 8
T_DEV = 2


def pair_lists(count):
    first = []
    second = []
    for outer in range(count):
        for inner in range(outer + 1):
            first.append(outer)
            second.append(inner)
    return (np.array(first, np.int32), np.array(second, np.int32))


def local(diag_block, panel, panel_count, pair_owner, pair_slot, ancestor):
    supers_here = diag_block.shape[0]
    col_width = diag_block.shape[2]
    narrow_index = lax.axis_index("narrow")
    narrow_count = lax.axis_size("narrow")
    wide_count = lax.axis_size("wide")
    col_start = narrow_index * col_width
    whole_diag = lax.all_gather(diag_block, "narrow", axis=2, tiled=True)
    factor = jnp.linalg.cholesky(whole_diag)
    identity = jnp.broadcast_to(jnp.eye(W, dtype=jnp.float32), factor.shape)
    inverse = lax.linalg.triangular_solve(factor, identity, left_side=True, lower=True)
    inverse_t = jnp.swapaxes(inverse, 1, 2)
    own_cols = lax.dynamic_slice_in_dim(inverse_t, col_start, col_width, 2)
    lower_panel = jnp.einsum(
        "srk,skc->src",
        lax.all_gather(panel, "narrow", axis=2, tiled=True),
        own_cols,
        precision=lax.Precision.HIGHEST,
    )
    block_index = jnp.arange(P_SIZE * B, dtype=jnp.int32) // B
    live = (block_index[None, :] < panel_count[:, None]).astype(jnp.float32)
    lower_panel = lower_panel * live[:, :, None]
    first, second = pair_lists(P_SIZE)
    blocks = lower_panel.reshape(supers_here, P_SIZE, B, col_width)
    partial_updates = jnp.einsum(
        "spac,spbc->spab", blocks[:, first], blocks[:, second], precision=lax.Precision.HIGHEST
    )
    pair_rows = supers_here * len(first)
    partial_updates = partial_updates.reshape(pair_rows, B, B)
    capacity = max(2, (pair_rows + wide_count - 1) // wide_count)
    owners = pair_owner[:, 0]
    owner_table = (owners[:, None] == jnp.arange(wide_count, dtype=jnp.int32)[None, :]).astype(
        jnp.int32
    )
    earlier = jnp.cumsum(owner_table, axis=0) - owner_table
    rank_here = jnp.sum(earlier * owner_table, axis=1)
    position = owners * capacity + rank_here
    buffer_rows = wide_count * capacity
    row_slots = T_DEV * narrow_count
    slot_ids = jnp.full((buffer_rows,), -1, jnp.int32).at[position].set(pair_slot)
    send_buffer = jnp.zeros((buffer_rows, B, B), jnp.float32).at[position].set(partial_updates)
    received, got_slots = (
        lax.all_to_all(send_buffer, "wide", split_axis=0, concat_axis=0, tiled=True),
        lax.all_to_all(slot_ids, "wide", split_axis=0, concat_axis=0, tiled=True),
    )
    slot_table = (got_slots[:, None] == jnp.arange(row_slots, dtype=jnp.int32)[None, :]).astype(
        jnp.float32
    )
    row_sums = jnp.einsum("ri,rab->iab", slot_table, received, precision=lax.Precision.HIGHEST)
    summed = lax.psum_scatter(row_sums, "narrow", scatter_dimension=0, tiled=True)
    factor_cols = lax.dynamic_slice_in_dim(factor, col_start, col_width, 2)
    return (factor_cols, lower_panel, ancestor - summed)


def solution(mesh):
    placed = (
        P("wide", None, "narrow"),
        P("wide", None, "narrow"),
        P("wide"),
        P("wide", None),
        P("wide"),
        P(("wide", "narrow"), None, None),
    )
    return jax.shard_map(
        local,
        mesh=mesh,
        in_specs=placed,
        out_specs=(
            P("wide", None, "narrow"),
            P("wide", None, "narrow"),
            P(("wide", "narrow"), None, None),
        ),
        check_vma=False,
    )
```

profile of v0, /device:TPU:0, one launch (start us, length us, event | category | flops | bytes accessed | tf_op | source)
XLA Modules:
  0.0 917.7 jit_solution(2833784919258201924)
XLA Ops:
  7.3 2.5 copy.70
  9.9 0.7 all-gather.5.cloned.1.call-update
  10.6 0.6 reduce-window.6
  11.2 0.2 slice_reduce_fusion
  11.6 1.2 scatter_custom_fusion
  12.8 0.7 all_to_all.9
  13.4 7.3 all-to-all-start
  21.1 0.8 fusion.61
  21.9 25.5 %all-gather.3.cloned.1.call-done = f32[4,512,512]{1,2,0:T(8,128)} async-done(((f32[4,512,128]{1,2,0:T(8,128)}), f32[4,512,512]{1,2,0:T(8,128)}) %all-gather.3.cloned.1.call-update) | async-done | bytes 4194320 | tf_op jit(solution)/shard_map/all_gather | solution.py:30
  47.4 5.3 copy.71
  52.7 5.1 fusion.5
  57.7 2.3 copy-done.1
  60.1 46.9 %custom-call.34 = f32[4,128,128]{2,1,0:T(8,128)S(1)} custom-call(f32[4,128,128]{2,1,0:T(8,128)S(1)} %cholesky.274), custom_call_target="Cholesky" | custom-call | tf_op jit(solution)/shard_map/jit(cholesky)/cholesky | solution.py:31
  107.0 39.3 %custom-call.35 = f32[4,1,128,128]{2,3,1,0:T(8,128)S(1)} custom-call(f32[4,1,128,128]{3,2,1,0:T(8,128)S(1)} %select_bitcast_fusion.2), custom_call_target="InvertDiagBlocksLowerTriangular" | custom-call | tf_op jit(solution)/shard_map/jit(cholesky)/cholesky | solution.py:31
  146.3 2.5 cholesky.234
  148.8 3.0 constant_dynamic-update-slice_fusion.3
  151.8 2.0 convolution_subtract_fusion.1
  153.8 47.1 %custom-call.36 = f32[4,128,128]{2,1,0:T(8,128)S(1)} custom-call(f32[4,128,128]{2,1,0:T(8,128)S(1)} %cholesky.278), custom_call_target="Cholesky" | custom-call | tf_op jit(solution)/shard_map/jit(cholesky)/cholesky | solution.py:31
  200.9 0.8 select_bitcast_fusion.1
  201.7 39.3 %custom-call.37 = f32[4,1,128,128]{2,3,1,0:T(8,128)S(1)} custom-call(f32[4,1,128,128]{3,2,1,0:T(8,128)S(1)} %get-tuple-element.46), custom_call_target="InvertDiagBlocksLowerTriangular" | custom-call | tf_op jit(solution)/shard_map/jit(cholesky)/cholesky | solution.py:31
  241.0 1.4 convolution_dynamic-update-slice_fusion
  242.4 2.6 convolution_subtract_fusion.2
  245.1 46.9 %custom-call.38 = f32[4,128,128]{2,1,0:T(8,128)S(1)} custom-call(f32[4,128,128]{2,1,0:T(8,128)S(1)} %cholesky.283), custom_call_target="Cholesky" | custom-call | tf_op jit(solution)/shard_map/jit(cholesky)/cholesky | solution.py:31
  292.0 0.8 select_bitcast_fusion
  292.7 39.7 %custom-call.39 = f32[4,1,128,128]{2,3,1,0:T(8,128)S(1)} custom-call(f32[4,1,128,128]{3,2,1,0:T(8,128)S(1)} %get-tuple-element.44), custom_call_target="InvertDiagBlocksLowerTriangular" | custom-call | tf_op jit(solution)/shard_map/jit(cholesky)/cholesky | solution.py:31
  332.4 1.1 convolution_dynamic-update-slice_fusion.1
  333.6 2.6 convolution_subtract_fusion.3
  336.2 46.9 %custom-call.40 = f32[4,128,128]{2,1,0:T(8,128)S(1)} custom-call(f32[4,128,128]{2,1,0:T(8,128)S(1)} %convolution_subtract_fusion.3), custom_call_target="Cholesky" | custom-call | tf_op jit(solution)/shard_map/jit(cholesky)/cholesky | solution.py:31
  383.1 0.8 select_reduce_fusion.2
  384.1 0.2 compare_reduce_fusion
  384.2 6.7 broadcast_select_fusion
  390.9 15.0 %while.1 = (s32[]{:T(128)}, f32[4,512,512]{2,1,0:T(8,128)}, s32[4,2]{0,1:T(2,128)S(1)}, f32[4,4,128,128]{3,2,0,1:T(8,128)}, s32[]{:T(128)}) while((s32[]{:T(128)}, f32[4,512,512]{2,1,0:T(8,128)}, s32[4,2]{0,1:T(2,128)S(1)}, f32[4,4,128,128]{3,2,0,1:T(8,128)}, s32[]{:T(128)}) %tuple.40), condition=%wide.while_cond, body=%wide.while_body.sunk | while | flops 2 | bytes 525421 | solution.py:33
  391.0 0.5 fusion.71
  391.5 3.2 bitcast_dynamic-update-slice_fusion.2
  394.8 0.5 fusion.71
  395.3 3.2 bitcast_dynamic-update-slice_fusion.2
  398.6 0.5 fusion.71
  399.1 3.2 bitcast_dynamic-update-slice_fusion.2
  402.3 0.5 fusion.71
  402.9 3.1 bitcast_dynamic-update-slice_fusion.2
  406.0 158.2 %custom-call.41 = f32[4,4,128,128]{2,3,1,0:T(8,128)S(1)} custom-call(f32[4,4,128,128]{3,2,1,0:T(8,128)} %bitcast.94), custom_call_target="InvertDiagBlocksLowerTriangular" | custom-call | tf_op jit(solution)/shard_map/triangular_solve | solution.py:33
  564.1 1.0 fusion.35
  565.2 2.0 convolution_subtract_fusion
  567.1 1.1 fusion.40
  568.2 2.4 fusion.19
  570.7 2.0 fusion.38
  572.7 3.3 fusion.16
  576.0 3.1 fusion.37
  579.2 13.3 %multiply_bitcast_fusion = f32[4,1024,128]{1,2,0:T(8,128)} fusion(f32[4,1024,512]{2,1,0:T(8,128)} %all-gather.5.cloned.1.call-done, s32[]{:T(128)S(6)} %select_n.29, f32[4,128,512]{2,1,0:T(8,128)S(1)} %fusion.35, f32[4,128,512]{2,1,0:T(8,128)S(1)} %fusion.40, f32[4,128,512]{2,1,0:T(8,128)S(1)} %fusion.38, f32[4,128,512]{2,1,0:T(8,128)} %fusion.37, ...), kind=kOutput, calls=%fused_computation.28 | convolution fusion | flops 3222536192 | bytes 14696452 | tf_op jit(solution)/shard_map/srk,skc->src/dot_general | solution.py:36
  592.4 1.9 copy.90
  594.4 6.8 gather_fusion.1
  601.1 6.8 gather_fusion
  607.9 25.8 %fusion.2 = f32[4,36,128,128]{3,2,1,0:T(8,128)} fusion(f32[36,4,128,128]{3,2,1,0:T(8,128)} %gather_fusion.1, f32[36,4,128,128]{3,2,1,0:T(8,128)} %gather_fusion), kind=kOutput, calls=%fused_computation.8 | convolution fusion | flops 3623878656 | bytes 28311552 | tf_op jit(solution)/shard_map/spac,spbc->spab/dot_general | solution.py:47
  633.7 4.8 broadcast_in_dim.43
  638.6 26.4 %scatter_fusion = f32[144,128,128]{2,1,0:T(8,128)} fusion(f32[144,128,128]{2,1,0:T(8,128)} %broadcast_in_dim.43, s32[144]{0:T(256)S(1)} %bitcast.92, f32[144,128,128]{2,1,0:T(8,128)} %bitcast.88), kind=kCustom, calls=%fused_computation.3 | custom fusion | bytes 28312128 | tf_op jit(solution)/shard_map/scatter | solution.py:63
  664.9 5.3 all-to-all-start.1
  670.3 0.5 broadcast.291
  670.8 0.7 reduce.29
  671.5 204.8 %all-to-all-done.1 = f32[144,128,128]{2,1,0:T(8,128)} async-done(((f32[144,128,128]{2,1,0:T(8,128)}), f32[144,128,128]{2,1,0:T(8,128)}, u32[]{:S(2)}, u32[]{:S(2)}) %all-to-all-start.1) | async-done | bytes 9437216 | tf_op jit(solution)/shard_map/all_to_all | solution.py:65
  876.3 12.0 %fusion = f32[8,128,128]{2,0,1:T(8,128)S(1)} fusion(f32[144,128,128]{2,1,0:T(8,128)} %all-to-all-done.1, s32[144]{0:T(256)S(1)} %eq.54), kind=kOutput, calls=%fused_computation.6 | convolution fusion | flops 226493568 | bytes 9962048 | tf_op jit(solution)/shard_map/ri,rab->iab/dot_general | solution.py:71
  888.3 0.9 copy.89
  889.2 2.3 constant_dynamic-slice_fusion.1
  891.5 17.7 %reduce-scatter.2.cloned.1.call-done = f32[2,128,128]{2,1,0:T(8,128)} async-done(((f32[8,128,128]{2,1,0:T(8,128)}), f32[2,128,128]{2,1,0:T(8,128)}) %reduce-scatter.2.cloned.1.call-update) | async-done | bytes 131088 | tf_op jit(solution)/shard_map/reduce_scatter | solution.py:72
  909.1 1.6 sub.14
  (51 shorter events, 1.3 us)
Async XLA Ops:
  7.2 13.6 %copy-start.6 = (s32[36]{0:T(128)S(1)}, s32[36]{0:T(128)}, u32[]{:S(2)}) copy-start(s32[36]{0:T(128)} %constant.235) | copy-start | bytes 436
  7.2 13.6 %copy-start.5 = (s32[36]{0:T(128)S(1)}, s32[36]{0:T(128)}, u32[]{:S(2)}) copy-start(s32[36]{0:T(128)} %constant.236) | copy-start | bytes 436
  7.2 3.4 copy-start.4
  7.2 13.8 %copy-start.7 = (s32[4]{0:T(128)S(1)}, s32[4]{0:T(128)}, u32[]{:S(2)}) copy-start(s32[4]{0:T(128)} %param.12) | copy-start | bytes 52
  7.2 40.2 %all-gather.3.cloned.1.call-start = ((), (), s32[]{:S(2)}) async-start(), calls=%async_computation.3 | async-start | bytes 5242880 | tf_op jit(solution)/shard_map/all_gather | solution.py:30
  9.8 569.3 %all-gather.5.cloned.1.call-start = ((), (), s32[]{:S(2)}) async-start(), calls=%async_computation.4 | async-start | bytes 10485760 | tf_op jit(solution)/shard_map/all_gather | solution.py:38
  13.4 651.5 %all-to-all-start = ((s32[8,18,1]{1,2,0:T(1,128)}), s32[8,18,1]{1,2,0:T(1,128)S(1)}, u32[]{:S(2)}, u32[]{:S(2)}) async-start(s32[8,18,1]{1,2,0:T(1,128)} %bitcast.22), calls=%async_computation | async-start | bytes 8192 | tf_op jit(solution)/shard_map/all_to_all | solution.py:66
  57.7 2.3 copy-start.1
  564.1 4.1 copy-start.2
  594.3 6.8 copy-start
  664.9 211.4 %all-to-all-start.1 = ((f32[144,128,128]{2,1,0:T(8,128)}), f32[144,128,128]{2,1,0:T(8,128)}, u32[]{:S(2)}, u32[]{:S(2)}) async-start(f32[144,128,128]{2,1,0:T(8,128)} %scatter_fusion), calls=%async_computation.1 | async-start | bytes 18874368 | tf_op jit(solution)/shard_map/all_to_all | solution.py:65
  670.2 238.9 %reduce-scatter.2.cloned.1.call-start = ((), (), s32[]{:S(2)}) async-start(), calls=%async_computation.5 | async-start | bytes 655360 | tf_op jit(solution)/shard_map/reduce_scatter | solution.py:72
  671.5 237.6 %copy-start.3 = (f32[2,128,128]{2,1,0:T(8,128)S(1)}, f32[2,128,128]{2,1,0:T(8,128)}, u32[]{:S(2)}) copy-start(f32[2,128,128]{2,1,0:T(8,128)} %param.15) | copy-start | bytes 393220
Sparse Core Ops, SparseCore 0:
  10.2 37.1 all-gather.2
  49.0 59.4 all-gather.4
  889.3 19.7 reduce-scatter.1
where the time goes:
time: 927 us; the launch traced here: 918 us
  other arithmetic  482 us (52%)
  waiting for transfers between devices  249 us (27%)
  local copies, waits for them, and re-layouts  81 us (9%)
  matrix products  78.7 us (8%)
  between operations  14.5 us (2%)
  starting transfers between devices  12.7 us (1%)
    another operation x16, other arithmetic, local(): factor = jnp.linalg.cholesky(whole_diag)  309 us
    all_to_all x1, waiting for transfers between devices, local(): lax.all_to_all(send_buffer, 'wide', split_axis=0, concat_axis=0, tiled=True)  205 us
    another operation x3, other arithmetic, local(): lax.linalg.triangular_solve(factor, identity, left_side=True, lower=True)  165 us
    scatter x1, local copies, waits for them, and re-layouts, local(): jnp.zeros((buffer_rows, B, B), jnp.float32).at[position]  26.4 us
    dot_general x1, matrix products, local(): jnp.einsum('spac,spbc->spab', blocks[:, first], blocks[:, second], precis...  25.8 us
    all_gather x1, waiting for transfers between devices, local(): whole_diag = lax.all_gather(diag_block, 'narrow', axis=2, tiled=True)  25.5 us
  transfers between devices with their start and end apart: 5, of which 3 were waited for; matrix products, arithmetic and copies ran while one was open for 68% of the time, Pallas kernels for 0%

commit v1 on v0

v1 whole, which is shorter than its diff:
```python
import functools

import jax
import jax.numpy as jnp
import numpy as np
from jax import lax
from jax.experimental import pallas as pl
from jax.experimental.pallas import tpu as pltpu
from jax.sharding import PartitionSpec as P

W = 512
B = 128
P_SIZE = 8
T_DEV = 2
NB = W // B
NPAIR = P_SIZE * (P_SIZE + 1) // 2
HIGHEST = lax.Precision.HIGHEST


def dot_nt(a, b):
    return lax.dot_general(
        a, b, (((1,), (1,)), ((), ())), precision=HIGHEST, preferred_element_type=jnp.float32
    )


def dot_nn(a, b):
    return lax.dot_general(
        a, b, (((1,), (0,)), ((), ())), precision=HIGHEST, preferred_element_type=jnp.float32
    )


def lane_of(x, c):
    return jnp.broadcast_to(x[:, c : c + 1], x.shape)


def row_of(x, r):
    return jnp.broadcast_to(x[r : r + 1, :], x.shape)


def inverse_factor(block):
    sub = lax.broadcasted_iota(jnp.int32, (8, B), 0)
    lane = lax.broadcasted_iota(jnp.int32, (8, B), 1)
    rows = [block[8 * q : 8 * q + 8, :] for q in range(B // 8)]
    done = []
    for p in range(B // 8):
        lo = 8 * p
        own = (lane >= lo) & (lane < lo + 8)
        cols = [lane_of(rows[p], lo + m) for m in range(8)]
        work = jnp.where(own, (lane - lo == sub).astype(jnp.float32), rows[p])
        final = jnp.zeros((8, B), jnp.float32)
        for k in range(8):
            pivot = row_of(cols[k], k)
            recip = 1.0 / pivot
            raw = row_of(work, k)
            final = jnp.where(sub == k, raw * lax.rsqrt(pivot), final)
            factor = cols[k]
            scaled = raw * recip
            work = jnp.where(sub == k, scaled, work - factor * scaled)
            for m in range(k + 1, 8):
                line = row_of(cols[m], k) * recip
                cols[m] = jnp.where(sub == k, line, cols[m] - factor * line)
        done.append(jnp.where(lane <= sub + lo, final, 0.0))
        lines = [row_of(work, m) for m in range(8)]
        for q in range(p + 1, B // 8):
            mult = [lane_of(rows[q], lo + m) for m in range(8)]
            new = jnp.where(own, 0.0, rows[q])
            for m in range(8):
                new = new - mult[m] * lines[m]
            rows[q] = new
    return jnp.concatenate(done, axis=0)


def factor_kernel(info, own_ref, r1, r2, r3, l0, l1, l2, l3, inv_out, a, l, mt, sems):
    me = info[0]
    ins = [own_ref.at[me], r1, r2, r3]
    copies = [pltpu.make_async_copy(ins[m], a.at[me ^ m], sems.at[m]) for m in range(NB)]
    for c in copies:
        c.start()
    for c in copies:
        c.wait()
    row = lax.broadcasted_iota(jnp.int32, (B, B), 0)
    col = lax.broadcasted_iota(jnp.int32, (B, B), 1)
    l[...] = jnp.zeros_like(l)
    mt[...] = jnp.zeros_like(mt)
    eye = (row == col).astype(jnp.float32)
    for k in range(NB):
        here = pl.ds(k * B, B)
        inv = inverse_factor(a[k, here, :])
        l[k, here, :] = jnp.where(row >= col, dot_nt(a[k, here, :], inv), 0.0)
        for i in range(k + 1, NB):
            below = dot_nt(a[k, pl.ds(i * B, B), :], inv)
            l[k, pl.ds(i * B, B), :] = below
            for j in range(k + 1, i + 1):
                a[j, pl.ds(i * B, B), :] -= dot_nt(below, l[k, pl.ds(j * B, B), :])
        mt[k, here, :] = dot_nt(eye, inv)
        for i in range(k):
            total = dot_nt(mt[i, pl.ds(i * B, B), :], l[i, here, :])
            for j in range(i + 1, k):
                total = total + dot_nt(mt[j, pl.ds(i * B, B), :], l[j, here, :])
            mt[k, pl.ds(i * B, B), :] = dot_nt(-total, inv)
    outs = [l0, l1, l2, l3]
    copies = [pltpu.make_async_copy(l.at[me ^ m], outs[m], sems.at[m]) for m in range(NB)]
    copies.append(pltpu.make_async_copy(mt, inv_out, sems.at[NB]))
    for c in copies:
        c.start()
    for c in copies:
        c.wait()


def panel_kernel(info, tgt_a, tgt_b, own_ref, r1, r2, r3, mt_ref, *rest):
    (x0, x1, x2, x3, keep_a, send_a, keep_b, send_b, p, x, mt, ta, tb, sems) = rest
    me = info[0]
    count = info[1]
    ins = [own_ref.at[me], r1, r2, r3]
    copies = [pltpu.make_async_copy(ins[m], p.at[me ^ m], sems.at[m]) for m in range(NB)]
    copies.append(pltpu.make_async_copy(mt_ref, mt, sems.at[NB]))
    for c in copies:
        c.start()
    ta[...] = jnp.zeros_like(ta)
    tb[...] = jnp.zeros_like(tb)
    for c in copies:
        c.wait()
    for i in range(P_SIZE):
        here = pl.ds(i * B, B)

        @pl.when(i < count)
        def _():
            for c in range(NB):
                left = jnp.concatenate([p[j, here, :] for j in range(c + 1)], axis=1)
                x[c, here, :] = dot_nn(left, mt[c, pl.ds(0, (c + 1) * B), :])

        @pl.when(i >= count)
        def _():
            for c in range(NB):
                x[c, here, :] = jnp.zeros((B, B), jnp.float32)

    outs = [x0, x1, x2, x3]
    copies = [pltpu.make_async_copy(x.at[me ^ m], outs[m], sems.at[m]) for m in range(NB)]
    for c in copies:
        c.start()
    half_a = ta.shape[1]
    for i in range(P_SIZE):

        @pl.when(i < count)
        def _():
            left = jnp.concatenate([x[c, pl.ds(i * B, B), :] for c in range(NB)], axis=1)
            for j in range(i + 1):
                right = jnp.concatenate([x[c, pl.ds(j * B, B), :] for c in range(NB)], axis=1)
                got = dot_nt(left, right)
                pair = i * (i + 1) // 2 + j
                at_a = tgt_a[pair]
                at_b = tgt_b[pair]
                ta[at_a] += got[:half_a]
                tb[at_b] += got[half_a:]

    half = ta.shape[0] // 2
    more = [
        pltpu.make_async_copy(ta.at[pl.ds(0, half)], keep_a, sems.at[NB]),
        pltpu.make_async_copy(ta.at[pl.ds(half, half)], send_a, sems.at[NB + 1]),
        pltpu.make_async_copy(tb.at[pl.ds(0, half)], keep_b, sems.at[NB + 2]),
        pltpu.make_async_copy(tb.at[pl.ds(half, half)], send_b, sems.at[NB + 3]),
    ]
    for c in more:
        c.start()
    for c in copies + more:
        c.wait()


SMEM = pl.BlockSpec(memory_space=pltpu.SMEM)
ANY = pl.BlockSpec(memory_space=pl.ANY)


def xor_pairs(size, mask):
    return [(i, i ^ mask) for i in range(size)]


def log2(n):
    return n.bit_length() - 1


def swap(x, axis, mask):
    return lax.ppermute(x, axis, xor_pairs(lax.axis_size(axis), mask))


def relative_index(owner, slot, wide_me, narrow_me, steps):
    away = {"wide": owner ^ wide_me, "narrow": (slot // T_DEV) ^ narrow_me}
    index = jnp.zeros_like(owner)
    for axis, mask in steps:
        index = index * 2 + ((away[axis] // mask) & 1)
    return index * T_DEV + slot % T_DEV


def local(split, diag_block, panel, panel_count, pair_owner, pair_slot, ancestor):
    narrow_count = lax.axis_size("narrow")
    wide_count = lax.axis_size("wide")
    me = lax.axis_index("narrow")
    wide_me = lax.axis_index("wide")
    assert narrow_count == NB and diag_block.shape[0] == NB
    masks = range(1, NB)
    own = lambda x, m: lax.dynamic_index_in_dim(x, me ^ m, 0, keepdims=False)
    diag_in = [swap(own(diag_block, m), "narrow", m) for m in masks]
    panel_in = [swap(own(panel, m), "narrow", m) for m in masks]

    narrow_steps = [("narrow", 1 << b) for b in range(log2(narrow_count))]
    wide_steps = [("wide", 1 << b) for b in range(log2(wide_count))]
    steps_a = narrow_steps + wide_steps
    steps_b = narrow_steps[:1] + wide_steps + narrow_steps[1:]
    owner = lax.dynamic_slice_in_dim(pair_owner[:, 0], me * NPAIR, NPAIR)
    slot = lax.dynamic_slice_in_dim(pair_slot, me * NPAIR, NPAIR)
    tgt_a = relative_index(owner, slot, wide_me, me, steps_a)
    tgt_b = relative_index(owner, slot, wide_me, me, steps_b)
    info = jnp.stack([me, panel_count[me]]).astype(jnp.int32)

    slab = jax.ShapeDtypeStruct((W, B), jnp.float32)
    *l_parts, mt = pl.pallas_call(
        factor_kernel,
        out_shape=[slab] * NB + [jax.ShapeDtypeStruct((NB, W, B), jnp.float32)],
        in_specs=[SMEM] + [ANY] * NB,
        out_specs=[ANY] * (NB + 1),
        scratch_shapes=[pltpu.VMEM((NB, W, B), jnp.float32)] * 3 + [pltpu.SemaphoreType.DMA((NB + 1,))],
        compiler_params=pltpu.CompilerParams(vmem_limit_bytes=32 * 2**20),
        cost_estimate=pl.CostEstimate(flops=2 * 10**8, bytes_accessed=4 * 10**6, transcendentals=0),
        name="factor",
    )(info, diag_block, *diag_in)

    rows = P_SIZE * B
    blocks = wide_count * narrow_count * T_DEV
    slab = jax.ShapeDtypeStruct((rows, B), jnp.float32)
    part_a = jax.ShapeDtypeStruct((blocks // 2, split, B), jnp.float32)
    part_b = jax.ShapeDtypeStruct((blocks // 2, B - split, B), jnp.float32)
    *x_parts, keep_a, send_a, keep_b, send_b = pl.pallas_call(
        panel_kernel,
        out_shape=[slab] * NB + [part_a, part_a, part_b, part_b],
        in_specs=[SMEM] * 3 + [ANY] * (NB + 1),
        out_specs=[ANY] * (NB + 4),
        scratch_shapes=[
            pltpu.VMEM((NB, rows, B), jnp.float32),
            pltpu.VMEM((NB, rows, B), jnp.float32),
            pltpu.VMEM((NB, W, B), jnp.float32),
            pltpu.VMEM((blocks, split, B), jnp.float32),
            pltpu.VMEM((blocks, B - split, B), jnp.float32),
            pltpu.SemaphoreType.DMA((NB + 4,)),
        ],
        compiler_params=pltpu.CompilerParams(vmem_limit_bytes=52 * 2**20),
        cost_estimate=pl.CostEstimate(flops=10**9, bytes_accessed=10 * 10**6, transcendentals=0),
        name="panel",
    )(info, tgt_a, tgt_b, panel, *panel_in, mt)

    def reduce(keep, send, steps):
        for n, (axis, mask) in enumerate(steps):
            got = swap(send, axis, mask)
            if n + 1 < len(steps):
                half = keep.shape[0] // 2
                send = keep[half:] + got[half:]
                keep = keep[:half] + got[:half]
            else:
                keep = keep + got
        return keep

    sum_a = reduce(keep_a, send_a, steps_a)
    sum_b = reduce(keep_b, send_b, steps_b)
    updated = ancestor - jnp.concatenate([sum_a, sum_b], axis=1)

    def give_back(parts):
        back = [parts[0]] + [swap(parts[m], "narrow", m) for m in masks]
        out = jnp.zeros((NB,) + parts[0].shape, jnp.float32)
        for m in range(NB):
            out = lax.dynamic_update_index_in_dim(out, back[m], me ^ m, 0)
        return out

    return (give_back(l_parts), give_back(x_parts), updated)


def solution(mesh):
    placed = (
        P("wide", None, "narrow"),
        P("wide", None, "narrow"),
        P("wide"),
        P("wide", None),
        P("wide"),
        P(("wide", "narrow"), None, None),
    )
    return jax.shard_map(
        functools.partial(local, 64),
        mesh=mesh,
        in_specs=placed,
        out_specs=(
            P("wide", None, "narrow"),
            P("wide", None, "narrow"),
            P(("wide", "narrow"), None, None),
        ),
        check_vma=False,
    )
```

time: 927 us -> 158 us (0.17)
  other arithmetic: 482 us -> 34.4 us
  waiting for transfers between devices: 249 us -> 79.9 us
  matrix products: 78.7 us -> 0 us
  local copies, waits for them, and re-layouts: 81 us -> 6.77 us
  starting transfers between devices: 12.7 us -> 35.9 us
  between operations: 14.5 us -> 0.89 us
    another operation x23 -> x1, other arithmetic: 474 us -> 0.62 us  [local(): info = jnp.stack([me, panel_count[me]]).astype(jnp.int32)]
    all_to_all x2 -> x0, waiting for transfers between devices: 205 us -> none  [the longest x1 205 us: local(): lax.all_to_all(send_buffer, 'wide', split_axis=0, concat_axis=0, tiled=True)]
    ppermute x0 -> x22, waiting for transfers between devices: none -> 79.9 us  [swap(): return lax.ppermute(x, axis, xor_pairs(lax.axis_size(axis), mask))]
    dot_general x3 -> x0, matrix products: 51 us -> none  [the longest x1 25.8 us: local(): jnp.einsum('spac,spbc->spab', blocks[:, first], blocks[:, second], precis...]
    ppermute x0 -> x22, starting transfers between devices: none -> 35.9 us  [swap(): return lax.ppermute(x, axis, xor_pairs(lax.axis_size(axis), mask))]
    pallas_call x0 -> x2, other arithmetic: none -> 32.3 us  [the longest x1 26.1 us: local(): pl.pallas_call(factor_kernel, out_shape=[slab] * NB + [jax.ShapeDtypeStru...]
    another operation x13 -> x0, matrix products: 27.7 us -> none  [the longest x7 15 us: local(): lax.linalg.triangular_solve(factor, identity, left_side=True, lower=True)]
    scatter x2 -> x0, local copies, waits for them, and re-layouts: 27.5 us -> none  [the longest x1 26.4 us: local(): jnp.zeros((buffer_rows, B, B), jnp.float32).at[position]]
  transfers between devices with their start and end apart: 5 -> 22, of which waited for: 3 -> 10; matrix products, arithmetic and copies ran while one was open for 68% -> 19% of each run, Pallas kernels for 0% -> 0%
where the time goes in v1:
time: 158 us
  waiting for transfers between devices  79.9 us (51%)
  starting transfers between devices  35.9 us (23%)
  other arithmetic  34.4 us (22%)
  local copies, waits for them, and re-layouts  6.77 us (4%)
    ppermute x22, waiting for transfers between devices, swap(): return lax.ppermute(x, axis, xor_pairs(lax.axis_size(axis), mask))  79.9 us
    ppermute x22, starting transfers between devices, swap(): return lax.ppermute(x, axis, xor_pairs(lax.axis_size(axis), mask))  35.9 us
    pallas_call x1, other arithmetic, local(): pl.pallas_call(factor_kernel, out_shape=[slab] * NB + [jax.ShapeDtypeStru...  26.1 us
    pallas_call x1, other arithmetic, local(): pl.pallas_call(panel_kernel, out_shape=[slab] * NB + [part_a, part_a, par...  6.26 us
    squeeze x2, local copies, waits for them, and re-layouts, local(): own = lambda x, m: lax.dynamic_index_in_dim(x, me ^ m, 0, keepdims=False)  4.48 us
  transfers between devices with their start and end apart: 22, of which 10 were waited for; matrix products, arithmetic and copies ran while one was open for 19% of the time, Pallas kernels for 0%

profile of v1, /device:TPU:0, one launch (start us, length us, event | category | flops | bytes accessed | tf_op | source)
XLA Modules:
  0.0 157.9 jit_solution(16214901131205520305)
XLA Ops:
  0.7 2.1 %dynamic-slice_bitcast_fusion.3 = (f32[512,128]{1,0:T(8,128)}, f32[512,128]{1,0:T(8,128)}, f32[512,128]{1,0:T(8,128)}) fusion(f32[4,512,128]{2,1,0:T(8,128)} %param.6, s32[]{:T(128)S(6)} %select_n.65, s32[]{:T(128)S(6)} %select_n.64, s32[]{:T(128)S(6)} %select_n.63), kind=kLoop, calls=%fused_computation.19 | loop fusion | bytes 1572876 | tf_op jit(solution)/shard_map/jit(dynamic_index_in_dim)/squeeze | solution.py:200
  2.7 2.4 %collective-permute-start.2 = (f32[512,128]{1,0:T(8,128)}, f32[512,128]{1,0:T(8,128)S(1)}, u32[]{:S(2)}, u32[]{:S(2)}) collective-permute-start(f32[512,128]{1,0:T(8,128)} %get-tuple-element.53), channel_id=1, source_target_pairs={{0,3},{1,2},{2,1},{3,0},{4,7},{5,6},{6,5},{7,4},{8,11},{9,10},{10,... | collective-permute-start | bytes 786440 | tf_op jit(solution)/shard_map/ppermute | solution.py:182
  5.1 2.4 %dynamic-slice_bitcast_fusion = (f32[1024,128]{1,0:T(8,128)}, f32[1024,128]{1,0:T(8,128)}, f32[1024,128]{1,0:T(8,128)S(1)}) fusion(f32[4,1024,128]{2,1,0:T(8,128)} %param.7, s32[]{:T(128)S(6)} %select_n.65, s32[]{:T(128)S(6)} %select_n.64, s32[]{:T(128)S(6)} %select_n.63), kind=kLoop, calls=%fused_computation.8 | loop fusion | bytes 3145740 | tf_op jit(solution)/shard_map/jit(dynamic_index_in_dim)/squeeze | solution.py:200
  7.5 0.1 collective-permute-start.8
  7.6 2.2 %collective-permute-start.7 = (f32[1024,128]{1,0:T(8,128)}, f32[1024,128]{1,0:T(8,128)S(1)}, u32[]{:S(2)}, u32[]{:S(2)}) collective-permute-start(f32[1024,128]{1,0:T(8,128)} %get-tuple-element.47), channel_id=1, source_target_pairs={{0,2},{1,3},{2,0},{3,1},{4,6},{5,7},{6,4},{7,5},{8,10},{9,11},{10,... | collective-permute-start | bytes 1572872 | tf_op jit(solution)/shard_map/ppermute | solution.py:182
  9.9 0.0 collective-permute-start.6
  9.9 0.2 collective-permute-start.1
  10.1 0.6 dynamic_slice.29
  10.6 0.1 multiply_add_fusion
  10.7 1.4 collective-permute-done.2
  12.1 1.0 collective-permute-start
  13.1 0.6 pad_add_fusion
  13.8 0.1 multiply_add_fusion.1
  13.9 26.5 %collective-permute-done.1 = f32[512,128]{1,0:T(8,128)} collective-permute-done((f32[512,128]{1,0:T(8,128)}, f32[512,128]{1,0:T(8,128)}, u32[]{:S(2)}, u32[]{:S(2)}) %collective-permute-start.1) | collective-permute-done | bytes 262176 | tf_op jit(solution)/shard_map/ppermute | solution.py:182
  40.4 0.1 broadcast_in_dim.32
  40.5 0.0 copy-start
  40.5 26.1 %factor.1 = (f32[4,512,128]{2,1,0:T(8,128)S(1)}, f32[512,128]{1,0:T(8,128)}, f32[512,128]{1,0:T(8,128)}, f32[512,128]{1,0:T(8,128)}, f32[4,512,128]{2,1,0:T(8,128)S(1)}) fusion(f32[4,512,128]{2,1,0:T(8,128)S(1)} %broadcast_in_dim.32, s32[]{:T(128)S(6)} %select_n.62, s32[2]{0:T(128)S(1)} %pad_add_fusion, f32[4,512,128]{2,1,0:T(8,128)S(1)} %copy-done.1, ...), kind=kCustom, calls=%fused_computation.18 | custom fusion | flops 200000000 | bytes 3932676 | tf_op jit(solution)/shard_map/factor/pallas_call | solution.py:215
  66.6 0.0 collective-permute-done.7
  66.6 0.0 collective-permute-done.6
  66.6 0.0 copy-start.4
  66.6 0.8 copy-done.4
  67.4 0.1 broadcast_in_dim.37
  67.6 6.3 %panel.1 = (f32[4,1024,128]{2,1,0:T(8,128)S(1)}, f32[1024,128]{1,0:T(8,128)}, f32[1024,128]{1,0:T(8,128)}, f32[1024,128]{1,0:T(8,128)S(1)}, f32[32,64,128]{2,1,0...) fusion(f32[4,1024,128]{2,1,0:T(8,128)S(1)} %broadcast_in_dim.37, ...), kind=kCustom, calls=%fused_computation.7 | custom fusion | flops 1000000000 | bytes 11011588 | tf_op jit(solution)/shard_map/panel/pallas_call | solution.py:231
  73.8 3.5 %collective-permute-start.12 = (f32[32,64,128]{2,1,0:T(8,128)S(1)}, f32[32,64,128]{2,1,0:T(8,128)S(1)}, u32[]{:S(2)}, u32[]{:S(2)}) collective-permute-start(f32[32,64,128]{2,1,0:T(8,128)S(1)} %get-tuple-element.71), channel_id=1, source_target_pairs={{0,1},{1,0},{2,3},{3,2},{4,5},{5,4},{6,7},{7,6},{8,9},{9,8},{10,11... | collective-permute-start | bytes 3145736 | tf_op jit(solution)/shard_map/ppermute | solution.py:182
  77.3 0.1 collective-permute-start.3
  77.4 0.4 collective-permute-start.17
  77.8 9.3 %collective-permute-start.4 = (f32[512,128]{1,0:T(8,128)}, f32[512,128]{1,0:T(8,128)S(1)}, u32[]{:S(2)}, u32[]{:S(2)}) collective-permute-start(f32[512,128]{1,0:T(8,128)} %get-tuple-element.34), channel_id=1, source_target_pairs={{0,2},{1,3},{2,0},{3,1},{4,6},{5,7},{6,4},{7,5},{8,10},{9,11},{10,... | collective-permute-start | bytes 786440 | tf_op jit(solution)/shard_map/ppermute | solution.py:182
  87.1 0.1 collective-permute-start.5
  87.2 0.0 collective-permute-done.3
  87.2 0.2 collective-permute-start.9
  87.4 7.1 %collective-permute-done.4 = f32[512,128]{1,0:T(8,128)S(1)} collective-permute-done((f32[512,128]{1,0:T(8,128)}, f32[512,128]{1,0:T(8,128)S(1)}, u32[]{:S(2)}, u32[]{:S(2)}) %collective-permute-start.4) | collective-permute-done | bytes 262176 | tf_op jit(solution)/shard_map/ppermute | solution.py:182
  94.5 2.0 %collective-permute-start.10 = (f32[1024,128]{1,0:T(8,128)}, f32[1024,128]{1,0:T(8,128)S(1)}, u32[]{:S(2)}, u32[]{:S(2)}) collective-permute-start(f32[1024,128]{1,0:T(8,128)} %get-tuple-element.65), channel_id=1, source_target_pairs={{0,2},{1,3},{2,0},{3,1},{4,6},{5,7},{6,4},{7,5},{8,10},{9,11},{10,... | collective-permute-start | bytes 1572872 | tf_op jit(solution)/shard_map/ppermute | solution.py:182
  96.4 3.1 %collective-permute-done.5 = f32[512,128]{1,0:T(8,128)S(1)} collective-permute-done((f32[512,128]{1,0:T(8,128)S(1)}, f32[512,128]{1,0:T(8,128)S(1)}, u32[]{:S(2)}, u32[]{:S(2)}) %collective-permute-start.5) | collective-permute-done | bytes 262176 | tf_op jit(solution)/shard_map/ppermute | solution.py:182
  99.6 1.9 %collective-permute-start.11 = (f32[1024,128]{1,0:T(8,128)S(1)}, f32[1024,128]{1,0:T(8,128)S(1)}, u32[]{:S(2)}, u32[]{:S(2)}) collective-permute-start(f32[1024,128]{1,0:T(8,128)S(1)} %get-tuple-element.67), channel_id=1, source_target_pairs={{0,3},{1,2},{2,1},{3,0},{4,7},{5,6},{6,5},{7,4},{8,11},{9,10},{10,... | collective-permute-start | bytes 1572872 | tf_op jit(solution)/shard_map/ppermute | solution.py:182
  101.5 0.0 copy-start.3
  101.5 0.0 collective-permute-done.12
  101.5 0.1 slice_add_fusion.3
  101.7 0.1 collective-permute-start.13
  101.8 0.0 collective-permute-done.17
  101.8 0.1 slice_add_fusion.1
  101.9 0.5 copy-done.3
  102.5 1.5 collective-permute-start.18
  104.0 0.0 collective-permute-done.9
  104.0 7.3 %collective-permute-done.10 = f32[1024,128]{1,0:T(8,128)S(1)} collective-permute-done((f32[1024,128]{1,0:T(8,128)}, f32[1024,128]{1,0:T(8,128)S(1)}, u32[]{:S(2)}, u32[]{:S(2)}) %collective-permute-start.10) | collective-permute-done | bytes 524320 | tf_op jit(solution)/shard_map/ppermute | solution.py:182
  111.4 22.2 %collective-permute-done.13 = f32[16,64,128]{2,1,0:T(8,128)S(1)} collective-permute-done((f32[16,64,128]{2,1,0:T(8,128)S(1)}, f32[16,64,128]{2,1,0:T(8,128)S(1)}, u32[]{:S(2)}, u32[]{:S(2)}) %collective-permute-start.13) | collective-permute-done | bytes 524320 | tf_op jit(solution)/shard_map/ppermute | solution.py:182
  133.5 0.1 slice_add_fusion.7
  133.6 1.9 %collective-permute-start.14 = (f32[8,64,128]{2,1,0:T(8,128)S(1)}, f32[8,64,128]{2,1,0:T(8,128)S(1)}, u32[]{:S(2)}, u32[]{:S(2)}) collective-permute-start(f32[8,64,128]{2,1,0:T(8,128)S(1)} %get-tuple-element.50), channel_id=1, source_target_pairs={{0,4},{4,0},{8,12},{12,8},{16,20},{20,16},{24,28},{28,24},{1,5},{5... | collective-permute-start | bytes 786440 | tf_op jit(solution)/shard_map/ppermute | solution.py:182
  135.5 0.0 collective-permute-done.18
  135.5 0.1 slice_add_fusion.5
  135.5 0.0 copy-start.6
  135.6 1.4 collective-permute-start.19
  136.9 0.0 collective-permute-done.11
  137.0 0.0 copy-start.2
  137.0 4.7 %collective-permute-done.14 = f32[8,64,128]{2,1,0:T(8,128)S(1)} collective-permute-done((f32[8,64,128]{2,1,0:T(8,128)S(1)}, f32[8,64,128]{2,1,0:T(8,128)S(1)}, u32[]{:S(2)}, u32[]{:S(2)}) %collective-permute-start.14) | collective-permute-done | bytes 262176 | tf_op jit(solution)/shard_map/ppermute | solution.py:182
  141.8 1.4 collective-permute-start.15
  143.2 0.0 collective-permute-done.19
  143.2 2.9 %collective-permute-start.20 = (f32[4,64,128]{2,1,0:T(8,128)S(1)}, f32[4,64,128]{2,1,0:T(8,128)S(1)}, u32[]{:S(2)}, u32[]{:S(2)}) collective-permute-start(f32[4,64,128]{2,1,0:T(8,128)S(1)} %get-tuple-element.59), channel_id=1, source_target_pairs={{0,16},{4,20},{8,24},{12,28},{16,0},{20,4},{24,8},{28,12},{1,17},{... | collective-permute-start | bytes 393224 | tf_op jit(solution)/shard_map/ppermute | solution.py:182
  146.2 2.0 %collective-permute-done.15 = f32[4,64,128]{2,1,0:T(8,128)S(1)} collective-permute-done((f32[4,64,128]{2,1,0:T(8,128)S(1)}, f32[4,64,128]{2,1,0:T(8,128)S(1)}, u32[]{:S(2)}, u32[]{:S(2)}) %collective-permute-start.15) | collective-permute-done | bytes 131104 | tf_op jit(solution)/shard_map/ppermute | solution.py:182
  148.2 2.0 %collective-permute-start.16 = (f32[2,64,128]{2,1,0:T(8,128)S(1)}, f32[2,64,128]{2,1,0:T(8,128)S(1)}, u32[]{:S(2)}, u32[]{:S(2)}) collective-permute-start(f32[2,64,128]{2,1,0:T(8,128)S(1)} %slice_add_fusion.14), channel_id=1, source_target_pairs={{0,16},{4,20},{8,24},{12,28},{16,0},{20,4},{24,8},{28,12},{1,17},{... | collective-permute-start | bytes 196616 | tf_op jit(solution)/shard_map/ppermute | solution.py:182
  150.2 2.6 %collective-permute-done.20 = f32[4,64,128]{2,1,0:T(8,128)S(1)} collective-permute-done((f32[4,64,128]{2,1,0:T(8,128)S(1)}, f32[4,64,128]{2,1,0:T(8,128)S(1)}, u32[]{:S(2)}, u32[]{:S(2)}) %collective-permute-start.20) | collective-permute-done | bytes 131104 | tf_op jit(solution)/shard_map/ppermute | solution.py:182
  152.9 1.4 collective-permute-start.21
  154.3 0.0 collective-permute-done.16
  154.3 2.9 %collective-permute-done.21 = f32[2,64,128]{2,1,0:T(8,128)S(1)} collective-permute-done((f32[2,64,128]{2,1,0:T(8,128)S(1)}, f32[2,64,128]{2,1,0:T(8,128)S(1)}, u32[]{:S(2)}, u32[]{:S(2)}) %collective-permute-start.21) | collective-permute-done | bytes 65568 | tf_op jit(solution)/shard_map/ppermute | solution.py:182
  157.2 0.7 maximum_subtract_fusion
  (27 shorter events, 0.3 us)
Async XLA Ops:
  0.7 9.4 %copy-start.9 = (s32[4]{0:T(128)S(1)}, s32[4]{0:T(128)}, u32[]{:S(2)}) copy-start(s32[4]{0:T(128)} %param.8) | copy-start | bytes 52
  0.7 10.0 %copy-start.7 = (s32[144,1]{0,1:T(1,128)S(1)}, s32[144,1]{0,1:T(1,128)}, u32[]{:S(2)}) copy-start(s32[144,1]{0,1:T(1,128)} %param.9) | copy-start | bytes 1732
  0.7 10.0 %copy-start.8 = (s32[144]{0:T(256)S(1)}, s32[144]{0:T(256)}, u32[]{:S(2)}) copy-start(s32[144]{0:T(256)} %param.10) | copy-start | bytes 1732
  2.7 37.7 %copy-start.1 = (f32[4,512,128]{2,1,0:T(8,128)S(1)}, f32[4,512,128]{2,1,0:T(8,128)}, u32[]{:S(2)}) copy-start(f32[4,512,128]{2,1,0:T(8,128)} %param.6) | copy-start | bytes 3145732
  2.7 9.4 %collective-permute-start.2 = (f32[512,128]{1,0:T(8,128)}, f32[512,128]{1,0:T(8,128)S(1)}, u32[]{:S(2)}, u32[]{:S(2)}) collective-permute-start(f32[512,128]{1,0:T(8,128)} %get-tuple-element.53), channel_id=1, source_target_pairs={{0,3},{1,2},{2,1},{3,0},{4,7},{5,6},{6,5},{7,4},{8,11},{9,10},{10,... | collective-permute-start | bytes 786440 | tf_op jit(solution)/shard_map/ppermute | solution.py:182
  7.5 59.0 %collective-permute-start.8 = (f32[1024,128]{1,0:T(8,128)}, f32[1024,128]{1,0:T(8,128)S(1)}, u32[]{:S(2)}, u32[]{:S(2)}) collective-permute-start(f32[1024,128]{1,0:T(8,128)} %get-tuple-element.46), channel_id=1, source_target_pairs={{0,3},{1,2},{2,1},{3,0},{4,7},{5,6},{6,5},{7,4},{8,11},{9,10},{10,... | collective-permute-start | bytes 1572872 | tf_op jit(solution)/shard_map/ppermute | solution.py:182
  7.6 59.0 %collective-permute-start.7 = (f32[1024,128]{1,0:T(8,128)}, f32[1024,128]{1,0:T(8,128)S(1)}, u32[]{:S(2)}, u32[]{:S(2)}) collective-permute-start(f32[1024,128]{1,0:T(8,128)} %get-tuple-element.47), channel_id=1, source_target_pairs={{0,2},{1,3},{2,0},{3,1},{4,6},{5,7},{6,4},{7,5},{8,10},{9,11},{10,... | collective-permute-start | bytes 1572872 | tf_op jit(solution)/shard_map/ppermute | solution.py:182
  9.9 56.8 %collective-permute-start.6 = (f32[1024,128]{1,0:T(8,128)S(1)}, f32[1024,128]{1,0:T(8,128)S(1)}, u32[]{:S(2)}, u32[]{:S(2)}) collective-permute-start(f32[1024,128]{1,0:T(8,128)S(1)} %get-tuple-element.48), channel_id=1, source_target_pairs={{0,1},{1,0},{2,3},{3,2},{4,5},{5,4},{6,7},{7,6},{8,9},{9,8},{10,11... | collective-permute-start | bytes 1572872 | tf_op jit(solution)/shard_map/ppermute | solution.py:182
  9.9 30.5 %collective-permute-start.1 = (f32[512,128]{1,0:T(8,128)}, f32[512,128]{1,0:T(8,128)}, u32[]{:S(2)}, u32[]{:S(2)}) collective-permute-start(f32[512,128]{1,0:T(8,128)} %get-tuple-element.54), channel_id=1, source_target_pairs={{0,2},{1,3},{2,0},{3,1},{4,6},{5,7},{6,4},{7,5},{8,10},{9,11},{10,... | collective-permute-start | bytes 786440 | tf_op jit(solution)/shard_map/ppermute | solution.py:182
  12.1 28.3 %collective-permute-start = (f32[512,128]{1,0:T(8,128)}, f32[512,128]{1,0:T(8,128)S(1)}, u32[]{:S(2)}, u32[]{:S(2)}) collective-permute-start(f32[512,128]{1,0:T(8,128)} %get-tuple-element.55), channel_id=1, source_target_pairs={{0,1},{1,0},{2,3},{3,2},{4,5},{5,4},{6,7},{7,6},{8,9},{9,8},{10,11... | collective-permute-start | bytes 786440 | tf_op jit(solution)/shard_map/ppermute | solution.py:182
  40.5 27.1 %copy-start = (f32[4,1024,128]{2,1,0:T(8,128)S(1)}, f32[4,1024,128]{2,1,0:T(8,128)}, u32[]{:S(2)}) copy-start(f32[4,1024,128]{2,1,0:T(8,128)} %param.7) | copy-start | bytes 6291460
  66.6 0.8 copy-start.4
  67.6 19.5 %copy-start.5 = (f32[512,128]{1,0:T(8,128)S(1)}, f32[512,128]{1,0:T(8,128)}, u32[]{:S(2)}) copy-start(f32[512,128]{1,0:T(8,128)} %get-tuple-element.36) | copy-start | bytes 786436
  73.8 27.7 %collective-permute-start.12 = (f32[32,64,128]{2,1,0:T(8,128)S(1)}, f32[32,64,128]{2,1,0:T(8,128)S(1)}, u32[]{:S(2)}, u32[]{:S(2)}) collective-permute-start(f32[32,64,128]{2,1,0:T(8,128)S(1)} %get-tuple-element.71), channel_id=1, source_target_pairs={{0,1},{1,0},{2,3},{3,2},{4,5},{5,4},{6,7},{7,6},{8,9},{9,8},{10,11... | collective-permute-start | bytes 3145736 | tf_op jit(solution)/shard_map/ppermute | solution.py:182
  77.3 9.8 %collective-permute-start.3 = (f32[512,128]{1,0:T(8,128)}, f32[512,128]{1,0:T(8,128)S(1)}, u32[]{:S(2)}, u32[]{:S(2)}) collective-permute-start(f32[512,128]{1,0:T(8,128)} %get-tuple-element.32), channel_id=1, source_target_pairs={{0,1},{1,0},{2,3},{3,2},{4,5},{5,4},{6,7},{7,6},{8,9},{9,8},{10,11... | collective-permute-start | bytes 786440 | tf_op jit(solution)/shard_map/ppermute | solution.py:182
  77.4 24.4 %collective-permute-start.17 = (f32[32,64,128]{2,1,0:T(8,128)S(1)}, f32[32,64,128]{2,1,0:T(8,128)S(1)}, u32[]{:S(2)}, u32[]{:S(2)}) collective-permute-start(f32[32,64,128]{2,1,0:T(8,128)S(1)} %get-tuple-element.75), channel_id=1, source_target_pairs={{0,1},{1,0},{2,3},{3,2},{4,5},{5,4},{6,7},{7,6},{8,9},{9,8},{10,11... | collective-permute-start | bytes 3145736 | tf_op jit(solution)/shard_map/ppermute | solution.py:182
  77.8 16.6 %collective-permute-start.4 = (f32[512,128]{1,0:T(8,128)}, f32[512,128]{1,0:T(8,128)S(1)}, u32[]{:S(2)}, u32[]{:S(2)}) collective-permute-start(f32[512,128]{1,0:T(8,128)} %get-tuple-element.34), channel_id=1, source_target_pairs={{0,2},{1,3},{2,0},{3,1},{4,6},{5,7},{6,4},{7,5},{8,10},{9,11},{10,... | collective-permute-start | bytes 786440 | tf_op jit(solution)/shard_map/ppermute | solution.py:182
  87.1 12.5 %collective-permute-start.5 = (f32[512,128]{1,0:T(8,128)S(1)}, f32[512,128]{1,0:T(8,128)S(1)}, u32[]{:S(2)}, u32[]{:S(2)}) collective-permute-start(f32[512,128]{1,0:T(8,128)S(1)} %copy-done.5), channel_id=1, source_target_pairs={{0,3},{1,2},{2,1},{3,0},{4,7},{5,6},{6,5},{7,4},{8,11},{9,10},{10,... | collective-permute-start | bytes 786440 | tf_op jit(solution)/shard_map/ppermute | solution.py:182
  87.2 16.8 %collective-permute-start.9 = (f32[1024,128]{1,0:T(8,128)}, f32[1024,128]{1,0:T(8,128)S(1)}, u32[]{:S(2)}, u32[]{:S(2)}) collective-permute-start(f32[1024,128]{1,0:T(8,128)} %get-tuple-element.63), channel_id=1, source_target_pairs={{0,1},{1,0},{2,3},{3,2},{4,5},{5,4},{6,7},{7,6},{8,9},{9,8},{10,11... | collective-permute-start | bytes 1572872 | tf_op jit(solution)/shard_map/ppermute | solution.py:182
  94.5 16.9 %collective-permute-start.10 = (f32[1024,128]{1,0:T(8,128)}, f32[1024,128]{1,0:T(8,128)S(1)}, u32[]{:S(2)}, u32[]{:S(2)}) collective-permute-start(f32[1024,128]{1,0:T(8,128)} %get-tuple-element.65), channel_id=1, source_target_pairs={{0,2},{1,3},{2,0},{3,1},{4,6},{5,7},{6,4},{7,5},{8,10},{9,11},{10,... | collective-permute-start | bytes 1572872 | tf_op jit(solution)/shard_map/ppermute | solution.py:182
  99.6 37.4 %collective-permute-start.11 = (f32[1024,128]{1,0:T(8,128)S(1)}, f32[1024,128]{1,0:T(8,128)S(1)}, u32[]{:S(2)}, u32[]{:S(2)}) collective-permute-start(f32[1024,128]{1,0:T(8,128)S(1)} %get-tuple-element.67), channel_id=1, source_target_pairs={{0,3},{1,2},{2,1},{3,0},{4,7},{5,6},{6,5},{7,4},{8,11},{9,10},{10,... | collective-permute-start | bytes 1572872 | tf_op jit(solution)/shard_map/ppermute | solution.py:182
  101.5 1.0 copy-start.3
  101.7 31.9 %collective-permute-start.13 = (f32[16,64,128]{2,1,0:T(8,128)S(1)}, f32[16,64,128]{2,1,0:T(8,128)S(1)}, u32[]{:S(2)}, u32[]{:S(2)}) collective-permute-start(f32[16,64,128]{2,1,0:T(8,128)S(1)} %get-tuple-element.43), channel_id=1, source_target_pairs={{0,2},{1,3},{2,0},{3,1},{4,6},{5,7},{6,4},{7,5},{8,10},{9,11},{10,... | collective-permute-start | bytes 1572872 | tf_op jit(solution)/shard_map/ppermute | solution.py:182
  102.5 33.0 %collective-permute-start.18 = (f32[16,64,128]{2,1,0:T(8,128)S(1)}, f32[16,64,128]{2,1,0:T(8,128)S(1)}, u32[]{:S(2)}, u32[]{:S(2)}) collective-permute-start(f32[16,64,128]{2,1,0:T(8,128)S(1)} %get-tuple-element.45), channel_id=1, source_target_pairs={{0,4},{4,0},{8,12},{12,8},{16,20},{20,16},{24,28},{28,24},{1,5},{5... | collective-permute-start | bytes 1572872 | tf_op jit(solution)/shard_map/ppermute | solution.py:182
  133.6 8.1 %collective-permute-start.14 = (f32[8,64,128]{2,1,0:T(8,128)S(1)}, f32[8,64,128]{2,1,0:T(8,128)S(1)}, u32[]{:S(2)}, u32[]{:S(2)}) collective-permute-start(f32[8,64,128]{2,1,0:T(8,128)S(1)} %get-tuple-element.50), channel_id=1, source_target_pairs={{0,4},{4,0},{8,12},{12,8},{16,20},{20,16},{24,28},{28,24},{1,5},{5... | collective-permute-start | bytes 786440 | tf_op jit(solution)/shard_map/ppermute | solution.py:182
  135.5 21.7 %copy-start.6 = (f32[2,128,128]{2,1,0:T(8,128)S(1)}, f32[2,128,128]{2,1,0:T(8,128)}, u32[]{:S(2)}) copy-start(f32[2,128,128]{2,1,0:T(8,128)} %param.11) | copy-start | bytes 393220
  135.6 7.7 %collective-permute-start.19 = (f32[8,64,128]{2,1,0:T(8,128)S(1)}, f32[8,64,128]{2,1,0:T(8,128)S(1)}, u32[]{:S(2)}, u32[]{:S(2)}) collective-permute-start(f32[8,64,128]{2,1,0:T(8,128)S(1)} %get-tuple-element.52), channel_id=1, source_target_pairs={{0,8},{4,12},{8,0},{12,4},{16,24},{20,28},{24,16},{28,20},{1,9},{5... | collective-permute-start | bytes 786440 | tf_op jit(solution)/shard_map/ppermute | solution.py:182
  137.0 20.9 %copy-start.2 = (f32[4,1024,128]{2,1,0:T(8,128)}, f32[4,1024,128]{2,1,0:T(8,128)S(1)}, u32[]{:S(2)}) copy-start(f32[4,1024,128]{2,1,0:T(8,128)S(1)} %bitcast_dynamic-update-slice_fusion) | copy-start | bytes 6291460
  141.8 6.4 %collective-permute-start.15 = (f32[4,64,128]{2,1,0:T(8,128)S(1)}, f32[4,64,128]{2,1,0:T(8,128)S(1)}, u32[]{:S(2)}, u32[]{:S(2)}) collective-permute-start(f32[4,64,128]{2,1,0:T(8,128)S(1)} %get-tuple-element.57), channel_id=1, source_target_pairs={{0,8},{4,12},{8,0},{12,4},{16,24},{20,28},{24,16},{28,20},{1,9},{5... | collective-permute-start | bytes 393224 | tf_op jit(solution)/shard_map/ppermute | solution.py:182
  143.2 9.6 %collective-permute-start.20 = (f32[4,64,128]{2,1,0:T(8,128)S(1)}, f32[4,64,128]{2,1,0:T(8,128)S(1)}, u32[]{:S(2)}, u32[]{:S(2)}) collective-permute-start(f32[4,64,128]{2,1,0:T(8,128)S(1)} %get-tuple-element.59), channel_id=1, source_target_pairs={{0,16},{4,20},{8,24},{12,28},{16,0},{20,4},{24,8},{28,12},{1,17},{... | collective-permute-start | bytes 393224 | tf_op jit(solution)/shard_map/ppermute | solution.py:182
  148.2 6.1 %collective-permute-start.16 = (f32[2,64,128]{2,1,0:T(8,128)S(1)}, f32[2,64,128]{2,1,0:T(8,128)S(1)}, u32[]{:S(2)}, u32[]{:S(2)}) collective-permute-start(f32[2,64,128]{2,1,0:T(8,128)S(1)} %slice_add_fusion.14), channel_id=1, source_target_pairs={{0,16},{4,20},{8,24},{12,28},{16,0},{20,4},{24,8},{28,12},{1,17},{... | collective-permute-start | bytes 196616 | tf_op jit(solution)/shard_map/ppermute | solution.py:182
  152.9 4.3 %collective-permute-start.21 = (f32[2,64,128]{2,1,0:T(8,128)S(1)}, f32[2,64,128]{2,1,0:T(8,128)S(1)}, u32[]{:S(2)}, u32[]{:S(2)}) collective-permute-start(f32[2,64,128]{2,1,0:T(8,128)S(1)} %slice_add_fusion.12), channel_id=1, source_target_pairs={{0,2},{1,3},{2,0},{3,1},{4,6},{5,7},{6,4},{7,5},{8,10},{9,11},{10,... | collective-permute-start | bytes 196616 | tf_op jit(solution)/shard_map/ppermute | solution.py:182

commit v2 on v1

--- a/solution.py
+++ b/solution.py
@@ -40,44 +40,98 @@
 def inverse_factor(block):
     sub = lax.broadcasted_iota(jnp.int32, (8, B), 0)
     lane = lax.broadcasted_iota(jnp.int32, (8, B), 1)
-    rows = [block[8 * q : 8 * q + 8, :] for q in range(B // 8)]
-    done = []
-    for p in range(B // 8):
-        lo = 8 * p
-        own = (lane >= lo) & (lane < lo + 8)
-        cols = [lane_of(rows[p], lo + m) for m in range(8)]
-        work = jnp.where(own, (lane - lo == sub).astype(jnp.float32), rows[p])
-        final = jnp.zeros((8, B), jnp.float32)
-        for k in range(8):
-            pivot = row_of(cols[k], k)
-            recip = 1.0 / pivot
-            raw = row_of(work, k)
-            final = jnp.where(sub == k, raw * lax.rsqrt(pivot), final)
-            factor = cols[k]
-            scaled = raw * recip
-            work = jnp.where(sub == k, scaled, work - factor * scaled)
-            for m in range(k + 1, 8):
-                line = row_of(cols[m], k) * recip
-                cols[m] = jnp.where(sub == k, line, cols[m] - factor * line)
-        done.append(jnp.where(lane <= sub + lo, final, 0.0))
-        lines = [row_of(work, m) for m in range(8)]
-        for q in range(p + 1, B // 8):
-            mult = [lane_of(rows[q], lo + m) for m in range(8)]
-            new = jnp.where(own, 0.0, rows[q])
-            for m in range(8):
-                new = new - mult[m] * lines[m]
-            rows[q] = new
+    total, strip = B // 8, 2
+    rows = [block[8 * q : 8 * q + 8, :] for q in range(total)]
+    done = [None] * total
+    for b in range(0, total, strip):
+        mine = range(b, b + strip)
+        near = range(b + strip, min(b + 2 * strip, total))
+        far = range(b + 2 * strip, total)
+        in_strip = (lane >= 8 * b) & (lane < 8 * (b + strip))
+        ahead = {q: [lane_of(rows[q], 8 * b + m) for m in range(8 * strip)] for q in near}
+        for p in mine:
+            lo = 8 * p
+            own = (lane >= lo) & (lane < lo + 8)
+            cols = [lane_of(rows[p], lo + m) for m in range(8)]
+            others = [q for q in mine if q != p]
+            mult = {q: [lane_of(rows[q], lo + m) for m in range(8)] for q in others}
+            work = jnp.where(own, (lane - lo == sub).astype(jnp.float32), rows[p])
+            final = jnp.zeros((8, B), jnp.float32)
+            for k in range(0, 8, 2):
+                f0, f1 = cols[k], cols[k + 1]
+                a, h, c = row_of(f0, k), row_of(f0, k + 1), row_of(f1, k + 1)
+                det = a * c - h * h
+                recip = 1.0 / det
+                ar, hr, cr = a * recip, h * recip, c * recip
+                first, second = sub == k, sub == k + 1
+
+                def eliminate(v):
+                    r0, r1 = row_of(v, k), row_of(v, k + 1)
+                    s0, s1 = cr * r0 - hr * r1, ar * r1 - hr * r0
+                    return r0, r1, jnp.where(first, s0, jnp.where(second, s1, v - f0 * s0 - f1 * s1))
+
+                for m in range(k + 2, 8):
+                    cols[m] = eliminate(cols[m])[2]
+                r0, r1, work = eliminate(work)
+                root = lax.rsqrt(a)
+                lower = (a * r1 - h * r0) * (root * lax.rsqrt(det))
+                final = jnp.where(first, r0 * root, jnp.where(second, lower, final))
+            done[p] = jnp.where(lane <= sub + lo, final, 0.0)
+            rows[p] = work
+            lines = [row_of(work, m) for m in range(8)]
+            for q in others:
+                new = jnp.where(own, 0.0, rows[q])
+                for m in range(8):
+                    new = new - mult[q][m] * lines[m]
+                rows[q] = new
+        lines = [row_of(rows[q], m) for q in mine for m in range(8)]
+        for q in near:
+            parts = [ahead[q][m] * lines[m] for m in range(4)]
+            for m in range(4, 8 * strip):
+                parts[m % 4] = parts[m % 4] + ahead[q][m] * lines[m]
+            rows[q] = jnp.where(in_strip, 0.0, rows[q]) - ((parts[0] + parts[1]) + (parts[2] + parts[3]))
+        if far:
+            stack = jnp.concatenate([rows[q] for q in far], axis=0)
+            lane_far = lax.broadcasted_iota(jnp.int32, stack.shape, 1)
+            in_far = (lane_far >= 8 * b) & (lane_far < 8 * (b + strip))
+            zero = jnp.zeros((8, B), jnp.float32)
+            tall = jnp.concatenate([rows[q] if q in mine else zero for q in range(total)], axis=0)
+            stack = jnp.where(in_far, 0.0, stack) - dot_nn(jnp.where(in_far, stack, 0.0), tall)
+            for n, q in enumerate(far):
+                rows[q] = stack[8 * n : 8 * n + 8]
     return jnp.concatenate(done, axis=0)
+
+
+def split_bf16(v):
+    high = v.astype(jnp.bfloat16)
+    return high, (v - high.astype(jnp.float32)).astype(jnp.bfloat16)
+
+
+def dot3(left, right, contract):
+    dot = lambda a, b: lax.dot_general(
+        a, b, (contract, ((), ())), preferred_element_type=jnp.float32
+    )
+    return dot(left[0], right[0]) + (dot(left[0], right[1]) + dot(left[1], right[0]))
 
 
 def factor_kernel(info, own_ref, r1, r2, r3, l0, l1, l2, l3, inv_out, a, l, mt, sems):
     me = info[0]
+    side = me // 2
+    far_rows = pl.ds((1 - side) * (W // 2), W // 2)
+    places = [a.at[me], a.at[me ^ 1], a.at[me ^ 2, far_rows], a.at[me ^ 3, far_rows]]
     ins = [own_ref.at[me], r1, r2, r3]
-    copies = [pltpu.make_async_copy(ins[m], a.at[me ^ m], sems.at[m]) for m in range(NB)]
+    copies = [pltpu.make_async_copy(ins[m], places[m], sems.at[m]) for m in range(NB)]
     for c in copies:
         c.start()
     for c in copies:
         c.wait()
+
+    @pl.when(side == 1)
+    def _():
+        for j in range(NB // 2):
+            for i in range(NB // 2, NB):
+                a[j, pl.ds(i * B, B), :] = a[i, pl.ds(j * B, B), :].T
+
     row = lax.broadcasted_iota(jnp.int32, (B, B), 0)
     col = lax.broadcasted_iota(jnp.int32, (B, B), 1)
     l[...] = jnp.zeros_like(l)
@@ -108,7 +162,7 @@
 
 
 def panel_kernel(info, tgt_a, tgt_b, own_ref, r1, r2, r3, mt_ref, *rest):
-    (x0, x1, x2, x3, keep_a, send_a, keep_b, send_b, p, x, mt, ta, tb, sems) = rest
+    (x0, x1, x2, x3, keep_a, send_a, keep_b, send_b, p, x, mt, xh, xl, ta, tb, sems) = rest
     me = info[0]
     count = info[1]
     ins = [own_ref.at[me], r1, r2, r3]
@@ -120,38 +174,41 @@
     tb[...] = jnp.zeros_like(tb)
     for c in copies:
         c.wait()
-    for i in range(P_SIZE):
-        here = pl.ds(i * B, B)
-
-        @pl.when(i < count)
-        def _():
-            for c in range(NB):
-                left = jnp.concatenate([p[j, here, :] for j in range(c + 1)], axis=1)
-                x[c, here, :] = dot_nn(left, mt[c, pl.ds(0, (c + 1) * B), :])
-
-        @pl.when(i >= count)
-        def _():
-            for c in range(NB):
-                x[c, here, :] = jnp.zeros((B, B), jnp.float32)
+    rows = P_SIZE * B
+    live = lax.broadcasted_iota(jnp.int32, (rows, B), 0) < count * B
+    parts = [split_bf16(jnp.where(live, p[c], 0.0)) for c in range(NB)]
+    for c in range(0, NB, 2):
+        left = [jnp.concatenate([parts[j][n] for j in range(c + 2)], axis=1) for n in range(2)]
+        right = split_bf16(
+            jnp.concatenate([mt[c, pl.ds(0, (c + 2) * B), :], mt[c + 1, pl.ds(0, (c + 2) * B), :]], axis=1)
+        )
+        got = dot3(left, right, ((1,), (0,)))
+        x[c] = got[:, :B]
+        x[c + 1] = got[:, B:]
+        high, low = split_bf16(got)
+        xh[:, pl.ds(c * B, 2 * B)] = high
+        xl[:, pl.ds(c * B, 2 * B)] = low
 
     outs = [x0, x1, x2, x3]
     copies = [pltpu.make_async_copy(x.at[me ^ m], outs[m], sems.at[m]) for m in range(NB)]
     for c in copies:
         c.start()
     half_a = ta.shape[1]
-    for i in range(P_SIZE):
-
-        @pl.when(i < count)
+    for j in range(0, P_SIZE, 2):
+
+        @pl.when(j < count)
         def _():
-            left = jnp.concatenate([x[c, pl.ds(i * B, B), :] for c in range(NB)], axis=1)
-            for j in range(i + 1):
-                right = jnp.concatenate([x[c, pl.ds(j * B, B), :] for c in range(NB)], axis=1)
-                got = dot_nt(left, right)
-                pair = i * (i + 1) // 2 + j
-                at_a = tgt_a[pair]
-                at_b = tgt_b[pair]
-                ta[at_a] += got[:half_a]
-                tb[at_b] += got[half_a:]
+            left = (xh[pl.ds(j * B, rows - j * B), :], xl[pl.ds(j * B, rows - j * B), :])
+            right = (xh[pl.ds(j * B, 2 * B), :], xl[pl.ds(j * B, 2 * B), :])
+            got = dot3(left, right, ((1,), (1,)))
+            for i in range(j, P_SIZE):
+                for n in range(2 if i > j else 1):
+                    block = got[(i - j) * B : (i - j + 1) * B, n * B : (n + 1) * B]
+                    pair = i * (i + 1) // 2 + j + n
+                    at_a = tgt_a[pair]
+                    at_b = tgt_b[pair]
+                    ta[at_a] += block[:half_a]
+                    tb[at_b] += block[half_a:]
 
     half = ta.shape[0] // 2
     more = [
@@ -198,13 +255,17 @@
     assert narrow_count == NB and diag_block.shape[0] == NB
     masks = range(1, NB)
     own = lambda x, m: lax.dynamic_index_in_dim(x, me ^ m, 0, keepdims=False)
-    diag_in = [swap(own(diag_block, m), "narrow", m) for m in masks]
+    half_of = lambda x, m: lax.dynamic_slice(
+        x, (me ^ m, (me // 2) * (W // 2), 0), (1, W // 2, B)
+    ).reshape(W // 2, B)
+    diag_in = [swap(own(diag_block, m) if m == 1 else half_of(diag_block, m), "narrow", m) for m in masks]
+    diag_in[0], panel = lax.optimization_barrier((diag_in[0], panel))
     panel_in = [swap(own(panel, m), "narrow", m) for m in masks]
 
     narrow_steps = [("narrow", 1 << b) for b in range(log2(narrow_count))]
     wide_steps = [("wide", 1 << b) for b in range(log2(wide_count))]
-    steps_a = narrow_steps + wide_steps
-    steps_b = narrow_steps[:1] + wide_steps + narrow_steps[1:]
+    steps_a = narrow_steps[:1] + wide_steps + narrow_steps[1:]
+    steps_b = narrow_steps[:1] + wide_steps[1:] + wide_steps[:1] + narrow_steps[1:]
     owner = lax.dynamic_slice_in_dim(pair_owner[:, 0], me * NPAIR, NPAIR)
     slot = lax.dynamic_slice_in_dim(pair_slot, me * NPAIR, NPAIR)
     tgt_a = relative_index(owner, slot, wide_me, me, steps_a)
@@ -237,6 +298,8 @@
             pltpu.VMEM((NB, rows, B), jnp.float32),
             pltpu.VMEM((NB, rows, B), jnp.float32),
             pltpu.VMEM((NB, W, B), jnp.float32),
+            pltpu.VMEM((rows, W), jnp.bfloat16),
+            pltpu.VMEM((rows, W), jnp.bfloat16),
             pltpu.VMEM((blocks, split, B), jnp.float32),
             pltpu.VMEM((blocks, B - split, B), jnp.float32),
             pltpu.SemaphoreType.DMA((NB + 4,)),
@@ -281,7 +344,7 @@
         P(("wide", "narrow"), None, None),
     )
     return jax.shard_map(
-        functools.partial(local, 64),
+        functools.partial(local, 72),
         mesh=mesh,
         in_specs=placed,
         out_specs=(

time: 158 us -> 127 us (0.80)
  waiting for transfers between devices: 79.9 us -> 68.3 us
  starting transfers between devices: 35.9 us -> 25 us
  other arithmetic: 34.4 us -> 28.3 us
  local copies, waits for them, and re-layouts: 6.77 us -> 4.68 us
    ppermute x22, waiting for transfers between devices: 79.9 us -> 68.3 us  [swap(): return lax.ppermute(x, axis, xor_pairs(lax.axis_size(axis), mask))]
    ppermute x22, starting transfers between devices: 35.9 us -> 25 us  [swap(): return lax.ppermute(x, axis, xor_pairs(lax.axis_size(axis), mask))]
    pallas_call x1, other arithmetic: 26.1 us -> 21 us  [local(): pl.pallas_call(factor_kernel, out_shape=[slab] * NB + [jax.ShapeDtypeStru...]
  transfers between devices with their start and end apart: 22 -> 22, of which waited for: 10 -> 14; matrix products, arithmetic and copies ran while one was open for 19% -> 23% of each run, Pallas kernels for 0% -> 0%
where the time goes in v2:
time: 127 us
  waiting for transfers between devices  68.3 us (54%)
  other arithmetic  28.3 us (22%)
  starting transfers between devices  25 us (20%)
  local copies, waits for them, and re-layouts  4.68 us (4%)
    ppermute x22, waiting for transfers between devices, swap(): return lax.ppermute(x, axis, xor_pairs(lax.axis_size(axis), mask))  68.3 us
    ppermute x22, starting transfers between devices, swap(): return lax.ppermute(x, axis, xor_pairs(lax.axis_size(axis), mask))  25 us
    pallas_call x1, other arithmetic, local(): pl.pallas_call(factor_kernel, out_shape=[slab] * NB + [jax.ShapeDtypeStru...  21 us
    pallas_call x1, other arithmetic, local(): pl.pallas_call(panel_kernel, out_shape=[slab] * NB + [part_a, part_a, par...  5.27 us
    squeeze x2, local copies, waits for them, and re-layouts, local(): own = lambda x, m: lax.dynamic_index_in_dim(x, me ^ m, 0, keepdims=False)  3.59 us
  transfers between devices with their start and end apart: 22, of which 14 were waited for; matrix products, arithmetic and copies ran while one was open for 23% of the time, Pallas kernels for 0%

profile of v2, /device:TPU:0, one launch (start us, length us, event | category | flops | bytes accessed | tf_op | source)
XLA Modules:
  0.0 127.2 jit_solution(16385943674029945647)
XLA Ops:
  0.6 0.0 copy-start.1
  0.7 0.0 copy-start.7
  0.7 1.1 dynamic-slice_bitcast_fusion.3
  1.7 0.5 collective-permute-start
  2.3 1.2 collective-permute-done
  3.4 2.5 %dynamic-slice_bitcast_fusion = (f32[1024,128]{1,0:T(8,128)}, f32[1024,128]{1,0:T(8,128)}, f32[1024,128]{1,0:T(8,128)}) fusion(f32[4,1024,128]{2,1,0:T(8,128)} %param.7, s32[]{:T(128)S(6)} %select_n.76, s32[]{:T(128)S(6)} %select_n.73, s32[]{:T(128)S(6)} %select_n.72), kind=kLoop, calls=%fused_computation.6 | loop fusion | bytes 3145740 | tf_op jit(solution)/shard_map/jit(dynamic_index_in_dim)/squeeze | solution.py:257
  6.0 2.6 %collective-permute-start.8 = (f32[1024,128]{1,0:T(8,128)}, f32[1024,128]{1,0:T(8,128)S(1)}, u32[]{:S(2)}, u32[]{:S(2)}) collective-permute-start(f32[1024,128]{1,0:T(8,128)} %get-tuple-element.48), channel_id=1, source_target_pairs={{0,3},{1,2},{2,1},{3,0},{4,7},{5,6},{6,5},{7,4},{8,11},{9,10},{10,... | collective-permute-start | bytes 1572872 | tf_op jit(solution)/shard_map/ppermute | solution.py:239
  8.6 0.3 collective-permute-start.7
  8.9 0.1 collective-permute-start.6
  9.0 1.9 %collective-permute-start.2 = (f32[256,128]{1,0:T(8,128)S(1)}, f32[256,128]{1,0:T(8,128)S(1)}, u32[]{:S(2)}, u32[]{:S(2)}) collective-permute-start(f32[256,128]{1,0:T(8,128)S(1)} %get-tuple-element.55), channel_id=1, source_target_pairs={{0,3},{1,2},{2,1},{3,0},{4,7},{5,6},{6,5},{7,4},{8,11},{9,10},{10,... | collective-permute-start | bytes 393224 | tf_op jit(solution)/shard_map/ppermute | solution.py:239
  10.8 0.3 collective-permute-start.1
  11.1 0.6 dynamic_slice.29
  11.8 0.7 pad_add_fusion
  12.5 0.1 multiply_add_fusion
  12.6 22.5 %collective-permute-done.2 = f32[256,128]{1,0:T(8,128)S(1)} collective-permute-done((f32[256,128]{1,0:T(8,128)S(1)}, f32[256,128]{1,0:T(8,128)S(1)}, u32[]{:S(2)}, u32[]{:S(2)}) %collective-permute-start.2) | collective-permute-done | bytes 131104 | tf_op jit(solution)/shard_map/ppermute | solution.py:239
  35.1 3.1 %collective-permute-done.1 = f32[256,128]{1,0:T(8,128)} collective-permute-done((f32[256,128]{1,0:T(8,128)S(1)}, f32[256,128]{1,0:T(8,128)}, u32[]{:S(2)}, u32[]{:S(2)}) %collective-permute-start.1) | collective-permute-done | bytes 131104 | tf_op jit(solution)/shard_map/ppermute | solution.py:239
  38.2 0.1 broadcast_in_dim.32
  38.3 0.0 copy-start
  38.3 21.0 %factor.1 = (f32[4,512,128]{2,1,0:T(8,128)S(1)}, f32[512,128]{1,0:T(8,128)}, f32[512,128]{1,0:T(8,128)}, f32[512,128]{1,0:T(8,128)}, f32[4,512,128]{2,1,0:T(8,128)S(1)}) fusion(f32[4,512,128]{2,1,0:T(8,128)S(1)} %broadcast_in_dim.32, s32[]{:T(128)S(6)} %select_n.71, s32[2]{0:T(128)S(1)} %pad_add_fusion, f32[4,512,128]{2,1,0:T(8,128)S(1)} %copy-done.1, ...), kind=kCustom, calls=%fused_computation.16 | custom fusion | flops 200000000 | bytes 3670532 | tf_op jit(solution)/shard_map/factor/pallas_call | solution.py:276
  59.3 0.1 collective-permute-start.3
  59.3 0.1 multiply_add_fusion.1
  59.4 0.0 collective-permute-done.8
  59.5 0.0 collective-permute-done.7
  59.5 0.0 collective-permute-done.6
  59.5 0.1 broadcast_in_dim.37
  59.6 5.3 %panel.1 = (f32[4,1024,128]{2,1,0:T(8,128)S(1)}, f32[1024,128]{1,0:T(8,128)}, f32[1024,128]{1,0:T(8,128)}, f32[1024,128]{1,0:T(8,128)S(1)}, f32[32,72,128]{2,1,0...) fusion(f32[4,1024,128]{2,1,0:T(8,128)S(1)} %broadcast_in_dim.37, ...), kind=kCustom, calls=%fused_computation.5 | custom fusion | flops 1000000000 | bytes 11011588 | tf_op jit(solution)/shard_map/panel/pallas_call | solution.py:292
  64.9 2.0 %collective-permute-start.17 = (f32[32,56,128]{2,1,0:T(8,128)S(1)}, f32[32,56,128]{2,1,0:T(8,128)S(1)}, u32[]{:S(2)}, u32[]{:S(2)}) collective-permute-start(f32[32,56,128]{2,1,0:T(8,128)S(1)} %get-tuple-element.78), channel_id=1, source_target_pairs={{0,1},{1,0},{2,3},{3,2},{4,5},{5,4},{6,7},{7,6},{8,9},{9,8},{10,11... | collective-permute-start | bytes 2752520 | tf_op jit(solution)/shard_map/ppermute | solution.py:239
  66.9 0.1 collective-permute-start.12
  67.0 1.5 %collective-permute-start.4 = (f32[512,128]{1,0:T(8,128)}, f32[512,128]{1,0:T(8,128)S(1)}, u32[]{:S(2)}, u32[]{:S(2)}) collective-permute-start(f32[512,128]{1,0:T(8,128)} %get-tuple-element.38), channel_id=1, source_target_pairs={{0,2},{1,3},{2,0},{3,1},{4,6},{5,7},{6,4},{7,5},{8,10},{9,11},{10,... | collective-permute-start | bytes 786440 | tf_op jit(solution)/shard_map/ppermute | solution.py:239
  68.4 0.3 collective-permute-start.5
  68.8 0.0 collective-permute-done.3
  68.8 7.5 %collective-permute-done.4 = f32[512,128]{1,0:T(8,128)S(1)} collective-permute-done((f32[512,128]{1,0:T(8,128)}, f32[512,128]{1,0:T(8,128)S(1)}, u32[]{:S(2)}, u32[]{:S(2)}) %collective-permute-start.4) | collective-permute-done | bytes 262176 | tf_op jit(solution)/shard_map/ppermute | solution.py:239
  76.3 4.7 %collective-permute-done.5 = f32[512,128]{1,0:T(8,128)S(1)} collective-permute-done((f32[512,128]{1,0:T(8,128)}, f32[512,128]{1,0:T(8,128)S(1)}, u32[]{:S(2)}, u32[]{:S(2)}) %collective-permute-start.5) | collective-permute-done | bytes 262176 | tf_op jit(solution)/shard_map/ppermute | solution.py:239
  81.0 0.0 copy-start.3
  81.0 0.3 collective-permute-start.9
  81.4 1.1 collective-permute-start.10
  82.5 0.5 collective-permute-start.11
  83.0 0.0 collective-permute-done.17
  83.0 0.1 slice_add_fusion.3
  83.1 2.6 %collective-permute-start.18 = (f32[16,56,128]{2,1,0:T(8,128)S(1)}, f32[16,56,128]{2,1,0:T(8,128)S(1)}, u32[]{:S(2)}, u32[]{:S(2)}) collective-permute-start(f32[16,56,128]{2,1,0:T(8,128)S(1)} %get-tuple-element.52), channel_id=1, source_target_pairs={{0,8},{4,12},{8,0},{12,4},{16,24},{20,28},{24,16},{28,20},{1,9},{5... | collective-permute-start | bytes 1376264 | tf_op jit(solution)/shard_map/ppermute | solution.py:239
  85.7 0.0 collective-permute-done.12
  85.7 0.1 slice_add_fusion.1
  85.8 1.5 %collective-permute-start.13 = (f32[16,72,128]{2,1,0:T(8,128)S(1)}, f32[16,72,128]{2,1,0:T(8,128)S(1)}, u32[]{:S(2)}, u32[]{:S(2)}) collective-permute-start(f32[16,72,128]{2,1,0:T(8,128)S(1)} %get-tuple-element.47), channel_id=1, source_target_pairs={{0,4},{4,0},{8,12},{12,8},{16,20},{20,16},{24,28},{28,24},{1,5},{5... | collective-permute-start | bytes 1769480 | tf_op jit(solution)/shard_map/ppermute | solution.py:239
  87.4 0.0 collective-permute-done.9
  87.4 8.9 %collective-permute-done.10 = f32[1024,128]{1,0:T(8,128)S(1)} collective-permute-done((f32[1024,128]{1,0:T(8,128)}, f32[1024,128]{1,0:T(8,128)S(1)}, u32[]{:S(2)}, u32[]{:S(2)}) %collective-permute-start.10) | collective-permute-done | bytes 524320 | tf_op jit(solution)/shard_map/ppermute | solution.py:239
  96.4 0.5 collective-permute-done.18
  96.9 2.7 %collective-permute-start.19 = (f32[8,56,128]{2,1,0:T(8,128)S(1)}, f32[8,56,128]{2,1,0:T(8,128)S(1)}, u32[]{:S(2)}, u32[]{:S(2)}) collective-permute-start(f32[8,56,128]{2,1,0:T(8,128)S(1)} %get-tuple-element.58), channel_id=1, source_target_pairs={{0,16},{4,20},{8,24},{12,28},{16,0},{20,4},{24,8},{28,12},{1,17},{... | collective-permute-start | bytes 688136 | tf_op jit(solution)/shard_map/ppermute | solution.py:239
  99.6 1.7 %collective-permute-done.13 = f32[16,72,128]{2,1,0:T(8,128)S(1)} collective-permute-done((f32[16,72,128]{2,1,0:T(8,128)S(1)}, f32[16,72,128]{2,1,0:T(8,128)S(1)}, u32[]{:S(2)}, u32[]{:S(2)}) %collective-permute-start.13) | collective-permute-done | bytes 589856 | tf_op jit(solution)/shard_map/ppermute | solution.py:239
  101.4 0.1 slice_add_fusion.5
  101.4 0.0 copy-start.4
  101.4 0.4 collective-permute-start.14
  101.8 4.4 %collective-permute-done.11 = f32[1024,128]{1,0:T(8,128)S(1)} collective-permute-done((f32[1024,128]{1,0:T(8,128)S(1)}, f32[1024,128]{1,0:T(8,128)S(1)}, u32[]{:S(2)}, u32[]{:S(2)}) %collective-permute-start.11) | collective-permute-done | bytes 524320 | tf_op jit(solution)/shard_map/ppermute | solution.py:239
  106.2 0.0 copy-start.2
  106.2 4.1 %collective-permute-done.19 = f32[8,56,128]{2,1,0:T(8,128)S(1)} collective-permute-done((f32[8,56,128]{2,1,0:T(8,128)S(1)}, f32[8,56,128]{2,1,0:T(8,128)S(1)}, u32[]{:S(2)}, u32[]{:S(2)}) %collective-permute-start.19) | collective-permute-done | bytes 229408 | tf_op jit(solution)/shard_map/ppermute | solution.py:239
  110.4 1.6 %collective-permute-start.20 = (f32[4,56,128]{2,1,0:T(8,128)S(1)}, f32[4,56,128]{2,1,0:T(8,128)S(1)}, u32[]{:S(2)}, u32[]{:S(2)}) collective-permute-start(f32[4,56,128]{2,1,0:T(8,128)S(1)} %get-tuple-element.62), channel_id=1, source_target_pairs={{0,4},{4,0},{8,12},{12,8},{16,20},{20,16},{24,28},{28,24},{1,5},{5... | collective-permute-start | bytes 344072 | tf_op jit(solution)/shard_map/ppermute | solution.py:239
  111.9 1.8 %collective-permute-done.14 = f32[8,72,128]{2,1,0:T(8,128)S(1)} collective-permute-done((f32[8,72,128]{2,1,0:T(8,128)S(1)}, f32[8,72,128]{2,1,0:T(8,128)S(1)}, u32[]{:S(2)}, u32[]{:S(2)}) %collective-permute-start.14) | collective-permute-done | bytes 294944 | tf_op jit(solution)/shard_map/ppermute | solution.py:239
  113.7 1.2 collective-permute-start.15
  114.9 0.3 collective-permute-done.20
  115.2 1.8 %collective-permute-start.21 = (f32[2,56,128]{2,1,0:T(8,128)S(1)}, f32[2,56,128]{2,1,0:T(8,128)S(1)}, u32[]{:S(2)}, u32[]{:S(2)}) collective-permute-start(f32[2,56,128]{2,1,0:T(8,128)S(1)} %slice_add_fusion.14), channel_id=1, source_target_pairs={{0,2},{1,3},{2,0},{3,1},{4,6},{5,7},{6,4},{7,5},{8,10},{9,11},{10,... | collective-permute-start | bytes 172040 | tf_op jit(solution)/shard_map/ppermute | solution.py:239
  117.0 5.1 %collective-permute-done.15 = f32[4,72,128]{2,1,0:T(8,128)S(1)} collective-permute-done((f32[4,72,128]{2,1,0:T(8,128)S(1)}, f32[4,72,128]{2,1,0:T(8,128)S(1)}, u32[]{:S(2)}, u32[]{:S(2)}) %collective-permute-start.15) | collective-permute-done | bytes 147488 | tf_op jit(solution)/shard_map/ppermute | solution.py:239
  122.1 1.8 %collective-permute-start.16 = (f32[2,72,128]{2,1,0:T(8,128)S(1)}, f32[2,72,128]{2,1,0:T(8,128)S(1)}, u32[]{:S(2)}, u32[]{:S(2)}) collective-permute-start(f32[2,72,128]{2,1,0:T(8,128)S(1)} %slice_add_fusion.12), channel_id=1, source_target_pairs={{0,2},{1,3},{2,0},{3,1},{4,6},{5,7},{6,4},{7,5},{8,10},{9,11},{10,... | collective-permute-start | bytes 221192 | tf_op jit(solution)/shard_map/ppermute | solution.py:239
  123.9 0.0 collective-permute-done.21
  123.9 2.6 %collective-permute-done.16 = f32[2,72,128]{2,1,0:T(8,128)S(1)} collective-permute-done((f32[2,72,128]{2,1,0:T(8,128)S(1)}, f32[2,72,128]{2,1,0:T(8,128)S(1)}, u32[]{:S(2)}, u32[]{:S(2)}) %collective-permute-start.16) | collective-permute-done | bytes 73760 | tf_op jit(solution)/shard_map/ppermute | solution.py:239
  126.5 0.7 maximum_subtract_fusion
  (24 shorter events, 0.4 us)
Async XLA Ops:
  0.6 8.3 %copy-start.1 = (f32[4,512,128]{2,1,0:T(8,128)S(1)}, f32[4,512,128]{2,1,0:T(8,128)}, u32[]{:S(2)}) copy-start(f32[4,512,128]{2,1,0:T(8,128)} %param.6) | copy-start | bytes 3145732
  0.7 10.5 %copy-start.7 = (s32[4]{0:T(128)S(1)}, s32[4]{0:T(128)}, u32[]{:S(2)}) copy-start(s32[4]{0:T(128)} %param.8) | copy-start | bytes 52
  0.7 11.8 %copy-start.5 = (s32[144,1]{0,1:T(1,128)S(1)}, s32[144,1]{0,1:T(1,128)}, u32[]{:S(2)}) copy-start(s32[144,1]{0,1:T(1,128)} %param.9) | copy-start | bytes 1732
  0.7 11.8 %copy-start.6 = (s32[144]{0:T(256)S(1)}, s32[144]{0:T(256)}, u32[]{:S(2)}) copy-start(s32[144]{0:T(256)} %param.10) | copy-start | bytes 1732
  1.7 1.7 %collective-permute-start = (f32[512,128]{1,0:T(8,128)S(1)}, f32[512,128]{1,0:T(8,128)S(1)}, u32[]{:S(2)}, u32[]{:S(2)}) collective-permute-start(f32[512,128]{1,0:T(8,128)S(1)} %dynamic-slice_bitcast_fusion.3), channel_id=1, source_target_pairs={{0,1},{1,0},{2,3},{3,2},{4,5},{5,4},{6,7},{7,6},{8,9},{9,8},{10,11... | collective-permute-start | bytes 786440 | tf_op jit(solution)/shard_map/ppermute | solution.py:239
  6.0 53.5 %collective-permute-start.8 = (f32[1024,128]{1,0:T(8,128)}, f32[1024,128]{1,0:T(8,128)S(1)}, u32[]{:S(2)}, u32[]{:S(2)}) collective-permute-start(f32[1024,128]{1,0:T(8,128)} %get-tuple-element.48), channel_id=1, source_target_pairs={{0,3},{1,2},{2,1},{3,0},{4,7},{5,6},{6,5},{7,4},{8,11},{9,10},{10,... | collective-permute-start | bytes 1572872 | tf_op jit(solution)/shard_map/ppermute | solution.py:239
  8.6 50.9 %collective-permute-start.7 = (f32[1024,128]{1,0:T(8,128)}, f32[1024,128]{1,0:T(8,128)S(1)}, u32[]{:S(2)}, u32[]{:S(2)}) collective-permute-start(f32[1024,128]{1,0:T(8,128)} %get-tuple-element.49), channel_id=1, source_target_pairs={{0,2},{1,3},{2,0},{3,1},{4,6},{5,7},{6,4},{7,5},{8,10},{9,11},{10,... | collective-permute-start | bytes 1572872 | tf_op jit(solution)/shard_map/ppermute | solution.py:239
  8.9 50.6 %collective-permute-start.6 = (f32[1024,128]{1,0:T(8,128)}, f32[1024,128]{1,0:T(8,128)}, u32[]{:S(2)}, u32[]{:S(2)}) collective-permute-start(f32[1024,128]{1,0:T(8,128)} %get-tuple-element.50), channel_id=1, source_target_pairs={{0,1},{1,0},{2,3},{3,2},{4,5},{5,4},{6,7},{7,6},{8,9},{9,8},{10,11... | collective-permute-start | bytes 1572872 | tf_op jit(solution)/shard_map/ppermute | solution.py:239
  9.0 26.2 %collective-permute-start.2 = (f32[256,128]{1,0:T(8,128)S(1)}, f32[256,128]{1,0:T(8,128)S(1)}, u32[]{:S(2)}, u32[]{:S(2)}) collective-permute-start(f32[256,128]{1,0:T(8,128)S(1)} %get-tuple-element.55), channel_id=1, source_target_pairs={{0,3},{1,2},{2,1},{3,0},{4,7},{5,6},{6,5},{7,4},{8,11},{9,10},{10,... | collective-permute-start | bytes 393224 | tf_op jit(solution)/shard_map/ppermute | solution.py:239
  10.8 27.4 %collective-permute-start.1 = (f32[256,128]{1,0:T(8,128)S(1)}, f32[256,128]{1,0:T(8,128)}, u32[]{:S(2)}, u32[]{:S(2)}) collective-permute-start(f32[256,128]{1,0:T(8,128)S(1)} %get-tuple-element.56), channel_id=1, source_target_pairs={{0,2},{1,3},{2,0},{3,1},{4,6},{5,7},{6,4},{7,5},{8,10},{9,11},{10,... | collective-permute-start | bytes 393224 | tf_op jit(solution)/shard_map/ppermute | solution.py:239
  38.3 21.3 %copy-start = (f32[4,1024,128]{2,1,0:T(8,128)S(1)}, f32[4,1024,128]{2,1,0:T(8,128)}, u32[]{:S(2)}) copy-start(f32[4,1024,128]{2,1,0:T(8,128)} %param.7) | copy-start | bytes 6291460
  59.3 9.5 %collective-permute-start.3 = (f32[512,128]{1,0:T(8,128)}, f32[512,128]{1,0:T(8,128)S(1)}, u32[]{:S(2)}, u32[]{:S(2)}) collective-permute-start(f32[512,128]{1,0:T(8,128)} %get-tuple-element.36), channel_id=1, source_target_pairs={{0,1},{1,0},{2,3},{3,2},{4,5},{5,4},{6,7},{7,6},{8,9},{9,8},{10,11... | collective-permute-start | bytes 786440 | tf_op jit(solution)/shard_map/ppermute | solution.py:239
  64.9 18.1 %collective-permute-start.17 = (f32[32,56,128]{2,1,0:T(8,128)S(1)}, f32[32,56,128]{2,1,0:T(8,128)S(1)}, u32[]{:S(2)}, u32[]{:S(2)}) collective-permute-start(f32[32,56,128]{2,1,0:T(8,128)S(1)} %get-tuple-element.78), channel_id=1, source_target_pairs={{0,1},{1,0},{2,3},{3,2},{4,5},{5,4},{6,7},{7,6},{8,9},{9,8},{10,11... | collective-permute-start | bytes 2752520 | tf_op jit(solution)/shard_map/ppermute | solution.py:239
  66.9 18.8 %collective-permute-start.12 = (f32[32,72,128]{2,1,0:T(8,128)S(1)}, f32[32,72,128]{2,1,0:T(8,128)S(1)}, u32[]{:S(2)}, u32[]{:S(2)}) collective-permute-start(f32[32,72,128]{2,1,0:T(8,128)S(1)} %get-tuple-element.74), channel_id=1, source_target_pairs={{0,1},{1,0},{2,3},{3,2},{4,5},{5,4},{6,7},{7,6},{8,9},{9,8},{10,11... | collective-permute-start | bytes 3538952 | tf_op jit(solution)/shard_map/ppermute | solution.py:239
  67.0 9.3 %collective-permute-start.4 = (f32[512,128]{1,0:T(8,128)}, f32[512,128]{1,0:T(8,128)S(1)}, u32[]{:S(2)}, u32[]{:S(2)}) collective-permute-start(f32[512,128]{1,0:T(8,128)} %get-tuple-element.38), channel_id=1, source_target_pairs={{0,2},{1,3},{2,0},{3,1},{4,6},{5,7},{6,4},{7,5},{8,10},{9,11},{10,... | collective-permute-start | bytes 786440 | tf_op jit(solution)/shard_map/ppermute | solution.py:239
  68.4 12.6 %collective-permute-start.5 = (f32[512,128]{1,0:T(8,128)}, f32[512,128]{1,0:T(8,128)S(1)}, u32[]{:S(2)}, u32[]{:S(2)}) collective-permute-start(f32[512,128]{1,0:T(8,128)} %get-tuple-element.40), channel_id=1, source_target_pairs={{0,3},{1,2},{2,1},{3,0},{4,7},{5,6},{6,5},{7,4},{8,11},{9,10},{10,... | collective-permute-start | bytes 786440 | tf_op jit(solution)/shard_map/ppermute | solution.py:239
  81.0 4.8 %copy-start.3 = (f32[4,512,128]{2,1,0:T(8,128)}, f32[4,512,128]{2,1,0:T(8,128)S(1)}, u32[]{:S(2)}) copy-start(f32[4,512,128]{2,1,0:T(8,128)S(1)} %bitcast_dynamic-update-slice_fusion.4) | copy-start | bytes 3145732
  81.0 6.3 %collective-permute-start.9 = (f32[1024,128]{1,0:T(8,128)}, f32[1024,128]{1,0:T(8,128)S(1)}, u32[]{:S(2)}, u32[]{:S(2)}) collective-permute-start(f32[1024,128]{1,0:T(8,128)} %get-tuple-element.66), channel_id=1, source_target_pairs={{0,1},{1,0},{2,3},{3,2},{4,5},{5,4},{6,7},{7,6},{8,9},{9,8},{10,11... | collective-permute-start | bytes 1572872 | tf_op jit(solution)/shard_map/ppermute | solution.py:239
  81.4 15.0 %collective-permute-start.10 = (f32[1024,128]{1,0:T(8,128)}, f32[1024,128]{1,0:T(8,128)S(1)}, u32[]{:S(2)}, u32[]{:S(2)}) collective-permute-start(f32[1024,128]{1,0:T(8,128)} %get-tuple-element.68), channel_id=1, source_target_pairs={{0,2},{1,3},{2,0},{3,1},{4,6},{5,7},{6,4},{7,5},{8,10},{9,11},{10,... | collective-permute-start | bytes 1572872 | tf_op jit(solution)/shard_map/ppermute | solution.py:239
  82.5 23.7 %collective-permute-start.11 = (f32[1024,128]{1,0:T(8,128)S(1)}, f32[1024,128]{1,0:T(8,128)S(1)}, u32[]{:S(2)}, u32[]{:S(2)}) collective-permute-start(f32[1024,128]{1,0:T(8,128)S(1)} %get-tuple-element.70), channel_id=1, source_target_pairs={{0,3},{1,2},{2,1},{3,0},{4,7},{5,6},{6,5},{7,4},{8,11},{9,10},{10,... | collective-permute-start | bytes 1572872 | tf_op jit(solution)/shard_map/ppermute | solution.py:239
  83.1 13.8 %collective-permute-start.18 = (f32[16,56,128]{2,1,0:T(8,128)S(1)}, f32[16,56,128]{2,1,0:T(8,128)S(1)}, u32[]{:S(2)}, u32[]{:S(2)}) collective-permute-start(f32[16,56,128]{2,1,0:T(8,128)S(1)} %get-tuple-element.52), channel_id=1, source_target_pairs={{0,8},{4,12},{8,0},{12,4},{16,24},{20,28},{24,16},{28,20},{1,9},{5... | collective-permute-start | bytes 1376264 | tf_op jit(solution)/shard_map/ppermute | solution.py:239
  85.8 15.5 %collective-permute-start.13 = (f32[16,72,128]{2,1,0:T(8,128)S(1)}, f32[16,72,128]{2,1,0:T(8,128)S(1)}, u32[]{:S(2)}, u32[]{:S(2)}) collective-permute-start(f32[16,72,128]{2,1,0:T(8,128)S(1)} %get-tuple-element.47), channel_id=1, source_target_pairs={{0,4},{4,0},{8,12},{12,8},{16,20},{20,16},{24,28},{28,24},{1,5},{5... | collective-permute-start | bytes 1769480 | tf_op jit(solution)/shard_map/ppermute | solution.py:239
  96.9 13.4 %collective-permute-start.19 = (f32[8,56,128]{2,1,0:T(8,128)S(1)}, f32[8,56,128]{2,1,0:T(8,128)S(1)}, u32[]{:S(2)}, u32[]{:S(2)}) collective-permute-start(f32[8,56,128]{2,1,0:T(8,128)S(1)} %get-tuple-element.58), channel_id=1, source_target_pairs={{0,16},{4,20},{8,24},{12,28},{16,0},{20,4},{24,8},{28,12},{1,17},{... | collective-permute-start | bytes 688136 | tf_op jit(solution)/shard_map/ppermute | solution.py:239
  101.4 25.1 %copy-start.4 = (f32[2,128,128]{2,1,0:T(8,128)S(1)}, f32[2,128,128]{2,1,0:T(8,128)}, u32[]{:S(2)}) copy-start(f32[2,128,128]{2,1,0:T(8,128)} %param.11) | copy-start | bytes 393220
  101.4 12.2 %collective-permute-start.14 = (f32[8,72,128]{2,1,0:T(8,128)S(1)}, f32[8,72,128]{2,1,0:T(8,128)S(1)}, u32[]{:S(2)}, u32[]{:S(2)}) collective-permute-start(f32[8,72,128]{2,1,0:T(8,128)S(1)} %get-tuple-element.54), channel_id=1, source_target_pairs={{0,8},{4,12},{8,0},{12,4},{16,24},{20,28},{24,16},{28,20},{1,9},{5... | collective-permute-start | bytes 884744 | tf_op jit(solution)/shard_map/ppermute | solution.py:239
  106.2 21.0 %copy-start.2 = (f32[4,1024,128]{2,1,0:T(8,128)}, f32[4,1024,128]{2,1,0:T(8,128)S(1)}, u32[]{:S(2)}) copy-start(f32[4,1024,128]{2,1,0:T(8,128)S(1)} %bitcast_dynamic-update-slice_fusion) | copy-start | bytes 6291460
  110.4 4.9 %collective-permute-start.20 = (f32[4,56,128]{2,1,0:T(8,128)S(1)}, f32[4,56,128]{2,1,0:T(8,128)S(1)}, u32[]{:S(2)}, u32[]{:S(2)}) collective-permute-start(f32[4,56,128]{2,1,0:T(8,128)S(1)} %get-tuple-element.62), channel_id=1, source_target_pairs={{0,4},{4,0},{8,12},{12,8},{16,20},{20,16},{24,28},{28,24},{1,5},{5... | collective-permute-start | bytes 344072 | tf_op jit(solution)/shard_map/ppermute | solution.py:239
  113.7 8.4 %collective-permute-start.15 = (f32[4,72,128]{2,1,0:T(8,128)S(1)}, f32[4,72,128]{2,1,0:T(8,128)S(1)}, u32[]{:S(2)}, u32[]{:S(2)}) collective-permute-start(f32[4,72,128]{2,1,0:T(8,128)S(1)} %get-tuple-element.60), channel_id=1, source_target_pairs={{0,16},{4,20},{8,24},{12,28},{16,0},{20,4},{24,8},{28,12},{1,17},{... | collective-permute-start | bytes 442376 | tf_op jit(solution)/shard_map/ppermute | solution.py:239
  115.2 8.7 %collective-permute-start.21 = (f32[2,56,128]{2,1,0:T(8,128)S(1)}, f32[2,56,128]{2,1,0:T(8,128)S(1)}, u32[]{:S(2)}, u32[]{:S(2)}) collective-permute-start(f32[2,56,128]{2,1,0:T(8,128)S(1)} %slice_add_fusion.14), channel_id=1, source_target_pairs={{0,2},{1,3},{2,0},{3,1},{4,6},{5,7},{6,4},{7,5},{8,10},{9,11},{10,... | collective-permute-start | bytes 172040 | tf_op jit(solution)/shard_map/ppermute | solution.py:239
  122.1 4.4 %collective-permute-start.16 = (f32[2,72,128]{2,1,0:T(8,128)S(1)}, f32[2,72,128]{2,1,0:T(8,128)S(1)}, u32[]{:S(2)}, u32[]{:S(2)}) collective-permute-start(f32[2,72,128]{2,1,0:T(8,128)S(1)} %slice_add_fusion.12), channel_id=1, source_target_pairs={{0,2},{1,3},{2,0},{3,1},{4,6},{5,7},{6,4},{7,5},{8,10},{9,11},{10,... | collective-permute-start | bytes 221192 | tf_op jit(solution)/shard_map/ppermute | solution.py:239

commit v3 on v2

--- a/solution.py
+++ b/solution.py
@@ -1,5 +1,3 @@
-import functools
-
 import jax
 import jax.numpy as jnp
 import numpy as np
@@ -162,7 +160,7 @@
 
 
 def panel_kernel(info, tgt_a, tgt_b, own_ref, r1, r2, r3, mt_ref, *rest):
-    (x0, x1, x2, x3, keep_a, send_a, keep_b, send_b, p, x, mt, xh, xl, ta, tb, sems) = rest
+    (x0, x1, x2, x3, keep, send, p, x, mt, xh, xl, total, sems) = rest
     me = info[0]
     count = info[1]
     ins = [own_ref.at[me], r1, r2, r3]
@@ -170,8 +168,7 @@
     copies.append(pltpu.make_async_copy(mt_ref, mt, sems.at[NB]))
     for c in copies:
         c.start()
-    ta[...] = jnp.zeros_like(ta)
-    tb[...] = jnp.zeros_like(tb)
+    total[...] = jnp.zeros_like(total)
     for c in copies:
         c.wait()
     rows = P_SIZE * B
@@ -193,7 +190,7 @@
     copies = [pltpu.make_async_copy(x.at[me ^ m], outs[m], sems.at[m]) for m in range(NB)]
     for c in copies:
         c.start()
-    half_a = ta.shape[1]
+    strip = total.shape[2]
     for j in range(0, P_SIZE, 2):
 
         @pl.when(j < count)
@@ -207,16 +204,15 @@
                     pair = i * (i + 1) // 2 + j + n
                     at_a = tgt_a[pair]
                     at_b = tgt_b[pair]
-                    ta[at_a] += block[:half_a]
-                    tb[at_b] += block[half_a:]
-
-    half = ta.shape[0] // 2
-    more = [
-        pltpu.make_async_copy(ta.at[pl.ds(0, half)], keep_a, sems.at[NB]),
-        pltpu.make_async_copy(ta.at[pl.ds(half, half)], send_a, sems.at[NB + 1]),
-        pltpu.make_async_copy(tb.at[pl.ds(0, half)], keep_b, sems.at[NB + 2]),
-        pltpu.make_async_copy(tb.at[pl.ds(half, half)], send_b, sems.at[NB + 3]),
-    ]
+                    total[0, at_a] += block[:strip]
+                    total[1, at_b] += block[strip:]
+
+    half = total.shape[1] // 2
+    more = []
+    for n in range(2):
+        at = NB + 2 * n
+        more.append(pltpu.make_async_copy(total.at[n, pl.ds(half, half)], send.at[n], sems.at[at]))
+        more.append(pltpu.make_async_copy(total.at[n, pl.ds(0, half)], keep.at[n], sems.at[at + 1]))
     for c in more:
         c.start()
     for c in copies + more:
@@ -247,7 +243,7 @@
     return index * T_DEV + slot % T_DEV
 
 
-def local(split, diag_block, panel, panel_count, pair_owner, pair_slot, ancestor):
+def local(diag_block, panel, panel_count, pair_owner, pair_slot, ancestor):
     narrow_count = lax.axis_size("narrow")
     wide_count = lax.axis_size("wide")
     me = lax.axis_index("narrow")
@@ -259,13 +255,15 @@
         x, (me ^ m, (me // 2) * (W // 2), 0), (1, W // 2, B)
     ).reshape(W // 2, B)
     diag_in = [swap(own(diag_block, m) if m == 1 else half_of(diag_block, m), "narrow", m) for m in masks]
-    diag_in[0], panel = lax.optimization_barrier((diag_in[0], panel))
-    panel_in = [swap(own(panel, m), "narrow", m) for m in masks]
+    panel_out = [own(panel, m) for m in masks]
+    diag_in, panel_out = lax.optimization_barrier((diag_in, panel_out))
+    panel_in = [swap(panel_out[m - 1], "narrow", m) for m in masks]
 
     narrow_steps = [("narrow", 1 << b) for b in range(log2(narrow_count))]
     wide_steps = [("wide", 1 << b) for b in range(log2(wide_count))]
-    steps_a = narrow_steps[:1] + wide_steps + narrow_steps[1:]
-    steps_b = narrow_steps[:1] + wide_steps[1:] + wide_steps[:1] + narrow_steps[1:]
+    first, last = narrow_steps[:1], wide_steps[2:] + narrow_steps[1:]
+    steps_a = first + wide_steps[:2] + last
+    steps_b = first + wide_steps[1::-1] + last
     owner = lax.dynamic_slice_in_dim(pair_owner[:, 0], me * NPAIR, NPAIR)
     slot = lax.dynamic_slice_in_dim(pair_slot, me * NPAIR, NPAIR)
     tgt_a = relative_index(owner, slot, wide_me, me, steps_a)
@@ -287,21 +285,19 @@
     rows = P_SIZE * B
     blocks = wide_count * narrow_count * T_DEV
     slab = jax.ShapeDtypeStruct((rows, B), jnp.float32)
-    part_a = jax.ShapeDtypeStruct((blocks // 2, split, B), jnp.float32)
-    part_b = jax.ShapeDtypeStruct((blocks // 2, B - split, B), jnp.float32)
-    *x_parts, keep_a, send_a, keep_b, send_b = pl.pallas_call(
+    part = jax.ShapeDtypeStruct((2, blocks // 2, B // 2, B), jnp.float32)
+    *x_parts, keep, send = pl.pallas_call(
         panel_kernel,
-        out_shape=[slab] * NB + [part_a, part_a, part_b, part_b],
+        out_shape=[slab] * NB + [part, part],
         in_specs=[SMEM] * 3 + [ANY] * (NB + 1),
-        out_specs=[ANY] * (NB + 4),
+        out_specs=[ANY] * (NB + 2),
         scratch_shapes=[
             pltpu.VMEM((NB, rows, B), jnp.float32),
             pltpu.VMEM((NB, rows, B), jnp.float32),
             pltpu.VMEM((NB, W, B), jnp.float32),
             pltpu.VMEM((rows, W), jnp.bfloat16),
             pltpu.VMEM((rows, W), jnp.bfloat16),
-            pltpu.VMEM((blocks, split, B), jnp.float32),
-            pltpu.VMEM((blocks, B - split, B), jnp.float32),
+            pltpu.VMEM((2, blocks, B // 2, B), jnp.float32),
             pltpu.SemaphoreType.DMA((NB + 4,)),
         ],
         compiler_params=pltpu.CompilerParams(vmem_limit_bytes=52 * 2**20),
@@ -309,29 +305,51 @@
         name="panel",
     )(info, tgt_a, tgt_b, panel, *panel_in, mt)
 
-    def reduce(keep, send, steps):
-        for n, (axis, mask) in enumerate(steps):
-            got = swap(send, axis, mask)
-            if n + 1 < len(steps):
-                half = keep.shape[0] // 2
-                send = keep[half:] + got[half:]
-                keep = keep[:half] + got[:half]
-            else:
-                keep = keep + got
-        return keep
-
-    sum_a = reduce(keep_a, send_a, steps_a)
-    sum_b = reduce(keep_b, send_b, steps_b)
-    updated = ancestor - jnp.concatenate([sum_a, sum_b], axis=1)
-
-    def give_back(parts):
-        back = [parts[0]] + [swap(parts[m], "narrow", m) for m in masks]
-        out = jnp.zeros((NB,) + parts[0].shape, jnp.float32)
+    l_back = [swap(l_parts[m], "narrow", m) for m in masks]
+    x_back = [swap(x_parts[m], "narrow", m) for m in masks]
+
+    got = swap(send, "narrow", 1)
+    half = blocks // 4
+    upper = lambda u, n: u[n, half:]
+    lower = lambda u, n: u[n, :half]
+    send_a = upper(keep, 0) + upper(got, 0)
+    send_b = upper(keep, 1) + upper(got, 1)
+    keep_a = lower(keep, 0) + lower(got, 0)
+    keep_b = lower(keep, 1) + lower(got, 1)
+    for n in (1, 2):
+        if n == 2:
+            send_a, send_b, l_back[1], l_back[2] = lax.optimization_barrier(
+                (send_a, send_b, l_back[1], l_back[2])
+            )
+        else:
+            send_a, send_b = lax.optimization_barrier((send_a, send_b))
+        got_a = swap(send_a, *steps_a[n])
+        got_b = swap(send_b, *steps_b[n])
+        half = half // 2
+        send_a, send_b = keep_a[half:] + got_a[half:], keep_b[half:] + got_b[half:]
+        keep_a, keep_b = keep_a[:half] + got_a[:half], keep_b[:half] + got_b[:half]
+    send = jnp.stack([send_a, send_b], axis=1)
+    keep = jnp.stack([keep_a, keep_b], axis=1)
+    for n in range(3, len(steps_a)):
+        if n == 3:
+            send, x_back[1] = lax.optimization_barrier((send, x_back[1]))
+        if n == len(steps_a) - 1:
+            send, x_back[2], x_back[0] = lax.optimization_barrier((send, x_back[2], x_back[0]))
+        got = swap(send, *steps_a[n])
+        if n + 1 < len(steps_a):
+            half = half // 2
+            send = keep[half:] + got[half:]
+            keep = keep[:half] + got[:half]
+    updated = ancestor - (keep + got).reshape(ancestor.shape)
+
+    def give_back(own_part, others):
+        back = [own_part] + others
+        out = jnp.zeros((NB,) + own_part.shape, jnp.float32)
         for m in range(NB):
             out = lax.dynamic_update_index_in_dim(out, back[m], me ^ m, 0)
         return out
 
-    return (give_back(l_parts), give_back(x_parts), updated)
+    return (give_back(l_parts[0], l_back), give_back(x_parts[0], x_back), updated)
 
 
 def solution(mesh):
@@ -344,7 +362,7 @@
         P(("wide", "narrow"), None, None),
     )
     return jax.shard_map(
-        functools.partial(local, 72),
+        local,
         mesh=mesh,
         in_specs=placed,
         out_specs=(

time: 127 us -> 101 us (0.80)
  waiting for transfers between devices: 68.3 us -> 46.5 us
  starting transfers between devices: 25 us -> 19.3 us
    ppermute x22 -> x19, waiting for transfers between devices: 68.3 us -> 46.5 us  [swap(): return lax.ppermute(x, axis, xor_pairs(lax.axis_size(axis), mask))]
    ppermute x22 -> x19, starting transfers between devices: 25 us -> 19.3 us  [swap(): return lax.ppermute(x, axis, xor_pairs(lax.axis_size(axis), mask))]
  transfers between devices with their start and end apart: 22 -> 19, of which waited for: 14 -> 12; matrix products, arithmetic and copies ran while one was open for 23% -> 26% of each run, Pallas kernels for 0% -> 0%
where the time goes in v3:
time: 101 us; the launch traced here: 100 us
  waiting for transfers between devices  46.5 us (46%)
  other arithmetic  28.4 us (28%)
  starting transfers between devices  19.3 us (19%)
  local copies, waits for them, and re-layouts  5.34 us (5%)
    ppermute x19, waiting for transfers between devices, swap(): return lax.ppermute(x, axis, xor_pairs(lax.axis_size(axis), mask))  46.5 us
    pallas_call x1, other arithmetic, local(): pl.pallas_call(factor_kernel, out_shape=[slab] * NB + [jax.ShapeDtypeStru...  20.4 us
    ppermute x19, starting transfers between devices, swap(): return lax.ppermute(x, axis, xor_pairs(lax.axis_size(axis), mask))  19.3 us
    pallas_call x1, other arithmetic, local(): pl.pallas_call(panel_kernel, out_shape=[slab] * NB + [part, part], in_spe...  5.83 us
    squeeze x2, local copies, waits for them, and re-layouts, local(): own = lambda x, m: lax.dynamic_index_in_dim(x, me ^ m, 0, keepdims=False)  3.32 us
  transfers between devices with their start and end apart: 19, of which 12 were waited for; matrix products, arithmetic and copies ran while one was open for 26% of the time, Pallas kernels for 0%

profile of v3, /device:TPU:0, one launch (start us, length us, event | category | flops | bytes accessed | tf_op | source)
XLA Modules:
  0.0 100.4 jit_solution(6693066868070490790)
XLA Ops:
  0.6 0.0 copy-start.10
  0.7 1.0 dynamic-slice_bitcast_fusion.3
  1.7 0.5 collective-permute-start
  2.2 1.0 dynamic-slice_bitcast_fusion.4
  3.2 2.7 %collective-permute-start.2 = (f32[256,128]{1,0:T(8,128)S(1)}, f32[256,128]{1,0:T(8,128)S(1)}, u32[]{:S(2)}, u32[]{:S(2)}) collective-permute-start(f32[256,128]{1,0:T(8,128)S(1)} %get-tuple-element.83), channel_id=1, source_target_pairs={{0,3},{1,2},{2,1},{3,0},{4,7},{5,6},{6,5},{7,4},{8,11},{9,10},{10,... | collective-permute-start | bytes 393224 | tf_op jit(solution)/shard_map/ppermute | solution.py:235
  5.8 0.0 collective-permute-start.1
  5.9 2.3 %dynamic-slice_bitcast_fusion = (f32[1024,128]{1,0:T(8,128)S(1)}, f32[1024,128]{1,0:T(8,128)S(1)}, f32[1024,128]{1,0:T(8,128)}) fusion(f32[4,1024,128]{2,1,0:T(8,128)} %param.7, s32[]{:T(128)S(6)} %select_n.76, s32[]{:T(128)S(6)} %select_n.73, s32[]{:T(128)S(6)} %select_n.72), kind=kLoop, calls=%fused_computation.10 | loop fusion | bytes 3145740 | tf_op jit(solution)/shard_map/jit(dynamic_index_in_dim)/squeeze | solution.py:253
  8.2 1.5 %collective-permute-done.2 = f32[256,128]{1,0:T(8,128)S(1)} collective-permute-done((f32[256,128]{1,0:T(8,128)S(1)}, f32[256,128]{1,0:T(8,128)S(1)}, u32[]{:S(2)}, u32[]{:S(2)}) %collective-permute-start.2) | collective-permute-done | bytes 131104 | tf_op jit(solution)/shard_map/ppermute | solution.py:235
  9.7 3.0 %collective-permute-done.1 = f32[256,128]{1,0:T(8,128)S(1)} collective-permute-done((f32[256,128]{1,0:T(8,128)S(1)}, f32[256,128]{1,0:T(8,128)S(1)}, u32[]{:S(2)}, u32[]{:S(2)}) %collective-permute-start.1) | collective-permute-done | bytes 131104 | tf_op jit(solution)/shard_map/ppermute | solution.py:235
  12.7 0.0 collective-permute-done
  12.7 0.0 collective-permute-start.4
  12.7 1.7 %collective-permute-start.5 = (f32[1024,128]{1,0:T(8,128)S(1)}, f32[1024,128]{1,0:T(8,128)}, u32[]{:S(2)}, u32[]{:S(2)}) collective-permute-start(f32[1024,128]{1,0:T(8,128)S(1)} %get-tuple-element.37), channel_id=1, source_target_pairs={{0,2},{1,3},{2,0},{3,1},{4,6},{5,7},{6,4},{7,5},{8,10},{9,11},{10,... | collective-permute-start | bytes 1572872 | tf_op jit(solution)/shard_map/ppermute | solution.py:235
  14.4 0.2 collective-permute-start.6
  14.6 0.6 dynamic_slice.29
  15.2 0.7 pad_add_fusion
  15.9 0.0 copy-done.8
  15.9 0.1 multiply_add_fusion
  16.0 0.1 multiply_add_fusion.1
  16.1 0.1 broadcast_in_dim.32
  16.2 0.0 copy-start
  16.2 20.4 %factor.1 = (f32[4,512,128]{2,1,0:T(8,128)S(1)}, f32[512,128]{1,0:T(8,128)}, f32[4,512,128]{2,1,0:T(8,128)S(1)}, f32[512,128]{1,0:T(8,128)}, f32[512,128]{1,0:T(8,128)}) fusion(f32[4,512,128]{2,1,0:T(8,128)S(1)} %broadcast_in_dim.32, s32[]{:T(128)S(6)} %select_n.71, s32[2]{0:T(128)S(1)} %pad_add_fusion, f32[4,512,128]{2,1,0:T(8,128)S(1)} %copy-done.1, ...), kind=kCustom, calls=%fused_computation.27 | custom fusion | flops 200000000 | bytes 3670532 | tf_op jit(solution)/shard_map/factor/pallas_call | solution.py:274
  36.5 0.0 collective-permute-done.4
  36.6 0.0 collective-permute-done.5
  36.6 1.4 %collective-permute-done.6 = f32[1024,128]{1,0:T(8,128)} collective-permute-done((f32[1024,128]{1,0:T(8,128)S(1)}, f32[1024,128]{1,0:T(8,128)}, u32[]{:S(2)}, u32[]{:S(2)}) %collective-permute-start.6) | collective-permute-done | bytes 524320 | tf_op jit(solution)/shard_map/ppermute | solution.py:235
  38.0 0.1 broadcast_in_dim.37
  38.1 5.8 %panel.1 = (f32[4,1024,128]{2,1,0:T(8,128)S(1)}, f32[2,32,64,128]{3,2,1,0:T(8,128)S(1)}, f32[2,32,64,128]{3,2,1,0:T(8,128)S(1)}, f32[1024,128]{1,0:T(8,128)S(1)}...) fusion(f32[4,1024,128]{2,1,0:T(8,128)S(1)} %broadcast_in_dim.37, s32[]{:T(128)S(6)} %select_n.71, ...), kind=kCustom, calls=%fused_computation.9 | custom fusion | flops 1000000000 | bytes 11011588 | tf_op jit(solution)/shard_map/panel/pallas_call | solution.py:289
  44.0 0.9 collective-permute-start.7
  44.9 3.8 %collective-permute-done.7 = f32[2,32,64,128]{3,2,1,0:T(8,128)S(1)} collective-permute-done((f32[2,32,64,128]{3,2,1,0:T(8,128)S(1)}, f32[2,32,64,128]{3,2,1,0:T(8,128)S(1)}, u32[]{:S(2)}, u32[]{:S(2)}) %collective-permute-start.7) | collective-permute-done | bytes 2097184 | tf_op jit(solution)/shard_map/ppermute | solution.py:235
  48.7 0.4 slice_add_fusion
  49.1 1.3 %collective-permute-start.8 = (f32[16,64,128]{2,1,0:T(8,128)S(1)}, f32[16,64,128]{2,1,0:T(8,128)S(1)}, u32[]{:S(2)}, u32[]{:S(2)}) collective-permute-start(f32[16,64,128]{2,1,0:T(8,128)S(1)} %get-tuple-element.42), channel_id=1, source_target_pairs={{0,4},{4,0},{8,12},{12,8},{16,20},{20,16},{24,28},{28,24},{1,5},{5... | collective-permute-start | bytes 1572872 | tf_op jit(solution)/shard_map/ppermute | solution.py:235
  50.4 1.6 %collective-permute-start.9 = (f32[16,64,128]{2,1,0:T(8,128)S(1)}, f32[16,64,128]{2,1,0:T(8,128)S(1)}, u32[]{:S(2)}, u32[]{:S(2)}) collective-permute-start(f32[16,64,128]{2,1,0:T(8,128)S(1)} %get-tuple-element.43), channel_id=1, source_target_pairs={{0,8},{4,12},{8,0},{12,4},{16,24},{20,28},{24,16},{28,20},{1,9},{5... | collective-permute-start | bytes 1572872 | tf_op jit(solution)/shard_map/ppermute | solution.py:235
  52.0 0.0 collective-permute-start.3
  52.0 0.0 copy-done.6
  52.0 2.6 %collective-permute-start.10 = (f32[512,128]{1,0:T(8,128)S(1)}, f32[512,128]{1,0:T(8,128)S(1)}, u32[]{:S(2)}, u32[]{:S(2)}) collective-permute-start(f32[512,128]{1,0:T(8,128)S(1)} %copy-done.6), channel_id=1, source_target_pairs={{0,2},{1,3},{2,0},{3,1},{4,6},{5,7},{6,4},{7,5},{8,10},{9,11},{10,... | collective-permute-start | bytes 786440 | tf_op jit(solution)/shard_map/ppermute | solution.py:235
  54.5 0.0 copy-done.5
  54.5 0.1 collective-permute-start.11
  54.7 8.7 %collective-permute-done.8 = f32[16,64,128]{2,1,0:T(8,128)S(1)} collective-permute-done((f32[16,64,128]{2,1,0:T(8,128)S(1)}, f32[16,64,128]{2,1,0:T(8,128)S(1)}, u32[]{:S(2)}, u32[]{:S(2)}) %collective-permute-start.8) | collective-permute-done | bytes 524320 | tf_op jit(solution)/shard_map/ppermute | solution.py:235
  63.3 0.1 slice_add_fusion.5
  63.4 0.7 collective-permute-done.9
  64.1 0.1 slice_add_fusion.4
  64.2 0.0 collective-permute-done.10
  64.2 2.6 %collective-permute-done.11 = f32[512,128]{1,0:T(8,128)S(1)} collective-permute-done((f32[512,128]{1,0:T(8,128)S(1)}, f32[512,128]{1,0:T(8,128)S(1)}, u32[]{:S(2)}, u32[]{:S(2)}) %collective-permute-start.11) | collective-permute-done | bytes 262176 | tf_op jit(solution)/shard_map/ppermute | solution.py:235
  66.8 0.4 collective-permute-start.12
  67.3 0.5 collective-permute-start.13
  67.8 0.0 collective-permute-done.3
  67.8 1.6 %collective-permute-start.14 = (f32[1024,128]{1,0:T(8,128)S(1)}, f32[1024,128]{1,0:T(8,128)S(1)}, u32[]{:S(2)}, u32[]{:S(2)}) collective-permute-start(f32[1024,128]{1,0:T(8,128)S(1)} %get-tuple-element.96), channel_id=1, source_target_pairs={{0,2},{1,3},{2,0},{3,1},{4,6},{5,7},{6,4},{7,5},{8,10},{9,11},{10,... | collective-permute-start | bytes 1572872 | tf_op jit(solution)/shard_map/ppermute | solution.py:235
  69.4 0.0 collective-permute-start.16
  69.4 0.6 collective-permute-start.17
  70.0 5.1 %collective-permute-done.12 = f32[8,64,128]{2,1,0:T(8,128)S(1)} collective-permute-done((f32[8,64,128]{2,1,0:T(8,128)S(1)}, f32[8,64,128]{2,1,0:T(8,128)S(1)}, u32[]{:S(2)}, u32[]{:S(2)}) %collective-permute-start.12) | collective-permute-done | bytes 262176 | tf_op jit(solution)/shard_map/ppermute | solution.py:235
  75.2 0.1 collective-permute-done.13
  75.4 7.3 %collective-permute-done.14 = f32[1024,128]{1,0:T(8,128)S(1)} collective-permute-done((f32[1024,128]{1,0:T(8,128)S(1)}, f32[1024,128]{1,0:T(8,128)S(1)}, u32[]{:S(2)}, u32[]{:S(2)}) %collective-permute-start.14) | collective-permute-done | bytes 524320 | tf_op jit(solution)/shard_map/ppermute | solution.py:235
  82.7 2.6 %collective-permute-start.15 = (f32[4,2,64,128]{3,2,0,1:T(8,128)S(1)}, f32[4,2,64,128]{3,2,0,1:T(8,128)S(1)}, u32[]{:S(2)}, u32[]{:S(2)}) collective-permute-start(f32[4,2,64,128]{3,2,0,1:T(8,128)S(1)} %pad_maximum_fusion), channel_id=1, source_target_pairs={{0,16},{4,20},{8,24},{12,28},{16,0},{20,4},{24,8},{28,12},{1,17},{... | collective-permute-start | bytes 786440 | tf_op jit(solution)/shard_map/ppermute | solution.py:235
  85.3 0.0 copy-start.3
  85.3 9.3 %collective-permute-done.15 = f32[4,2,64,128]{3,2,0,1:T(8,128)S(1)} collective-permute-done((f32[4,2,64,128]{3,2,0,1:T(8,128)S(1)}, f32[4,2,64,128]{3,2,0,1:T(8,128)S(1)}, u32[]{:S(2)}, u32[]{:S(2)}) %collective-permute-start.15) | collective-permute-done | bytes 262176 | tf_op jit(solution)/shard_map/ppermute | solution.py:235
  94.6 0.0 copy-start.7
  94.7 0.0 collective-permute-done.16
  94.7 0.0 collective-permute-done.17
  94.7 2.0 %collective-permute-start.18 = (f32[2,2,64,128]{3,2,0,1:T(8,128)S(1)}, f32[2,2,64,128]{3,2,0,1:T(8,128)S(1)}, u32[]{:S(2)}, u32[]{:S(2)}) collective-permute-start(f32[2,2,64,128]{3,2,0,1:T(8,128)S(1)} %fusion.3), channel_id=1, source_target_pairs={{0,2},{1,3},{2,0},{3,1},{4,6},{5,7},{6,4},{7,5},{8,10},{9,11},{10,... | collective-permute-start | bytes 393224 | tf_op jit(solution)/shard_map/ppermute | solution.py:235
  96.8 0.0 copy-start.2
  96.8 2.9 %collective-permute-done.18 = f32[2,2,64,128]{3,2,0,1:T(8,128)S(1)} collective-permute-done((f32[2,2,64,128]{3,2,0,1:T(8,128)S(1)}, f32[2,2,64,128]{3,2,0,1:T(8,128)S(1)}, u32[]{:S(2)}, u32[]{:S(2)}) %collective-permute-start.18) | collective-permute-done | bytes 131104 | tf_op jit(solution)/shard_map/ppermute | solution.py:235
  99.7 0.0 copy-done.3
  99.8 0.0 copy-done.7
  99.8 0.7 bitcast_subtract_fusion
  100.4 0.0 copy-done.2
  (23 shorter events, 0.3 us)
Async XLA Ops:
  0.6 13.9 %copy-start.10 = (s32[4]{0:T(128)S(1)}, s32[4]{0:T(128)}, u32[]{:S(2)}) copy-start(s32[4]{0:T(128)} %param.8) | copy-start | bytes 52
  0.7 15.2 %copy-start.8 = (s32[144,1]{0,1:T(1,128)S(1)}, s32[144,1]{0,1:T(1,128)}, u32[]{:S(2)}) copy-start(s32[144,1]{0,1:T(1,128)} %param.9) | copy-start | bytes 1732
  0.7 15.2 %copy-start.9 = (s32[144]{0:T(256)S(1)}, s32[144]{0:T(256)}, u32[]{:S(2)}) copy-start(s32[144]{0:T(256)} %param.10) | copy-start | bytes 1732
  1.7 11.0 %collective-permute-start = (f32[512,128]{1,0:T(8,128)S(1)}, f32[512,128]{1,0:T(8,128)S(1)}, u32[]{:S(2)}, u32[]{:S(2)}) collective-permute-start(f32[512,128]{1,0:T(8,128)S(1)} %dynamic-slice_bitcast_fusion.3), channel_id=1, source_target_pairs={{0,1},{1,0},{2,3},{3,2},{4,5},{5,4},{6,7},{7,6},{8,9},{9,8},{10,11... | collective-permute-start | bytes 786440 | tf_op jit(solution)/shard_map/ppermute | solution.py:235
  3.2 6.5 %collective-permute-start.2 = (f32[256,128]{1,0:T(8,128)S(1)}, f32[256,128]{1,0:T(8,128)S(1)}, u32[]{:S(2)}, u32[]{:S(2)}) collective-permute-start(f32[256,128]{1,0:T(8,128)S(1)} %get-tuple-element.83), channel_id=1, source_target_pairs={{0,3},{1,2},{2,1},{3,0},{4,7},{5,6},{6,5},{7,4},{8,11},{9,10},{10,... | collective-permute-start | bytes 393224 | tf_op jit(solution)/shard_map/ppermute | solution.py:235
  5.8 10.3 %copy-start.1 = (f32[4,512,128]{2,1,0:T(8,128)S(1)}, f32[4,512,128]{2,1,0:T(8,128)}, u32[]{:S(2)}) copy-start(f32[4,512,128]{2,1,0:T(8,128)} %param.6) | copy-start | bytes 3145732
  5.8 6.9 %collective-permute-start.1 = (f32[256,128]{1,0:T(8,128)S(1)}, f32[256,128]{1,0:T(8,128)S(1)}, u32[]{:S(2)}, u32[]{:S(2)}) collective-permute-start(f32[256,128]{1,0:T(8,128)S(1)} %get-tuple-element.84), channel_id=1, source_target_pairs={{0,2},{1,3},{2,0},{3,1},{4,6},{5,7},{6,4},{7,5},{8,10},{9,11},{10,... | collective-permute-start | bytes 393224 | tf_op jit(solution)/shard_map/ppermute | solution.py:235
  12.7 23.8 %collective-permute-start.4 = (f32[1024,128]{1,0:T(8,128)}, f32[1024,128]{1,0:T(8,128)}, u32[]{:S(2)}, u32[]{:S(2)}) collective-permute-start(f32[1024,128]{1,0:T(8,128)} %get-tuple-element.36), channel_id=1, source_target_pairs={{0,1},{1,0},{2,3},{3,2},{4,5},{5,4},{6,7},{7,6},{8,9},{9,8},{10,11... | collective-permute-start | bytes 1572872 | tf_op jit(solution)/shard_map/ppermute | solution.py:235
  12.7 23.9 %collective-permute-start.5 = (f32[1024,128]{1,0:T(8,128)S(1)}, f32[1024,128]{1,0:T(8,128)}, u32[]{:S(2)}, u32[]{:S(2)}) collective-permute-start(f32[1024,128]{1,0:T(8,128)S(1)} %get-tuple-element.37), channel_id=1, source_target_pairs={{0,2},{1,3},{2,0},{3,1},{4,6},{5,7},{6,4},{7,5},{8,10},{9,11},{10,... | collective-permute-start | bytes 1572872 | tf_op jit(solution)/shard_map/ppermute | solution.py:235
  14.4 23.6 %collective-permute-start.6 = (f32[1024,128]{1,0:T(8,128)S(1)}, f32[1024,128]{1,0:T(8,128)}, u32[]{:S(2)}, u32[]{:S(2)}) collective-permute-start(f32[1024,128]{1,0:T(8,128)S(1)} %get-tuple-element.38), channel_id=1, source_target_pairs={{0,3},{1,2},{2,1},{3,0},{4,7},{5,6},{6,5},{7,4},{8,11},{9,10},{10,... | collective-permute-start | bytes 1572872 | tf_op jit(solution)/shard_map/ppermute | solution.py:235
  16.2 22.0 %copy-start = (f32[4,1024,128]{2,1,0:T(8,128)S(1)}, f32[4,1024,128]{2,1,0:T(8,128)}, u32[]{:S(2)}) copy-start(f32[4,1024,128]{2,1,0:T(8,128)} %param.7) | copy-start | bytes 6291460
  44.0 4.7 %collective-permute-start.7 = (f32[2,32,64,128]{3,2,1,0:T(8,128)S(1)}, f32[2,32,64,128]{3,2,1,0:T(8,128)S(1)}, u32[]{:S(2)}, u32[]{:S(2)}) collective-permute-start(f32[2,32,64,128]{3,2,1,0:T(8,128)S(1)} %get-tuple-element.93), channel_id=1, source_target_pairs={{0,1},{1,0},{2,3},{3,2},{4,5},{5,4},{6,7},{7,6},{8,9},{9,8},{10,11... | collective-permute-start | bytes 6291464 | tf_op jit(solution)/shard_map/ppermute | solution.py:235
  48.7 3.3 %copy-start.4 = (f32[512,128]{1,0:T(8,128)S(1)}, f32[512,128]{1,0:T(8,128)}, u32[]{:S(2)}) copy-start(f32[512,128]{1,0:T(8,128)} %get-tuple-element.62) | copy-start | bytes 786436
  48.7 3.3 %copy-start.6 = (f32[512,128]{1,0:T(8,128)S(1)}, f32[512,128]{1,0:T(8,128)}, u32[]{:S(2)}) copy-start(f32[512,128]{1,0:T(8,128)} %get-tuple-element.66) | copy-start | bytes 786436
  48.7 5.9 %copy-start.5 = (f32[512,128]{1,0:T(8,128)S(1)}, f32[512,128]{1,0:T(8,128)}, u32[]{:S(2)}) copy-start(f32[512,128]{1,0:T(8,128)} %get-tuple-element.68) | copy-start | bytes 786436
  49.1 14.3 %collective-permute-start.8 = (f32[16,64,128]{2,1,0:T(8,128)S(1)}, f32[16,64,128]{2,1,0:T(8,128)S(1)}, u32[]{:S(2)}, u32[]{:S(2)}) collective-permute-start(f32[16,64,128]{2,1,0:T(8,128)S(1)} %get-tuple-element.42), channel_id=1, source_target_pairs={{0,4},{4,0},{8,12},{12,8},{16,20},{20,16},{24,28},{28,24},{1,5},{5... | collective-permute-start | bytes 1572872 | tf_op jit(solution)/shard_map/ppermute | solution.py:235
  50.4 13.8 %collective-permute-start.9 = (f32[16,64,128]{2,1,0:T(8,128)S(1)}, f32[16,64,128]{2,1,0:T(8,128)S(1)}, u32[]{:S(2)}, u32[]{:S(2)}) collective-permute-start(f32[16,64,128]{2,1,0:T(8,128)S(1)} %get-tuple-element.43), channel_id=1, source_target_pairs={{0,8},{4,12},{8,0},{12,4},{16,24},{20,28},{24,16},{28,20},{1,9},{5... | collective-permute-start | bytes 1572872 | tf_op jit(solution)/shard_map/ppermute | solution.py:235
  52.0 15.8 %collective-permute-start.3 = (f32[512,128]{1,0:T(8,128)S(1)}, f32[512,128]{1,0:T(8,128)S(1)}, u32[]{:S(2)}, u32[]{:S(2)}) collective-permute-start(f32[512,128]{1,0:T(8,128)S(1)} %copy-done.4), channel_id=1, source_target_pairs={{0,1},{1,0},{2,3},{3,2},{4,5},{5,4},{6,7},{7,6},{8,9},{9,8},{10,11... | collective-permute-start | bytes 786440 | tf_op jit(solution)/shard_map/ppermute | solution.py:235
  52.0 12.2 %collective-permute-start.10 = (f32[512,128]{1,0:T(8,128)S(1)}, f32[512,128]{1,0:T(8,128)S(1)}, u32[]{:S(2)}, u32[]{:S(2)}) collective-permute-start(f32[512,128]{1,0:T(8,128)S(1)} %copy-done.6), channel_id=1, source_target_pairs={{0,2},{1,3},{2,0},{3,1},{4,6},{5,7},{6,4},{7,5},{8,10},{9,11},{10,... | collective-permute-start | bytes 786440 | tf_op jit(solution)/shard_map/ppermute | solution.py:235
  54.5 12.3 %collective-permute-start.11 = (f32[512,128]{1,0:T(8,128)S(1)}, f32[512,128]{1,0:T(8,128)S(1)}, u32[]{:S(2)}, u32[]{:S(2)}) collective-permute-start(f32[512,128]{1,0:T(8,128)S(1)} %copy-done.5), channel_id=1, source_target_pairs={{0,3},{1,2},{2,1},{3,0},{4,7},{5,6},{6,5},{7,4},{8,11},{9,10},{10,... | collective-permute-start | bytes 786440 | tf_op jit(solution)/shard_map/ppermute | solution.py:235
  66.8 8.3 %collective-permute-start.12 = (f32[8,64,128]{2,1,0:T(8,128)S(1)}, f32[8,64,128]{2,1,0:T(8,128)S(1)}, u32[]{:S(2)}, u32[]{:S(2)}) collective-permute-start(f32[8,64,128]{2,1,0:T(8,128)S(1)} %get-tuple-element.49), channel_id=1, source_target_pairs={{0,8},{4,12},{8,0},{12,4},{16,24},{20,28},{24,16},{28,20},{1,9},{5... | collective-permute-start | bytes 786440 | tf_op jit(solution)/shard_map/ppermute | solution.py:235
  67.3 8.0 %collective-permute-start.13 = (f32[8,64,128]{2,1,0:T(8,128)S(1)}, f32[8,64,128]{2,1,0:T(8,128)S(1)}, u32[]{:S(2)}, u32[]{:S(2)}) collective-permute-start(f32[8,64,128]{2,1,0:T(8,128)S(1)} %get-tuple-element.50), channel_id=1, source_target_pairs={{0,4},{4,0},{8,12},{12,8},{16,20},{20,16},{24,28},{28,24},{1,5},{5... | collective-permute-start | bytes 786440 | tf_op jit(solution)/shard_map/ppermute | solution.py:235
  67.8 14.9 %collective-permute-start.14 = (f32[1024,128]{1,0:T(8,128)S(1)}, f32[1024,128]{1,0:T(8,128)S(1)}, u32[]{:S(2)}, u32[]{:S(2)}) collective-permute-start(f32[1024,128]{1,0:T(8,128)S(1)} %get-tuple-element.96), channel_id=1, source_target_pairs={{0,2},{1,3},{2,0},{3,1},{4,6},{5,7},{6,4},{7,5},{8,10},{9,11},{10,... | collective-permute-start | bytes 1572872 | tf_op jit(solution)/shard_map/ppermute | solution.py:235
  69.4 25.3 %collective-permute-start.16 = (f32[1024,128]{1,0:T(8,128)S(1)}, f32[1024,128]{1,0:T(8,128)S(1)}, u32[]{:S(2)}, u32[]{:S(2)}) collective-permute-start(f32[1024,128]{1,0:T(8,128)S(1)} %get-tuple-element.98), channel_id=1, source_target_pairs={{0,3},{1,2},{2,1},{3,0},{4,7},{5,6},{6,5},{7,4},{8,11},{9,10},{10,... | collective-permute-start | bytes 1572872 | tf_op jit(solution)/shard_map/ppermute | solution.py:235
  69.4 25.3 %collective-permute-start.17 = (f32[1024,128]{1,0:T(8,128)S(1)}, f32[1024,128]{1,0:T(8,128)S(1)}, u32[]{:S(2)}, u32[]{:S(2)}) collective-permute-start(f32[1024,128]{1,0:T(8,128)S(1)} %get-tuple-element.100), channel_id=1, source_target_pairs={{0,1},{1,0},{2,3},{3,2},{4,5},{5,4},{6,7},{7,6},{8,9},{9,8},{10,11... | collective-permute-start | bytes 1572872 | tf_op jit(solution)/shard_map/ppermute | solution.py:235
  82.7 11.9 %collective-permute-start.15 = (f32[4,2,64,128]{3,2,0,1:T(8,128)S(1)}, f32[4,2,64,128]{3,2,0,1:T(8,128)S(1)}, u32[]{:S(2)}, u32[]{:S(2)}) collective-permute-start(f32[4,2,64,128]{3,2,0,1:T(8,128)S(1)} %pad_maximum_fusion), channel_id=1, source_target_pairs={{0,16},{4,20},{8,24},{12,28},{16,0},{20,4},{24,8},{28,12},{1,17},{... | collective-permute-start | bytes 786440 | tf_op jit(solution)/shard_map/ppermute | solution.py:235
  85.3 14.4 %copy-start.3 = (f32[4,512,128]{2,1,0:T(8,128)}, f32[4,512,128]{2,1,0:T(8,128)S(1)}, u32[]{:S(2)}) copy-start(f32[4,512,128]{2,1,0:T(8,128)S(1)} %bitcast_dynamic-update-slice_fusion.4) | copy-start | bytes 3145732
  94.6 5.1 %copy-start.7 = (f32[2,128,128]{2,1,0:T(8,128)S(1)}, f32[2,128,128]{2,1,0:T(8,128)}, u32[]{:S(2)}) copy-start(f32[2,128,128]{2,1,0:T(8,128)} %param.11) | copy-start | bytes 393220
  94.7 5.0 %collective-permute-start.18 = (f32[2,2,64,128]{3,2,0,1:T(8,128)S(1)}, f32[2,2,64,128]{3,2,0,1:T(8,128)S(1)}, u32[]{:S(2)}, u32[]{:S(2)}) collective-permute-start(f32[2,2,64,128]{3,2,0,1:T(8,128)S(1)} %fusion.3), channel_id=1, source_target_pairs={{0,2},{1,3},{2,0},{3,1},{4,6},{5,7},{6,4},{7,5},{8,10},{9,11},{10,... | collective-permute-start | bytes 393224 | tf_op jit(solution)/shard_map/ppermute | solution.py:235
  96.8 3.7 %copy-start.2 = (f32[4,1024,128]{2,1,0:T(8,128)}, f32[4,1024,128]{2,1,0:T(8,128)S(1)}, u32[]{:S(2)}) copy-start(f32[4,1024,128]{2,1,0:T(8,128)S(1)} %bitcast_dynamic-update-slice_fusion) | copy-start | bytes 6291460

commit v4 on v3

--- a/solution.py
+++ b/solution.py
@@ -112,7 +112,7 @@
     return dot(left[0], right[0]) + (dot(left[0], right[1]) + dot(left[1], right[0]))
 
 
-def factor_kernel(info, own_ref, r1, r2, r3, l0, l1, l2, l3, inv_out, a, l, mt, sems):
+def factor_kernel(info, own_ref, r1, r2, r3, l0, l1, l2, l3, mt, a, l, sems):
     me = info[0]
     side = me // 2
     far_rows = pl.ds((1 - side) * (W // 2), W // 2)
@@ -152,45 +152,36 @@
             mt[k, pl.ds(i * B, B), :] = dot_nt(-total, inv)
     outs = [l0, l1, l2, l3]
     copies = [pltpu.make_async_copy(l.at[me ^ m], outs[m], sems.at[m]) for m in range(NB)]
-    copies.append(pltpu.make_async_copy(mt, inv_out, sems.at[NB]))
     for c in copies:
         c.start()
     for c in copies:
         c.wait()
 
 
-def panel_kernel(info, tgt_a, tgt_b, own_ref, r1, r2, r3, mt_ref, *rest):
-    (x0, x1, x2, x3, keep, send, p, x, mt, xh, xl, total, sems) = rest
+def panel_kernel(info, counts, tgt_a, tgt_b, own_ref, r1, r2, r3, mt, x0, x1, x2, x3, keep, send, xh, xl):
     me = info[0]
-    count = info[1]
+    count = counts[me]
+    rows = P_SIZE * B
     ins = [own_ref.at[me], r1, r2, r3]
-    copies = [pltpu.make_async_copy(ins[m], p.at[me ^ m], sems.at[m]) for m in range(NB)]
-    copies.append(pltpu.make_async_copy(mt_ref, mt, sems.at[NB]))
-    for c in copies:
-        c.start()
-    total[...] = jnp.zeros_like(total)
-    for c in copies:
-        c.wait()
-    rows = P_SIZE * B
+    outs = [x0, x1, x2, x3]
     live = lax.broadcasted_iota(jnp.int32, (rows, B), 0) < count * B
-    parts = [split_bf16(jnp.where(live, p[c], 0.0)) for c in range(NB)]
+    parts = [split_bf16(jnp.where(live, ref[...], 0.0)) for ref in ins]
+    left = [jnp.concatenate([part[n] for part in parts], axis=1) for n in range(2)]
     for c in range(0, NB, 2):
-        left = [jnp.concatenate([parts[j][n] for j in range(c + 2)], axis=1) for n in range(2)]
-        right = split_bf16(
-            jnp.concatenate([mt[c, pl.ds(0, (c + 2) * B), :], mt[c + 1, pl.ds(0, (c + 2) * B), :]], axis=1)
-        )
-        got = dot3(left, right, ((1,), (0,)))
-        x[c] = got[:, :B]
-        x[c + 1] = got[:, B:]
+        right = [
+            jnp.concatenate([mt[me ^ m, pl.ds((me ^ k) * B, B), :] for m in (c, c + 1)], axis=1)
+            for k in range(NB)
+        ]
+        got = dot3(left, split_bf16(jnp.concatenate(right, axis=0)), ((1,), (0,)))
+        outs[c][...] = got[:, :B]
+        outs[c + 1][...] = got[:, B:]
         high, low = split_bf16(got)
         xh[:, pl.ds(c * B, 2 * B)] = high
         xl[:, pl.ds(c * B, 2 * B)] = low
 
-    outs = [x0, x1, x2, x3]
-    copies = [pltpu.make_async_copy(x.at[me ^ m], outs[m], sems.at[m]) for m in range(NB)]
-    for c in copies:
-        c.start()
-    strip = total.shape[2]
+    keep[...] = jnp.zeros_like(keep)
+    send[...] = jnp.zeros_like(send)
+    half, strip = keep.shape[1:3]
     for j in range(0, P_SIZE, 2):
 
         @pl.when(j < count)
@@ -202,25 +193,17 @@
                 for n in range(2 if i > j else 1):
                     block = got[(i - j) * B : (i - j + 1) * B, n * B : (n + 1) * B]
                     pair = i * (i + 1) // 2 + j + n
-                    at_a = tgt_a[pair]
-                    at_b = tgt_b[pair]
-                    total[0, at_a] += block[:strip]
-                    total[1, at_b] += block[strip:]
-
-    half = total.shape[1] // 2
-    more = []
-    for n in range(2):
-        at = NB + 2 * n
-        more.append(pltpu.make_async_copy(total.at[n, pl.ds(half, half)], send.at[n], sems.at[at]))
-        more.append(pltpu.make_async_copy(total.at[n, pl.ds(0, half)], keep.at[n], sems.at[at + 1]))
-    for c in more:
-        c.start()
-    for c in copies + more:
-        c.wait()
+                    away = (tgt_a[pair] >= half).astype(jnp.float32)
+                    for stream, tgt in enumerate((tgt_a, tgt_b)):
+                        at = lax.rem(tgt[pair], half)
+                        piece = block[stream * strip : (stream + 1) * strip]
+                        keep[stream, at] += piece * (1.0 - away)
+                        send[stream, at] += piece * away
 
 
 SMEM = pl.BlockSpec(memory_space=pltpu.SMEM)
 ANY = pl.BlockSpec(memory_space=pl.ANY)
+VMEM = pl.BlockSpec(memory_space=pltpu.VMEM)
 
 
 def xor_pairs(size, mask):
@@ -268,15 +251,15 @@
     slot = lax.dynamic_slice_in_dim(pair_slot, me * NPAIR, NPAIR)
     tgt_a = relative_index(owner, slot, wide_me, me, steps_a)
     tgt_b = relative_index(owner, slot, wide_me, me, steps_b)
-    info = jnp.stack([me, panel_count[me]]).astype(jnp.int32)
+    info = me.astype(jnp.int32).reshape(1)
 
     slab = jax.ShapeDtypeStruct((W, B), jnp.float32)
     *l_parts, mt = pl.pallas_call(
         factor_kernel,
         out_shape=[slab] * NB + [jax.ShapeDtypeStruct((NB, W, B), jnp.float32)],
         in_specs=[SMEM] + [ANY] * NB,
-        out_specs=[ANY] * (NB + 1),
-        scratch_shapes=[pltpu.VMEM((NB, W, B), jnp.float32)] * 3 + [pltpu.SemaphoreType.DMA((NB + 1,))],
+        out_specs=[ANY] * NB + [VMEM],
+        scratch_shapes=[pltpu.VMEM((NB, W, B), jnp.float32)] * 2 + [pltpu.SemaphoreType.DMA((NB,))],
         compiler_params=pltpu.CompilerParams(vmem_limit_bytes=32 * 2**20),
         cost_estimate=pl.CostEstimate(flops=2 * 10**8, bytes_accessed=4 * 10**6, transcendentals=0),
         name="factor",
@@ -289,21 +272,13 @@
     *x_parts, keep, send = pl.pallas_call(
         panel_kernel,
         out_shape=[slab] * NB + [part, part],
-        in_specs=[SMEM] * 3 + [ANY] * (NB + 1),
-        out_specs=[ANY] * (NB + 2),
-        scratch_shapes=[
-            pltpu.VMEM((NB, rows, B), jnp.float32),
-            pltpu.VMEM((NB, rows, B), jnp.float32),
-            pltpu.VMEM((NB, W, B), jnp.float32),
-            pltpu.VMEM((rows, W), jnp.bfloat16),
-            pltpu.VMEM((rows, W), jnp.bfloat16),
-            pltpu.VMEM((2, blocks, B // 2, B), jnp.float32),
-            pltpu.SemaphoreType.DMA((NB + 4,)),
-        ],
+        in_specs=[SMEM] * 4 + [VMEM] * (NB + 1),
+        out_specs=[VMEM] * (NB + 2),
+        scratch_shapes=[pltpu.VMEM((rows, W), jnp.bfloat16)] * 2,
         compiler_params=pltpu.CompilerParams(vmem_limit_bytes=52 * 2**20),
         cost_estimate=pl.CostEstimate(flops=10**9, bytes_accessed=10 * 10**6, transcendentals=0),
         name="panel",
-    )(info, tgt_a, tgt_b, panel, *panel_in, mt)
+    )(info, panel_count, tgt_a, tgt_b, panel, *panel_in, mt)
 
     l_back = [swap(l_parts[m], "narrow", m) for m in masks]
     x_back = [swap(x_parts[m], "narrow", m) for m in masks]
@@ -318,9 +293,7 @@
     keep_b = lower(keep, 1) + lower(got, 1)
     for n in (1, 2):
         if n == 2:
-            send_a, send_b, l_back[1], l_back[2] = lax.optimization_barrier(
-                (send_a, send_b, l_back[1], l_back[2])
-            )
+            send_a, send_b, x_back[1] = lax.optimization_barrier((send_a, send_b, x_back[1]))
         else:
             send_a, send_b = lax.optimization_barrier((send_a, send_b))
         got_a = swap(send_a, *steps_a[n])
@@ -332,7 +305,7 @@
     keep = jnp.stack([keep_a, keep_b], axis=1)
     for n in range(3, len(steps_a)):
         if n == 3:
-            send, x_back[1] = lax.optimization_barrier((send, x_back[1]))
+            send, l_back[1] = lax.optimization_barrier((send, l_back[1]))
         if n == len(steps_a) - 1:
             send, x_back[2], x_back[0] = lax.optimization_barrier((send, x_back[2], x_back[0]))
         got = swap(send, *steps_a[n])

time: 101 us -> 98.4 us (0.974)
  starting transfers between devices: 19.3 us -> 16.7 us
    ppermute x19, starting transfers between devices: 19.3 us -> 16.7 us  [swap(): return lax.ppermute(x, axis, xor_pairs(lax.axis_size(axis), mask))]
    pallas_call x1, other arithmetic: 5.83 us -> 7 us  [local(): pl.pallas_call(panel_kernel, out_shape=[slab] * NB + [part, part], in_spe...]
  transfers between devices with their start and end apart: 19 -> 19, of which waited for: 12 -> 12; matrix products, arithmetic and copies ran while one was open for 26% -> 25% of each run, Pallas kernels for 0% -> 0%
where the time goes in v4:
time: 98.4 us; the launch traced here: 98.2 us
  waiting for transfers between devices  46.6 us (47%)
  other arithmetic  29 us (29%)
  starting transfers between devices  16.7 us (17%)
  local copies, waits for them, and re-layouts  4.92 us (5%)
    ppermute x19, waiting for transfers between devices, swap(): return lax.ppermute(x, axis, xor_pairs(lax.axis_size(axis), mask))  46.6 us
    pallas_call x1, other arithmetic, local(): pl.pallas_call(factor_kernel, out_shape=[slab] * NB + [jax.ShapeDtypeStru...  20.5 us
    ppermute x19, starting transfers between devices, swap(): return lax.ppermute(x, axis, xor_pairs(lax.axis_size(axis), mask))  16.7 us
    pallas_call x1, other arithmetic, local(): pl.pallas_call(panel_kernel, out_shape=[slab] * NB + [part, part], in_spe...  7 us
    squeeze x2, local copies, waits for them, and re-layouts, local(): own = lambda x, m: lax.dynamic_index_in_dim(x, me ^ m, 0, keepdims=False)  3.48 us
  transfers between devices with their start and end apart: 19, of which 12 were waited for; matrix products, arithmetic and copies ran while one was open for 25% of the time, Pallas kernels for 0%

profile of v4, /device:TPU:0, one launch (start us, length us, event | category | flops | bytes accessed | tf_op | source)
XLA Modules:
  0.0 98.2 jit_solution(567266545539718895)
XLA Ops:
  0.6 0.0 copy-start.8
  0.7 0.0 copy-start.9
  0.7 1.0 dynamic-slice_bitcast_fusion.3
  1.6 0.5 collective-permute-start
  2.2 1.0 %dynamic-slice_bitcast_fusion.4 = (f32[256,128]{1,0:T(8,128)S(1)}, f32[256,128]{1,0:T(8,128)S(1)}) fusion(f32[4,512,128]{2,1,0:T(8,128)} %param.6, s32[]{:T(128)S(6)} %select_n.74, s32[]{:T(128)S(6)} %select_n.73, s32[]{:T(128)S(6)} %select_n.71), kind=kLoop, calls=%fused_computation.43 | loop fusion | bytes 524300 | tf_op jit(solution)/shard_map/reshape | solution.py:239
  3.1 2.7 %collective-permute-start.2 = (f32[256,128]{1,0:T(8,128)S(1)}, f32[256,128]{1,0:T(8,128)S(1)}, u32[]{:S(2)}, u32[]{:S(2)}) collective-permute-start(f32[256,128]{1,0:T(8,128)S(1)} %get-tuple-element.81), channel_id=1, source_target_pairs={{0,3},{1,2},{2,1},{3,0},{4,7},{5,6},{6,5},{7,4},{8,11},{9,10},{10,... | collective-permute-start | bytes 393224 | tf_op jit(solution)/shard_map/ppermute | solution.py:218
  5.8 0.0 collective-permute-start.1
  5.9 2.5 %dynamic-slice_bitcast_fusion = (f32[1024,128]{1,0:T(8,128)S(1)}, f32[1024,128]{1,0:T(8,128)}, f32[1024,128]{1,0:T(8,128)}) fusion(f32[4,1024,128]{2,1,0:T(8,128)} %param.7, s32[]{:T(128)S(6)} %select_n.74, s32[]{:T(128)S(6)} %select_n.71, s32[]{:T(128)S(6)} %select_n.70), kind=kLoop, calls=%fused_computation.10 | loop fusion | bytes 3145740 | tf_op jit(solution)/shard_map/jit(dynamic_index_in_dim)/squeeze | solution.py:236
  8.4 1.3 %collective-permute-done.2 = f32[256,128]{1,0:T(8,128)S(1)} collective-permute-done((f32[256,128]{1,0:T(8,128)S(1)}, f32[256,128]{1,0:T(8,128)S(1)}, u32[]{:S(2)}, u32[]{:S(2)}) %collective-permute-start.2) | collective-permute-done | bytes 131104 | tf_op jit(solution)/shard_map/ppermute | solution.py:218
  9.6 3.1 %collective-permute-done.1 = f32[256,128]{1,0:T(8,128)} collective-permute-done((f32[256,128]{1,0:T(8,128)S(1)}, f32[256,128]{1,0:T(8,128)}, u32[]{:S(2)}, u32[]{:S(2)}) %collective-permute-start.1) | collective-permute-done | bytes 131104 | tf_op jit(solution)/shard_map/ppermute | solution.py:218
  12.8 0.0 collective-permute-done
  12.8 0.0 collective-permute-start.4
  12.8 1.7 %collective-permute-start.5 = (f32[1024,128]{1,0:T(8,128)}, f32[1024,128]{1,0:T(8,128)}, u32[]{:S(2)}, u32[]{:S(2)}) collective-permute-start(f32[1024,128]{1,0:T(8,128)} %get-tuple-element.36), channel_id=1, source_target_pairs={{0,2},{1,3},{2,0},{3,1},{4,6},{5,7},{6,4},{7,5},{8,10},{9,11},{10,... | collective-permute-start | bytes 1572872 | tf_op jit(solution)/shard_map/ppermute | solution.py:218
  14.5 0.2 collective-permute-start.6
  14.7 0.1 multiply_add_fusion
  14.8 0.1 multiply_add_fusion.1
  14.9 0.1 broadcast_in_dim.32
  14.9 0.0 copy-done.1
  14.9 0.0 copy-start
  15.0 0.0 copy-start.10
  15.0 20.5 %factor.1 = (f32[4,512,128]{2,1,0:T(8,128)S(1)}, f32[512,128]{1,0:T(8,128)}, f32[4,512,128]{2,1,0:T(8,128)S(1)}, f32[512,128]{1,0:T(8,128)}, f32[512,128]{1,0:T(8,128)S(1)}) fusion(f32[4,512,128]{2,1,0:T(8,128)S(1)} %broadcast_in_dim.32, s32[]{:T(128)S(6)} %select_n.75, s32[1]{0:T(128)} %bitcast, f32[4,512,128]{2,1,0:T(8,128)S(1)} %copy-done.1, ...), kind=kCustom, calls=%fused_computation.27 | custom fusion | flops 200000000 | bytes 3670024 | tf_op jit(solution)/shard_map/factor/pallas_call | solution.py:257
  35.5 0.0 collective-permute-done.4
  35.5 0.0 collective-permute-done.5
  35.5 2.8 %collective-permute-done.6 = f32[1024,128]{1,0:T(8,128)} collective-permute-done((f32[1024,128]{1,0:T(8,128)S(1)}, f32[1024,128]{1,0:T(8,128)}, u32[]{:S(2)}, u32[]{:S(2)}) %collective-permute-start.6) | collective-permute-done | bytes 524320 | tf_op jit(solution)/shard_map/ppermute | solution.py:218
  38.3 0.1 broadcast_in_dim.37
  38.4 0.0 copy-done
  38.4 0.0 copy-done.10
  38.5 7.0 %panel.1 = (f32[4,1024,128]{2,1,0:T(8,128)S(1)}, f32[2,32,64,128]{3,2,1,0:T(8,128)S(1)}, f32[2,32,64,128]{3,2,1,0:T(8,128)S(1)}, f32[1024,128]{1,0:T(8,128)}, f3...) fusion(f32[4,1024,128]{2,1,0:T(8,128)S(1)} %broadcast_in_dim.37, s32[]{:T(128)S(6)} %select_n.75, s32[1]{0:T(128)} %bitcast, ...), kind=kCustom, calls=%fused_computation.9 | custom fusion | flops 1000000000 | bytes 11011592 | tf_op jit(solution)/shard_map/panel/pallas_call | solution.py:272
  45.5 0.0 collective-permute-start.7
  45.5 4.2 %collective-permute-done.7 = f32[2,32,64,128]{3,2,1,0:T(8,128)S(1)} collective-permute-done((f32[2,32,64,128]{3,2,1,0:T(8,128)S(1)}, f32[2,32,64,128]{3,2,1,0:T(8,128)S(1)}, u32[]{:S(2)}, u32[]{:S(2)}) %collective-permute-start.7) | collective-permute-done | bytes 2097184 | tf_op jit(solution)/shard_map/ppermute | solution.py:218
  49.6 0.4 slice_add_fusion
  50.0 0.0 copy-start.5
  50.0 1.6 %collective-permute-start.8 = (f32[16,64,128]{2,1,0:T(8,128)S(1)}, f32[16,64,128]{2,1,0:T(8,128)S(1)}, u32[]{:S(2)}, u32[]{:S(2)}) collective-permute-start(f32[16,64,128]{2,1,0:T(8,128)S(1)} %get-tuple-element.41), channel_id=1, source_target_pairs={{0,4},{4,0},{8,12},{12,8},{16,20},{20,16},{24,28},{28,24},{1,5},{5... | collective-permute-start | bytes 1572872 | tf_op jit(solution)/shard_map/ppermute | solution.py:218
  51.6 1.3 %collective-permute-start.9 = (f32[16,64,128]{2,1,0:T(8,128)S(1)}, f32[16,64,128]{2,1,0:T(8,128)S(1)}, u32[]{:S(2)}, u32[]{:S(2)}) collective-permute-start(f32[16,64,128]{2,1,0:T(8,128)S(1)} %get-tuple-element.42), channel_id=1, source_target_pairs={{0,8},{4,12},{8,0},{12,4},{16,24},{20,28},{24,16},{28,20},{1,9},{5... | collective-permute-start | bytes 1572872 | tf_op jit(solution)/shard_map/ppermute | solution.py:218
  53.0 0.7 collective-permute-start.10
  53.7 0.0 collective-permute-start.3
  53.7 10.4 %collective-permute-done.8 = f32[16,64,128]{2,1,0:T(8,128)S(1)} collective-permute-done((f32[16,64,128]{2,1,0:T(8,128)S(1)}, f32[16,64,128]{2,1,0:T(8,128)S(1)}, u32[]{:S(2)}, u32[]{:S(2)}) %collective-permute-start.8) | collective-permute-done | bytes 524320 | tf_op jit(solution)/shard_map/ppermute | solution.py:218
  64.1 0.1 slice_add_fusion.7
  64.1 1.4 %collective-permute-done.9 = f32[16,64,128]{2,1,0:T(8,128)S(1)} collective-permute-done((f32[16,64,128]{2,1,0:T(8,128)S(1)}, f32[16,64,128]{2,1,0:T(8,128)S(1)}, u32[]{:S(2)}, u32[]{:S(2)}) %collective-permute-start.9) | collective-permute-done | bytes 524320 | tf_op jit(solution)/shard_map/ppermute | solution.py:218
  65.5 0.1 slice_add_fusion.4
  65.6 0.8 collective-permute-done.10
  66.4 0.9 collective-permute-start.11
  67.3 0.0 copy-done.5
  67.3 1.4 %collective-permute-start.13 = (f32[512,128]{1,0:T(8,128)S(1)}, f32[512,128]{1,0:T(8,128)S(1)}, u32[]{:S(2)}, u32[]{:S(2)}) collective-permute-start(f32[512,128]{1,0:T(8,128)S(1)} %copy-done.5), channel_id=1, source_target_pairs={{0,2},{1,3},{2,0},{3,1},{4,6},{5,7},{6,4},{7,5},{8,10},{9,11},{10,... | collective-permute-start | bytes 786440 | tf_op jit(solution)/shard_map/ppermute | solution.py:218
  68.7 0.0 collective-permute-start.14
  68.7 0.5 collective-permute-start.12
  69.2 0.0 collective-permute-done.3
  69.2 1.5 %collective-permute-start.16 = (f32[1024,128]{1,0:T(8,128)S(1)}, f32[1024,128]{1,0:T(8,128)S(1)}, u32[]{:S(2)}, u32[]{:S(2)}) collective-permute-start(f32[1024,128]{1,0:T(8,128)S(1)} %get-tuple-element.96), channel_id=1, source_target_pairs={{0,3},{1,2},{2,1},{3,0},{4,7},{5,6},{6,5},{7,4},{8,11},{9,10},{10,... | collective-permute-start | bytes 1572872 | tf_op jit(solution)/shard_map/ppermute | solution.py:218
  70.8 2.5 %collective-permute-done.11 = f32[8,64,128]{2,1,0:T(8,128)S(1)} collective-permute-done((f32[8,64,128]{2,1,0:T(8,128)S(1)}, f32[8,64,128]{2,1,0:T(8,128)S(1)}, u32[]{:S(2)}, u32[]{:S(2)}) %collective-permute-start.11) | collective-permute-done | bytes 262176 | tf_op jit(solution)/shard_map/ppermute | solution.py:218
  73.2 0.0 collective-permute-start.17
  73.3 4.4 %collective-permute-done.12 = f32[8,64,128]{2,1,0:T(8,128)S(1)} collective-permute-done((f32[8,64,128]{2,1,0:T(8,128)S(1)}, f32[8,64,128]{2,1,0:T(8,128)S(1)}, u32[]{:S(2)}, u32[]{:S(2)}) %collective-permute-start.12) | collective-permute-done | bytes 262176 | tf_op jit(solution)/shard_map/ppermute | solution.py:218
  77.7 0.0 collective-permute-done.13
  77.7 2.4 %collective-permute-start.15 = (f32[4,2,64,128]{3,2,0,1:T(8,128)S(1)}, f32[4,2,64,128]{3,2,0,1:T(8,128)S(1)}, u32[]{:S(2)}, u32[]{:S(2)}) collective-permute-start(f32[4,2,64,128]{3,2,0,1:T(8,128)S(1)} %pad_maximum_fusion), channel_id=1, source_target_pairs={{0,16},{4,20},{8,24},{12,28},{16,0},{20,4},{24,8},{28,12},{1,17},{... | collective-permute-start | bytes 786440 | tf_op jit(solution)/shard_map/ppermute | solution.py:218
  80.1 1.0 collective-permute-done.14
  81.1 0.0 copy-start.3
  81.1 11.2 %collective-permute-done.15 = f32[4,2,64,128]{3,2,0,1:T(8,128)S(1)} collective-permute-done((f32[4,2,64,128]{3,2,0,1:T(8,128)S(1)}, f32[4,2,64,128]{3,2,0,1:T(8,128)S(1)}, u32[]{:S(2)}, u32[]{:S(2)}) %collective-permute-start.15) | collective-permute-done | bytes 262176 | tf_op jit(solution)/shard_map/ppermute | solution.py:218
  92.4 0.0 copy-start.7
  92.4 0.0 collective-permute-done.16
  92.4 0.0 collective-permute-done.17
  92.4 1.2 %collective-permute-start.18 = (f32[2,2,64,128]{3,2,0,1:T(8,128)S(1)}, f32[2,2,64,128]{3,2,0,1:T(8,128)S(1)}, u32[]{:S(2)}, u32[]{:S(2)}) collective-permute-start(f32[2,2,64,128]{3,2,0,1:T(8,128)S(1)} %fusion.3), channel_id=1, source_target_pairs={{0,2},{1,3},{2,0},{3,1},{4,6},{5,7},{6,4},{7,5},{8,10},{9,11},{10,... | collective-permute-start | bytes 393224 | tf_op jit(solution)/shard_map/ppermute | solution.py:218
  93.7 0.0 copy-start.2
  93.7 3.7 %collective-permute-done.18 = f32[2,2,64,128]{3,2,0,1:T(8,128)S(1)} collective-permute-done((f32[2,2,64,128]{3,2,0,1:T(8,128)S(1)}, f32[2,2,64,128]{3,2,0,1:T(8,128)S(1)}, u32[]{:S(2)}, u32[]{:S(2)}) %collective-permute-start.18) | collective-permute-done | bytes 131104 | tf_op jit(solution)/shard_map/ppermute | solution.py:218
  97.5 0.0 copy-done.7
  97.5 0.7 bitcast_subtract_fusion
  (21 shorter events, 0.3 us)
Async XLA Ops:
  0.6 14.0 %copy-start.8 = (s32[144,1]{0,1:T(1,128)S(1)}, s32[144,1]{0,1:T(1,128)}, u32[]{:S(2)}) copy-start(s32[144,1]{0,1:T(1,128)} %param.9) | copy-start | bytes 1732
  0.7 14.0 %copy-start.9 = (s32[144]{0:T(256)S(1)}, s32[144]{0:T(256)}, u32[]{:S(2)}) copy-start(s32[144]{0:T(256)} %param.10) | copy-start | bytes 1732
  1.6 11.1 %collective-permute-start = (f32[512,128]{1,0:T(8,128)S(1)}, f32[512,128]{1,0:T(8,128)}, u32[]{:S(2)}, u32[]{:S(2)}) collective-permute-start(f32[512,128]{1,0:T(8,128)S(1)} %dynamic-slice_bitcast_fusion.3), channel_id=1, source_target_pairs={{0,1},{1,0},{2,3},{3,2},{4,5},{5,4},{6,7},{7,6},{8,9},{9,8},{10,11... | collective-permute-start | bytes 786440 | tf_op jit(solution)/shard_map/ppermute | solution.py:218
  3.1 6.5 %collective-permute-start.2 = (f32[256,128]{1,0:T(8,128)S(1)}, f32[256,128]{1,0:T(8,128)S(1)}, u32[]{:S(2)}, u32[]{:S(2)}) collective-permute-start(f32[256,128]{1,0:T(8,128)S(1)} %get-tuple-element.81), channel_id=1, source_target_pairs={{0,3},{1,2},{2,1},{3,0},{4,7},{5,6},{6,5},{7,4},{8,11},{9,10},{10,... | collective-permute-start | bytes 393224 | tf_op jit(solution)/shard_map/ppermute | solution.py:218
  5.8 9.1 %copy-start.1 = (f32[4,512,128]{2,1,0:T(8,128)S(1)}, f32[4,512,128]{2,1,0:T(8,128)}, u32[]{:S(2)}) copy-start(f32[4,512,128]{2,1,0:T(8,128)} %param.6) | copy-start | bytes 3145732
  5.8 7.0 %collective-permute-start.1 = (f32[256,128]{1,0:T(8,128)S(1)}, f32[256,128]{1,0:T(8,128)}, u32[]{:S(2)}, u32[]{:S(2)}) collective-permute-start(f32[256,128]{1,0:T(8,128)S(1)} %get-tuple-element.82), channel_id=1, source_target_pairs={{0,2},{1,3},{2,0},{3,1},{4,6},{5,7},{6,4},{7,5},{8,10},{9,11},{10,... | collective-permute-start | bytes 393224 | tf_op jit(solution)/shard_map/ppermute | solution.py:218
  12.8 22.7 %collective-permute-start.4 = (f32[1024,128]{1,0:T(8,128)}, f32[1024,128]{1,0:T(8,128)S(1)}, u32[]{:S(2)}, u32[]{:S(2)}) collective-permute-start(f32[1024,128]{1,0:T(8,128)} %get-tuple-element.35), channel_id=1, source_target_pairs={{0,1},{1,0},{2,3},{3,2},{4,5},{5,4},{6,7},{7,6},{8,9},{9,8},{10,11... | collective-permute-start | bytes 1572872 | tf_op jit(solution)/shard_map/ppermute | solution.py:218
  12.8 22.7 %collective-permute-start.5 = (f32[1024,128]{1,0:T(8,128)}, f32[1024,128]{1,0:T(8,128)}, u32[]{:S(2)}, u32[]{:S(2)}) collective-permute-start(f32[1024,128]{1,0:T(8,128)} %get-tuple-element.36), channel_id=1, source_target_pairs={{0,2},{1,3},{2,0},{3,1},{4,6},{5,7},{6,4},{7,5},{8,10},{9,11},{10,... | collective-permute-start | bytes 1572872 | tf_op jit(solution)/shard_map/ppermute | solution.py:218
  14.5 23.8 %collective-permute-start.6 = (f32[1024,128]{1,0:T(8,128)S(1)}, f32[1024,128]{1,0:T(8,128)}, u32[]{:S(2)}, u32[]{:S(2)}) collective-permute-start(f32[1024,128]{1,0:T(8,128)S(1)} %get-tuple-element.37), channel_id=1, source_target_pairs={{0,3},{1,2},{2,1},{3,0},{4,7},{5,6},{6,5},{7,4},{8,11},{9,10},{10,... | collective-permute-start | bytes 1572872 | tf_op jit(solution)/shard_map/ppermute | solution.py:218
  14.9 23.5 %copy-start = (f32[4,1024,128]{2,1,0:T(8,128)S(1)}, f32[4,1024,128]{2,1,0:T(8,128)}, u32[]{:S(2)}) copy-start(f32[4,1024,128]{2,1,0:T(8,128)} %param.7) | copy-start | bytes 6291460
  15.0 23.5 %copy-start.10 = (s32[4]{0:T(128)S(1)}, s32[4]{0:T(128)}, u32[]{:S(2)}) copy-start(s32[4]{0:T(128)} %param.8) | copy-start | bytes 52
  45.5 4.2 %collective-permute-start.7 = (f32[2,32,64,128]{3,2,1,0:T(8,128)S(1)}, f32[2,32,64,128]{3,2,1,0:T(8,128)S(1)}, u32[]{:S(2)}, u32[]{:S(2)}) collective-permute-start(f32[2,32,64,128]{3,2,1,0:T(8,128)S(1)} %get-tuple-element.91), channel_id=1, source_target_pairs={{0,1},{1,0},{2,3},{3,2},{4,5},{5,4},{6,7},{7,6},{8,9},{9,8},{10,11... | collective-permute-start | bytes 6291464 | tf_op jit(solution)/shard_map/ppermute | solution.py:218
  49.6 3.3 %copy-start.4 = (f32[1024,128]{1,0:T(8,128)S(1)}, f32[1024,128]{1,0:T(8,128)}, u32[]{:S(2)}) copy-start(f32[1024,128]{1,0:T(8,128)} %get-tuple-element.93) | copy-start | bytes 1572868
  49.6 4.1 %copy-start.6 = (f32[512,128]{1,0:T(8,128)S(1)}, f32[512,128]{1,0:T(8,128)}, u32[]{:S(2)}) copy-start(f32[512,128]{1,0:T(8,128)} %get-tuple-element.60) | copy-start | bytes 786436
  50.0 17.3 %copy-start.5 = (f32[512,128]{1,0:T(8,128)S(1)}, f32[512,128]{1,0:T(8,128)}, u32[]{:S(2)}) copy-start(f32[512,128]{1,0:T(8,128)} %get-tuple-element.64) | copy-start | bytes 786436
  50.0 14.0 %collective-permute-start.8 = (f32[16,64,128]{2,1,0:T(8,128)S(1)}, f32[16,64,128]{2,1,0:T(8,128)S(1)}, u32[]{:S(2)}, u32[]{:S(2)}) collective-permute-start(f32[16,64,128]{2,1,0:T(8,128)S(1)} %get-tuple-element.41), channel_id=1, source_target_pairs={{0,4},{4,0},{8,12},{12,8},{16,20},{20,16},{24,28},{28,24},{1,5},{5... | collective-permute-start | bytes 1572872 | tf_op jit(solution)/shard_map/ppermute | solution.py:218
  51.6 13.9 %collective-permute-start.9 = (f32[16,64,128]{2,1,0:T(8,128)S(1)}, f32[16,64,128]{2,1,0:T(8,128)S(1)}, u32[]{:S(2)}, u32[]{:S(2)}) collective-permute-start(f32[16,64,128]{2,1,0:T(8,128)S(1)} %get-tuple-element.42), channel_id=1, source_target_pairs={{0,8},{4,12},{8,0},{12,4},{16,24},{20,28},{24,16},{28,20},{1,9},{5... | collective-permute-start | bytes 1572872 | tf_op jit(solution)/shard_map/ppermute | solution.py:218
  53.0 13.4 %collective-permute-start.10 = (f32[1024,128]{1,0:T(8,128)S(1)}, f32[1024,128]{1,0:T(8,128)S(1)}, u32[]{:S(2)}, u32[]{:S(2)}) collective-permute-start(f32[1024,128]{1,0:T(8,128)S(1)} %copy-done.4), channel_id=1, source_target_pairs={{0,2},{1,3},{2,0},{3,1},{4,6},{5,7},{6,4},{7,5},{8,10},{9,11},{10,... | collective-permute-start | bytes 1572872 | tf_op jit(solution)/shard_map/ppermute | solution.py:218
  53.7 15.5 %collective-permute-start.3 = (f32[512,128]{1,0:T(8,128)S(1)}, f32[512,128]{1,0:T(8,128)S(1)}, u32[]{:S(2)}, u32[]{:S(2)}) collective-permute-start(f32[512,128]{1,0:T(8,128)S(1)} %copy-done.6), channel_id=1, source_target_pairs={{0,1},{1,0},{2,3},{3,2},{4,5},{5,4},{6,7},{7,6},{8,9},{9,8},{10,11... | collective-permute-start | bytes 786440 | tf_op jit(solution)/shard_map/ppermute | solution.py:218
  66.4 6.9 %collective-permute-start.11 = (f32[8,64,128]{2,1,0:T(8,128)S(1)}, f32[8,64,128]{2,1,0:T(8,128)S(1)}, u32[]{:S(2)}, u32[]{:S(2)}) collective-permute-start(f32[8,64,128]{2,1,0:T(8,128)S(1)} %get-tuple-element.44), channel_id=1, source_target_pairs={{0,8},{4,12},{8,0},{12,4},{16,24},{20,28},{24,16},{28,20},{1,9},{5... | collective-permute-start | bytes 786440 | tf_op jit(solution)/shard_map/ppermute | solution.py:218
  67.3 10.4 %collective-permute-start.13 = (f32[512,128]{1,0:T(8,128)S(1)}, f32[512,128]{1,0:T(8,128)S(1)}, u32[]{:S(2)}, u32[]{:S(2)}) collective-permute-start(f32[512,128]{1,0:T(8,128)S(1)} %copy-done.5), channel_id=1, source_target_pairs={{0,2},{1,3},{2,0},{3,1},{4,6},{5,7},{6,4},{7,5},{8,10},{9,11},{10,... | collective-permute-start | bytes 786440 | tf_op jit(solution)/shard_map/ppermute | solution.py:218
  68.7 12.4 %collective-permute-start.14 = (f32[512,128]{1,0:T(8,128)S(1)}, f32[512,128]{1,0:T(8,128)S(1)}, u32[]{:S(2)}, u32[]{:S(2)}) collective-permute-start(f32[512,128]{1,0:T(8,128)S(1)} %get-tuple-element.66), channel_id=1, source_target_pairs={{0,3},{1,2},{2,1},{3,0},{4,7},{5,6},{6,5},{7,4},{8,11},{9,10},{10,... | collective-permute-start | bytes 786440 | tf_op jit(solution)/shard_map/ppermute | solution.py:218
  68.7 8.9 %collective-permute-start.12 = (f32[8,64,128]{2,1,0:T(8,128)S(1)}, f32[8,64,128]{2,1,0:T(8,128)S(1)}, u32[]{:S(2)}, u32[]{:S(2)}) collective-permute-start(f32[8,64,128]{2,1,0:T(8,128)S(1)} %get-tuple-element.45), channel_id=1, source_target_pairs={{0,4},{4,0},{8,12},{12,8},{16,20},{20,16},{24,28},{28,24},{1,5},{5... | collective-permute-start | bytes 786440 | tf_op jit(solution)/shard_map/ppermute | solution.py:218
  69.2 23.1 %collective-permute-start.16 = (f32[1024,128]{1,0:T(8,128)S(1)}, f32[1024,128]{1,0:T(8,128)S(1)}, u32[]{:S(2)}, u32[]{:S(2)}) collective-permute-start(f32[1024,128]{1,0:T(8,128)S(1)} %get-tuple-element.96), channel_id=1, source_target_pairs={{0,3},{1,2},{2,1},{3,0},{4,7},{5,6},{6,5},{7,4},{8,11},{9,10},{10,... | collective-permute-start | bytes 1572872 | tf_op jit(solution)/shard_map/ppermute | solution.py:218
  73.2 19.1 %collective-permute-start.17 = (f32[1024,128]{1,0:T(8,128)S(1)}, f32[1024,128]{1,0:T(8,128)S(1)}, u32[]{:S(2)}, u32[]{:S(2)}) collective-permute-start(f32[1024,128]{1,0:T(8,128)S(1)} %get-tuple-element.98), channel_id=1, source_target_pairs={{0,1},{1,0},{2,3},{3,2},{4,5},{5,4},{6,7},{7,6},{8,9},{9,8},{10,11... | collective-permute-start | bytes 1572872 | tf_op jit(solution)/shard_map/ppermute | solution.py:218
  77.7 14.6 %collective-permute-start.15 = (f32[4,2,64,128]{3,2,0,1:T(8,128)S(1)}, f32[4,2,64,128]{3,2,0,1:T(8,128)S(1)}, u32[]{:S(2)}, u32[]{:S(2)}) collective-permute-start(f32[4,2,64,128]{3,2,0,1:T(8,128)S(1)} %pad_maximum_fusion), channel_id=1, source_target_pairs={{0,16},{4,20},{8,24},{12,28},{16,0},{20,4},{24,8},{28,12},{1,17},{... | collective-permute-start | bytes 786440 | tf_op jit(solution)/shard_map/ppermute | solution.py:218
  81.1 16.3 %copy-start.3 = (f32[4,512,128]{2,1,0:T(8,128)}, f32[4,512,128]{2,1,0:T(8,128)S(1)}, u32[]{:S(2)}) copy-start(f32[4,512,128]{2,1,0:T(8,128)S(1)} %bitcast_dynamic-update-slice_fusion.4) | copy-start | bytes 3145732
  92.4 5.1 %copy-start.7 = (f32[2,128,128]{2,1,0:T(8,128)S(1)}, f32[2,128,128]{2,1,0:T(8,128)}, u32[]{:S(2)}) copy-start(f32[2,128,128]{2,1,0:T(8,128)} %param.11) | copy-start | bytes 393220
  92.4 5.0 %collective-permute-start.18 = (f32[2,2,64,128]{3,2,0,1:T(8,128)S(1)}, f32[2,2,64,128]{3,2,0,1:T(8,128)S(1)}, u32[]{:S(2)}, u32[]{:S(2)}) collective-permute-start(f32[2,2,64,128]{3,2,0,1:T(8,128)S(1)} %fusion.3), channel_id=1, source_target_pairs={{0,2},{1,3},{2,0},{3,1},{4,6},{5,7},{6,4},{7,5},{8,10},{9,11},{10,... | collective-permute-start | bytes 393224 | tf_op jit(solution)/shard_map/ppermute | solution.py:218
  93.7 4.4 %copy-start.2 = (f32[4,1024,128]{2,1,0:T(8,128)}, f32[4,1024,128]{2,1,0:T(8,128)S(1)}, u32[]{:S(2)}) copy-start(f32[4,1024,128]{2,1,0:T(8,128)S(1)} %bitcast_dynamic-update-slice_fusion) | copy-start | bytes 6291460

commit v5 on v4

--- a/solution.py
+++ b/solution.py
@@ -112,7 +112,7 @@
     return dot(left[0], right[0]) + (dot(left[0], right[1]) + dot(left[1], right[0]))
 
 
-def factor_kernel(info, own_ref, r1, r2, r3, l0, l1, l2, l3, mt, a, l, sems):
+def factor_kernel(info, own_ref, r1, r2, r3, l, mt, a, sems):
     me = info[0]
     side = me // 2
     far_rows = pl.ds((1 - side) * (W // 2), W // 2)
@@ -150,20 +150,18 @@
             for j in range(i + 1, k):
                 total = total + dot_nt(mt[j, pl.ds(i * B, B), :], l[j, here, :])
             mt[k, pl.ds(i * B, B), :] = dot_nt(-total, inv)
-    outs = [l0, l1, l2, l3]
-    copies = [pltpu.make_async_copy(l.at[me ^ m], outs[m], sems.at[m]) for m in range(NB)]
-    for c in copies:
-        c.start()
-    for c in copies:
-        c.wait()
-
-
-def panel_kernel(info, counts, tgt_a, tgt_b, own_ref, r1, r2, r3, mt, x0, x1, x2, x3, keep, send, xh, xl):
+
+
+def panel_kernel(
+    info, counts, tgt_a, tgt_b, own_ref, r1, r2, r3, mt, l, own, near, far, keep, send_a, send_b, xh, xl
+):
     me = info[0]
     count = counts[me]
     rows = P_SIZE * B
     ins = [own_ref.at[me], r1, r2, r3]
-    outs = [x0, x1, x2, x3]
+    outs = [own, near, far.at[0], far.at[1]]
+    for m in range(NB):
+        outs[m][pl.ds(rows, W), :] = l[me ^ m]
     live = lax.broadcasted_iota(jnp.int32, (rows, B), 0) < count * B
     parts = [split_bf16(jnp.where(live, ref[...], 0.0)) for ref in ins]
     left = [jnp.concatenate([part[n] for part in parts], axis=1) for n in range(2)]
@@ -173,14 +171,15 @@
             for k in range(NB)
         ]
         got = dot3(left, split_bf16(jnp.concatenate(right, axis=0)), ((1,), (0,)))
-        outs[c][...] = got[:, :B]
-        outs[c + 1][...] = got[:, B:]
+        outs[c][pl.ds(0, rows), :] = got[:, :B]
+        outs[c + 1][pl.ds(0, rows), :] = got[:, B:]
         high, low = split_bf16(got)
         xh[:, pl.ds(c * B, 2 * B)] = high
         xl[:, pl.ds(c * B, 2 * B)] = low
 
     keep[...] = jnp.zeros_like(keep)
-    send[...] = jnp.zeros_like(send)
+    send_a[...] = jnp.zeros_like(send_a)
+    send_b[...] = jnp.zeros_like(send_b)
     half, strip = keep.shape[1:3]
     for j in range(0, P_SIZE, 2):
 
@@ -194,11 +193,11 @@
                     block = got[(i - j) * B : (i - j + 1) * B, n * B : (n + 1) * B]
                     pair = i * (i + 1) // 2 + j + n
                     away = (tgt_a[pair] >= half).astype(jnp.float32)
-                    for stream, tgt in enumerate((tgt_a, tgt_b)):
+                    for stream, (tgt, send) in enumerate(((tgt_a, send_a), (tgt_b, send_b))):
                         at = lax.rem(tgt[pair], half)
                         piece = block[stream * strip : (stream + 1) * strip]
                         keep[stream, at] += piece * (1.0 - away)
-                        send[stream, at] += piece * away
+                        send[at] += piece * away
 
 
 SMEM = pl.BlockSpec(memory_space=pltpu.SMEM)
@@ -237,7 +236,10 @@
     half_of = lambda x, m: lax.dynamic_slice(
         x, (me ^ m, (me // 2) * (W // 2), 0), (1, W // 2, B)
     ).reshape(W // 2, B)
-    diag_in = [swap(own(diag_block, m) if m == 1 else half_of(diag_block, m), "narrow", m) for m in masks]
+    halves = [half_of(diag_block, m) for m in masks[1:]]
+    halves, near_block = lax.optimization_barrier((halves, diag_block))
+    diag_in = [swap(own(near_block, 1), "narrow", 1)]
+    diag_in += [swap(part, "narrow", m) for m, part in zip(masks[1:], halves)]
     panel_out = [own(panel, m) for m in masks]
     diag_in, panel_out = lax.optimization_barrier((diag_in, panel_out))
     panel_in = [swap(panel_out[m - 1], "narrow", m) for m in masks]
@@ -253,76 +255,78 @@
     tgt_b = relative_index(owner, slot, wide_me, me, steps_b)
     info = me.astype(jnp.int32).reshape(1)
 
-    slab = jax.ShapeDtypeStruct((W, B), jnp.float32)
-    *l_parts, mt = pl.pallas_call(
+    whole = jax.ShapeDtypeStruct((NB, W, B), jnp.float32)
+    l, mt = pl.pallas_call(
         factor_kernel,
-        out_shape=[slab] * NB + [jax.ShapeDtypeStruct((NB, W, B), jnp.float32)],
+        out_shape=[whole, whole],
         in_specs=[SMEM] + [ANY] * NB,
-        out_specs=[ANY] * NB + [VMEM],
-        scratch_shapes=[pltpu.VMEM((NB, W, B), jnp.float32)] * 2 + [pltpu.SemaphoreType.DMA((NB,))],
-        compiler_params=pltpu.CompilerParams(vmem_limit_bytes=32 * 2**20),
+        out_specs=[VMEM] * 2,
+        scratch_shapes=[pltpu.VMEM((NB, W, B), jnp.float32), pltpu.SemaphoreType.DMA((NB,))],
+        compiler_params=pltpu.CompilerParams(vmem_limit_bytes=16 * 2**20),
         cost_estimate=pl.CostEstimate(flops=2 * 10**8, bytes_accessed=4 * 10**6, transcendentals=0),
         name="factor",
     )(info, diag_block, *diag_in)
 
     rows = P_SIZE * B
     blocks = wide_count * narrow_count * T_DEV
-    slab = jax.ShapeDtypeStruct((rows, B), jnp.float32)
-    part = jax.ShapeDtypeStruct((2, blocks // 2, B // 2, B), jnp.float32)
-    *x_parts, keep, send = pl.pallas_call(
+    slab = jax.ShapeDtypeStruct((rows + W, B), jnp.float32)
+    pair = jax.ShapeDtypeStruct((2, rows + W, B), jnp.float32)
+    part = jax.ShapeDtypeStruct((blocks // 2, B // 2, B), jnp.float32)
+    parts = jax.ShapeDtypeStruct((2, blocks // 2, B // 2, B), jnp.float32)
+    home, near, far, keep, send_a, send_b = pl.pallas_call(
         panel_kernel,
-        out_shape=[slab] * NB + [part, part],
-        in_specs=[SMEM] * 4 + [VMEM] * (NB + 1),
-        out_specs=[VMEM] * (NB + 2),
+        out_shape=[slab, slab, pair, parts, part, part],
+        in_specs=[SMEM] * 4 + [VMEM] * (NB + 2),
+        out_specs=[VMEM] * 6,
         scratch_shapes=[pltpu.VMEM((rows, W), jnp.bfloat16)] * 2,
-        compiler_params=pltpu.CompilerParams(vmem_limit_bytes=52 * 2**20),
+        compiler_params=pltpu.CompilerParams(vmem_limit_bytes=20 * 2**20 + 4 * blocks * B * B),
         cost_estimate=pl.CostEstimate(flops=10**9, bytes_accessed=10 * 10**6, transcendentals=0),
         name="panel",
-    )(info, panel_count, tgt_a, tgt_b, panel, *panel_in, mt)
-
-    l_back = [swap(l_parts[m], "narrow", m) for m in masks]
-    x_back = [swap(x_parts[m], "narrow", m) for m in masks]
-
-    got = swap(send, "narrow", 1)
+    )(info, panel_count, tgt_a, tgt_b, panel, *panel_in, mt, l)
+
+    far = swap(far, "narrow", 2)
+    near = swap(near, "narrow", 1)
+
+    got_a, got_b = swap(send_a, "narrow", 1), swap(send_b, "narrow", 1)
+    keep_a, keep_b = keep[0], keep[1]
     half = blocks // 4
-    upper = lambda u, n: u[n, half:]
-    lower = lambda u, n: u[n, :half]
-    send_a = upper(keep, 0) + upper(got, 0)
-    send_b = upper(keep, 1) + upper(got, 1)
-    keep_a = lower(keep, 0) + lower(got, 0)
-    keep_b = lower(keep, 1) + lower(got, 1)
     for n in (1, 2):
-        if n == 2:
-            send_a, send_b, x_back[1] = lax.optimization_barrier((send_a, send_b, x_back[1]))
-        else:
-            send_a, send_b = lax.optimization_barrier((send_a, send_b))
-        got_a = swap(send_a, *steps_a[n])
-        got_b = swap(send_b, *steps_b[n])
-        half = half // 2
         send_a, send_b = keep_a[half:] + got_a[half:], keep_b[half:] + got_b[half:]
         keep_a, keep_b = keep_a[:half] + got_a[:half], keep_b[:half] + got_b[:half]
-    send = jnp.stack([send_a, send_b], axis=1)
-    keep = jnp.stack([keep_a, keep_b], axis=1)
-    for n in range(3, len(steps_a)):
-        if n == 3:
-            send, l_back[1] = lax.optimization_barrier((send, l_back[1]))
-        if n == len(steps_a) - 1:
-            send, x_back[2], x_back[0] = lax.optimization_barrier((send, x_back[2], x_back[0]))
-        got = swap(send, *steps_a[n])
-        if n + 1 < len(steps_a):
-            half = half // 2
-            send = keep[half:] + got[half:]
-            keep = keep[:half] + got[:half]
-    updated = ancestor - (keep + got).reshape(ancestor.shape)
-
-    def give_back(own_part, others):
-        back = [own_part] + others
-        out = jnp.zeros((NB,) + own_part.shape, jnp.float32)
-        for m in range(NB):
-            out = lax.dynamic_update_index_in_dim(out, back[m], me ^ m, 0)
+        if n == 2:
+            send_a, send_b = lax.optimization_barrier((send_a, send_b))
+        got_a, got_b = swap(send_a, *steps_a[n]), swap(send_b, *steps_b[n])
+        half = half // 2
+
+    def rows_of(n, size):
+        at = slice(n * size, (n + 1) * size)
+        return jnp.concatenate([keep_a[at] + got_a[at], keep_b[at] + got_b[at]], axis=1)
+
+    rest = steps_a[3:]
+    while len(rest) > 2:
+        got = swap(rows_of(1, half), *rest.pop(0))
+        total = rows_of(0, half) + got
+        half = half // 2
+        keep_a, keep_b = total[:, : B // 2], total[:, B // 2 :]
+        got_a, got_b = jnp.zeros_like(keep_a), jnp.zeros_like(keep_b)
+    (_, wide_mask), (_, narrow_mask) = rest
+    both = wide_mask * narrow_count + narrow_mask
+    got = [
+        lax.ppermute(rows_of(3, T_DEV), ("wide", "narrow"), xor_pairs(wide_count * narrow_count, both)),
+        swap(rows_of(2, T_DEV), *rest[0]),
+        swap(rows_of(1, T_DEV), *rest[1]),
+    ]
+    got, far = lax.optimization_barrier((got, far))
+    relayed = swap(far[1], "narrow", 1)
+    updated = ancestor - (rows_of(0, T_DEV) + (got[0] + (got[1] + got[2])))
+
+    def assemble(at, size):
+        out = jnp.zeros((NB, size, B), jnp.float32)
+        for m, piece in enumerate((home, near, far[0], relayed)):
+            out = lax.dynamic_update_index_in_dim(out, piece[at : at + size], me ^ m, 0)
         return out
 
-    return (give_back(l_parts[0], l_back), give_back(x_parts[0], x_back), updated)
+    return (assemble(rows, W), assemble(0, rows), updated)
 
 
 def solution(mesh):

time: 98.4 us -> 101 us (1.026)
  other arithmetic: 29 us -> 4.48 us
  Pallas kernels: 0 us -> 24.3 us
  local copies, waits for them, and re-layouts: 4.92 us -> 9.62 us
  waiting for transfers between devices: 46.6 us -> 42.9 us
  starting transfers between devices: 16.7 us -> 19 us
    pallas_call x2 -> x0, other arithmetic: 27.5 us -> none  [the longest x1 20.5 us: local(): pl.pallas_call(factor_kernel, out_shape=[slab] * NB + [jax.ShapeDtypeStru...]
    pallas_call x0 -> x2, Pallas kernels: none -> 24.3 us  [the longest x1 18.9 us: local(): pl.pallas_call(factor_kernel, out_shape=[whole, whole], in_specs=[SMEM] +...]
    unnamed x22 -> x24, local copies, waits for them, and re-layouts: 0.06 us -> 3.85 us
    ppermute x19 -> x17, waiting for transfers between devices: 46.6 us -> 42.9 us  [swap(): return lax.ppermute(x, axis, xor_pairs(lax.axis_size(axis), mask))]
    add x1 -> x2, other arithmetic: 0.07 us -> 2.4 us  [local(): keep_b[:half] + got_b[:half]]
    ppermute x19 -> x17, starting transfers between devices: 16.7 us -> 18.6 us  [swap(): return lax.ppermute(x, axis, xor_pairs(lax.axis_size(axis), mask))]
    add x1, other arithmetic: 0.07 us -> 1.09 us  [local(): keep_a[:half] + got_a[:half]]
  transfers between devices with their start and end apart: 19 -> 18, of which waited for: 12 -> 12; matrix products, arithmetic and copies ran while one was open for 25% -> 6% of each run, Pallas kernels for 0% -> 19%
where the time goes in v5:
time: 101 us
  waiting for transfers between devices  42.9 us (42%)
  Pallas kernels  24.3 us (24%)
  starting transfers between devices  19 us (19%)
  local copies, waits for them, and re-layouts  9.62 us (10%)
  other arithmetic  4.48 us (4%)
    ppermute x17, waiting for transfers between devices, swap(): return lax.ppermute(x, axis, xor_pairs(lax.axis_size(axis), mask))  42.9 us
    pallas_call x1, Pallas kernels, local(): pl.pallas_call(factor_kernel, out_shape=[whole, whole], in_specs=[SMEM] +...  18.9 us
    ppermute x17, starting transfers between devices, swap(): return lax.ppermute(x, axis, xor_pairs(lax.axis_size(axis), mask))  18.6 us
    pallas_call x1, Pallas kernels, local(): pl.pallas_call(panel_kernel, out_shape=[slab, slab, pair, parts, part, pa...  5.41 us
    unnamed x24, local copies, waits for them, and re-layouts  3.85 us
    squeeze x2, local copies, waits for them, and re-layouts, local(): own = lambda x, m: lax.dynamic_index_in_dim(x, me ^ m, 0, keepdims=False)  3.49 us
    add x2, other arithmetic, local(): keep_b[:half] + got_b[:half]  2.4 us
  transfers between devices with their start and end apart: 18, of which 12 were waited for; matrix products, arithmetic and copies ran while one was open for 6% of the time, Pallas kernels for 19%

profile of v5, /device:TPU:0, one launch (start us, length us, event | category | flops | bytes accessed | tf_op | source)
XLA Modules:
  0.0 101.3 jit_solution(13557858477761212202)
XLA Ops:
  0.7 0.0 copy-start.10
  0.7 0.0 copy-start.11
  0.7 0.0 copy-start.1
  0.7 1.8 %dynamic-slice_bitcast_fusion.4 = (f32[256,128]{1,0:T(8,128)}, f32[256,128]{1,0:T(8,128)}) fusion(f32[4,512,128]{2,1,0:T(8,128)} %own_ref.2, s32[]{:T(128)S(6)} %select_n.79, s32[]{:T(128)S(6)} %select_n.78, s32[]{:T(128)S(6)} %select_n.76), kind=kLoop, calls=%fused_computation.30 | loop fusion | bytes 524300 | tf_op jit(solution)/shard_map/reshape | solution.py:238
  2.5 1.0 dynamic-slice_bitcast_fusion.3
  3.4 0.0 copy-start
  3.5 0.0 copy-start.4
  3.5 0.5 collective-permute-start
  4.0 2.6 %collective-permute-start.1 = (f32[256,128]{1,0:T(8,128)}, f32[256,128]{1,0:T(8,128)S(1)}, u32[]{:S(2)}, u32[]{:S(2)}) collective-permute-start(f32[256,128]{1,0:T(8,128)} %get-tuple-element.27), channel_id=1, source_target_pairs={{0,2},{1,3},{2,0},{3,1},{4,6},{5,7},{6,4},{7,5},{8,10},{9,11},{10,... | collective-permute-start | bytes 393224 | tf_op jit(solution)/shard_map/ppermute | solution.py:217
  6.6 0.1 collective-permute-start.2
  6.6 2.5 %dynamic-slice_bitcast_fusion = (f32[1024,128]{1,0:T(8,128)}, f32[1024,128]{1,0:T(8,128)}, f32[1024,128]{1,0:T(8,128)}) fusion(f32[4,1024,128]{2,1,0:T(8,128)} %own_ref.3, s32[]{:T(128)S(6)} %select_n.79, s32[]{:T(128)S(6)} %select_n.76, s32[]{:T(128)S(6)} %select_n.80), kind=kLoop, calls=%fused_computation.11 | loop fusion | bytes 3145740 | tf_op jit(solution)/shard_map/jit(dynamic_index_in_dim)/squeeze | solution.py:235
  9.1 2.0 %collective-permute-done.1.r2 = f32[256,128]{1,0:T(8,128)S(1)} collective-permute-done((f32[256,128]{1,0:T(8,128)}, f32[256,128]{1,0:T(8,128)S(1)}, u32[]{:S(2)}, u32[]{:S(2)}) %collective-permute-start.1) | collective-permute-done | bytes 131104 | tf_op jit(solution)/shard_map/ppermute | solution.py:217
  11.1 2.3 %collective-permute-done.2.r3 = f32[256,128]{1,0:T(8,128)S(1)} collective-permute-done((f32[256,128]{1,0:T(8,128)}, f32[256,128]{1,0:T(8,128)S(1)}, u32[]{:S(2)}, u32[]{:S(2)}) %collective-permute-start.2) | collective-permute-done | bytes 131104 | tf_op jit(solution)/shard_map/ppermute | solution.py:217
  13.4 0.7 copy-done.2
  14.1 0.0 collective-permute-done.r1
  14.1 0.1 collective-permute-start.3
  14.2 1.7 %collective-permute-start.4 = (f32[1024,128]{1,0:T(8,128)}, f32[1024,128]{1,0:T(8,128)}, u32[]{:S(2)}, u32[]{:S(2)}) collective-permute-start(f32[1024,128]{1,0:T(8,128)} %get-tuple-element.30), channel_id=1, source_target_pairs={{0,2},{1,3},{2,0},{3,1},{4,6},{5,7},{6,4},{7,5},{8,10},{9,11},{10,... | collective-permute-start | bytes 1572872 | tf_op jit(solution)/shard_map/ppermute | solution.py:217
  15.9 0.0 collective-permute-start.5
  15.9 0.0 copy-done.11
  15.9 0.1 multiply_add_fusion
  16.0 0.1 multiply_add_fusion.1.tgt_a
  16.1 0.0 copy-start.3
  16.2 0.9 copy-done.3
  17.1 18.9 %factor.1 = (f32[4,512,128]{2,1,0:T(8,128)S(1)}, f32[4,512,128]{2,1,0:T(8,128)S(1)}) custom-call(s32[1]{0:T(128)} %bitcast.info, f32[4,512,128]{2,1,0:T(8,128)S(1)} %copy-done.1, f32[512,128]{1,0:T(8,128)S(1)} %collective-permute-done.r1, f32[256,128]{1,0:T(8,128)S(1)} %collective-permute-done.1.r2, f32[256,128]{1,0:T(8,128)S(1)} %copy-done.3), custom_call_target="tpu_custom_call" | custom-call | flops 200000000 | bytes 4000000 | tf_op jit(solution)/shard_map/factor/pallas_call | solution.py:259
  36.0 0.0 collective-permute-done.3.r1
  36.0 0.0 collective-permute-done.4.r2
  36.0 3.4 %collective-permute-done.5.r3 = f32[1024,128]{1,0:T(8,128)} collective-permute-done((f32[1024,128]{1,0:T(8,128)}, f32[1024,128]{1,0:T(8,128)}, u32[]{:S(2)}, u32[]{:S(2)}) %collective-permute-start.5) | collective-permute-done | bytes 524320 | tf_op jit(solution)/shard_map/ppermute | solution.py:217
  39.4 5.4 %panel.1 = (f32[1536,128]{1,0:T(8,128)S(1)}, f32[1536,128]{1,0:T(8,128)S(1)}, f32[2,1536,128]{2,1,0:T(8,128)S(1)}, f32[2,32,64,128]{3,2,1,0:T(8,128)S(1)}, f32[3...) custom-call(s32[1]{0:T(128)} %bitcast.info, s32[4]{0:T(128)S(1)} %copy-done.4, s32[36]{0:T(128)S(1)} %multiply_add_fusion.1.tgt_a, ...), custom_call_target="tpu_custom_call" | custom-call | flops 1000000000 | bytes 10000000 | tf_op jit(solution)/shard_map/panel/pallas_call | solution.py:276
  44.8 0.0 copy-start.5
  44.8 0.0 copy-start.6
  44.8 0.1 collective-permute-start.7
  44.9 0.5 collective-permute-start.9
  45.4 2.1 %collective-permute-done.7 = f32[32,64,128]{2,1,0:T(8,128)S(1)} collective-permute-done((f32[32,64,128]{2,1,0:T(8,128)S(1)}, f32[32,64,128]{2,1,0:T(8,128)S(1)}, u32[]{:S(2)}, u32[]{:S(2)}) %collective-permute-start.7) | collective-permute-done | bytes 1048608 | tf_op jit(solution)/shard_map/ppermute | solution.py:217
  47.6 1.5 %collective-permute-done.9 = f32[32,64,128]{2,1,0:T(8,128)S(1)} collective-permute-done((f32[32,64,128]{2,1,0:T(8,128)S(1)}, f32[32,64,128]{2,1,0:T(8,128)S(1)}, u32[]{:S(2)}, u32[]{:S(2)}) %collective-permute-start.9) | collective-permute-done | bytes 1048608 | tf_op jit(solution)/shard_map/ppermute | solution.py:217
  49.1 1.3 %slice_add_fusion.1 = (f32[16,64,128]{2,1,0:T(8,128)S(1)}, f32[16,64,128]{2,1,0:T(8,128)}, f32[16,64,128]{2,1,0:T(8,128)S(1)}, f32[16,64,128]{2,1,0:T(8,128)S(1)}) fusion(f32[32,64,128]{2,1,0:T(8,128)S(1)} %collective-permute-done.9, f32[2,32,64,128]{3,2,1,0:T(8,128)S(1)} %get-tuple-element.39, f32[32,64,128]{2,1,0:T(8,128)S(1)} %collective-permute-done.7), kind=kLoop, calls=%fused_computation.6 | loop fusion | flops 524288 | bytes 6291456 | tf_op jit(solution)/shard_map/add | solution.py:295
  50.4 2.7 %collective-permute-start.10 = (f32[16,64,128]{2,1,0:T(8,128)}, f32[16,64,128]{2,1,0:T(8,128)}, u32[]{:S(2)}, u32[]{:S(2)}) collective-permute-start(f32[16,64,128]{2,1,0:T(8,128)} %get-tuple-element.53), channel_id=1, source_target_pairs={{0,8},{4,12},{8,0},{12,4},{16,24},{20,28},{24,16},{28,20},{1,9},{5... | collective-permute-start | bytes 1572872 | tf_op jit(solution)/shard_map/ppermute | solution.py:217
  53.1 1.5 %collective-permute-start.8 = (f32[16,64,128]{2,1,0:T(8,128)S(1)}, f32[16,64,128]{2,1,0:T(8,128)}, u32[]{:S(2)}, u32[]{:S(2)}) collective-permute-start(f32[16,64,128]{2,1,0:T(8,128)S(1)} %get-tuple-element.56), channel_id=1, source_target_pairs={{0,4},{4,0},{8,12},{12,8},{16,20},{20,16},{24,28},{28,24},{1,5},{5... | collective-permute-start | bytes 1572872 | tf_op jit(solution)/shard_map/ppermute | solution.py:217
  54.6 1.3 %collective-permute-start.16 = (f32[2,1536,128]{2,1,0:T(8,128)}, f32[2,1536,128]{2,1,0:T(8,128)S(1)}, u32[]{:S(2)}, u32[]{:S(2)}) collective-permute-start(f32[2,1536,128]{2,1,0:T(8,128)} %copy-done.5), channel_id=1, source_target_pairs={{0,2},{1,3},{2,0},{3,1},{4,6},{5,7},{6,4},{7,5},{8,10},{9,11},{10,... | collective-permute-start | bytes 4718600 | tf_op jit(solution)/shard_map/ppermute | solution.py:217
  55.9 0.0 collective-permute-start.6
  55.9 9.9 %collective-permute-done.10 = f32[16,64,128]{2,1,0:T(8,128)} collective-permute-done((f32[16,64,128]{2,1,0:T(8,128)}, f32[16,64,128]{2,1,0:T(8,128)}, u32[]{:S(2)}, u32[]{:S(2)}) %collective-permute-start.10) | collective-permute-done | bytes 524320 | tf_op jit(solution)/shard_map/ppermute | solution.py:217
  65.8 1.1 %slice_add_fusion.4 = (f32[8,64,128]{2,1,0:T(8,128)S(1)}, f32[8,64,128]{2,1,0:T(8,128)S(1)}) fusion(f32[16,64,128]{2,1,0:T(8,128)} %collective-permute-done.10, f32[16,64,128]{2,1,0:T(8,128)S(1)} %get-tuple-element.52), kind=kLoop, calls=%fused_computation.16 | loop fusion | flops 131072 | bytes 1572864 | tf_op jit(solution)/shard_map/add | solution.py:295
  66.9 0.2 collective-permute-done.8
  67.1 1.1 %slice_add_fusion.7 = (f32[8,64,128]{2,1,0:T(8,128)S(1)}, f32[8,64,128]{2,1,0:T(8,128)S(1)}) fusion(f32[16,64,128]{2,1,0:T(8,128)} %collective-permute-done.8, f32[16,64,128]{2,1,0:T(8,128)S(1)} %get-tuple-element.57), kind=kLoop, calls=%fused_computation.19 | loop fusion | flops 131072 | bytes 1572864 | tf_op jit(solution)/shard_map/add | solution.py:295
  68.2 1.7 %collective-permute-start.11 = (f32[8,64,128]{2,1,0:T(8,128)S(1)}, f32[8,64,128]{2,1,0:T(8,128)S(1)}, u32[]{:S(2)}, u32[]{:S(2)}) collective-permute-start(f32[8,64,128]{2,1,0:T(8,128)S(1)} %get-tuple-element.42), channel_id=1, source_target_pairs={{0,8},{4,12},{8,0},{12,4},{16,24},{20,28},{24,16},{28,20},{1,9},{5... | collective-permute-start | bytes 786440 | tf_op jit(solution)/shard_map/ppermute | solution.py:217
  69.8 0.1 broadcast_in_dim.32
  70.0 1.6 %collective-permute-start.12 = (f32[8,64,128]{2,1,0:T(8,128)S(1)}, f32[8,64,128]{2,1,0:T(8,128)S(1)}, u32[]{:S(2)}, u32[]{:S(2)}) collective-permute-start(f32[8,64,128]{2,1,0:T(8,128)S(1)} %get-tuple-element.43), channel_id=1, source_target_pairs={{0,4},{4,0},{8,12},{12,8},{16,20},{20,16},{24,28},{28,24},{1,5},{5... | collective-permute-start | bytes 786440 | tf_op jit(solution)/shard_map/ppermute | solution.py:217
  71.6 0.1 broadcast_in_dim.28
  71.7 4.4 %collective-permute-done.11 = f32[8,64,128]{2,1,0:T(8,128)S(1)} collective-permute-done((f32[8,64,128]{2,1,0:T(8,128)S(1)}, f32[8,64,128]{2,1,0:T(8,128)S(1)}, u32[]{:S(2)}, u32[]{:S(2)}) %collective-permute-start.11) | collective-permute-done | bytes 262176 | tf_op jit(solution)/shard_map/ppermute | solution.py:217
  76.1 1.4 %collective-permute-done.12 = f32[8,64,128]{2,1,0:T(8,128)S(1)} collective-permute-done((f32[8,64,128]{2,1,0:T(8,128)S(1)}, f32[8,64,128]{2,1,0:T(8,128)S(1)}, u32[]{:S(2)}, u32[]{:S(2)}) %collective-permute-start.12) | collective-permute-done | bytes 262176 | tf_op jit(solution)/shard_map/ppermute | solution.py:217
  77.6 0.7 collective-permute-start.15
  78.3 3.5 %collective-permute-start.14 = (f32[2,128,128]{2,1,0:T(8,128)S(1)}, f32[2,128,128]{2,1,0:T(8,128)S(1)}, u32[]{:S(2)}, u32[]{:S(2)}) collective-permute-start(f32[2,128,128]{2,1,0:T(8,128)S(1)} %pad_maximum_fusion.1), channel_id=1, source_target_pairs={{0,16},{4,20},{8,24},{12,28},{16,0},{20,4},{24,8},{28,12},{1,17},{... | collective-permute-start | bytes 393224 | tf_op jit(solution)/shard_map/ppermute | solution.py:217
  81.9 0.4 collective-permute-start.13
  82.2 0.0 collective-permute-done.6
  82.3 12.6 %collective-permute-done.16 = f32[2,1536,128]{2,1,0:T(8,128)S(1)} collective-permute-done((f32[2,1536,128]{2,1,0:T(8,128)}, f32[2,1536,128]{2,1,0:T(8,128)S(1)}, u32[]{:S(2)}, u32[]{:S(2)}) %collective-permute-start.16) | collective-permute-done | bytes 1572896 | tf_op jit(solution)/shard_map/ppermute | solution.py:217
  94.9 1.6 %collective-permute-done.15 = f32[2,128,128]{2,1,0:T(8,128)S(1)} collective-permute-done((f32[2,128,128]{2,1,0:T(8,128)S(1)}, f32[2,128,128]{2,1,0:T(8,128)S(1)}, u32[]{:S(2)}, u32[]{:S(2)}) %collective-permute-start.15) | collective-permute-done | bytes 131104 | tf_op jit(solution)/shard_map/ppermute | solution.py:217
  96.5 0.0 collective-permute-done.14
  96.5 0.0 collective-permute-done.13
  96.5 0.1 slice_bitcast_fusion
  96.6 0.1 collective-permute-start.17
  96.7 0.7 fusion.4
  97.5 1.5 %collective-permute-done.17 = f32[1536,128]{1,0:T(8,128)S(1)} collective-permute-done((f32[1536,128]{1,0:T(8,128)S(1)}, f32[1536,128]{1,0:T(8,128)S(1)}, u32[]{:S(2)}, u32[]{:S(2)}) %collective-permute-start.17) | collective-permute-done | bytes 786464 | tf_op jit(solution)/shard_map/ppermute | solution.py:217
  99.0 0.0 copy-start.7
  99.0 1.3 %copy-done.7 = f32[4,1024,128]{2,1,0:T(8,128)} copy-done((f32[4,1024,128]{2,1,0:T(8,128)}, f32[4,1024,128]{2,1,0:T(8,128)S(1)}, u32[]{:S(2)}) %copy-start.7) | copy-done | bytes 2097176
  100.3 1.0 copy-done.8
  (23 shorter events, 0.4 us)
Async XLA Ops:
  0.7 15.3 %copy-start.10 = (s32[144,1]{0,1:T(1,128)S(1)}, s32[144,1]{0,1:T(1,128)}, u32[]{:S(2)}) copy-start(s32[144,1]{0,1:T(1,128)} %param.9) | copy-start | bytes 1732
  0.7 15.3 %copy-start.11 = (s32[144]{0:T(256)S(1)}, s32[144]{0:T(256)}, u32[]{:S(2)}) copy-start(s32[144]{0:T(256)} %param.10) | copy-start | bytes 1732
  0.7 15.5 %copy-start.1 = (f32[4,512,128]{2,1,0:T(8,128)S(1)}, f32[4,512,128]{2,1,0:T(8,128)}, u32[]{:S(2)}) copy-start(f32[4,512,128]{2,1,0:T(8,128)} %own_ref.2) | copy-start | bytes 3145732
  3.4 36.0 %copy-start = (f32[4,1024,128]{2,1,0:T(8,128)S(1)}, f32[4,1024,128]{2,1,0:T(8,128)}, u32[]{:S(2)}) copy-start(f32[4,1024,128]{2,1,0:T(8,128)} %own_ref.3) | copy-start | bytes 6291460
  3.5 35.9 %copy-start.4 = (s32[4]{0:T(128)S(1)}, s32[4]{0:T(128)}, u32[]{:S(2)}) copy-start(s32[4]{0:T(128)} %counts.1) | copy-start | bytes 52
  3.5 10.6 %collective-permute-start = (f32[512,128]{1,0:T(8,128)S(1)}, f32[512,128]{1,0:T(8,128)S(1)}, u32[]{:S(2)}, u32[]{:S(2)}) collective-permute-start(f32[512,128]{1,0:T(8,128)S(1)} %dynamic-slice_bitcast_fusion.3), channel_id=1, source_target_pairs={{0,1},{1,0},{2,3},{3,2},{4,5},{5,4},{6,7},{7,6},{8,9},{9,8},{10,11... | collective-permute-start | bytes 786440 | tf_op jit(solution)/shard_map/ppermute | solution.py:217
  4.0 7.1 %collective-permute-start.1 = (f32[256,128]{1,0:T(8,128)}, f32[256,128]{1,0:T(8,128)S(1)}, u32[]{:S(2)}, u32[]{:S(2)}) collective-permute-start(f32[256,128]{1,0:T(8,128)} %get-tuple-element.27), channel_id=1, source_target_pairs={{0,2},{1,3},{2,0},{3,1},{4,6},{5,7},{6,4},{7,5},{8,10},{9,11},{10,... | collective-permute-start | bytes 393224 | tf_op jit(solution)/shard_map/ppermute | solution.py:217
  6.6 6.8 %collective-permute-start.2 = (f32[256,128]{1,0:T(8,128)}, f32[256,128]{1,0:T(8,128)S(1)}, u32[]{:S(2)}, u32[]{:S(2)}) collective-permute-start(f32[256,128]{1,0:T(8,128)} %get-tuple-element.28), channel_id=1, source_target_pairs={{0,3},{1,2},{2,1},{3,0},{4,7},{5,6},{6,5},{7,4},{8,11},{9,10},{10,... | collective-permute-start | bytes 393224 | tf_op jit(solution)/shard_map/ppermute | solution.py:217
  13.4 0.7 copy-start.2
  14.1 21.9 %collective-permute-start.3 = (f32[1024,128]{1,0:T(8,128)}, f32[1024,128]{1,0:T(8,128)}, u32[]{:S(2)}, u32[]{:S(2)}) collective-permute-start(f32[1024,128]{1,0:T(8,128)} %get-tuple-element.29), channel_id=1, source_target_pairs={{0,1},{1,0},{2,3},{3,2},{4,5},{5,4},{6,7},{7,6},{8,9},{9,8},{10,11... | collective-permute-start | bytes 1572872 | tf_op jit(solution)/shard_map/ppermute | solution.py:217
  14.2 21.8 %collective-permute-start.4 = (f32[1024,128]{1,0:T(8,128)}, f32[1024,128]{1,0:T(8,128)}, u32[]{:S(2)}, u32[]{:S(2)}) collective-permute-start(f32[1024,128]{1,0:T(8,128)} %get-tuple-element.30), channel_id=1, source_target_pairs={{0,2},{1,3},{2,0},{3,1},{4,6},{5,7},{6,4},{7,5},{8,10},{9,11},{10,... | collective-permute-start | bytes 1572872 | tf_op jit(solution)/shard_map/ppermute | solution.py:217
  15.9 23.5 %collective-permute-start.5 = (f32[1024,128]{1,0:T(8,128)}, f32[1024,128]{1,0:T(8,128)}, u32[]{:S(2)}, u32[]{:S(2)}) collective-permute-start(f32[1024,128]{1,0:T(8,128)} %get-tuple-element.31), channel_id=1, source_target_pairs={{0,3},{1,2},{2,1},{3,0},{4,7},{5,6},{6,5},{7,4},{8,11},{9,10},{10,... | collective-permute-start | bytes 1572872 | tf_op jit(solution)/shard_map/ppermute | solution.py:217
  16.1 0.9 copy-start.3
  44.8 5.6 %copy-start.5 = (f32[2,1536,128]{2,1,0:T(8,128)}, f32[2,1536,128]{2,1,0:T(8,128)S(1)}, u32[]{:S(2)}) copy-start(f32[2,1536,128]{2,1,0:T(8,128)S(1)} %get-tuple-element.44) | copy-start | bytes 4718596
  44.8 5.6 %copy-start.6 = (f32[1536,128]{1,0:T(8,128)}, f32[1536,128]{1,0:T(8,128)S(1)}, u32[]{:S(2)}) copy-start(f32[1536,128]{1,0:T(8,128)S(1)} %get-tuple-element.38) | copy-start | bytes 2359300
  44.8 2.7 %collective-permute-start.7 = (f32[32,64,128]{2,1,0:T(8,128)S(1)}, f32[32,64,128]{2,1,0:T(8,128)S(1)}, u32[]{:S(2)}, u32[]{:S(2)}) collective-permute-start(f32[32,64,128]{2,1,0:T(8,128)S(1)} %get-tuple-element.40), channel_id=1, source_target_pairs={{0,1},{1,0},{2,3},{3,2},{4,5},{5,4},{6,7},{7,6},{8,9},{9,8},{10,11... | collective-permute-start | bytes 3145736 | tf_op jit(solution)/shard_map/ppermute | solution.py:217
  44.9 4.1 %collective-permute-start.9 = (f32[32,64,128]{2,1,0:T(8,128)S(1)}, f32[32,64,128]{2,1,0:T(8,128)S(1)}, u32[]{:S(2)}, u32[]{:S(2)}) collective-permute-start(f32[32,64,128]{2,1,0:T(8,128)S(1)} %get-tuple-element.41), channel_id=1, source_target_pairs={{0,1},{1,0},{2,3},{3,2},{4,5},{5,4},{6,7},{7,6},{8,9},{9,8},{10,11... | collective-permute-start | bytes 3145736 | tf_op jit(solution)/shard_map/ppermute | solution.py:217
  50.4 15.5 %collective-permute-start.10 = (f32[16,64,128]{2,1,0:T(8,128)}, f32[16,64,128]{2,1,0:T(8,128)}, u32[]{:S(2)}, u32[]{:S(2)}) collective-permute-start(f32[16,64,128]{2,1,0:T(8,128)} %get-tuple-element.53), channel_id=1, source_target_pairs={{0,8},{4,12},{8,0},{12,4},{16,24},{20,28},{24,16},{28,20},{1,9},{5... | collective-permute-start | bytes 1572872 | tf_op jit(solution)/shard_map/ppermute | solution.py:217
  53.1 14.0 %collective-permute-start.8 = (f32[16,64,128]{2,1,0:T(8,128)S(1)}, f32[16,64,128]{2,1,0:T(8,128)}, u32[]{:S(2)}, u32[]{:S(2)}) collective-permute-start(f32[16,64,128]{2,1,0:T(8,128)S(1)} %get-tuple-element.56), channel_id=1, source_target_pairs={{0,4},{4,0},{8,12},{12,8},{16,20},{20,16},{24,28},{28,24},{1,5},{5... | collective-permute-start | bytes 1572872 | tf_op jit(solution)/shard_map/ppermute | solution.py:217
  54.6 40.3 %collective-permute-start.16 = (f32[2,1536,128]{2,1,0:T(8,128)}, f32[2,1536,128]{2,1,0:T(8,128)S(1)}, u32[]{:S(2)}, u32[]{:S(2)}) collective-permute-start(f32[2,1536,128]{2,1,0:T(8,128)} %copy-done.5), channel_id=1, source_target_pairs={{0,2},{1,3},{2,0},{3,1},{4,6},{5,7},{6,4},{7,5},{8,10},{9,11},{10,... | collective-permute-start | bytes 4718600 | tf_op jit(solution)/shard_map/ppermute | solution.py:217
  55.9 26.3 %collective-permute-start.6 = (f32[1536,128]{1,0:T(8,128)}, f32[1536,128]{1,0:T(8,128)S(1)}, u32[]{:S(2)}, u32[]{:S(2)}) collective-permute-start(f32[1536,128]{1,0:T(8,128)} %copy-done.6), channel_id=1, source_target_pairs={{0,1},{1,0},{2,3},{3,2},{4,5},{5,4},{6,7},{7,6},{8,9},{9,8},{10,11... | collective-permute-start | bytes 2359304 | tf_op jit(solution)/shard_map/ppermute | solution.py:217
  68.2 7.9 %collective-permute-start.11 = (f32[8,64,128]{2,1,0:T(8,128)S(1)}, f32[8,64,128]{2,1,0:T(8,128)S(1)}, u32[]{:S(2)}, u32[]{:S(2)}) collective-permute-start(f32[8,64,128]{2,1,0:T(8,128)S(1)} %get-tuple-element.42), channel_id=1, source_target_pairs={{0,8},{4,12},{8,0},{12,4},{16,24},{20,28},{24,16},{28,20},{1,9},{5... | collective-permute-start | bytes 786440 | tf_op jit(solution)/shard_map/ppermute | solution.py:217
  70.0 7.6 %collective-permute-start.12 = (f32[8,64,128]{2,1,0:T(8,128)S(1)}, f32[8,64,128]{2,1,0:T(8,128)S(1)}, u32[]{:S(2)}, u32[]{:S(2)}) collective-permute-start(f32[8,64,128]{2,1,0:T(8,128)S(1)} %get-tuple-element.43), channel_id=1, source_target_pairs={{0,4},{4,0},{8,12},{12,8},{16,20},{20,16},{24,28},{28,24},{1,5},{5... | collective-permute-start | bytes 786440 | tf_op jit(solution)/shard_map/ppermute | solution.py:217
  77.6 18.9 %collective-permute-start.15 = (f32[2,128,128]{2,1,0:T(8,128)S(1)}, f32[2,128,128]{2,1,0:T(8,128)S(1)}, u32[]{:S(2)}, u32[]{:S(2)}) collective-permute-start(f32[2,128,128]{2,1,0:T(8,128)S(1)} %pad_maximum_fusion.2), channel_id=1, source_target_pairs={{0,2},{1,3},{2,0},{3,1},{4,6},{5,7},{6,4},{7,5},{8,10},{9,11},{10,... | collective-permute-start | bytes 393224 | tf_op jit(solution)/shard_map/ppermute | solution.py:217
  78.3 18.4 %copy-start.9 = (f32[2,128,128]{2,1,0:T(8,128)S(1)}, f32[2,128,128]{2,1,0:T(8,128)}, u32[]{:S(2)}) copy-start(f32[2,128,128]{2,1,0:T(8,128)} %param.11) | copy-start | bytes 393220
  78.3 18.2 %collective-permute-start.14 = (f32[2,128,128]{2,1,0:T(8,128)S(1)}, f32[2,128,128]{2,1,0:T(8,128)S(1)}, u32[]{:S(2)}, u32[]{:S(2)}) collective-permute-start(f32[2,128,128]{2,1,0:T(8,128)S(1)} %pad_maximum_fusion.1), channel_id=1, source_target_pairs={{0,16},{4,20},{8,24},{12,28},{16,0},{20,4},{24,8},{28,12},{1,17},{... | collective-permute-start | bytes 393224 | tf_op jit(solution)/shard_map/ppermute | solution.py:217
  81.9 14.7 %collective-permute-start.13 = (f32[2,128,128]{2,1,0:T(8,128)S(1)}, f32[2,128,128]{2,1,0:T(8,128)S(1)}, u32[]{:S(2)}, u32[]{:S(2)}) collective-permute-start(f32[2,128,128]{2,1,0:T(8,128)S(1)} %pad_maximum_fusion), channel_id=1, source_target_pairs={{0,18},{1,19},{2,16},{3,17},{4,22},{5,23},{6,20},{7,21},{8,26},{9,... | collective-permute-start | bytes 393224 | tf_op jit(solution)/shard_map/ppermute | solution.py:315
  96.6 2.4 %collective-permute-start.17 = (f32[1536,128]{1,0:T(8,128)S(1)}, f32[1536,128]{1,0:T(8,128)S(1)}, u32[]{:S(2)}, u32[]{:S(2)}) collective-permute-start(f32[1536,128]{1,0:T(8,128)S(1)} %slice_bitcast_fusion), channel_id=1, source_target_pairs={{0,1},{1,0},{2,3},{3,2},{4,5},{5,4},{6,7},{7,6},{8,9},{9,8},{10,11... | collective-permute-start | bytes 2359304 | tf_op jit(solution)/shard_map/ppermute | solution.py:217
  99.0 1.3 %copy-start.7 = (f32[4,1024,128]{2,1,0:T(8,128)}, f32[4,1024,128]{2,1,0:T(8,128)S(1)}, u32[]{:S(2)}) copy-start(f32[4,1024,128]{2,1,0:T(8,128)S(1)} %fusion) | copy-start | bytes 6291460
  100.3 1.0 copy-start.8

commit v6 on v5

--- a/solution.py
+++ b/solution.py
@@ -153,15 +153,17 @@
 
 
 def panel_kernel(
-    info, counts, tgt_a, tgt_b, own_ref, r1, r2, r3, mt, l, own, near, far, keep, send_a, send_b, xh, xl
+    info, counts, tgt_a, tgt_b, own_ref, r1, r2, r3, mt, l, own, near, far_x, far_l, keep_a, keep_b, send_a, send_b, xh, xl
 ):
     me = info[0]
     count = counts[me]
     rows = P_SIZE * B
     ins = [own_ref.at[me], r1, r2, r3]
-    outs = [own, near, far.at[0], far.at[1]]
-    for m in range(NB):
-        outs[m][pl.ds(rows, W), :] = l[me ^ m]
+    outs = [own, near, far_x.at[0], far_x.at[1]]
+    own[pl.ds(rows, W), :] = l[me]
+    near[pl.ds(rows, W), :] = l[me ^ 1]
+    far_l[0] = l[me ^ 2]
+    far_l[1] = l[me ^ 3]
     live = lax.broadcasted_iota(jnp.int32, (rows, B), 0) < count * B
     parts = [split_bf16(jnp.where(live, ref[...], 0.0)) for ref in ins]
     left = [jnp.concatenate([part[n] for part in parts], axis=1) for n in range(2)]
@@ -177,10 +179,11 @@
         xh[:, pl.ds(c * B, 2 * B)] = high
         xl[:, pl.ds(c * B, 2 * B)] = low
 
-    keep[...] = jnp.zeros_like(keep)
+    keep_a[...] = jnp.zeros_like(keep_a)
+    keep_b[...] = jnp.zeros_like(keep_b)
     send_a[...] = jnp.zeros_like(send_a)
     send_b[...] = jnp.zeros_like(send_b)
-    half, strip = keep.shape[1:3]
+    half, strip = keep_a.shape[:2]
     for j in range(0, P_SIZE, 2):
 
         @pl.when(j < count)
@@ -193,10 +196,12 @@
                     block = got[(i - j) * B : (i - j + 1) * B, n * B : (n + 1) * B]
                     pair = i * (i + 1) // 2 + j + n
                     away = (tgt_a[pair] >= half).astype(jnp.float32)
-                    for stream, (tgt, send) in enumerate(((tgt_a, send_a), (tgt_b, send_b))):
+                    for tgt, keep, send, piece in (
+                        (tgt_a, keep_a, send_a, block[:strip]),
+                        (tgt_b, keep_b, send_b, block[strip:]),
+                    ):
                         at = lax.rem(tgt[pair], half)
-                        piece = block[stream * strip : (stream + 1) * strip]
-                        keep[stream, at] += piece * (1.0 - away)
+                        keep[at] += piece * (1.0 - away)
                         send[at] += piece * away
 
 
@@ -237,11 +242,11 @@
         x, (me ^ m, (me // 2) * (W // 2), 0), (1, W // 2, B)
     ).reshape(W // 2, B)
     halves = [half_of(diag_block, m) for m in masks[1:]]
-    halves, near_block = lax.optimization_barrier((halves, diag_block))
+    _, near_block = lax.optimization_barrier((halves, diag_block))
     diag_in = [swap(own(near_block, 1), "narrow", 1)]
     diag_in += [swap(part, "narrow", m) for m, part in zip(masks[1:], halves)]
     panel_out = [own(panel, m) for m in masks]
-    diag_in, panel_out = lax.optimization_barrier((diag_in, panel_out))
+    _, panel_out = lax.optimization_barrier((diag_in, panel_out))
     panel_in = [swap(panel_out[m - 1], "narrow", m) for m in masks]
 
     narrow_steps = [("narrow", 1 << b) for b in range(log2(narrow_count))]
@@ -270,63 +275,62 @@
     rows = P_SIZE * B
     blocks = wide_count * narrow_count * T_DEV
     slab = jax.ShapeDtypeStruct((rows + W, B), jnp.float32)
-    pair = jax.ShapeDtypeStruct((2, rows + W, B), jnp.float32)
+    pair_x = jax.ShapeDtypeStruct((2, rows, B), jnp.float32)
+    pair_l = jax.ShapeDtypeStruct((2, W, B), jnp.float32)
     part = jax.ShapeDtypeStruct((blocks // 2, B // 2, B), jnp.float32)
-    parts = jax.ShapeDtypeStruct((2, blocks // 2, B // 2, B), jnp.float32)
-    home, near, far, keep, send_a, send_b = pl.pallas_call(
+    home, near, far_x, far_l, keep_a, keep_b, send_a, send_b = pl.pallas_call(
         panel_kernel,
-        out_shape=[slab, slab, pair, parts, part, part],
+        out_shape=[slab, slab, pair_x, pair_l] + [part] * 4,
         in_specs=[SMEM] * 4 + [VMEM] * (NB + 2),
-        out_specs=[VMEM] * 6,
+        out_specs=[VMEM] * 8,
         scratch_shapes=[pltpu.VMEM((rows, W), jnp.bfloat16)] * 2,
         compiler_params=pltpu.CompilerParams(vmem_limit_bytes=20 * 2**20 + 4 * blocks * B * B),
         cost_estimate=pl.CostEstimate(flops=10**9, bytes_accessed=10 * 10**6, transcendentals=0),
         name="panel",
     )(info, panel_count, tgt_a, tgt_b, panel, *panel_in, mt, l)
 
-    far = swap(far, "narrow", 2)
+    far_x = swap(far_x, "narrow", 2)
+    far_l = swap(far_l, "narrow", 2)
     near = swap(near, "narrow", 1)
 
     got_a, got_b = swap(send_a, "narrow", 1), swap(send_b, "narrow", 1)
-    keep_a, keep_b = keep[0], keep[1]
     half = blocks // 4
     for n in (1, 2):
-        send_a, send_b = keep_a[half:] + got_a[half:], keep_b[half:] + got_b[half:]
+        send_a = keep_a[half:] + got_a[half:]
+        send_a, got_b = lax.optimization_barrier((send_a, got_b))
+        send_b = keep_b[half:] + got_b[half:]
         keep_a, keep_b = keep_a[:half] + got_a[:half], keep_b[:half] + got_b[:half]
         if n == 2:
             send_a, send_b = lax.optimization_barrier((send_a, send_b))
         got_a, got_b = swap(send_a, *steps_a[n]), swap(send_b, *steps_b[n])
         half = half // 2
-
-    def rows_of(n, size):
-        at = slice(n * size, (n + 1) * size)
-        return jnp.concatenate([keep_a[at] + got_a[at], keep_b[at] + got_b[at]], axis=1)
-
-    rest = steps_a[3:]
-    while len(rest) > 2:
-        got = swap(rows_of(1, half), *rest.pop(0))
-        total = rows_of(0, half) + got
-        half = half // 2
-        keep_a, keep_b = total[:, : B // 2], total[:, B // 2 :]
-        got_a, got_b = jnp.zeros_like(keep_a), jnp.zeros_like(keep_b)
-    (_, wide_mask), (_, narrow_mask) = rest
-    both = wide_mask * narrow_count + narrow_mask
-    got = [
-        lax.ppermute(rows_of(3, T_DEV), ("wide", "narrow"), xor_pairs(wide_count * narrow_count, both)),
-        swap(rows_of(2, T_DEV), *rest[0]),
-        swap(rows_of(1, T_DEV), *rest[1]),
-    ]
-    got, far = lax.optimization_barrier((got, far))
-    relayed = swap(far[1], "narrow", 1)
-    updated = ancestor - (rows_of(0, T_DEV) + (got[0] + (got[1] + got[2])))
-
-    def assemble(at, size):
-        out = jnp.zeros((NB, size, B), jnp.float32)
-        for m, piece in enumerate((home, near, far[0], relayed)):
-            out = lax.dynamic_update_index_in_dim(out, piece[at : at + size], me ^ m, 0)
+    send = jnp.concatenate([keep_a[half:] + got_a[half:], keep_b[half:] + got_b[half:]], axis=1)
+    keep = jnp.concatenate([keep_a[:half] + got_a[:half], keep_b[:half] + got_b[:half]], axis=1)
+    for n in range(3, len(steps_a)):
+        if n == 3:
+            send, far_x = lax.optimization_barrier((send, far_x))
+        if n == len(steps_a) - 1:
+            send, far_l = lax.optimization_barrier((send, far_l))
+        got = swap(send, *steps_a[n])
+        if n + 1 < len(steps_a):
+            half = half // 2
+            send = keep[half:] + got[half:]
+            keep = keep[:half] + got[:half]
+    relayed_x = swap(far_x[1], "narrow", 1)
+    relayed_l = swap(far_l[1], "narrow", 1)
+    updated = ancestor - (keep + got)
+
+    def assemble(pieces):
+        out = jnp.zeros((NB,) + pieces[0].shape, jnp.float32)
+        for m, piece in enumerate(pieces):
+            out = lax.dynamic_update_index_in_dim(out, piece, me ^ m, 0)
         return out
 
-    return (assemble(rows, W), assemble(0, rows), updated)
+    return (
+        assemble([home[rows:], near[rows:], far_l[0], relayed_l]),
+        assemble([home[:rows], near[:rows], far_x[0], relayed_x]),
+        updated,
+    )
 
 
 def solution(mesh):

time: 101 us -> 101 us (level)
  starting transfers between devices: 19 us -> 15.9 us
    ppermute x17 -> x19, starting transfers between devices: 18.6 us -> 15.9 us  [swap(): return lax.ppermute(x, axis, xor_pairs(lax.axis_size(axis), mask))]
    ppermute x17 -> x19, waiting for transfers between devices: 42.9 us -> 43.7 us  [swap(): return lax.ppermute(x, axis, xor_pairs(lax.axis_size(axis), mask))]
  transfers between devices with their start and end apart: 18 -> 19, of which waited for: 12 -> 12; matrix products, arithmetic and copies ran while one was open for 6% -> 8% of each run, Pallas kernels for 19% -> 19%
where the time goes in v6:
time: 101 us; the launch traced here: 100 us
  waiting for transfers between devices  43.7 us (43%)
  Pallas kernels  25.3 us (25%)
  starting transfers between devices  15.9 us (16%)
  local copies, waits for them, and re-layouts  9.57 us (9%)
  other arithmetic  5.02 us (5%)
    ppermute x19, waiting for transfers between devices, swap(): return lax.ppermute(x, axis, xor_pairs(lax.axis_size(axis), mask))  43.7 us
    pallas_call x1, Pallas kernels, local(): pl.pallas_call(factor_kernel, out_shape=[whole, whole], in_specs=[SMEM] +...  18.9 us
    ppermute x19, starting transfers between devices, swap(): return lax.ppermute(x, axis, xor_pairs(lax.axis_size(axis), mask))  15.9 us
    pallas_call x1, Pallas kernels, local(): pl.pallas_call(panel_kernel, out_shape=[slab, slab, pair_x, pair_l] + [pa...  6.4 us
    unnamed x24, local copies, waits for them, and re-layouts  3.82 us
    squeeze x2, local copies, waits for them, and re-layouts, local(): own = lambda x, m: lax.dynamic_index_in_dim(x, me ^ m, 0, keepdims=False)  3.48 us
  transfers between devices with their start and end apart: 19, of which 12 were waited for; matrix products, arithmetic and copies ran while one was open for 8% of the time, Pallas kernels for 19%

profile of v6, /device:TPU:0, one launch (start us, length us, event | category | flops | bytes accessed | tf_op | source)
XLA Modules:
  0.0 100.4 jit_solution(3395431603412735207)
XLA Ops:
  0.7 0.0 copy-start.1
  0.7 1.8 %dynamic-slice_bitcast_fusion.4 = (f32[256,128]{1,0:T(8,128)}, f32[256,128]{1,0:T(8,128)}) fusion(f32[4,512,128]{2,1,0:T(8,128)} %own_ref.2, s32[]{:T(128)S(6)} %select_n.79, s32[]{:T(128)S(6)} %select_n.78, s32[]{:T(128)S(6)} %select_n.76), kind=kLoop, calls=%fused_computation.37 | loop fusion | bytes 524300 | tf_op jit(solution)/shard_map/reshape | solution.py:243
  2.5 1.0 dynamic-slice_bitcast_fusion.3
  3.4 0.0 copy-start
  3.4 0.0 copy-start.4
  3.5 0.5 collective-permute-start
  4.0 2.6 %collective-permute-start.1 = (f32[256,128]{1,0:T(8,128)}, f32[256,128]{1,0:T(8,128)S(1)}, u32[]{:S(2)}, u32[]{:S(2)}) collective-permute-start(f32[256,128]{1,0:T(8,128)} %get-tuple-element.68), channel_id=1, source_target_pairs={{0,2},{1,3},{2,0},{3,1},{4,6},{5,7},{6,4},{7,5},{8,10},{9,11},{10,... | collective-permute-start | bytes 393224 | tf_op jit(solution)/shard_map/ppermute | solution.py:222
  6.5 0.1 collective-permute-start.2
  6.6 2.5 %dynamic-slice_bitcast_fusion = (f32[1024,128]{1,0:T(8,128)}, f32[1024,128]{1,0:T(8,128)}, f32[1024,128]{1,0:T(8,128)}) fusion(f32[4,1024,128]{2,1,0:T(8,128)} %own_ref.3, s32[]{:T(128)S(6)} %select_n.79, s32[]{:T(128)S(6)} %select_n.76, s32[]{:T(128)S(6)} %select_n.80), kind=kLoop, calls=%fused_computation.10 | loop fusion | bytes 3145740 | tf_op jit(solution)/shard_map/jit(dynamic_index_in_dim)/squeeze | solution.py:240
  9.1 2.0 %collective-permute-done.1.r2 = f32[256,128]{1,0:T(8,128)S(1)} collective-permute-done((f32[256,128]{1,0:T(8,128)}, f32[256,128]{1,0:T(8,128)S(1)}, u32[]{:S(2)}, u32[]{:S(2)}) %collective-permute-start.1) | collective-permute-done | bytes 131104 | tf_op jit(solution)/shard_map/ppermute | solution.py:222
  11.1 2.3 %collective-permute-done.2.r3 = f32[256,128]{1,0:T(8,128)S(1)} collective-permute-done((f32[256,128]{1,0:T(8,128)}, f32[256,128]{1,0:T(8,128)S(1)}, u32[]{:S(2)}, u32[]{:S(2)}) %collective-permute-start.2) | collective-permute-done | bytes 131104 | tf_op jit(solution)/shard_map/ppermute | solution.py:222
  13.4 0.7 copy-done.2
  14.0 0.0 collective-permute-done.r1
  14.0 0.1 collective-permute-start.3
  14.2 1.7 %collective-permute-start.4 = (f32[1024,128]{1,0:T(8,128)}, f32[1024,128]{1,0:T(8,128)}, u32[]{:S(2)}, u32[]{:S(2)}) collective-permute-start(f32[1024,128]{1,0:T(8,128)} %get-tuple-element.29), channel_id=1, source_target_pairs={{0,2},{1,3},{2,0},{3,1},{4,6},{5,7},{6,4},{7,5},{8,10},{9,11},{10,... | collective-permute-start | bytes 1572872 | tf_op jit(solution)/shard_map/ppermute | solution.py:222
  15.9 0.0 collective-permute-start.5
  15.9 0.1 multiply_add_fusion
  16.0 0.1 multiply_add_fusion.1.tgt_a
  16.1 0.0 copy-start.3
  16.1 0.9 copy-done.3
  17.0 18.9 %factor.1 = (f32[4,512,128]{2,1,0:T(8,128)S(1)}, f32[4,512,128]{2,1,0:T(8,128)S(1)}) custom-call(s32[1]{0:T(128)} %bitcast.info, f32[4,512,128]{2,1,0:T(8,128)S(1)} %copy-done.1, f32[512,128]{1,0:T(8,128)S(1)} %collective-permute-done.r1, f32[256,128]{1,0:T(8,128)S(1)} %collective-permute-done.1.r2, f32[256,128]{1,0:T(8,128)S(1)} %copy-done.3), custom_call_target="tpu_custom_call" | custom-call | flops 200000000 | bytes 4000000 | tf_op jit(solution)/shard_map/factor/pallas_call | solution.py:264
  36.0 0.0 collective-permute-done.3.r1
  36.0 0.0 collective-permute-done.4.r2
  36.0 3.4 %collective-permute-done.5.r3 = f32[1024,128]{1,0:T(8,128)} collective-permute-done((f32[1024,128]{1,0:T(8,128)}, f32[1024,128]{1,0:T(8,128)}, u32[]{:S(2)}, u32[]{:S(2)}) %collective-permute-start.5) | collective-permute-done | bytes 524320 | tf_op jit(solution)/shard_map/ppermute | solution.py:222
  39.4 6.4 %panel.1 = (f32[1536,128]{1,0:T(8,128)S(1)}, f32[1536,128]{1,0:T(8,128)S(1)}, f32[2,1024,128]{2,1,0:T(8,128)S(1)}, f32[2,512,128]{2,1,0:T(8,128)S(1)}, f32[32,64...) custom-call(s32[1]{0:T(128)} %bitcast.info, ...), custom_call_target="tpu_custom_call" | custom-call | flops 1000000000 | bytes 10000000 | tf_op jit(solution)/shard_map/panel/pallas_call | solution.py:281
  45.8 0.0 copy-start.5
  45.8 0.0 copy-start.6
  45.8 0.1 collective-permute-start.7
  45.9 0.5 collective-permute-start.8
  46.4 2.1 %collective-permute-done.7 = f32[32,64,128]{2,1,0:T(8,128)S(1)} collective-permute-done((f32[32,64,128]{2,1,0:T(8,128)S(1)}, f32[32,64,128]{2,1,0:T(8,128)S(1)}, u32[]{:S(2)}, u32[]{:S(2)}) %collective-permute-start.7) | collective-permute-done | bytes 1048608 | tf_op jit(solution)/shard_map/ppermute | solution.py:222
  48.5 0.9 slice_add_fusion.1
  49.5 0.6 collective-permute-done.8
  50.0 1.6 %collective-permute-start.9 = (f32[16,64,128]{2,1,0:T(8,128)}, f32[16,64,128]{2,1,0:T(8,128)}, u32[]{:S(2)}, u32[]{:S(2)}) collective-permute-start(f32[16,64,128]{2,1,0:T(8,128)} %get-tuple-element.38), channel_id=1, source_target_pairs={{0,4},{4,0},{8,12},{12,8},{16,20},{20,16},{24,28},{28,24},{1,5},{5... | collective-permute-start | bytes 1572872 | tf_op jit(solution)/shard_map/ppermute | solution.py:222
  51.6 0.9 slice_add_fusion.2
  52.6 0.0 collective-permute-start.10
  52.6 2.9 %collective-permute-start.13 = (f32[2,1024,128]{2,1,0:T(8,128)}, f32[2,1024,128]{2,1,0:T(8,128)S(1)}, u32[]{:S(2)}, u32[]{:S(2)}) collective-permute-start(f32[2,1024,128]{2,1,0:T(8,128)} %copy-done.5), channel_id=1, source_target_pairs={{0,2},{1,3},{2,0},{3,1},{4,6},{5,7},{6,4},{7,5},{8,10},{9,11},{10,... | collective-permute-start | bytes 3145736 | tf_op jit(solution)/shard_map/ppermute | solution.py:222
  55.5 0.0 collective-permute-start.15
  55.5 0.0 collective-permute-start.6
  55.5 0.1 broadcast_in_dim.32
  55.7 8.7 %collective-permute-done.9 = f32[16,64,128]{2,1,0:T(8,128)} collective-permute-done((f32[16,64,128]{2,1,0:T(8,128)}, f32[16,64,128]{2,1,0:T(8,128)}, u32[]{:S(2)}, u32[]{:S(2)}) %collective-permute-start.9) | collective-permute-done | bytes 524320 | tf_op jit(solution)/shard_map/ppermute | solution.py:222
  64.4 1.1 %slice_add_fusion.7 = (f32[8,64,128]{2,1,0:T(8,128)S(1)}, f32[8,64,128]{2,1,0:T(8,128)S(1)}) fusion(f32[16,64,128]{2,1,0:T(8,128)} %collective-permute-done.9, f32[16,64,128]{2,1,0:T(8,128)S(1)} %get-tuple-element.56), kind=kLoop, calls=%fused_computation.16 | loop fusion | flops 131072 | bytes 1572864 | tf_op jit(solution)/shard_map/add | solution.py:302
  65.5 1.3 %collective-permute-done.10 = f32[16,64,128]{2,1,0:T(8,128)} collective-permute-done((f32[16,64,128]{2,1,0:T(8,128)}, f32[16,64,128]{2,1,0:T(8,128)}, u32[]{:S(2)}, u32[]{:S(2)}) %collective-permute-start.10) | collective-permute-done | bytes 524320 | tf_op jit(solution)/shard_map/ppermute | solution.py:222
  66.8 1.1 %slice_add_fusion.4 = (f32[8,64,128]{2,1,0:T(8,128)S(1)}, f32[8,64,128]{2,1,0:T(8,128)S(1)}) fusion(f32[16,64,128]{2,1,0:T(8,128)S(1)} %get-tuple-element.54, f32[16,64,128]{2,1,0:T(8,128)} %collective-permute-done.10), kind=kLoop, calls=%fused_computation.13 | loop fusion | flops 131072 | bytes 1572864 | tf_op jit(solution)/shard_map/add | solution.py:302
  67.9 0.5 collective-permute-start.12
  68.4 0.1 broadcast_in_dim.28
  68.5 1.3 %collective-permute-start.11 = (f32[8,64,128]{2,1,0:T(8,128)S(1)}, f32[8,64,128]{2,1,0:T(8,128)S(1)}, u32[]{:S(2)}, u32[]{:S(2)}) collective-permute-start(f32[8,64,128]{2,1,0:T(8,128)S(1)} %get-tuple-element.43), channel_id=1, source_target_pairs={{0,8},{4,12},{8,0},{12,4},{16,24},{20,28},{24,16},{28,20},{1,9},{5... | collective-permute-start | bytes 786440 | tf_op jit(solution)/shard_map/ppermute | solution.py:222
  69.8 0.0 collective-permute-done.6
  69.9 5.5 %collective-permute-done.12 = f32[8,64,128]{2,1,0:T(8,128)S(1)} collective-permute-done((f32[8,64,128]{2,1,0:T(8,128)S(1)}, f32[8,64,128]{2,1,0:T(8,128)S(1)}, u32[]{:S(2)}, u32[]{:S(2)}) %collective-permute-start.12) | collective-permute-done | bytes 262176 | tf_op jit(solution)/shard_map/ppermute | solution.py:222
  75.4 0.6 collective-permute-done.11
  76.1 0.0 copy-start.9
  76.1 3.6 %collective-permute-done.13 = f32[2,1024,128]{2,1,0:T(8,128)S(1)} collective-permute-done((f32[2,1024,128]{2,1,0:T(8,128)}, f32[2,1024,128]{2,1,0:T(8,128)S(1)}, u32[]{:S(2)}, u32[]{:S(2)}) %collective-permute-start.13) | collective-permute-done | bytes 1048608 | tf_op jit(solution)/shard_map/ppermute | solution.py:222
  79.7 2.3 %collective-permute-start.14 = (f32[4,128,128]{2,1,0:T(8,128)S(1)}, f32[4,128,128]{2,1,0:T(8,128)S(1)}, u32[]{:S(2)}, u32[]{:S(2)}) collective-permute-start(f32[4,128,128]{2,1,0:T(8,128)S(1)} %pad_maximum_fusion), channel_id=1, source_target_pairs={{0,16},{4,20},{8,24},{12,28},{16,0},{20,4},{24,8},{28,12},{1,17},{... | collective-permute-start | bytes 786440 | tf_op jit(solution)/shard_map/ppermute | solution.py:222
  82.0 0.1 slice_bitcast_fusion.1
  82.1 0.1 collective-permute-start.17
  82.2 10.1 %collective-permute-done.14 = f32[4,128,128]{2,1,0:T(8,128)S(1)} collective-permute-done((f32[4,128,128]{2,1,0:T(8,128)S(1)}, f32[4,128,128]{2,1,0:T(8,128)S(1)}, u32[]{:S(2)}, u32[]{:S(2)}) %collective-permute-start.14) | collective-permute-done | bytes 262176 | tf_op jit(solution)/shard_map/ppermute | solution.py:222
  92.3 0.0 collective-permute-done.15
  92.4 1.5 %collective-permute-start.18 = (f32[2,128,128]{2,1,0:T(8,128)S(1)}, f32[2,128,128]{2,1,0:T(8,128)S(1)}, u32[]{:S(2)}, u32[]{:S(2)}) collective-permute-start(f32[2,128,128]{2,1,0:T(8,128)S(1)} %fusion.3), channel_id=1, source_target_pairs={{0,2},{1,3},{2,0},{3,1},{4,6},{5,7},{6,4},{7,5},{8,10},{9,11},{10,... | collective-permute-start | bytes 393224 | tf_op jit(solution)/shard_map/ppermute | solution.py:222
  93.9 0.1 collective-permute-start.16
  94.0 3.4 %collective-permute-done.18 = f32[2,128,128]{2,1,0:T(8,128)S(1)} collective-permute-done((f32[2,128,128]{2,1,0:T(8,128)S(1)}, f32[2,128,128]{2,1,0:T(8,128)S(1)}, u32[]{:S(2)}, u32[]{:S(2)}) %collective-permute-start.18) | collective-permute-done | bytes 131104 | tf_op jit(solution)/shard_map/ppermute | solution.py:222
  97.4 0.7 fusion.5
  98.1 0.0 collective-permute-done.16
  98.1 0.0 copy-start.8
  98.2 0.9 copy-done.8
  99.1 1.3 %copy-done.7 = f32[4,1024,128]{2,1,0:T(8,128)} copy-done((f32[4,1024,128]{2,1,0:T(8,128)}, f32[4,1024,128]{2,1,0:T(8,128)S(1)}, u32[]{:S(2)}) %copy-start.7) | copy-done | bytes 2097176
  (24 shorter events, 0.4 us)
Async XLA Ops:
  0.7 15.3 %copy-start.10 = (s32[144,1]{0,1:T(1,128)S(1)}, s32[144,1]{0,1:T(1,128)}, u32[]{:S(2)}) copy-start(s32[144,1]{0,1:T(1,128)} %param.9) | copy-start | bytes 1732
  0.7 15.2 %copy-start.11 = (s32[144]{0:T(256)S(1)}, s32[144]{0:T(256)}, u32[]{:S(2)}) copy-start(s32[144]{0:T(256)} %param.10) | copy-start | bytes 1732
  0.7 15.4 %copy-start.1 = (f32[4,512,128]{2,1,0:T(8,128)S(1)}, f32[4,512,128]{2,1,0:T(8,128)}, u32[]{:S(2)}) copy-start(f32[4,512,128]{2,1,0:T(8,128)} %own_ref.2) | copy-start | bytes 3145732
  3.4 36.0 %copy-start = (f32[4,1024,128]{2,1,0:T(8,128)S(1)}, f32[4,1024,128]{2,1,0:T(8,128)}, u32[]{:S(2)}) copy-start(f32[4,1024,128]{2,1,0:T(8,128)} %own_ref.3) | copy-start | bytes 6291460
  3.4 35.9 %copy-start.4 = (s32[4]{0:T(128)S(1)}, s32[4]{0:T(128)}, u32[]{:S(2)}) copy-start(s32[4]{0:T(128)} %counts.1) | copy-start | bytes 52
  3.5 10.6 %collective-permute-start = (f32[512,128]{1,0:T(8,128)S(1)}, f32[512,128]{1,0:T(8,128)S(1)}, u32[]{:S(2)}, u32[]{:S(2)}) collective-permute-start(f32[512,128]{1,0:T(8,128)S(1)} %dynamic-slice_bitcast_fusion.3), channel_id=1, source_target_pairs={{0,1},{1,0},{2,3},{3,2},{4,5},{5,4},{6,7},{7,6},{8,9},{9,8},{10,11... | collective-permute-start | bytes 786440 | tf_op jit(solution)/shard_map/ppermute | solution.py:222
  4.0 7.1 %collective-permute-start.1 = (f32[256,128]{1,0:T(8,128)}, f32[256,128]{1,0:T(8,128)S(1)}, u32[]{:S(2)}, u32[]{:S(2)}) collective-permute-start(f32[256,128]{1,0:T(8,128)} %get-tuple-element.68), channel_id=1, source_target_pairs={{0,2},{1,3},{2,0},{3,1},{4,6},{5,7},{6,4},{7,5},{8,10},{9,11},{10,... | collective-permute-start | bytes 393224 | tf_op jit(solution)/shard_map/ppermute | solution.py:222
  6.5 6.8 %collective-permute-start.2 = (f32[256,128]{1,0:T(8,128)}, f32[256,128]{1,0:T(8,128)S(1)}, u32[]{:S(2)}, u32[]{:S(2)}) collective-permute-start(f32[256,128]{1,0:T(8,128)} %get-tuple-element.67), channel_id=1, source_target_pairs={{0,3},{1,2},{2,1},{3,0},{4,7},{5,6},{6,5},{7,4},{8,11},{9,10},{10,... | collective-permute-start | bytes 393224 | tf_op jit(solution)/shard_map/ppermute | solution.py:222
  13.4 0.7 copy-start.2
  14.0 21.9 %collective-permute-start.3 = (f32[1024,128]{1,0:T(8,128)}, f32[1024,128]{1,0:T(8,128)}, u32[]{:S(2)}, u32[]{:S(2)}) collective-permute-start(f32[1024,128]{1,0:T(8,128)} %get-tuple-element.28), channel_id=1, source_target_pairs={{0,1},{1,0},{2,3},{3,2},{4,5},{5,4},{6,7},{7,6},{8,9},{9,8},{10,11... | collective-permute-start | bytes 1572872 | tf_op jit(solution)/shard_map/ppermute | solution.py:222
  14.2 21.8 %collective-permute-start.4 = (f32[1024,128]{1,0:T(8,128)}, f32[1024,128]{1,0:T(8,128)}, u32[]{:S(2)}, u32[]{:S(2)}) collective-permute-start(f32[1024,128]{1,0:T(8,128)} %get-tuple-element.29), channel_id=1, source_target_pairs={{0,2},{1,3},{2,0},{3,1},{4,6},{5,7},{6,4},{7,5},{8,10},{9,11},{10,... | collective-permute-start | bytes 1572872 | tf_op jit(solution)/shard_map/ppermute | solution.py:222
  15.9 23.5 %collective-permute-start.5 = (f32[1024,128]{1,0:T(8,128)}, f32[1024,128]{1,0:T(8,128)}, u32[]{:S(2)}, u32[]{:S(2)}) collective-permute-start(f32[1024,128]{1,0:T(8,128)} %get-tuple-element.30), channel_id=1, source_target_pairs={{0,3},{1,2},{2,1},{3,0},{4,7},{5,6},{6,5},{7,4},{8,11},{9,10},{10,... | collective-permute-start | bytes 1572872 | tf_op jit(solution)/shard_map/ppermute | solution.py:222
  16.1 0.9 copy-start.3
  45.8 6.8 %copy-start.5 = (f32[2,1024,128]{2,1,0:T(8,128)}, f32[2,1024,128]{2,1,0:T(8,128)S(1)}, u32[]{:S(2)}) copy-start(f32[2,1024,128]{2,1,0:T(8,128)S(1)} %get-tuple-element.45) | copy-start | bytes 3145732
  45.8 6.8 %copy-start.6 = (f32[1536,128]{1,0:T(8,128)}, f32[1536,128]{1,0:T(8,128)S(1)}, u32[]{:S(2)}) copy-start(f32[1536,128]{1,0:T(8,128)S(1)} %get-tuple-element.34) | copy-start | bytes 2359300
  45.8 2.7 %collective-permute-start.7 = (f32[32,64,128]{2,1,0:T(8,128)S(1)}, f32[32,64,128]{2,1,0:T(8,128)S(1)}, u32[]{:S(2)}, u32[]{:S(2)}) collective-permute-start(f32[32,64,128]{2,1,0:T(8,128)S(1)} %get-tuple-element.36), channel_id=1, source_target_pairs={{0,1},{1,0},{2,3},{3,2},{4,5},{5,4},{6,7},{7,6},{8,9},{9,8},{10,11... | collective-permute-start | bytes 3145736 | tf_op jit(solution)/shard_map/ppermute | solution.py:222
  45.9 4.1 %collective-permute-start.8 = (f32[32,64,128]{2,1,0:T(8,128)S(1)}, f32[32,64,128]{2,1,0:T(8,128)S(1)}, u32[]{:S(2)}, u32[]{:S(2)}) collective-permute-start(f32[32,64,128]{2,1,0:T(8,128)S(1)} %get-tuple-element.37), channel_id=1, source_target_pairs={{0,1},{1,0},{2,3},{3,2},{4,5},{5,4},{6,7},{7,6},{8,9},{9,8},{10,11... | collective-permute-start | bytes 3145736 | tf_op jit(solution)/shard_map/ppermute | solution.py:222
  50.0 14.4 %collective-permute-start.9 = (f32[16,64,128]{2,1,0:T(8,128)}, f32[16,64,128]{2,1,0:T(8,128)}, u32[]{:S(2)}, u32[]{:S(2)}) collective-permute-start(f32[16,64,128]{2,1,0:T(8,128)} %get-tuple-element.38), channel_id=1, source_target_pairs={{0,4},{4,0},{8,12},{12,8},{16,20},{20,16},{24,28},{28,24},{1,5},{5... | collective-permute-start | bytes 1572872 | tf_op jit(solution)/shard_map/ppermute | solution.py:222
  52.6 14.2 %collective-permute-start.10 = (f32[16,64,128]{2,1,0:T(8,128)}, f32[16,64,128]{2,1,0:T(8,128)}, u32[]{:S(2)}, u32[]{:S(2)}) collective-permute-start(f32[16,64,128]{2,1,0:T(8,128)} %get-tuple-element.55), channel_id=1, source_target_pairs={{0,8},{4,12},{8,0},{12,4},{16,24},{20,28},{24,16},{28,20},{1,9},{5... | collective-permute-start | bytes 1572872 | tf_op jit(solution)/shard_map/ppermute | solution.py:222
  52.6 27.1 %collective-permute-start.13 = (f32[2,1024,128]{2,1,0:T(8,128)}, f32[2,1024,128]{2,1,0:T(8,128)S(1)}, u32[]{:S(2)}, u32[]{:S(2)}) collective-permute-start(f32[2,1024,128]{2,1,0:T(8,128)} %copy-done.5), channel_id=1, source_target_pairs={{0,2},{1,3},{2,0},{3,1},{4,6},{5,7},{6,4},{7,5},{8,10},{9,11},{10,... | collective-permute-start | bytes 3145736 | tf_op jit(solution)/shard_map/ppermute | solution.py:222
  55.5 36.8 %collective-permute-start.15 = (f32[2,512,128]{2,1,0:T(8,128)S(1)}, f32[2,512,128]{2,1,0:T(8,128)S(1)}, u32[]{:S(2)}, u32[]{:S(2)}) collective-permute-start(f32[2,512,128]{2,1,0:T(8,128)S(1)} %get-tuple-element.47), channel_id=1, source_target_pairs={{0,2},{1,3},{2,0},{3,1},{4,6},{5,7},{6,4},{7,5},{8,10},{9,11},{10,... | collective-permute-start | bytes 1572872 | tf_op jit(solution)/shard_map/ppermute | solution.py:222
  55.5 14.3 %collective-permute-start.6 = (f32[1536,128]{1,0:T(8,128)}, f32[1536,128]{1,0:T(8,128)S(1)}, u32[]{:S(2)}, u32[]{:S(2)}) collective-permute-start(f32[1536,128]{1,0:T(8,128)} %copy-done.6), channel_id=1, source_target_pairs={{0,1},{1,0},{2,3},{3,2},{4,5},{5,4},{6,7},{7,6},{8,9},{9,8},{10,11... | collective-permute-start | bytes 2359304 | tf_op jit(solution)/shard_map/ppermute | solution.py:222
  67.9 7.5 %collective-permute-start.12 = (f32[8,64,128]{2,1,0:T(8,128)S(1)}, f32[8,64,128]{2,1,0:T(8,128)S(1)}, u32[]{:S(2)}, u32[]{:S(2)}) collective-permute-start(f32[8,64,128]{2,1,0:T(8,128)S(1)} %get-tuple-element.44), channel_id=1, source_target_pairs={{0,4},{4,0},{8,12},{12,8},{16,20},{20,16},{24,28},{28,24},{1,5},{5... | collective-permute-start | bytes 786440 | tf_op jit(solution)/shard_map/ppermute | solution.py:222
  68.5 7.6 %collective-permute-start.11 = (f32[8,64,128]{2,1,0:T(8,128)S(1)}, f32[8,64,128]{2,1,0:T(8,128)S(1)}, u32[]{:S(2)}, u32[]{:S(2)}) collective-permute-start(f32[8,64,128]{2,1,0:T(8,128)S(1)} %get-tuple-element.43), channel_id=1, source_target_pairs={{0,8},{4,12},{8,0},{12,4},{16,24},{20,28},{24,16},{28,20},{1,9},{5... | collective-permute-start | bytes 786440 | tf_op jit(solution)/shard_map/ppermute | solution.py:222
  76.1 21.3 %copy-start.9 = (f32[2,128,128]{2,1,0:T(8,128)S(1)}, f32[2,128,128]{2,1,0:T(8,128)}, u32[]{:S(2)}) copy-start(f32[2,128,128]{2,1,0:T(8,128)} %param.11) | copy-start | bytes 393220
  79.7 12.6 %collective-permute-start.14 = (f32[4,128,128]{2,1,0:T(8,128)S(1)}, f32[4,128,128]{2,1,0:T(8,128)S(1)}, u32[]{:S(2)}, u32[]{:S(2)}) collective-permute-start(f32[4,128,128]{2,1,0:T(8,128)S(1)} %pad_maximum_fusion), channel_id=1, source_target_pairs={{0,16},{4,20},{8,24},{12,28},{16,0},{20,4},{24,8},{28,12},{1,17},{... | collective-permute-start | bytes 786440 | tf_op jit(solution)/shard_map/ppermute | solution.py:222
  82.1 16.0 %collective-permute-start.17 = (f32[1024,128]{1,0:T(8,128)S(1)}, f32[1024,128]{1,0:T(8,128)S(1)}, u32[]{:S(2)}, u32[]{:S(2)}) collective-permute-start(f32[1024,128]{1,0:T(8,128)S(1)} %get-tuple-element.61), channel_id=1, source_target_pairs={{0,1},{1,0},{2,3},{3,2},{4,5},{5,4},{6,7},{7,6},{8,9},{9,8},{10,11... | collective-permute-start | bytes 1572872 | tf_op jit(solution)/shard_map/ppermute | solution.py:222
  92.4 5.0 %collective-permute-start.18 = (f32[2,128,128]{2,1,0:T(8,128)S(1)}, f32[2,128,128]{2,1,0:T(8,128)S(1)}, u32[]{:S(2)}, u32[]{:S(2)}) collective-permute-start(f32[2,128,128]{2,1,0:T(8,128)S(1)} %fusion.3), channel_id=1, source_target_pairs={{0,2},{1,3},{2,0},{3,1},{4,6},{5,7},{6,4},{7,5},{8,10},{9,11},{10,... | collective-permute-start | bytes 393224 | tf_op jit(solution)/shard_map/ppermute | solution.py:222
  93.9 4.2 %collective-permute-start.16 = (f32[512,128]{1,0:T(8,128)S(1)}, f32[512,128]{1,0:T(8,128)S(1)}, u32[]{:S(2)}, u32[]{:S(2)}) collective-permute-start(f32[512,128]{1,0:T(8,128)S(1)} %get-tuple-element.69), channel_id=1, source_target_pairs={{0,1},{1,0},{2,3},{3,2},{4,5},{5,4},{6,7},{7,6},{8,9},{9,8},{10,11... | collective-permute-start | bytes 786440 | tf_op jit(solution)/shard_map/ppermute | solution.py:222
  98.1 1.0 copy-start.8
  99.1 1.3 %copy-start.7 = (f32[4,1024,128]{2,1,0:T(8,128)}, f32[4,1024,128]{2,1,0:T(8,128)S(1)}, u32[]{:S(2)}) copy-start(f32[4,1024,128]{2,1,0:T(8,128)S(1)} %bitcast_dynamic-update-slice_fusion) | copy-start | bytes 6291460

commit v7 on v4

--- a/solution.py
+++ b/solution.py
@@ -112,6 +112,20 @@
     return dot(left[0], right[0]) + (dot(left[0], right[1]) + dot(left[1], right[0]))
 
 
+def cut_kernel(info, blocks, near, far_a, far_b, sems):
+    me = info[0]
+    half = pl.ds((me // 2) * (W // 2), W // 2)
+    copies = [
+        pltpu.make_async_copy(blocks.at[me ^ 2, half], far_a, sems.at[0]),
+        pltpu.make_async_copy(blocks.at[me ^ 3, half], far_b, sems.at[1]),
+        pltpu.make_async_copy(blocks.at[me ^ 1], near, sems.at[2]),
+    ]
+    for c in copies:
+        c.start()
+    for c in copies:
+        c.wait()
+
+
 def factor_kernel(info, own_ref, r1, r2, r3, l0, l1, l2, l3, mt, a, l, sems):
     me = info[0]
     side = me // 2
@@ -234,10 +248,19 @@
     assert narrow_count == NB and diag_block.shape[0] == NB
     masks = range(1, NB)
     own = lambda x, m: lax.dynamic_index_in_dim(x, me ^ m, 0, keepdims=False)
-    half_of = lambda x, m: lax.dynamic_slice(
-        x, (me ^ m, (me // 2) * (W // 2), 0), (1, W // 2, B)
-    ).reshape(W // 2, B)
-    diag_in = [swap(own(diag_block, m) if m == 1 else half_of(diag_block, m), "narrow", m) for m in masks]
+    info = me.astype(jnp.int32).reshape(1)
+    cut = [jax.ShapeDtypeStruct((rows, B), jnp.float32) for rows in (W, W // 2, W // 2)]
+    cut = pl.pallas_call(
+        cut_kernel,
+        out_shape=cut,
+        in_specs=[SMEM, pl.BlockSpec(memory_space=pltpu.HBM)],
+        out_specs=[VMEM] * 3,
+        scratch_shapes=[pltpu.SemaphoreType.DMA((3,))],
+        compiler_params=pltpu.CompilerParams(vmem_limit_bytes=8 * 2**20),
+        cost_estimate=pl.CostEstimate(flops=0, bytes_accessed=2**20, transcendentals=0),
+        name="cut",
+    )(info, diag_block)
+    diag_in = [swap(part, "narrow", m) for m, part in zip(masks, cut)]
     panel_out = [own(panel, m) for m in masks]
     diag_in, panel_out = lax.optimization_barrier((diag_in, panel_out))
     panel_in = [swap(panel_out[m - 1], "narrow", m) for m in masks]
@@ -251,7 +274,6 @@
     slot = lax.dynamic_slice_in_dim(pair_slot, me * NPAIR, NPAIR)
     tgt_a = relative_index(owner, slot, wide_me, me, steps_a)
     tgt_b = relative_index(owner, slot, wide_me, me, steps_b)
-    info = me.astype(jnp.int32).reshape(1)
 
     slab = jax.ShapeDtypeStruct((W, B), jnp.float32)
     *l_parts, mt = pl.pallas_call(
@@ -275,7 +297,7 @@
         in_specs=[SMEM] * 4 + [VMEM] * (NB + 1),
         out_specs=[VMEM] * (NB + 2),
         scratch_shapes=[pltpu.VMEM((rows, W), jnp.bfloat16)] * 2,
-        compiler_params=pltpu.CompilerParams(vmem_limit_bytes=52 * 2**20),
+        compiler_params=pltpu.CompilerParams(vmem_limit_bytes=20 * 2**20 + 4 * blocks * B * B),
         cost_estimate=pl.CostEstimate(flops=10**9, bytes_accessed=10 * 10**6, transcendentals=0),
         name="panel",
     )(info, panel_count, tgt_a, tgt_b, panel, *panel_in, mt)
@@ -291,29 +313,31 @@
     send_b = upper(keep, 1) + upper(got, 1)
     keep_a = lower(keep, 0) + lower(got, 0)
     keep_b = lower(keep, 1) + lower(got, 1)
-    for n in (1, 2):
-        if n == 2:
-            send_a, send_b, x_back[1] = lax.optimization_barrier((send_a, send_b, x_back[1]))
-        else:
-            send_a, send_b = lax.optimization_barrier((send_a, send_b))
+    for n, (box, at) in ((1, (l_back, 1)), (2, (x_back, 1))):
+        send_a, send_b, box[at] = lax.optimization_barrier((send_a, send_b, box[at]))
         got_a = swap(send_a, *steps_a[n])
         got_b = swap(send_b, *steps_b[n])
         half = half // 2
-        send_a, send_b = keep_a[half:] + got_a[half:], keep_b[half:] + got_b[half:]
-        keep_a, keep_b = keep_a[:half] + got_a[:half], keep_b[:half] + got_b[:half]
-    send = jnp.stack([send_a, send_b], axis=1)
-    keep = jnp.stack([keep_a, keep_b], axis=1)
-    for n in range(3, len(steps_a)):
-        if n == 3:
-            send, l_back[1] = lax.optimization_barrier((send, l_back[1]))
-        if n == len(steps_a) - 1:
-            send, x_back[2], x_back[0] = lax.optimization_barrier((send, x_back[2], x_back[0]))
-        got = swap(send, *steps_a[n])
-        if n + 1 < len(steps_a):
-            half = half // 2
-            send = keep[half:] + got[half:]
-            keep = keep[:half] + got[:half]
-    updated = ancestor - (keep + got).reshape(ancestor.shape)
+        if n == 1:
+            send_a, send_b = keep_a[half:] + got_a[half:], keep_b[half:] + got_b[half:]
+            keep_a, keep_b = keep_a[:half] + got_a[:half], keep_b[:half] + got_b[:half]
+    rest = steps_a[3:]
+    take = lambda n, size: jnp.concatenate(
+        [u[n * size : (n + 1) * size] + v[n * size : (n + 1) * size] for u, v in ((keep_a, got_a), (keep_b, got_b))],
+        axis=1,
+    )
+    while len(rest) > 2:
+        got = swap(take(1, half), *rest.pop(0))
+        keep_a = take(0, half) + got
+        half = half // 2
+        keep_a, keep_b = keep_a[:, : B // 2], keep_a[:, B // 2 :]
+        got_a, got_b = jnp.zeros_like(keep_a), jnp.zeros_like(keep_b)
+    onward, stay = take(3, T_DEV), take(2, T_DEV)
+    onward, stay, l_back[2] = lax.optimization_barrier((onward, stay, l_back[2]))
+    onward = take(1, T_DEV) + swap(onward, *rest[0])
+    stay = swap(stay, *rest[0])
+    onward, x_back[2], x_back[0] = lax.optimization_barrier((onward, x_back[2], x_back[0]))
+    updated = ancestor - (take(0, T_DEV) + stay + swap(onward, *rest[1]))
 
     def give_back(own_part, others):
         back = [own_part] + others

time: 98.4 us -> 98.7 us (level)
  starting transfers between devices: 16.7 us -> 19.7 us
  other arithmetic: 29 us -> 26.4 us
    ppermute x19 -> x20, starting transfers between devices: 16.7 us -> 19.7 us  [swap(): return lax.ppermute(x, axis, xor_pairs(lax.axis_size(axis), mask))]
    pallas_call x1, other arithmetic: 7 us -> 5.04 us  [local(): pl.pallas_call(panel_kernel, out_shape=[slab] * NB + [part, part], in_spe...]
    unnamed x22 -> x18, local copies, waits for them, and re-layouts: 0.06 us -> 1.26 us
    squeeze x2 -> x1, local copies, waits for them, and re-layouts: 3.48 us -> 2.34 us  [local(): own = lambda x, m: lax.dynamic_index_in_dim(x, me ^ m, 0, keepdims=False)]
    ppermute x19 -> x20, waiting for transfers between devices: 46.6 us -> 47.3 us  [swap(): return lax.ppermute(x, axis, xor_pairs(lax.axis_size(axis), mask))]
  transfers between devices with their start and end apart: 19 -> 20, of which waited for: 12 -> 13; matrix products, arithmetic and copies ran while one was open for 25% -> 24% of each run, Pallas kernels for 0% -> 0%
where the time goes in v7:
time: 98.7 us; the launch traced here: 98.6 us
  waiting for transfers between devices  47.3 us (48%)
  other arithmetic  26.4 us (27%)
  starting transfers between devices  19.7 us (20%)
  local copies, waits for them, and re-layouts  3.99 us (4%)
    ppermute x20, waiting for transfers between devices, swap(): return lax.ppermute(x, axis, xor_pairs(lax.axis_size(axis), mask))  47.3 us
    pallas_call x1, other arithmetic, local(): pl.pallas_call(factor_kernel, out_shape=[slab] * NB + [jax.ShapeDtypeStru...  19.8 us
    ppermute x20, starting transfers between devices, swap(): return lax.ppermute(x, axis, xor_pairs(lax.axis_size(axis), mask))  19.7 us
    pallas_call x1, other arithmetic, local(): pl.pallas_call(panel_kernel, out_shape=[slab] * NB + [part, part], in_spe...  5.04 us
    squeeze x1, local copies, waits for them, and re-layouts, local(): own = lambda x, m: lax.dynamic_index_in_dim(x, me ^ m, 0, keepdims=False)  2.34 us
  transfers between devices with their start and end apart: 20, of which 13 were waited for; matrix products, arithmetic and copies ran while one was open for 24% of the time, Pallas kernels for 0%

profile of v7, /device:TPU:0, one launch (start us, length us, event | category | flops | bytes accessed | tf_op | source)
XLA Modules:
  0.0 98.6 jit_solution(16837931870826856401)
XLA Ops:
  0.6 0.0 copy-start
  0.6 1.2 %copy-done = f32[4,512,128]{2,1,0:T(8,128)S(1)} copy-done((f32[4,512,128]{2,1,0:T(8,128)S(1)}, f32[4,512,128]{2,1,0:T(8,128)}, u32[]{:S(2)}) %copy-start) | copy-done | bytes 1048600
  1.9 0.4 cut.1
  2.2 0.5 collective-permute-start
  2.8 2.6 %collective-permute-start.1 = (f32[256,128]{1,0:T(8,128)S(1)}, f32[256,128]{1,0:T(8,128)S(1)}, u32[]{:S(2)}, u32[]{:S(2)}) collective-permute-start(f32[256,128]{1,0:T(8,128)S(1)} %get-tuple-element.36), channel_id=1, source_target_pairs={{0,2},{1,3},{2,0},{3,1},{4,6},{5,7},{6,4},{7,5},{8,10},{9,11},{10,... | collective-permute-start | bytes 393224 | tf_op jit(solution)/shard_map/ppermute | solution.py:232
  5.3 0.1 collective-permute-start.2
  5.4 2.3 %dynamic-slice_bitcast_fusion = (f32[1024,128]{1,0:T(8,128)S(1)}, f32[1024,128]{1,0:T(8,128)S(1)}, f32[1024,128]{1,0:T(8,128)}) fusion(f32[4,1024,128]{2,1,0:T(8,128)} %param.7, s32[]{:T(128)S(6)} %select_n.59, s32[]{:T(128)S(6)} %select_n.58, s32[]{:T(128)S(6)} %select_n.57), kind=kLoop, calls=%fused_computation.10 | loop fusion | bytes 3145740 | tf_op jit(solution)/shard_map/jit(dynamic_index_in_dim)/squeeze | solution.py:250
  7.7 1.9 %collective-permute-done.1 = f32[256,128]{1,0:T(8,128)S(1)} collective-permute-done((f32[256,128]{1,0:T(8,128)S(1)}, f32[256,128]{1,0:T(8,128)S(1)}, u32[]{:S(2)}, u32[]{:S(2)}) %collective-permute-start.1) | collective-permute-done | bytes 131104 | tf_op jit(solution)/shard_map/ppermute | solution.py:232
  9.7 2.4 %collective-permute-done.2 = f32[256,128]{1,0:T(8,128)} collective-permute-done((f32[256,128]{1,0:T(8,128)S(1)}, f32[256,128]{1,0:T(8,128)}, u32[]{:S(2)}, u32[]{:S(2)}) %collective-permute-start.2) | collective-permute-done | bytes 131104 | tf_op jit(solution)/shard_map/ppermute | solution.py:232
  12.1 0.0 collective-permute-done
  12.1 0.1 collective-permute-start.4
  12.2 1.7 %collective-permute-start.5 = (f32[1024,128]{1,0:T(8,128)S(1)}, f32[1024,128]{1,0:T(8,128)S(1)}, u32[]{:S(2)}, u32[]{:S(2)}) collective-permute-start(f32[1024,128]{1,0:T(8,128)S(1)} %get-tuple-element.44), channel_id=1, source_target_pairs={{0,2},{1,3},{2,0},{3,1},{4,6},{5,7},{6,4},{7,5},{8,10},{9,11},{10,... | collective-permute-start | bytes 1572872 | tf_op jit(solution)/shard_map/ppermute | solution.py:232
  13.9 0.0 collective-permute-start.6
  14.0 0.0 copy-done.6
  14.0 0.0 copy-done.7
  14.0 0.1 multiply_add_fusion
  14.1 0.1 multiply_add_fusion.1
  14.2 0.1 broadcast_in_dim.32
  14.2 0.0 copy-done.1
  14.2 0.0 copy-start.2
  14.3 0.0 copy-start.8
  14.3 19.8 %factor.1 = (f32[4,512,128]{2,1,0:T(8,128)S(1)}, f32[512,128]{1,0:T(8,128)S(1)}, f32[4,512,128]{2,1,0:T(8,128)S(1)}, f32[512,128]{1,0:T(8,128)S(1)}, f32[512,128]{1,0:T(8,128)S(1)}) fusion(f32[4,512,128]{2,1,0:T(8,128)S(1)} %broadcast_in_dim.32, s32[]{:T(128)S(6)} %select_n.60, s32[1]{0:T(128)} %bitcast.info, f32[4,512,128]{2,1,0:T(8,128)S(1)} %copy-done.1, ...), kind=kCustom, calls=%fused_computation.24 | custom fusion | flops 200000000 | bytes 3670024 | tf_op jit(solution)/shard_map/factor/pallas_call | solution.py:279
  34.1 0.0 collective-permute-done.4
  34.1 0.0 collective-permute-done.5
  34.1 3.1 %collective-permute-done.6 = f32[1024,128]{1,0:T(8,128)} collective-permute-done((f32[1024,128]{1,0:T(8,128)S(1)}, f32[1024,128]{1,0:T(8,128)}, u32[]{:S(2)}, u32[]{:S(2)}) %collective-permute-start.6) | collective-permute-done | bytes 524320 | tf_op jit(solution)/shard_map/ppermute | solution.py:232
  37.2 0.1 broadcast_in_dim.37
  37.4 5.0 %panel.1 = (f32[4,1024,128]{2,1,0:T(8,128)S(1)}, f32[2,32,64,128]{3,2,1,0:T(8,128)S(1)}, f32[2,32,64,128]{3,2,1,0:T(8,128)S(1)}, f32[1024,128]{1,0:T(8,128)S(1)}...) fusion(f32[4,1024,128]{2,1,0:T(8,128)S(1)} %broadcast_in_dim.37, s32[]{:T(128)S(6)} %select_n.60, s32[1]{0:T(128)} %bitcast.info, ...), kind=kCustom, calls=%fused_computation.9 | custom fusion | flops 1000000000 | bytes 11011592 | tf_op jit(solution)/shard_map/panel/pallas_call | solution.py:294
  42.4 0.1 collective-permute-start.7
  42.5 2.5 %collective-permute-start.8 = (f32[512,128]{1,0:T(8,128)S(1)}, f32[512,128]{1,0:T(8,128)S(1)}, u32[]{:S(2)}, u32[]{:S(2)}) collective-permute-start(f32[512,128]{1,0:T(8,128)S(1)} %get-tuple-element.74), channel_id=1, source_target_pairs={{0,2},{1,3},{2,0},{3,1},{4,6},{5,7},{6,4},{7,5},{8,10},{9,11},{10,... | collective-permute-start | bytes 786440 | tf_op jit(solution)/shard_map/ppermute | solution.py:232
  45.0 1.6 %collective-permute-done.7 = f32[2,32,64,128]{3,2,1,0:T(8,128)S(1)} collective-permute-done((f32[2,32,64,128]{3,2,1,0:T(8,128)S(1)}, f32[2,32,64,128]{3,2,1,0:T(8,128)S(1)}, u32[]{:S(2)}, u32[]{:S(2)}) %collective-permute-start.7) | collective-permute-done | bytes 2097184 | tf_op jit(solution)/shard_map/ppermute | solution.py:232
  46.6 0.4 slice_add_fusion
  47.0 4.9 %collective-permute-done.8 = f32[512,128]{1,0:T(8,128)S(1)} collective-permute-done((f32[512,128]{1,0:T(8,128)S(1)}, f32[512,128]{1,0:T(8,128)S(1)}, u32[]{:S(2)}, u32[]{:S(2)}) %collective-permute-start.8) | collective-permute-done | bytes 262176 | tf_op jit(solution)/shard_map/ppermute | solution.py:232
  51.9 1.8 %collective-permute-start.9 = (f32[16,64,128]{2,1,0:T(8,128)S(1)}, f32[16,64,128]{2,1,0:T(8,128)S(1)}, u32[]{:S(2)}, u32[]{:S(2)}) collective-permute-start(f32[16,64,128]{2,1,0:T(8,128)S(1)} %get-tuple-element.51), channel_id=1, source_target_pairs={{0,4},{4,0},{8,12},{12,8},{16,20},{20,16},{24,28},{28,24},{1,5},{5... | collective-permute-start | bytes 1572872 | tf_op jit(solution)/shard_map/ppermute | solution.py:232
  53.7 1.3 %collective-permute-start.10 = (f32[16,64,128]{2,1,0:T(8,128)S(1)}, f32[16,64,128]{2,1,0:T(8,128)S(1)}, u32[]{:S(2)}, u32[]{:S(2)}) collective-permute-start(f32[16,64,128]{2,1,0:T(8,128)S(1)} %get-tuple-element.52), channel_id=1, source_target_pairs={{0,8},{4,12},{8,0},{12,4},{16,24},{20,28},{24,16},{28,20},{1,9},{5... | collective-permute-start | bytes 1572872 | tf_op jit(solution)/shard_map/ppermute | solution.py:232
  55.0 1.8 %collective-permute-start.11 = (f32[1024,128]{1,0:T(8,128)S(1)}, f32[1024,128]{1,0:T(8,128)S(1)}, u32[]{:S(2)}, u32[]{:S(2)}) collective-permute-start(f32[1024,128]{1,0:T(8,128)S(1)} %get-tuple-element.107), channel_id=1, source_target_pairs={{0,2},{1,3},{2,0},{3,1},{4,6},{5,7},{6,4},{7,5},{8,10},{9,11},{10,... | collective-permute-start | bytes 1572872 | tf_op jit(solution)/shard_map/ppermute | solution.py:232
  56.7 0.0 collective-permute-start.3
  56.8 0.4 collective-permute-start.14
  57.1 8.4 %collective-permute-done.9 = f32[16,64,128]{2,1,0:T(8,128)S(1)} collective-permute-done((f32[16,64,128]{2,1,0:T(8,128)S(1)}, f32[16,64,128]{2,1,0:T(8,128)S(1)}, u32[]{:S(2)}, u32[]{:S(2)}) %collective-permute-start.9) | collective-permute-done | bytes 524320 | tf_op jit(solution)/shard_map/ppermute | solution.py:232
  65.6 0.1 slice_add_fusion.7
  65.6 1.3 %collective-permute-done.10 = f32[16,64,128]{2,1,0:T(8,128)S(1)} collective-permute-done((f32[16,64,128]{2,1,0:T(8,128)S(1)}, f32[16,64,128]{2,1,0:T(8,128)S(1)}, u32[]{:S(2)}, u32[]{:S(2)}) %collective-permute-start.10) | collective-permute-done | bytes 524320 | tf_op jit(solution)/shard_map/ppermute | solution.py:232
  66.9 0.1 slice_add_fusion.4
  67.0 2.9 %collective-permute-done.11 = f32[1024,128]{1,0:T(8,128)S(1)} collective-permute-done((f32[1024,128]{1,0:T(8,128)S(1)}, f32[1024,128]{1,0:T(8,128)S(1)}, u32[]{:S(2)}, u32[]{:S(2)}) %collective-permute-start.11) | collective-permute-done | bytes 524320 | tf_op jit(solution)/shard_map/ppermute | solution.py:232
  69.8 0.7 collective-permute-start.12
  70.6 0.0 collective-permute-done.3
  70.6 0.1 collective-permute-start.16
  70.7 1.1 %collective-permute-start.17 = (f32[1024,128]{1,0:T(8,128)S(1)}, f32[1024,128]{1,0:T(8,128)S(1)}, u32[]{:S(2)}, u32[]{:S(2)}) collective-permute-start(f32[1024,128]{1,0:T(8,128)S(1)} %get-tuple-element.112), channel_id=1, source_target_pairs={{0,1},{1,0},{2,3},{3,2},{4,5},{5,4},{6,7},{7,6},{8,9},{9,8},{10,11... | collective-permute-start | bytes 1572872 | tf_op jit(solution)/shard_map/ppermute | solution.py:232
  71.8 1.0 collective-permute-start.13
  72.8 3.4 %collective-permute-done.12 = f32[8,64,128]{2,1,0:T(8,128)S(1)} collective-permute-done((f32[8,64,128]{2,1,0:T(8,128)S(1)}, f32[8,64,128]{2,1,0:T(8,128)S(1)}, u32[]{:S(2)}, u32[]{:S(2)}) %collective-permute-start.12) | collective-permute-done | bytes 262176 | tf_op jit(solution)/shard_map/ppermute | solution.py:232
  76.3 3.8 %collective-permute-done.13 = f32[8,64,128]{2,1,0:T(8,128)S(1)} collective-permute-done((f32[8,64,128]{2,1,0:T(8,128)S(1)}, f32[8,64,128]{2,1,0:T(8,128)S(1)}, u32[]{:S(2)}, u32[]{:S(2)}) %collective-permute-start.13) | collective-permute-done | bytes 262176 | tf_op jit(solution)/shard_map/ppermute | solution.py:232
  80.1 0.0 copy-start.5
  80.1 0.0 collective-permute-done.14
  80.1 3.2 %collective-permute-start.15 = (f32[2,128,128]{2,1,0:T(8,128)S(1)}, f32[2,128,128]{2,1,0:T(8,128)S(1)}, u32[]{:S(2)}, u32[]{:S(2)}) collective-permute-start(f32[2,128,128]{2,1,0:T(8,128)S(1)} %get-tuple-element.59), channel_id=1, source_target_pairs={{0,16},{4,20},{8,24},{12,28},{16,0},{20,4},{24,8},{28,12},{1,17},{... | collective-permute-start | bytes 393224 | tf_op jit(solution)/shard_map/ppermute | solution.py:232
  83.3 0.1 collective-permute-start.18
  83.4 0.0 copy-start.4
  83.4 9.5 %collective-permute-done.15 = f32[2,128,128]{2,1,0:T(8,128)S(1)} collective-permute-done((f32[2,128,128]{2,1,0:T(8,128)S(1)}, f32[2,128,128]{2,1,0:T(8,128)S(1)}, u32[]{:S(2)}, u32[]{:S(2)}) %collective-permute-start.15) | collective-permute-done | bytes 131104 | tf_op jit(solution)/shard_map/ppermute | solution.py:232
  92.9 0.0 collective-permute-done.16
  92.9 0.0 collective-permute-done.17
  92.9 0.8 collective-permute-start.19
  93.8 0.0 copy-start.3
  93.8 0.7 collective-permute-done.18
  94.5 3.4 %collective-permute-done.19 = f32[2,128,128]{2,1,0:T(8,128)S(1)} collective-permute-done((f32[2,128,128]{2,1,0:T(8,128)S(1)}, f32[2,128,128]{2,1,0:T(8,128)S(1)}, u32[]{:S(2)}, u32[]{:S(2)}) %collective-permute-start.19) | collective-permute-done | bytes 131104 | tf_op jit(solution)/shard_map/ppermute | solution.py:232
  97.9 0.0 copy-done.5
  97.9 0.7 fusion.3
  98.6 0.0 copy-done.4
  (16 shorter events, 0.3 us)
Async XLA Ops:
  0.6 1.2 %copy-start = (f32[4,512,128]{2,1,0:T(8,128)S(1)}, f32[4,512,128]{2,1,0:T(8,128)}, u32[]{:S(2)}) copy-start(f32[4,512,128]{2,1,0:T(8,128)} %blocks.1) | copy-start | bytes 3145732
  1.9 12.1 %copy-start.6 = (s32[144,1]{0,1:T(1,128)S(1)}, s32[144,1]{0,1:T(1,128)}, u32[]{:S(2)}) copy-start(s32[144,1]{0,1:T(1,128)} %param.9) | copy-start | bytes 1732
  1.9 12.1 %copy-start.7 = (s32[144]{0:T(256)S(1)}, s32[144]{0:T(256)}, u32[]{:S(2)}) copy-start(s32[144]{0:T(256)} %param.10) | copy-start | bytes 1732
  2.2 9.8 %collective-permute-start = (f32[512,128]{1,0:T(8,128)S(1)}, f32[512,128]{1,0:T(8,128)S(1)}, u32[]{:S(2)}, u32[]{:S(2)}) collective-permute-start(f32[512,128]{1,0:T(8,128)S(1)} %get-tuple-element.35), channel_id=1, source_target_pairs={{0,1},{1,0},{2,3},{3,2},{4,5},{5,4},{6,7},{7,6},{8,9},{9,8},{10,11... | collective-permute-start | bytes 786440 | tf_op jit(solution)/shard_map/ppermute | solution.py:232
  2.8 6.9 %collective-permute-start.1 = (f32[256,128]{1,0:T(8,128)S(1)}, f32[256,128]{1,0:T(8,128)S(1)}, u32[]{:S(2)}, u32[]{:S(2)}) collective-permute-start(f32[256,128]{1,0:T(8,128)S(1)} %get-tuple-element.36), channel_id=1, source_target_pairs={{0,2},{1,3},{2,0},{3,1},{4,6},{5,7},{6,4},{7,5},{8,10},{9,11},{10,... | collective-permute-start | bytes 393224 | tf_op jit(solution)/shard_map/ppermute | solution.py:232
  5.3 6.7 %collective-permute-start.2 = (f32[256,128]{1,0:T(8,128)S(1)}, f32[256,128]{1,0:T(8,128)}, u32[]{:S(2)}, u32[]{:S(2)}) collective-permute-start(f32[256,128]{1,0:T(8,128)S(1)} %get-tuple-element.37), channel_id=1, source_target_pairs={{0,3},{1,2},{2,1},{3,0},{4,7},{5,6},{6,5},{7,4},{8,11},{9,10},{10,... | collective-permute-start | bytes 393224 | tf_op jit(solution)/shard_map/ppermute | solution.py:232
  5.4 8.8 %copy-start.1 = (f32[4,512,128]{2,1,0:T(8,128)S(1)}, f32[4,512,128]{2,1,0:T(8,128)}, u32[]{:S(2)}) copy-start(f32[4,512,128]{2,1,0:T(8,128)} %blocks.1) | copy-start | bytes 3145732
  12.1 22.0 %collective-permute-start.4 = (f32[1024,128]{1,0:T(8,128)}, f32[1024,128]{1,0:T(8,128)S(1)}, u32[]{:S(2)}, u32[]{:S(2)}) collective-permute-start(f32[1024,128]{1,0:T(8,128)} %get-tuple-element.43), channel_id=1, source_target_pairs={{0,1},{1,0},{2,3},{3,2},{4,5},{5,4},{6,7},{7,6},{8,9},{9,8},{10,11... | collective-permute-start | bytes 1572872 | tf_op jit(solution)/shard_map/ppermute | solution.py:232
  12.2 21.9 %collective-permute-start.5 = (f32[1024,128]{1,0:T(8,128)S(1)}, f32[1024,128]{1,0:T(8,128)S(1)}, u32[]{:S(2)}, u32[]{:S(2)}) collective-permute-start(f32[1024,128]{1,0:T(8,128)S(1)} %get-tuple-element.44), channel_id=1, source_target_pairs={{0,2},{1,3},{2,0},{3,1},{4,6},{5,7},{6,4},{7,5},{8,10},{9,11},{10,... | collective-permute-start | bytes 1572872 | tf_op jit(solution)/shard_map/ppermute | solution.py:232
  13.9 23.3 %collective-permute-start.6 = (f32[1024,128]{1,0:T(8,128)S(1)}, f32[1024,128]{1,0:T(8,128)}, u32[]{:S(2)}, u32[]{:S(2)}) collective-permute-start(f32[1024,128]{1,0:T(8,128)S(1)} %get-tuple-element.45), channel_id=1, source_target_pairs={{0,3},{1,2},{2,1},{3,0},{4,7},{5,6},{6,5},{7,4},{8,11},{9,10},{10,... | collective-permute-start | bytes 1572872 | tf_op jit(solution)/shard_map/ppermute | solution.py:232
  14.2 23.1 %copy-start.2 = (f32[4,1024,128]{2,1,0:T(8,128)S(1)}, f32[4,1024,128]{2,1,0:T(8,128)}, u32[]{:S(2)}) copy-start(f32[4,1024,128]{2,1,0:T(8,128)} %param.7) | copy-start | bytes 6291460
  14.3 23.1 %copy-start.8 = (s32[4]{0:T(128)S(1)}, s32[4]{0:T(128)}, u32[]{:S(2)}) copy-start(s32[4]{0:T(128)} %param.8) | copy-start | bytes 52
  42.4 4.2 %collective-permute-start.7 = (f32[2,32,64,128]{3,2,1,0:T(8,128)S(1)}, f32[2,32,64,128]{3,2,1,0:T(8,128)S(1)}, u32[]{:S(2)}, u32[]{:S(2)}) collective-permute-start(f32[2,32,64,128]{3,2,1,0:T(8,128)S(1)} %get-tuple-element.105), channel_id=1, source_target_pairs={{0,1},{1,0},{2,3},{3,2},{4,5},{5,4},{6,7},{7,6},{8,9},{9,8},{10,11... | collective-permute-start | bytes 6291464 | tf_op jit(solution)/shard_map/ppermute | solution.py:232
  42.5 9.4 %collective-permute-start.8 = (f32[512,128]{1,0:T(8,128)S(1)}, f32[512,128]{1,0:T(8,128)S(1)}, u32[]{:S(2)}, u32[]{:S(2)}) collective-permute-start(f32[512,128]{1,0:T(8,128)S(1)} %get-tuple-element.74), channel_id=1, source_target_pairs={{0,2},{1,3},{2,0},{3,1},{4,6},{5,7},{6,4},{7,5},{8,10},{9,11},{10,... | collective-permute-start | bytes 786440 | tf_op jit(solution)/shard_map/ppermute | solution.py:232
  51.9 13.7 %collective-permute-start.9 = (f32[16,64,128]{2,1,0:T(8,128)S(1)}, f32[16,64,128]{2,1,0:T(8,128)S(1)}, u32[]{:S(2)}, u32[]{:S(2)}) collective-permute-start(f32[16,64,128]{2,1,0:T(8,128)S(1)} %get-tuple-element.51), channel_id=1, source_target_pairs={{0,4},{4,0},{8,12},{12,8},{16,20},{20,16},{24,28},{28,24},{1,5},{5... | collective-permute-start | bytes 1572872 | tf_op jit(solution)/shard_map/ppermute | solution.py:232
  53.7 13.2 %collective-permute-start.10 = (f32[16,64,128]{2,1,0:T(8,128)S(1)}, f32[16,64,128]{2,1,0:T(8,128)S(1)}, u32[]{:S(2)}, u32[]{:S(2)}) collective-permute-start(f32[16,64,128]{2,1,0:T(8,128)S(1)} %get-tuple-element.52), channel_id=1, source_target_pairs={{0,8},{4,12},{8,0},{12,4},{16,24},{20,28},{24,16},{28,20},{1,9},{5... | collective-permute-start | bytes 1572872 | tf_op jit(solution)/shard_map/ppermute | solution.py:232
  55.0 14.9 %collective-permute-start.11 = (f32[1024,128]{1,0:T(8,128)S(1)}, f32[1024,128]{1,0:T(8,128)S(1)}, u32[]{:S(2)}, u32[]{:S(2)}) collective-permute-start(f32[1024,128]{1,0:T(8,128)S(1)} %get-tuple-element.107), channel_id=1, source_target_pairs={{0,2},{1,3},{2,0},{3,1},{4,6},{5,7},{6,4},{7,5},{8,10},{9,11},{10,... | collective-permute-start | bytes 1572872 | tf_op jit(solution)/shard_map/ppermute | solution.py:232
  56.7 13.8 %collective-permute-start.3 = (f32[512,128]{1,0:T(8,128)S(1)}, f32[512,128]{1,0:T(8,128)S(1)}, u32[]{:S(2)}, u32[]{:S(2)}) collective-permute-start(f32[512,128]{1,0:T(8,128)S(1)} %get-tuple-element.70), channel_id=1, source_target_pairs={{0,1},{1,0},{2,3},{3,2},{4,5},{5,4},{6,7},{7,6},{8,9},{9,8},{10,11... | collective-permute-start | bytes 786440 | tf_op jit(solution)/shard_map/ppermute | solution.py:232
  56.8 23.4 %collective-permute-start.14 = (f32[512,128]{1,0:T(8,128)S(1)}, f32[512,128]{1,0:T(8,128)S(1)}, u32[]{:S(2)}, u32[]{:S(2)}) collective-permute-start(f32[512,128]{1,0:T(8,128)S(1)} %get-tuple-element.76), channel_id=1, source_target_pairs={{0,3},{1,2},{2,1},{3,0},{4,7},{5,6},{6,5},{7,4},{8,11},{9,10},{10,... | collective-permute-start | bytes 786440 | tf_op jit(solution)/shard_map/ppermute | solution.py:232
  69.8 6.4 %collective-permute-start.12 = (f32[8,64,128]{2,1,0:T(8,128)S(1)}, f32[8,64,128]{2,1,0:T(8,128)S(1)}, u32[]{:S(2)}, u32[]{:S(2)}) collective-permute-start(f32[8,64,128]{2,1,0:T(8,128)S(1)} %get-tuple-element.54), channel_id=1, source_target_pairs={{0,8},{4,12},{8,0},{12,4},{16,24},{20,28},{24,16},{28,20},{1,9},{5... | collective-permute-start | bytes 786440 | tf_op jit(solution)/shard_map/ppermute | solution.py:232
  70.6 22.3 %collective-permute-start.16 = (f32[1024,128]{1,0:T(8,128)S(1)}, f32[1024,128]{1,0:T(8,128)S(1)}, u32[]{:S(2)}, u32[]{:S(2)}) collective-permute-start(f32[1024,128]{1,0:T(8,128)S(1)} %get-tuple-element.110), channel_id=1, source_target_pairs={{0,3},{1,2},{2,1},{3,0},{4,7},{5,6},{6,5},{7,4},{8,11},{9,10},{10,... | collective-permute-start | bytes 1572872 | tf_op jit(solution)/shard_map/ppermute | solution.py:232
  70.7 22.2 %collective-permute-start.17 = (f32[1024,128]{1,0:T(8,128)S(1)}, f32[1024,128]{1,0:T(8,128)S(1)}, u32[]{:S(2)}, u32[]{:S(2)}) collective-permute-start(f32[1024,128]{1,0:T(8,128)S(1)} %get-tuple-element.112), channel_id=1, source_target_pairs={{0,1},{1,0},{2,3},{3,2},{4,5},{5,4},{6,7},{7,6},{8,9},{9,8},{10,11... | collective-permute-start | bytes 1572872 | tf_op jit(solution)/shard_map/ppermute | solution.py:232
  71.8 8.2 %collective-permute-start.13 = (f32[8,64,128]{2,1,0:T(8,128)S(1)}, f32[8,64,128]{2,1,0:T(8,128)S(1)}, u32[]{:S(2)}, u32[]{:S(2)}) collective-permute-start(f32[8,64,128]{2,1,0:T(8,128)S(1)} %get-tuple-element.55), channel_id=1, source_target_pairs={{0,4},{4,0},{8,12},{12,8},{16,20},{20,16},{24,28},{28,24},{1,5},{5... | collective-permute-start | bytes 786440 | tf_op jit(solution)/shard_map/ppermute | solution.py:232
  80.1 17.9 %copy-start.5 = (f32[2,128,128]{2,1,0:T(8,128)S(1)}, f32[2,128,128]{2,1,0:T(8,128)}, u32[]{:S(2)}) copy-start(f32[2,128,128]{2,1,0:T(8,128)} %param.11) | copy-start | bytes 393220
  80.1 12.8 %collective-permute-start.15 = (f32[2,128,128]{2,1,0:T(8,128)S(1)}, f32[2,128,128]{2,1,0:T(8,128)S(1)}, u32[]{:S(2)}, u32[]{:S(2)}) collective-permute-start(f32[2,128,128]{2,1,0:T(8,128)S(1)} %get-tuple-element.59), channel_id=1, source_target_pairs={{0,16},{4,20},{8,24},{12,28},{16,0},{20,4},{24,8},{28,12},{1,17},{... | collective-permute-start | bytes 393224 | tf_op jit(solution)/shard_map/ppermute | solution.py:232
  83.3 11.2 %collective-permute-start.18 = (f32[2,128,128]{2,1,0:T(8,128)S(1)}, f32[2,128,128]{2,1,0:T(8,128)S(1)}, u32[]{:S(2)}, u32[]{:S(2)}) collective-permute-start(f32[2,128,128]{2,1,0:T(8,128)S(1)} %get-tuple-element.65), channel_id=1, source_target_pairs={{0,16},{4,20},{8,24},{12,28},{16,0},{20,4},{24,8},{28,12},{1,17},{... | collective-permute-start | bytes 393224 | tf_op jit(solution)/shard_map/ppermute | solution.py:232
  83.4 15.2 %copy-start.4 = (f32[4,512,128]{2,1,0:T(8,128)}, f32[4,512,128]{2,1,0:T(8,128)S(1)}, u32[]{:S(2)}) copy-start(f32[4,512,128]{2,1,0:T(8,128)S(1)} %bitcast_dynamic-update-slice_fusion.4) | copy-start | bytes 3145732
  92.9 5.0 %collective-permute-start.19 = (f32[2,128,128]{2,1,0:T(8,128)S(1)}, f32[2,128,128]{2,1,0:T(8,128)S(1)}, u32[]{:S(2)}, u32[]{:S(2)}) collective-permute-start(f32[2,128,128]{2,1,0:T(8,128)S(1)} %maximum_add_fusion), channel_id=1, source_target_pairs={{0,2},{1,3},{2,0},{3,1},{4,6},{5,7},{6,4},{7,5},{8,10},{9,11},{10,... | collective-permute-start | bytes 393224 | tf_op jit(solution)/shard_map/ppermute | solution.py:232
  93.8 4.8 %copy-start.3 = (f32[4,1024,128]{2,1,0:T(8,128)}, f32[4,1024,128]{2,1,0:T(8,128)S(1)}, u32[]{:S(2)}) copy-start(f32[4,1024,128]{2,1,0:T(8,128)S(1)} %bitcast_dynamic-update-slice_fusion) | copy-start | bytes 6291460

commit v8 on v7

--- a/solution.py
+++ b/solution.py
@@ -172,12 +172,15 @@
         c.wait()
 
 
-def panel_kernel(info, counts, tgt_a, tgt_b, own_ref, r1, r2, r3, mt, x0, x1, x2, x3, keep, send, xh, xl):
+def panel_kernel(
+    info, counts, tgt_a, tgt_b, own_ref, r1, r2, r3, mt, l3, x0, x1, x2, x3, keep, send, xh, xl
+):
     me = info[0]
     count = counts[me]
     rows = P_SIZE * B
     ins = [own_ref.at[me], r1, r2, r3]
     outs = [x0, x1, x2, x3]
+    x3[pl.ds(rows, W), :] = l3[...]
     live = lax.broadcasted_iota(jnp.int32, (rows, B), 0) < count * B
     parts = [split_bf16(jnp.where(live, ref[...], 0.0)) for ref in ins]
     left = [jnp.concatenate([part[n] for part in parts], axis=1) for n in range(2)]
@@ -187,8 +190,8 @@
             for k in range(NB)
         ]
         got = dot3(left, split_bf16(jnp.concatenate(right, axis=0)), ((1,), (0,)))
-        outs[c][...] = got[:, :B]
-        outs[c + 1][...] = got[:, B:]
+        outs[c][pl.ds(0, rows), :] = got[:, :B]
+        outs[c + 1][pl.ds(0, rows), :] = got[:, B:]
         high, low = split_bf16(got)
         xh[:, pl.ds(c * B, 2 * B)] = high
         xl[:, pl.ds(c * B, 2 * B)] = low
@@ -290,21 +293,23 @@
     rows = P_SIZE * B
     blocks = wide_count * narrow_count * T_DEV
     slab = jax.ShapeDtypeStruct((rows, B), jnp.float32)
+    longer = jax.ShapeDtypeStruct((rows + W, B), jnp.float32)
     part = jax.ShapeDtypeStruct((2, blocks // 2, B // 2, B), jnp.float32)
     *x_parts, keep, send = pl.pallas_call(
         panel_kernel,
-        out_shape=[slab] * NB + [part, part],
-        in_specs=[SMEM] * 4 + [VMEM] * (NB + 1),
+        out_shape=[slab] * (NB - 1) + [longer, part, part],
+        in_specs=[SMEM] * 4 + [VMEM] * (NB + 2),
         out_specs=[VMEM] * (NB + 2),
         scratch_shapes=[pltpu.VMEM((rows, W), jnp.bfloat16)] * 2,
         compiler_params=pltpu.CompilerParams(vmem_limit_bytes=20 * 2**20 + 4 * blocks * B * B),
         cost_estimate=pl.CostEstimate(flops=10**9, bytes_accessed=10 * 10**6, transcendentals=0),
         name="panel",
-    )(info, panel_count, tgt_a, tgt_b, panel, *panel_in, mt)
-
-    l_back = [swap(l_parts[m], "narrow", m) for m in masks]
+    )(info, panel_count, tgt_a, tgt_b, panel, *panel_in, mt, l_parts[3])
+
+    l_back = [swap(l_parts[m], "narrow", m) for m in (1, 2)]
     x_back = [swap(x_parts[m], "narrow", m) for m in masks]
 
+    send, l_back[1] = lax.optimization_barrier((send, l_back[1]))
     got = swap(send, "narrow", 1)
     half = blocks // 4
     upper = lambda u, n: u[n, half:]
@@ -313,8 +318,11 @@
     send_b = upper(keep, 1) + upper(got, 1)
     keep_a = lower(keep, 0) + lower(got, 0)
     keep_b = lower(keep, 1) + lower(got, 1)
-    for n, (box, at) in ((1, (l_back, 1)), (2, (x_back, 1))):
-        send_a, send_b, box[at] = lax.optimization_barrier((send_a, send_b, box[at]))
+    for n in (1, 2):
+        if n == 2:
+            send_a, send_b, x_back[1] = lax.optimization_barrier((send_a, send_b, x_back[1]))
+        else:
+            send_a, send_b = lax.optimization_barrier((send_a, send_b))
         got_a = swap(send_a, *steps_a[n])
         got_b = swap(send_b, *steps_b[n])
         half = half // 2
@@ -332,12 +340,17 @@
         half = half // 2
         keep_a, keep_b = keep_a[:, : B // 2], keep_a[:, B // 2 :]
         got_a, got_b = jnp.zeros_like(keep_a), jnp.zeros_like(keep_b)
-    onward, stay = take(3, T_DEV), take(2, T_DEV)
-    onward, stay, l_back[2] = lax.optimization_barrier((onward, stay, l_back[2]))
-    onward = take(1, T_DEV) + swap(onward, *rest[0])
-    stay = swap(stay, *rest[0])
-    onward, x_back[2], x_back[0] = lax.optimization_barrier((onward, x_back[2], x_back[0]))
-    updated = ancestor - (take(0, T_DEV) + stay + swap(onward, *rest[1]))
+    (_, wide_mask), (_, narrow_mask) = rest
+    both = wide_mask * narrow_count + narrow_mask
+    got = [
+        lax.ppermute(take(3, T_DEV), ("wide", "narrow"), xor_pairs(wide_count * narrow_count, both)),
+        swap(take(2, T_DEV), *rest[0]),
+        swap(take(1, T_DEV), *rest[1]),
+    ]
+    got, x_back[2], x_back[0] = lax.optimization_barrier((got, x_back[2], x_back[0]))
+    l_back.append(x_back[2][rows:])
+    x_back[2] = x_back[2][:rows]
+    updated = ancestor - (take(0, T_DEV) + (got[0] + (got[1] + got[2])))
 
     def give_back(own_part, others):
         back = [own_part] + others

time: 98.7 us -> 94.4 us (0.956)
  Pallas kernels: 0.37 us -> 20 us
  other arithmetic: 26.4 us -> 6.98 us
  waiting for transfers between devices: 47.3 us -> 41.7 us
  local copies, waits for them, and re-layouts: 3.99 us -> 5.06 us
    pallas_call x0 -> x1, Pallas kernels: none -> 19.6 us  [local(): pl.pallas_call(factor_kernel, out_shape=[slab] * NB + [jax.ShapeDtypeStru...]
    pallas_call x2 -> x1, other arithmetic: 24.9 us -> 5.38 us  [local(): pl.pallas_call(panel_kernel, out_shape=[slab] * (NB - 1) + [longer, part,...]
    ppermute x20 -> x18, waiting for transfers between devices: 47.3 us -> 41.7 us  [swap(): return lax.ppermute(x, axis, xor_pairs(lax.axis_size(axis), mask))]
    ppermute x20 -> x18, starting transfers between devices: 19.7 us -> 19.6 us  [swap(): return lax.ppermute(x, axis, xor_pairs(lax.axis_size(axis), mask))]
  transfers between devices with their start and end apart: 20 -> 19, of which waited for: 13 -> 12; matrix products, arithmetic and copies ran while one was open for 24% -> 9% of each run, Pallas kernels for 0% -> 21%
where the time goes in v8:
time: 94.4 us; the launch traced here: 94.5 us
  waiting for transfers between devices  41.7 us (44%)
  Pallas kernels  20 us (21%)
  starting transfers between devices  19.9 us (21%)
  other arithmetic  6.98 us (7%)
  local copies, waits for them, and re-layouts  5.06 us (5%)
    ppermute x18, waiting for transfers between devices, swap(): return lax.ppermute(x, axis, xor_pairs(lax.axis_size(axis), mask))  41.7 us
    pallas_call x1, Pallas kernels, local(): pl.pallas_call(factor_kernel, out_shape=[slab] * NB + [jax.ShapeDtypeStru...  19.6 us
    ppermute x18, starting transfers between devices, swap(): return lax.ppermute(x, axis, xor_pairs(lax.axis_size(axis), mask))  19.6 us
    pallas_call x1, other arithmetic, local(): pl.pallas_call(panel_kernel, out_shape=[slab] * (NB - 1) + [longer, part,...  5.38 us
    squeeze x1, local copies, waits for them, and re-layouts, local(): own = lambda x, m: lax.dynamic_index_in_dim(x, me ^ m, 0, keepdims=False)  2.55 us
    unnamed x18, local copies, waits for them, and re-layouts  2.09 us
  transfers between devices with their start and end apart: 19, of which 12 were waited for; matrix products, arithmetic and copies ran while one was open for 9% of the time, Pallas kernels for 21%

profile of v8, /device:TPU:0, one launch (start us, length us, event | category | flops | bytes accessed | tf_op | source)
XLA Modules:
  0.0 94.5 jit_solution(905762914955068481)
XLA Ops:
  0.6 0.0 copy-start
  0.6 1.2 %copy-done = f32[4,512,128]{2,1,0:T(8,128)S(1)} copy-done((f32[4,512,128]{2,1,0:T(8,128)S(1)}, f32[4,512,128]{2,1,0:T(8,128)}, u32[]{:S(2)}) %copy-start) | copy-done | bytes 1048600
  1.9 0.4 cut.1
  2.2 0.5 collective-permute-start
  2.8 2.6 %collective-permute-start.1 = (f32[256,128]{1,0:T(8,128)S(1)}, f32[256,128]{1,0:T(8,128)S(1)}, u32[]{:S(2)}, u32[]{:S(2)}) collective-permute-start(f32[256,128]{1,0:T(8,128)S(1)} %get-tuple-element.36), channel_id=1, source_target_pairs={{0,2},{1,3},{2,0},{3,1},{4,6},{5,7},{6,4},{7,5},{8,10},{9,11},{10,... | collective-permute-start | bytes 393224 | tf_op jit(solution)/shard_map/ppermute | solution.py:235
  5.3 0.1 collective-permute-start.2
  5.4 2.6 %dynamic-slice_bitcast_fusion = (f32[1024,128]{1,0:T(8,128)}, f32[1024,128]{1,0:T(8,128)}, f32[1024,128]{1,0:T(8,128)}) fusion(f32[4,1024,128]{2,1,0:T(8,128)} %param.7, s32[]{:T(128)S(6)} %select_n.59, s32[]{:T(128)S(6)} %select_n.58, s32[]{:T(128)S(6)} %select_n.57), kind=kLoop, calls=%fused_computation.10 | loop fusion | bytes 3145740 | tf_op jit(solution)/shard_map/jit(dynamic_index_in_dim)/squeeze | solution.py:253
  7.9 1.7 %collective-permute-done.1.r2 = f32[256,128]{1,0:T(8,128)S(1)} collective-permute-done((f32[256,128]{1,0:T(8,128)S(1)}, f32[256,128]{1,0:T(8,128)S(1)}, u32[]{:S(2)}, u32[]{:S(2)}) %collective-permute-start.1) | collective-permute-done | bytes 131104 | tf_op jit(solution)/shard_map/ppermute | solution.py:235
  9.7 2.3 %collective-permute-done.2.r3 = f32[256,128]{1,0:T(8,128)S(1)} collective-permute-done((f32[256,128]{1,0:T(8,128)S(1)}, f32[256,128]{1,0:T(8,128)S(1)}, u32[]{:S(2)}, u32[]{:S(2)}) %collective-permute-start.2) | collective-permute-done | bytes 131104 | tf_op jit(solution)/shard_map/ppermute | solution.py:235
  12.0 0.0 collective-permute-done.r1
  12.0 0.1 collective-permute-start.4
  12.1 1.7 %collective-permute-start.5 = (f32[1024,128]{1,0:T(8,128)}, f32[1024,128]{1,0:T(8,128)}, u32[]{:S(2)}, u32[]{:S(2)}) collective-permute-start(f32[1024,128]{1,0:T(8,128)} %get-tuple-element.44), channel_id=1, source_target_pairs={{0,2},{1,3},{2,0},{3,1},{4,6},{5,7},{6,4},{7,5},{8,10},{9,11},{10,... | collective-permute-start | bytes 1572872 | tf_op jit(solution)/shard_map/ppermute | solution.py:235
  13.8 0.0 collective-permute-start.6
  13.8 0.0 copy-done.1
  13.8 19.6 %factor.1 = (f32[512,128]{1,0:T(8,128)S(1)}, f32[512,128]{1,0:T(8,128)S(1)}, f32[512,128]{1,0:T(8,128)}, f32[512,128]{1,0:T(8,128)S(1)}, f32[4,512,128]{2,1,0:T(8,128)S(1)}) custom-call(s32[1]{0:T(128)} %bitcast.info, f32[4,512,128]{2,1,0:T(8,128)S(1)} %copy-done.1, f32[512,128]{1,0:T(8,128)S(1)} %collective-permute-done.r1, ...), custom_call_target="tpu_custom_call" | custom-call | flops 200000000 | bytes 4000000 | tf_op jit(solution)/shard_map/factor/pallas_call | solution.py:282
  33.5 1.7 %collective-permute-start.7 = (f32[512,128]{1,0:T(8,128)}, f32[512,128]{1,0:T(8,128)S(1)}, u32[]{:S(2)}, u32[]{:S(2)}) collective-permute-start(f32[512,128]{1,0:T(8,128)} %get-tuple-element.49), channel_id=1, source_target_pairs={{0,2},{1,3},{2,0},{3,1},{4,6},{5,7},{6,4},{7,5},{8,10},{9,11},{10,... | collective-permute-start | bytes 786440 | tf_op jit(solution)/shard_map/ppermute | solution.py:235
  35.2 0.0 copy-done.6
  35.2 0.0 copy-done.7
  35.2 0.1 multiply_add_fusion
  35.3 0.0 copy-start.2
  35.3 0.1 multiply_add_fusion.1
  35.4 0.0 collective-permute-done.4
  35.4 0.0 collective-permute-done.5
  35.5 2.2 %collective-permute-done.6 = f32[1024,128]{1,0:T(8,128)} collective-permute-done((f32[1024,128]{1,0:T(8,128)}, f32[1024,128]{1,0:T(8,128)}, u32[]{:S(2)}, u32[]{:S(2)}) %collective-permute-start.6) | collective-permute-done | bytes 524320 | tf_op jit(solution)/shard_map/ppermute | solution.py:235
  37.6 0.1 broadcast_in_dim.37
  37.8 0.0 copy-done.8
  37.8 0.0 copy-done.2
  37.8 5.4 %panel.1 = (f32[4,1024,128]{2,1,0:T(8,128)S(1)}, f32[2,32,64,128]{3,2,1,0:T(8,128)S(1)}, f32[2,32,64,128]{3,2,1,0:T(8,128)S(1)}, f32[1024,128]{1,0:T(8,128)S(1)}...) fusion(f32[4,1024,128]{2,1,0:T(8,128)S(1)} %broadcast_in_dim.37, s32[]{:T(128)S(6)} %select_n.60, s32[1]{0:T(128)} %bitcast.info, ...), kind=kCustom, calls=%fused_computation.9 | custom fusion | flops 1000000000 | bytes 11535880 | tf_op jit(solution)/shard_map/panel/pallas_call | solution.py:298
  43.2 0.2 collective-permute-done.7
  43.4 0.5 collective-permute-start.8
  43.8 3.8 %collective-permute-done.8 = f32[2,32,64,128]{3,2,1,0:T(8,128)S(1)} collective-permute-done((f32[2,32,64,128]{3,2,1,0:T(8,128)S(1)}, f32[2,32,64,128]{3,2,1,0:T(8,128)S(1)}, u32[]{:S(2)}, u32[]{:S(2)}) %collective-permute-start.8) | collective-permute-done | bytes 2097184 | tf_op jit(solution)/shard_map/ppermute | solution.py:235
  47.6 0.4 slice_add_fusion
  48.0 2.9 %collective-permute-start.10 = (f32[16,64,128]{2,1,0:T(8,128)S(1)}, f32[16,64,128]{2,1,0:T(8,128)S(1)}, u32[]{:S(2)}, u32[]{:S(2)}) collective-permute-start(f32[16,64,128]{2,1,0:T(8,128)S(1)} %get-tuple-element.54), channel_id=1, source_target_pairs={{0,8},{4,12},{8,0},{12,4},{16,24},{20,28},{24,16},{28,20},{1,9},{5... | collective-permute-start | bytes 1572872 | tf_op jit(solution)/shard_map/ppermute | solution.py:235
  50.9 1.5 %collective-permute-start.9 = (f32[16,64,128]{2,1,0:T(8,128)S(1)}, f32[16,64,128]{2,1,0:T(8,128)S(1)}, u32[]{:S(2)}, u32[]{:S(2)}) collective-permute-start(f32[16,64,128]{2,1,0:T(8,128)S(1)} %get-tuple-element.53), channel_id=1, source_target_pairs={{0,4},{4,0},{8,12},{12,8},{16,20},{20,16},{24,28},{28,24},{1,5},{5... | collective-permute-start | bytes 1572872 | tf_op jit(solution)/shard_map/ppermute | solution.py:235
  52.4 1.1 %collective-permute-start.11 = (f32[1024,128]{1,0:T(8,128)S(1)}, f32[1024,128]{1,0:T(8,128)S(1)}, u32[]{:S(2)}, u32[]{:S(2)}) collective-permute-start(f32[1024,128]{1,0:T(8,128)S(1)} %get-tuple-element.95), channel_id=1, source_target_pairs={{0,2},{1,3},{2,0},{3,1},{4,6},{5,7},{6,4},{7,5},{8,10},{9,11},{10,... | collective-permute-start | bytes 1572872 | tf_op jit(solution)/shard_map/ppermute | solution.py:235
  53.5 0.0 collective-permute-start.3
  53.5 9.9 %collective-permute-done.10 = f32[16,64,128]{2,1,0:T(8,128)S(1)} collective-permute-done((f32[16,64,128]{2,1,0:T(8,128)S(1)}, f32[16,64,128]{2,1,0:T(8,128)S(1)}, u32[]{:S(2)}, u32[]{:S(2)}) %collective-permute-start.10) | collective-permute-done | bytes 524320 | tf_op jit(solution)/shard_map/ppermute | solution.py:235
  63.4 0.1 slice_add_fusion.4
  63.4 1.4 %collective-permute-done.9 = f32[16,64,128]{2,1,0:T(8,128)S(1)} collective-permute-done((f32[16,64,128]{2,1,0:T(8,128)S(1)}, f32[16,64,128]{2,1,0:T(8,128)S(1)}, u32[]{:S(2)}, u32[]{:S(2)}) %collective-permute-start.9) | collective-permute-done | bytes 524320 | tf_op jit(solution)/shard_map/ppermute | solution.py:235
  64.8 0.1 slice_add_fusion.7
  64.9 1.2 %collective-permute-done.11 = f32[1024,128]{1,0:T(8,128)S(1)} collective-permute-done((f32[1024,128]{1,0:T(8,128)S(1)}, f32[1024,128]{1,0:T(8,128)S(1)}, u32[]{:S(2)}, u32[]{:S(2)}) %collective-permute-start.11) | collective-permute-done | bytes 524320 | tf_op jit(solution)/shard_map/ppermute | solution.py:235
  66.1 0.5 collective-permute-start.12
  66.5 0.1 broadcast_in_dim.32
  66.6 0.5 collective-permute-start.13
  67.1 0.0 collective-permute-done.3
  67.1 0.1 collective-permute-start.17
  67.2 1.6 %collective-permute-start.18 = (f32[1024,128]{1,0:T(8,128)S(1)}, f32[1024,128]{1,0:T(8,128)S(1)}, u32[]{:S(2)}, u32[]{:S(2)}) collective-permute-start(f32[1024,128]{1,0:T(8,128)S(1)} %get-tuple-element.99), channel_id=1, source_target_pairs={{0,1},{1,0},{2,3},{3,2},{4,5},{5,4},{6,7},{7,6},{8,9},{9,8},{10,11... | collective-permute-start | bytes 1572872 | tf_op jit(solution)/shard_map/ppermute | solution.py:235
  68.8 4.4 %collective-permute-done.12 = f32[8,64,128]{2,1,0:T(8,128)S(1)} collective-permute-done((f32[8,64,128]{2,1,0:T(8,128)S(1)}, f32[8,64,128]{2,1,0:T(8,128)S(1)}, u32[]{:S(2)}, u32[]{:S(2)}) %collective-permute-start.12) | collective-permute-done | bytes 262176 | tf_op jit(solution)/shard_map/ppermute | solution.py:235
  73.2 0.3 collective-permute-done.13
  73.6 1.4 %collective-permute-start.16 = (f32[2,128,128]{2,1,0:T(8,128)S(1)}, f32[2,128,128]{2,1,0:T(8,128)S(1)}, u32[]{:S(2)}, u32[]{:S(2)}) collective-permute-start(f32[2,128,128]{2,1,0:T(8,128)S(1)} %pad_maximum_fusion.2), channel_id=1, source_target_pairs={{0,2},{1,3},{2,0},{3,1},{4,6},{5,7},{6,4},{7,5},{8,10},{9,11},{10,... | collective-permute-start | bytes 393224 | tf_op jit(solution)/shard_map/ppermute | solution.py:235
  75.0 2.8 %collective-permute-start.15 = (f32[2,128,128]{2,1,0:T(8,128)S(1)}, f32[2,128,128]{2,1,0:T(8,128)S(1)}, u32[]{:S(2)}, u32[]{:S(2)}) collective-permute-start(f32[2,128,128]{2,1,0:T(8,128)S(1)} %pad_maximum_fusion.1), channel_id=1, source_target_pairs={{0,16},{4,20},{8,24},{12,28},{16,0},{20,4},{24,8},{28,12},{1,17},{... | collective-permute-start | bytes 393224 | tf_op jit(solution)/shard_map/ppermute | solution.py:235
  77.8 0.0 copy-start.5
  77.8 0.4 collective-permute-start.14
  78.2 0.0 collective-permute-done.18
  78.3 11.6 %collective-permute-done.17 = f32[1536,128]{1,0:T(8,128)S(1)} collective-permute-done((f32[1536,128]{1,0:T(8,128)S(1)}, f32[1536,128]{1,0:T(8,128)S(1)}, u32[]{:S(2)}, u32[]{:S(2)}) %collective-permute-start.17) | collective-permute-done | bytes 786464 | tf_op jit(solution)/shard_map/ppermute | solution.py:235
  89.8 2.8 %collective-permute-done.16 = f32[2,128,128]{2,1,0:T(8,128)S(1)} collective-permute-done((f32[2,128,128]{2,1,0:T(8,128)S(1)}, f32[2,128,128]{2,1,0:T(8,128)S(1)}, u32[]{:S(2)}, u32[]{:S(2)}) %collective-permute-start.16) | collective-permute-done | bytes 131104 | tf_op jit(solution)/shard_map/ppermute | solution.py:235
  92.7 0.0 collective-permute-done.15
  92.7 0.0 collective-permute-done.14
  92.8 0.0 copy-start.3
  92.9 0.0 copy-start.4
  92.9 0.0 copy-done.5
  92.9 0.8 fusion.2
  93.7 0.5 copy-done.3
  94.2 0.3 copy-done.4
  (16 shorter events, 0.3 us)
Async XLA Ops:
  0.6 1.2 %copy-start = (f32[4,512,128]{2,1,0:T(8,128)S(1)}, f32[4,512,128]{2,1,0:T(8,128)}, u32[]{:S(2)}) copy-start(f32[4,512,128]{2,1,0:T(8,128)} %own_ref.2) | copy-start | bytes 3145732
  1.9 12.0 %copy-start.1 = (f32[4,512,128]{2,1,0:T(8,128)S(1)}, f32[4,512,128]{2,1,0:T(8,128)}, u32[]{:S(2)}) copy-start(f32[4,512,128]{2,1,0:T(8,128)} %own_ref.2) | copy-start | bytes 3145732
  2.2 9.7 %collective-permute-start = (f32[512,128]{1,0:T(8,128)S(1)}, f32[512,128]{1,0:T(8,128)S(1)}, u32[]{:S(2)}, u32[]{:S(2)}) collective-permute-start(f32[512,128]{1,0:T(8,128)S(1)} %get-tuple-element.35), channel_id=1, source_target_pairs={{0,1},{1,0},{2,3},{3,2},{4,5},{5,4},{6,7},{7,6},{8,9},{9,8},{10,11... | collective-permute-start | bytes 786440 | tf_op jit(solution)/shard_map/ppermute | solution.py:235
  2.8 6.9 %collective-permute-start.1 = (f32[256,128]{1,0:T(8,128)S(1)}, f32[256,128]{1,0:T(8,128)S(1)}, u32[]{:S(2)}, u32[]{:S(2)}) collective-permute-start(f32[256,128]{1,0:T(8,128)S(1)} %get-tuple-element.36), channel_id=1, source_target_pairs={{0,2},{1,3},{2,0},{3,1},{4,6},{5,7},{6,4},{7,5},{8,10},{9,11},{10,... | collective-permute-start | bytes 393224 | tf_op jit(solution)/shard_map/ppermute | solution.py:235
  5.3 6.6 %collective-permute-start.2 = (f32[256,128]{1,0:T(8,128)S(1)}, f32[256,128]{1,0:T(8,128)S(1)}, u32[]{:S(2)}, u32[]{:S(2)}) collective-permute-start(f32[256,128]{1,0:T(8,128)S(1)} %get-tuple-element.37), channel_id=1, source_target_pairs={{0,3},{1,2},{2,1},{3,0},{4,7},{5,6},{6,5},{7,4},{8,11},{9,10},{10,... | collective-permute-start | bytes 393224 | tf_op jit(solution)/shard_map/ppermute | solution.py:235
  5.4 29.8 %copy-start.6 = (s32[144,1]{0,1:T(1,128)S(1)}, s32[144,1]{0,1:T(1,128)}, u32[]{:S(2)}) copy-start(s32[144,1]{0,1:T(1,128)} %param.9) | copy-start | bytes 1732
  5.4 29.8 %copy-start.7 = (s32[144]{0:T(256)S(1)}, s32[144]{0:T(256)}, u32[]{:S(2)}) copy-start(s32[144]{0:T(256)} %param.10) | copy-start | bytes 1732
  7.9 29.8 %copy-start.8 = (s32[4]{0:T(128)S(1)}, s32[4]{0:T(128)}, u32[]{:S(2)}) copy-start(s32[4]{0:T(128)} %param.8) | copy-start | bytes 52
  12.0 23.5 %collective-permute-start.4 = (f32[1024,128]{1,0:T(8,128)}, f32[1024,128]{1,0:T(8,128)}, u32[]{:S(2)}, u32[]{:S(2)}) collective-permute-start(f32[1024,128]{1,0:T(8,128)} %get-tuple-element.43), channel_id=1, source_target_pairs={{0,1},{1,0},{2,3},{3,2},{4,5},{5,4},{6,7},{7,6},{8,9},{9,8},{10,11... | collective-permute-start | bytes 1572872 | tf_op jit(solution)/shard_map/ppermute | solution.py:235
  12.1 23.4 %collective-permute-start.5 = (f32[1024,128]{1,0:T(8,128)}, f32[1024,128]{1,0:T(8,128)}, u32[]{:S(2)}, u32[]{:S(2)}) collective-permute-start(f32[1024,128]{1,0:T(8,128)} %get-tuple-element.44), channel_id=1, source_target_pairs={{0,2},{1,3},{2,0},{3,1},{4,6},{5,7},{6,4},{7,5},{8,10},{9,11},{10,... | collective-permute-start | bytes 1572872 | tf_op jit(solution)/shard_map/ppermute | solution.py:235
  13.8 23.8 %collective-permute-start.6 = (f32[1024,128]{1,0:T(8,128)}, f32[1024,128]{1,0:T(8,128)}, u32[]{:S(2)}, u32[]{:S(2)}) collective-permute-start(f32[1024,128]{1,0:T(8,128)} %get-tuple-element.45), channel_id=1, source_target_pairs={{0,3},{1,2},{2,1},{3,0},{4,7},{5,6},{6,5},{7,4},{8,11},{9,10},{10,... | collective-permute-start | bytes 1572872 | tf_op jit(solution)/shard_map/ppermute | solution.py:235
  33.5 9.9 %collective-permute-start.7 = (f32[512,128]{1,0:T(8,128)}, f32[512,128]{1,0:T(8,128)S(1)}, u32[]{:S(2)}, u32[]{:S(2)}) collective-permute-start(f32[512,128]{1,0:T(8,128)} %get-tuple-element.49), channel_id=1, source_target_pairs={{0,2},{1,3},{2,0},{3,1},{4,6},{5,7},{6,4},{7,5},{8,10},{9,11},{10,... | collective-permute-start | bytes 786440 | tf_op jit(solution)/shard_map/ppermute | solution.py:235
  35.3 2.5 %copy-start.2 = (f32[4,1024,128]{2,1,0:T(8,128)S(1)}, f32[4,1024,128]{2,1,0:T(8,128)}, u32[]{:S(2)}) copy-start(f32[4,1024,128]{2,1,0:T(8,128)} %param.7) | copy-start | bytes 6291460
  43.4 4.3 %collective-permute-start.8 = (f32[2,32,64,128]{3,2,1,0:T(8,128)S(1)}, f32[2,32,64,128]{3,2,1,0:T(8,128)S(1)}, u32[]{:S(2)}, u32[]{:S(2)}) collective-permute-start(f32[2,32,64,128]{3,2,1,0:T(8,128)S(1)} %get-tuple-element.52), channel_id=1, source_target_pairs={{0,1},{1,0},{2,3},{3,2},{4,5},{5,4},{6,7},{7,6},{8,9},{9,8},{10,11... | collective-permute-start | bytes 6291464 | tf_op jit(solution)/shard_map/ppermute | solution.py:235
  48.0 15.4 %collective-permute-start.10 = (f32[16,64,128]{2,1,0:T(8,128)S(1)}, f32[16,64,128]{2,1,0:T(8,128)S(1)}, u32[]{:S(2)}, u32[]{:S(2)}) collective-permute-start(f32[16,64,128]{2,1,0:T(8,128)S(1)} %get-tuple-element.54), channel_id=1, source_target_pairs={{0,8},{4,12},{8,0},{12,4},{16,24},{20,28},{24,16},{28,20},{1,9},{5... | collective-permute-start | bytes 1572872 | tf_op jit(solution)/shard_map/ppermute | solution.py:235
  50.9 13.9 %collective-permute-start.9 = (f32[16,64,128]{2,1,0:T(8,128)S(1)}, f32[16,64,128]{2,1,0:T(8,128)S(1)}, u32[]{:S(2)}, u32[]{:S(2)}) collective-permute-start(f32[16,64,128]{2,1,0:T(8,128)S(1)} %get-tuple-element.53), channel_id=1, source_target_pairs={{0,4},{4,0},{8,12},{12,8},{16,20},{20,16},{24,28},{28,24},{1,5},{5... | collective-permute-start | bytes 1572872 | tf_op jit(solution)/shard_map/ppermute | solution.py:235
  52.4 13.6 %collective-permute-start.11 = (f32[1024,128]{1,0:T(8,128)S(1)}, f32[1024,128]{1,0:T(8,128)S(1)}, u32[]{:S(2)}, u32[]{:S(2)}) collective-permute-start(f32[1024,128]{1,0:T(8,128)S(1)} %get-tuple-element.95), channel_id=1, source_target_pairs={{0,2},{1,3},{2,0},{3,1},{4,6},{5,7},{6,4},{7,5},{8,10},{9,11},{10,... | collective-permute-start | bytes 1572872 | tf_op jit(solution)/shard_map/ppermute | solution.py:235
  53.5 13.6 %collective-permute-start.3 = (f32[512,128]{1,0:T(8,128)S(1)}, f32[512,128]{1,0:T(8,128)S(1)}, u32[]{:S(2)}, u32[]{:S(2)}) collective-permute-start(f32[512,128]{1,0:T(8,128)S(1)} %get-tuple-element.42), channel_id=1, source_target_pairs={{0,1},{1,0},{2,3},{3,2},{4,5},{5,4},{6,7},{7,6},{8,9},{9,8},{10,11... | collective-permute-start | bytes 786440 | tf_op jit(solution)/shard_map/ppermute | solution.py:235
  66.1 7.1 %collective-permute-start.12 = (f32[8,64,128]{2,1,0:T(8,128)S(1)}, f32[8,64,128]{2,1,0:T(8,128)S(1)}, u32[]{:S(2)}, u32[]{:S(2)}) collective-permute-start(f32[8,64,128]{2,1,0:T(8,128)S(1)} %get-tuple-element.56), channel_id=1, source_target_pairs={{0,8},{4,12},{8,0},{12,4},{16,24},{20,28},{24,16},{28,20},{1,9},{5... | collective-permute-start | bytes 786440 | tf_op jit(solution)/shard_map/ppermute | solution.py:235
  66.6 6.9 %collective-permute-start.13 = (f32[8,64,128]{2,1,0:T(8,128)S(1)}, f32[8,64,128]{2,1,0:T(8,128)S(1)}, u32[]{:S(2)}, u32[]{:S(2)}) collective-permute-start(f32[8,64,128]{2,1,0:T(8,128)S(1)} %get-tuple-element.57), channel_id=1, source_target_pairs={{0,4},{4,0},{8,12},{12,8},{16,20},{20,16},{24,28},{28,24},{1,5},{5... | collective-permute-start | bytes 786440 | tf_op jit(solution)/shard_map/ppermute | solution.py:235
  67.1 22.7 %collective-permute-start.17 = (f32[1536,128]{1,0:T(8,128)S(1)}, f32[1536,128]{1,0:T(8,128)S(1)}, u32[]{:S(2)}, u32[]{:S(2)}) collective-permute-start(f32[1536,128]{1,0:T(8,128)S(1)} %get-tuple-element.97), channel_id=1, source_target_pairs={{0,3},{1,2},{2,1},{3,0},{4,7},{5,6},{6,5},{7,4},{8,11},{9,10},{10,... | collective-permute-start | bytes 2359304 | tf_op jit(solution)/shard_map/ppermute | solution.py:235
  67.2 11.0 %collective-permute-start.18 = (f32[1024,128]{1,0:T(8,128)S(1)}, f32[1024,128]{1,0:T(8,128)S(1)}, u32[]{:S(2)}, u32[]{:S(2)}) collective-permute-start(f32[1024,128]{1,0:T(8,128)S(1)} %get-tuple-element.99), channel_id=1, source_target_pairs={{0,1},{1,0},{2,3},{3,2},{4,5},{5,4},{6,7},{7,6},{8,9},{9,8},{10,11... | collective-permute-start | bytes 1572872 | tf_op jit(solution)/shard_map/ppermute | solution.py:235
  73.6 19.1 %collective-permute-start.16 = (f32[2,128,128]{2,1,0:T(8,128)S(1)}, f32[2,128,128]{2,1,0:T(8,128)S(1)}, u32[]{:S(2)}, u32[]{:S(2)}) collective-permute-start(f32[2,128,128]{2,1,0:T(8,128)S(1)} %pad_maximum_fusion.2), channel_id=1, source_target_pairs={{0,2},{1,3},{2,0},{3,1},{4,6},{5,7},{6,4},{7,5},{8,10},{9,11},{10,... | collective-permute-start | bytes 393224 | tf_op jit(solution)/shard_map/ppermute | solution.py:235
  75.0 17.7 %collective-permute-start.15 = (f32[2,128,128]{2,1,0:T(8,128)S(1)}, f32[2,128,128]{2,1,0:T(8,128)S(1)}, u32[]{:S(2)}, u32[]{:S(2)}) collective-permute-start(f32[2,128,128]{2,1,0:T(8,128)S(1)} %pad_maximum_fusion.1), channel_id=1, source_target_pairs={{0,16},{4,20},{8,24},{12,28},{16,0},{20,4},{24,8},{28,12},{1,17},{... | collective-permute-start | bytes 393224 | tf_op jit(solution)/shard_map/ppermute | solution.py:235
  77.8 15.0 %copy-start.5 = (f32[2,128,128]{2,1,0:T(8,128)S(1)}, f32[2,128,128]{2,1,0:T(8,128)}, u32[]{:S(2)}) copy-start(f32[2,128,128]{2,1,0:T(8,128)} %param.11) | copy-start | bytes 393220
  77.8 14.8 %collective-permute-start.14 = (f32[2,128,128]{2,1,0:T(8,128)S(1)}, f32[2,128,128]{2,1,0:T(8,128)S(1)}, u32[]{:S(2)}, u32[]{:S(2)}) collective-permute-start(f32[2,128,128]{2,1,0:T(8,128)S(1)} %pad_maximum_fusion), channel_id=1, source_target_pairs={{0,18},{1,19},{2,16},{3,17},{4,22},{5,23},{6,20},{7,21},{8,26},{9,... | collective-permute-start | bytes 393224 | tf_op jit(solution)/shard_map/ppermute | solution.py:346
  92.8 1.4 %copy-start.3 = (f32[4,1024,128]{2,1,0:T(8,128)}, f32[4,1024,128]{2,1,0:T(8,128)S(1)}, u32[]{:S(2)}) copy-start(f32[4,1024,128]{2,1,0:T(8,128)S(1)} %bitcast_dynamic-update-slice_fusion) | copy-start | bytes 6291460
  92.9 1.7 %copy-start.4 = (f32[4,512,128]{2,1,0:T(8,128)}, f32[4,512,128]{2,1,0:T(8,128)S(1)}, u32[]{:S(2)}) copy-start(f32[4,512,128]{2,1,0:T(8,128)S(1)} %bitcast_dynamic-update-slice_fusion.4) | copy-start | bytes 3145732

commit v9 on v8

--- a/solution.py
+++ b/solution.py
@@ -126,7 +126,7 @@
         c.wait()
 
 
-def factor_kernel(info, own_ref, r1, r2, r3, l0, l1, l2, l3, mt, a, l, sems):
+def factor_kernel(info, own_ref, r1, r2, r3, l0, l1, l2, l3a, l3b, mt, a, l, sems):
     me = info[0]
     side = me // 2
     far_rows = pl.ds((1 - side) * (W // 2), W // 2)
@@ -164,23 +164,42 @@
             for j in range(i + 1, k):
                 total = total + dot_nt(mt[j, pl.ds(i * B, B), :], l[j, here, :])
             mt[k, pl.ds(i * B, B), :] = dot_nt(-total, inv)
-    outs = [l0, l1, l2, l3]
-    copies = [pltpu.make_async_copy(l.at[me ^ m], outs[m], sems.at[m]) for m in range(NB)]
+    copies = [pltpu.make_async_copy(l.at[me ^ m], out, sems.at[m]) for m, out in enumerate((l0, l1, l2))]
+    for n, out in enumerate((l3a, l3b)):
+        piece = l.at[me ^ 3, pl.ds(n * (W // 2), W // 2)]
+        copies.append(pltpu.make_async_copy(piece, out, sems.at[3 + n]))
     for c in copies:
         c.start()
     for c in copies:
         c.wait()
 
 
-def panel_kernel(
-    info, counts, tgt_a, tgt_b, own_ref, r1, r2, r3, mt, l3, x0, x1, x2, x3, keep, send, xh, xl
-):
+def add_pairs(xh, xl, tgt, stream, keep, send):
+    keep[...] = jnp.zeros_like(keep)
+    send[...] = jnp.zeros_like(send)
+    half, strip = keep.shape[:2]
+    for j in range(0, P_SIZE, 2):
+        places = [pl.ds(i * B + stream * strip, strip) for i in range(j, P_SIZE)]
+        left = [jnp.concatenate([ref[at, :] for at in places], axis=0) for ref in (xh, xl)]
+        right = [ref[pl.ds(j * B, 2 * B), :] for ref in (xh, xl)]
+        got = dot3(left, right, ((1,), (1,)))
+        for i in range(j, P_SIZE):
+            for n in range(2 if i > j else 1):
+                piece = got[(i - j) * strip : (i - j + 1) * strip, n * B : (n + 1) * B]
+                where = tgt[i * (i + 1) // 2 + j + n]
+                away = (where >= half).astype(jnp.float32)
+                at = lax.rem(where, half)
+                keep[at] += piece * (1.0 - away)
+                send[at] += piece * away
+
+
+def panel_kernel(info, counts, tgt, own_ref, r1, r2, r3, mt, l3b, x0, x1, x2, x3, xh, xl, keep, send):
     me = info[0]
     count = counts[me]
     rows = P_SIZE * B
     ins = [own_ref.at[me], r1, r2, r3]
     outs = [x0, x1, x2, x3]
-    x3[pl.ds(rows, W), :] = l3[...]
+    x3[pl.ds(rows, W // 2), :] = l3b[...]
     live = lax.broadcasted_iota(jnp.int32, (rows, B), 0) < count * B
     parts = [split_bf16(jnp.where(live, ref[...], 0.0)) for ref in ins]
     left = [jnp.concatenate([part[n] for part in parts], axis=1) for n in range(2)]
@@ -195,27 +214,11 @@
         high, low = split_bf16(got)
         xh[:, pl.ds(c * B, 2 * B)] = high
         xl[:, pl.ds(c * B, 2 * B)] = low
-
-    keep[...] = jnp.zeros_like(keep)
-    send[...] = jnp.zeros_like(send)
-    half, strip = keep.shape[1:3]
-    for j in range(0, P_SIZE, 2):
-
-        @pl.when(j < count)
-        def _():
-            left = (xh[pl.ds(j * B, rows - j * B), :], xl[pl.ds(j * B, rows - j * B), :])
-            right = (xh[pl.ds(j * B, 2 * B), :], xl[pl.ds(j * B, 2 * B), :])
-            got = dot3(left, right, ((1,), (1,)))
-            for i in range(j, P_SIZE):
-                for n in range(2 if i > j else 1):
-                    block = got[(i - j) * B : (i - j + 1) * B, n * B : (n + 1) * B]
-                    pair = i * (i + 1) // 2 + j + n
-                    away = (tgt_a[pair] >= half).astype(jnp.float32)
-                    for stream, tgt in enumerate((tgt_a, tgt_b)):
-                        at = lax.rem(tgt[pair], half)
-                        piece = block[stream * strip : (stream + 1) * strip]
-                        keep[stream, at] += piece * (1.0 - away)
-                        send[stream, at] += piece * away
+    add_pairs(xh, xl, tgt, 0, keep, send)
+
+
+def second_kernel(tgt, xh, xl, keep, send):
+    add_pairs(xh, xl, tgt, 1, keep, send)
 
 
 SMEM = pl.BlockSpec(memory_space=pltpu.SMEM)
@@ -279,12 +282,13 @@
     tgt_b = relative_index(owner, slot, wide_me, me, steps_b)
 
     slab = jax.ShapeDtypeStruct((W, B), jnp.float32)
+    low = jax.ShapeDtypeStruct((W // 2, B), jnp.float32)
     *l_parts, mt = pl.pallas_call(
         factor_kernel,
-        out_shape=[slab] * NB + [jax.ShapeDtypeStruct((NB, W, B), jnp.float32)],
+        out_shape=[slab] * (NB - 1) + [low, low, jax.ShapeDtypeStruct((NB, W, B), jnp.float32)],
         in_specs=[SMEM] + [ANY] * NB,
-        out_specs=[ANY] * NB + [VMEM],
-        scratch_shapes=[pltpu.VMEM((NB, W, B), jnp.float32)] * 2 + [pltpu.SemaphoreType.DMA((NB,))],
+        out_specs=[ANY] * (NB + 1) + [VMEM],
+        scratch_shapes=[pltpu.VMEM((NB, W, B), jnp.float32)] * 2 + [pltpu.SemaphoreType.DMA((NB + 1,))],
         compiler_params=pltpu.CompilerParams(vmem_limit_bytes=32 * 2**20),
         cost_estimate=pl.CostEstimate(flops=2 * 10**8, bytes_accessed=4 * 10**6, transcendentals=0),
         name="factor",
@@ -293,42 +297,48 @@
     rows = P_SIZE * B
     blocks = wide_count * narrow_count * T_DEV
     slab = jax.ShapeDtypeStruct((rows, B), jnp.float32)
-    longer = jax.ShapeDtypeStruct((rows + W, B), jnp.float32)
-    part = jax.ShapeDtypeStruct((2, blocks // 2, B // 2, B), jnp.float32)
-    *x_parts, keep, send = pl.pallas_call(
+    longer = jax.ShapeDtypeStruct((rows + W // 2, B), jnp.float32)
+    split = jax.ShapeDtypeStruct((rows, W), jnp.bfloat16)
+    part = jax.ShapeDtypeStruct((blocks // 2, B // 2, B), jnp.float32)
+    room = pltpu.CompilerParams(vmem_limit_bytes=20 * 2**20 + 4 * blocks * B * B)
+    *x_parts, xh, xl, keep_a, send_a = pl.pallas_call(
         panel_kernel,
-        out_shape=[slab] * (NB - 1) + [longer, part, part],
-        in_specs=[SMEM] * 4 + [VMEM] * (NB + 2),
-        out_specs=[VMEM] * (NB + 2),
-        scratch_shapes=[pltpu.VMEM((rows, W), jnp.bfloat16)] * 2,
-        compiler_params=pltpu.CompilerParams(vmem_limit_bytes=20 * 2**20 + 4 * blocks * B * B),
+        out_shape=[slab] * (NB - 1) + [longer, split, split, part, part],
+        in_specs=[SMEM] * 3 + [VMEM] * (NB + 2),
+        out_specs=[VMEM] * (NB + 4),
+        compiler_params=room,
         cost_estimate=pl.CostEstimate(flops=10**9, bytes_accessed=10 * 10**6, transcendentals=0),
         name="panel",
-    )(info, panel_count, tgt_a, tgt_b, panel, *panel_in, mt, l_parts[3])
-
-    l_back = [swap(l_parts[m], "narrow", m) for m in (1, 2)]
+    )(info, panel_count, tgt_a, panel, *panel_in, mt, l_parts[4])
+    keep_b, send_b = pl.pallas_call(
+        second_kernel,
+        out_shape=[part, part],
+        in_specs=[SMEM] + [VMEM] * 2,
+        out_specs=[VMEM] * 2,
+        compiler_params=room,
+        cost_estimate=pl.CostEstimate(flops=10**6, bytes_accessed=10**4, transcendentals=0),
+        name="second",
+    )(tgt_b, xh, xl)
+
+    l_back = [swap(l_parts[m], "narrow", m) for m in (1, 2, 3)]
     x_back = [swap(x_parts[m], "narrow", m) for m in masks]
 
-    send, l_back[1] = lax.optimization_barrier((send, l_back[1]))
-    got = swap(send, "narrow", 1)
+    got_a = swap(send_a, "narrow", 1)
+    send_b, l_back[1] = lax.optimization_barrier((send_b, l_back[1]))
+    got_b = swap(send_b, "narrow", 1)
     half = blocks // 4
-    upper = lambda u, n: u[n, half:]
-    lower = lambda u, n: u[n, :half]
-    send_a = upper(keep, 0) + upper(got, 0)
-    send_b = upper(keep, 1) + upper(got, 1)
-    keep_a = lower(keep, 0) + lower(got, 0)
-    keep_b = lower(keep, 1) + lower(got, 1)
-    for n in (1, 2):
-        if n == 2:
-            send_a, send_b, x_back[1] = lax.optimization_barrier((send_a, send_b, x_back[1]))
-        else:
-            send_a, send_b = lax.optimization_barrier((send_a, send_b))
-        got_a = swap(send_a, *steps_a[n])
-        got_b = swap(send_b, *steps_b[n])
-        half = half // 2
-        if n == 1:
-            send_a, send_b = keep_a[half:] + got_a[half:], keep_b[half:] + got_b[half:]
-            keep_a, keep_b = keep_a[:half] + got_a[:half], keep_b[:half] + got_b[:half]
+    send_a, send_b = keep_a[half:] + got_a[half:], keep_b[half:] + got_b[half:]
+    keep_a, keep_b = keep_a[:half] + got_a[:half], keep_b[:half] + got_b[:half]
+    got_a = swap(send_a, *steps_a[1])
+    send_b, l_back[2] = lax.optimization_barrier((send_b, l_back[2]))
+    got_b = swap(send_b, *steps_b[1])
+    half = half // 2
+    send_a, send_b = keep_a[half:] + got_a[half:], keep_b[half:] + got_b[half:]
+    keep_a, keep_b = keep_a[:half] + got_a[:half], keep_b[:half] + got_b[:half]
+    send_a, send_b, x_back[1] = lax.optimization_barrier((send_a, send_b, x_back[1]))
+    got_a = swap(send_a, *steps_a[2])
+    got_b = swap(send_b, *steps_b[2])
+    half = half // 2
     rest = steps_a[3:]
     take = lambda n, size: jnp.concatenate(
         [u[n * size : (n + 1) * size] + v[n * size : (n + 1) * size] for u, v in ((keep_a, got_a), (keep_b, got_b))],
@@ -348,7 +358,7 @@
         swap(take(1, T_DEV), *rest[1]),
     ]
     got, x_back[2], x_back[0] = lax.optimization_barrier((got, x_back[2], x_back[0]))
-    l_back.append(x_back[2][rows:])
+    l_back[2] = jnp.concatenate([l_back[2], x_back[2][rows:]], axis=0)
     x_back[2] = x_back[2][:rows]
     updated = ancestor - (take(0, T_DEV) + (got[0] + (got[1] + got[2])))
 

time: 94.4 us -> 98.9 us (1.048)
  Pallas kernels: 20 us -> 27.7 us
  waiting for transfers between devices: 41.7 us -> 35.8 us
  local copies, waits for them, and re-layouts: 5.06 us -> 7.63 us
  other arithmetic: 6.98 us -> 5.21 us
  starting transfers between devices: 19.9 us -> 21.2 us
    ppermute x18 -> x20, waiting for transfers between devices: 41.7 us -> 33.2 us  [swap(): return lax.ppermute(x, axis, xor_pairs(lax.axis_size(axis), mask))]
    pallas_call x1 -> x3, Pallas kernels: 19.6 us -> 26.6 us  [the longest x1 20.1 us: local(): pl.pallas_call(factor_kernel, out_shape=[slab] * (NB - 1) + [low, low, ja...]
    pallas_call x1 -> x0, other arithmetic: 5.38 us -> none  [local(): pl.pallas_call(panel_kernel, out_shape=[slab] * (NB - 1) + [longer, part,...]
    ppermute x1, waiting for transfers between devices: 0.01 us -> 2.64 us  [local(): lax.ppermute(take(3, T_DEV), ('wide', 'narrow'), xor_pairs(wide_count * n...]
    unnamed x18 -> x38, local copies, waits for them, and re-layouts: 2.09 us -> 4.51 us
    add x1 -> x2, other arithmetic: 0.06 us -> 2.07 us  [local(): keep_a[:half] + got_a[:half]]
    add x1 -> x2, other arithmetic: 0.06 us -> 2.04 us  [local(): keep_b[:half] + got_b[:half]]
    ppermute x1, starting transfers between devices: 0.37 us -> 1.39 us  [local(): lax.ppermute(take(3, T_DEV), ('wide', 'narrow'), xor_pairs(wide_count * n...]
  transfers between devices with their start and end apart: 19 -> 21, of which waited for: 12 -> 14; matrix products, arithmetic and copies ran while one was open for 9% -> 7% of each run, Pallas kernels for 21% -> 27%
where the time goes in v9:
time: 98.9 us; the launch traced here: 98.6 us
  waiting for transfers between devices  35.8 us (36%)
  Pallas kernels  27.7 us (28%)
  starting transfers between devices  21.2 us (21%)
  local copies, waits for them, and re-layouts  7.63 us (8%)
  other arithmetic  5.21 us (5%)
    ppermute x20, waiting for transfers between devices, swap(): return lax.ppermute(x, axis, xor_pairs(lax.axis_size(axis), mask))  33.2 us
    pallas_call x1, Pallas kernels, local(): pl.pallas_call(factor_kernel, out_shape=[slab] * (NB - 1) + [low, low, ja...  20.1 us
    ppermute x20, starting transfers between devices, swap(): return lax.ppermute(x, axis, xor_pairs(lax.axis_size(axis), mask))  19.8 us
    unnamed x38, local copies, waits for them, and re-layouts  4.51 us
    pallas_call x1, Pallas kernels, local(): pl.pallas_call(panel_kernel, out_shape=[slab] * (NB - 1) + [longer, split...  4.5 us
    squeeze x1, local copies, waits for them, and re-layouts, local(): own = lambda x, m: lax.dynamic_index_in_dim(x, me ^ m, 0, keepdims=False)  2.68 us
    ppermute x1, waiting for transfers between devices, local(): lax.ppermute(take(3, T_DEV), ('wide', 'narrow'), xor_pairs(wide_count * n...  2.64 us
    add x2, other arithmetic, local(): keep_a[:half] + got_a[:half]  2.07 us
  transfers between devices with their start and end apart: 21, of which 14 were waited for; matrix products, arithmetic and copies ran while one was open for 7% of the time, Pallas kernels for 27%

profile of v9, /device:TPU:0, one launch (start us, length us, event | category | flops | bytes accessed | tf_op | source)
XLA Modules:
  0.0 98.6 jit_solution(16584292259682774963)
XLA Ops:
  0.6 1.2 %copy-done.1 = f32[4,512,128]{2,1,0:T(8,128)S(1)} copy-done((f32[4,512,128]{2,1,0:T(8,128)S(1)}, f32[4,512,128]{2,1,0:T(8,128)}, u32[]{:S(2)}) %copy-start.1) | copy-done | bytes 1048600
  1.9 1.2 %cut.1 = (f32[512,128]{1,0:T(8,128)}, f32[256,128]{1,0:T(8,128)}, f32[256,128]{1,0:T(8,128)}) custom-call(s32[1]{0:T(128)} %bitcast.info, f32[4,512,128]{2,1,0:T(8,128)S(1)} %copy-done.1), custom_call_target="tpu_custom_call" | custom-call | bytes 1048576 | tf_op jit(solution)/shard_map/cut/pallas_call | solution.py:259
  3.0 0.5 collective-permute-start
  3.6 2.6 %collective-permute-start.1 = (f32[256,128]{1,0:T(8,128)}, f32[256,128]{1,0:T(8,128)S(1)}, u32[]{:S(2)}, u32[]{:S(2)}) collective-permute-start(f32[256,128]{1,0:T(8,128)} %get-tuple-element.41), channel_id=1, source_target_pairs={{0,2},{1,3},{2,0},{3,1},{4,6},{5,7},{6,4},{7,5},{8,10},{9,11},{10,... | collective-permute-start | bytes 393224 | tf_op jit(solution)/shard_map/ppermute | solution.py:238
  6.1 0.1 collective-permute-start.2
  6.2 2.7 %dynamic-slice_bitcast_fusion = (f32[1024,128]{1,0:T(8,128)}, f32[1024,128]{1,0:T(8,128)}, f32[1024,128]{1,0:T(8,128)}) fusion(f32[4,1024,128]{2,1,0:T(8,128)} %own_ref.3, s32[]{:T(128)S(6)} %select_n.59, s32[]{:T(128)S(6)} %select_n.58, s32[]{:T(128)S(6)} %select_n.57), kind=kLoop, calls=%fused_computation.8 | loop fusion | bytes 3145740 | tf_op jit(solution)/shard_map/jit(dynamic_index_in_dim)/squeeze | solution.py:256
  8.9 1.8 %collective-permute-done.1.r2 = f32[256,128]{1,0:T(8,128)S(1)} collective-permute-done((f32[256,128]{1,0:T(8,128)}, f32[256,128]{1,0:T(8,128)S(1)}, u32[]{:S(2)}, u32[]{:S(2)}) %collective-permute-start.1) | collective-permute-done | bytes 131104 | tf_op jit(solution)/shard_map/ppermute | solution.py:238
  10.7 2.4 %collective-permute-done.2.r3 = f32[256,128]{1,0:T(8,128)} collective-permute-done((f32[256,128]{1,0:T(8,128)}, f32[256,128]{1,0:T(8,128)}, u32[]{:S(2)}, u32[]{:S(2)}) %collective-permute-start.2) | collective-permute-done | bytes 131104 | tf_op jit(solution)/shard_map/ppermute | solution.py:238
  13.1 0.7 copy-done.3
  13.8 0.1 collective-permute-start.4
  13.9 1.7 %collective-permute-start.5 = (f32[1024,128]{1,0:T(8,128)}, f32[1024,128]{1,0:T(8,128)}, u32[]{:S(2)}, u32[]{:S(2)}) collective-permute-start(f32[1024,128]{1,0:T(8,128)} %get-tuple-element.49), channel_id=1, source_target_pairs={{0,2},{1,3},{2,0},{3,1},{4,6},{5,7},{6,4},{7,5},{8,10},{9,11},{10,... | collective-permute-start | bytes 1572872 | tf_op jit(solution)/shard_map/ppermute | solution.py:238
  15.6 0.0 collective-permute-start.6
  15.7 0.1 multiply_add_fusion
  15.8 0.9 copy-done.4
  16.7 20.1 %factor.1 = (f32[512,128]{1,0:T(8,128)S(1)}, f32[512,128]{1,0:T(8,128)S(1)}, f32[512,128]{1,0:T(8,128)S(1)}, f32[256,128]{1,0:T(8,128)S(1)}, f32[256,128]{1,0:T(8,128)S(1)}, /*index=5*/f32[4,512,128]{2,1,0:T(8,128)S(1)}) custom-call(s32[1]{0:T(128)} %bitcast.info, f32[4,512,128]{2,1,0:T(8,128)S(1)} %copy-done.2, f32[512,128]{1,0:T(8,128)S(1)} %copy-done.4, ...), custom_call_target="tpu_custom_call" | custom-call | flops 200000000 | bytes 4000000 | tf_op jit(solution)/shard_map/factor/pallas_call | solution.py:286
  36.8 0.7 copy-done.10
  37.6 1.7 %collective-permute-start.7 = (f32[512,128]{1,0:T(8,128)S(1)}, f32[512,128]{1,0:T(8,128)S(1)}, u32[]{:S(2)}, u32[]{:S(2)}) collective-permute-start(f32[512,128]{1,0:T(8,128)S(1)} %get-tuple-element.56), channel_id=1, source_target_pairs={{0,2},{1,3},{2,0},{3,1},{4,6},{5,7},{6,4},{7,5},{8,10},{9,11},{10,... | collective-permute-start | bytes 786440 | tf_op jit(solution)/shard_map/ppermute | solution.py:238
  39.2 0.1 multiply_add_fusion.1.tgt
  39.3 0.0 collective-permute-done.4.r1
  39.4 0.0 collective-permute-done.5.r2
  39.4 4.5 %panel.1 = (f32[1024,128]{1,0:T(8,128)S(1)}, f32[1024,128]{1,0:T(8,128)S(1)}, f32[1024,128]{1,0:T(8,128)S(1)}, f32[1280,128]{1,0:T(8,128)S(1)}, bf16[1024,512]{1...) custom-call(s32[1]{0:T(128)} %bitcast.info, ...), custom_call_target="tpu_custom_call" | custom-call | flops 1000000000 | bytes 10000000 | tf_op jit(solution)/shard_map/panel/pallas_call | solution.py:304
  43.9 0.0 copy-start.6
  43.9 0.0 copy-start.8
  43.9 2.0 %second.1 = (f32[32,64,128]{2,1,0:T(8,128)S(1)}, f32[32,64,128]{2,1,0:T(8,128)S(1)}) custom-call(s32[36]{0:T(128)S(1)} %multiply_add_fusion.1.tgt, bf16[1024,512]{1,0:T(8,128)(2,1)S(1)} %get-tuple-element.53.xh, bf16[1024,512]{1,0:T(8,128)(2,1)S(1)} %get-tuple-element.54.xl), custom_call_target="tpu_custom_call" | custom-call | flops 1000000 | bytes 10000 | tf_op jit(solution)/shard_map/second/pallas_call | solution.py:313
  45.9 0.4 collective-permute-done.7
  46.3 0.5 collective-permute-start.10
  46.8 1.4 %collective-permute-start.9 = (f32[256,128]{1,0:T(8,128)S(1)}, f32[256,128]{1,0:T(8,128)S(1)}, u32[]{:S(2)}, u32[]{:S(2)}) collective-permute-start(f32[256,128]{1,0:T(8,128)S(1)} %get-tuple-element.60), channel_id=1, source_target_pairs={{0,3},{1,2},{2,1},{3,0},{4,7},{5,6},{6,5},{7,4},{8,11},{9,10},{10,... | collective-permute-start | bytes 393224 | tf_op jit(solution)/shard_map/ppermute | solution.py:238
  48.1 0.8 collective-permute-done.8
  48.9 0.9 slice_add_fusion
  49.9 2.4 %collective-permute-done.9 = f32[256,128]{1,0:T(8,128)S(1)} collective-permute-done((f32[256,128]{1,0:T(8,128)S(1)}, f32[256,128]{1,0:T(8,128)S(1)}, u32[]{:S(2)}, u32[]{:S(2)}) %collective-permute-start.9) | collective-permute-done | bytes 131104 | tf_op jit(solution)/shard_map/ppermute | solution.py:238
  52.3 1.8 %collective-permute-start.12 = (f32[16,64,128]{2,1,0:T(8,128)}, f32[16,64,128]{2,1,0:T(8,128)}, u32[]{:S(2)}, u32[]{:S(2)}) collective-permute-start(f32[16,64,128]{2,1,0:T(8,128)} %get-tuple-element.64), channel_id=1, source_target_pairs={{0,8},{4,12},{8,0},{12,4},{16,24},{20,28},{24,16},{28,20},{1,9},{5... | collective-permute-start | bytes 1572872 | tf_op jit(solution)/shard_map/ppermute | solution.py:238
  54.1 0.0 collective-permute-done.10
  54.1 1.0 slice_add_fusion.2
  55.1 1.5 %collective-permute-start.11 = (f32[16,64,128]{2,1,0:T(8,128)}, f32[16,64,128]{2,1,0:T(8,128)}, u32[]{:S(2)}, u32[]{:S(2)}) collective-permute-start(f32[16,64,128]{2,1,0:T(8,128)} %get-tuple-element.83), channel_id=1, source_target_pairs={{0,4},{4,0},{8,12},{12,8},{16,20},{20,16},{24,28},{28,24},{1,5},{5... | collective-permute-start | bytes 1572872 | tf_op jit(solution)/shard_map/ppermute | solution.py:238
  56.6 0.0 collective-permute-start.3
  56.6 1.7 %collective-permute-start.13 = (f32[1024,128]{1,0:T(8,128)S(1)}, f32[1024,128]{1,0:T(8,128)S(1)}, u32[]{:S(2)}, u32[]{:S(2)}) collective-permute-start(f32[1024,128]{1,0:T(8,128)S(1)} %copy-done.9), channel_id=1, source_target_pairs={{0,2},{1,3},{2,0},{3,1},{4,6},{5,7},{6,4},{7,5},{8,10},{9,11},{10,... | collective-permute-start | bytes 1572872 | tf_op jit(solution)/shard_map/ppermute | solution.py:238
  58.3 0.1 broadcast_in_dim.32
  58.4 0.0 copy-start.7
  58.4 8.2 %collective-permute-done.12 = f32[16,64,128]{2,1,0:T(8,128)} collective-permute-done((f32[16,64,128]{2,1,0:T(8,128)}, f32[16,64,128]{2,1,0:T(8,128)}, u32[]{:S(2)}, u32[]{:S(2)}) %collective-permute-start.12) | collective-permute-done | bytes 524320 | tf_op jit(solution)/shard_map/ppermute | solution.py:238
  66.6 1.1 %slice_add_fusion.4 = (f32[8,64,128]{2,1,0:T(8,128)S(1)}, f32[8,64,128]{2,1,0:T(8,128)S(1)}) fusion(f32[16,64,128]{2,1,0:T(8,128)} %collective-permute-done.12, f32[16,64,128]{2,1,0:T(8,128)S(1)} %get-tuple-element.80), kind=kLoop, calls=%fused_computation.11 | loop fusion | flops 131072 | bytes 1572864 | tf_op jit(solution)/shard_map/add | solution.py:337
  67.7 1.4 %collective-permute-done.11 = f32[16,64,128]{2,1,0:T(8,128)} collective-permute-done((f32[16,64,128]{2,1,0:T(8,128)}, f32[16,64,128]{2,1,0:T(8,128)}, u32[]{:S(2)}, u32[]{:S(2)}) %collective-permute-start.11) | collective-permute-done | bytes 524320 | tf_op jit(solution)/shard_map/ppermute | solution.py:238
  69.1 1.1 %slice_add_fusion.7 = (f32[8,64,128]{2,1,0:T(8,128)S(1)}, f32[8,64,128]{2,1,0:T(8,128)S(1)}) fusion(f32[16,64,128]{2,1,0:T(8,128)} %collective-permute-done.11, f32[16,64,128]{2,1,0:T(8,128)S(1)} %get-tuple-element.82), kind=kLoop, calls=%fused_computation.14 | loop fusion | flops 131072 | bytes 1572864 | tf_op jit(solution)/shard_map/add | solution.py:337
  70.2 0.8 collective-permute-done.13
  71.0 0.5 collective-permute-start.14
  71.4 0.0 collective-permute-done.3
  71.4 0.7 collective-permute-start.19
  72.1 1.1 %collective-permute-start.20 = (f32[1024,128]{1,0:T(8,128)S(1)}, f32[1024,128]{1,0:T(8,128)S(1)}, u32[]{:S(2)}, u32[]{:S(2)}) collective-permute-start(f32[1024,128]{1,0:T(8,128)S(1)} %get-tuple-element.69), channel_id=1, source_target_pairs={{0,1},{1,0},{2,3},{3,2},{4,5},{5,4},{6,7},{7,6},{8,9},{9,8},{10,11... | collective-permute-start | bytes 1572872 | tf_op jit(solution)/shard_map/ppermute | solution.py:238
  73.2 0.8 collective-permute-start.15
  74.0 0.1 broadcast_in_dim.37
  74.2 4.6 %collective-permute-done.14 = f32[8,64,128]{2,1,0:T(8,128)S(1)} collective-permute-done((f32[8,64,128]{2,1,0:T(8,128)S(1)}, f32[8,64,128]{2,1,0:T(8,128)S(1)}, u32[]{:S(2)}, u32[]{:S(2)}) %collective-permute-start.14) | collective-permute-done | bytes 262176 | tf_op jit(solution)/shard_map/ppermute | solution.py:238
  78.8 2.6 %collective-permute-done.15 = f32[8,64,128]{2,1,0:T(8,128)S(1)} collective-permute-done((f32[8,64,128]{2,1,0:T(8,128)S(1)}, f32[8,64,128]{2,1,0:T(8,128)S(1)}, u32[]{:S(2)}, u32[]{:S(2)}) %collective-permute-start.15) | collective-permute-done | bytes 262176 | tf_op jit(solution)/shard_map/ppermute | solution.py:238
  81.5 0.5 collective-permute-start.18
  82.1 2.7 %collective-permute-start.17 = (f32[2,128,128]{2,1,0:T(8,128)S(1)}, f32[2,128,128]{2,1,0:T(8,128)S(1)}, u32[]{:S(2)}, u32[]{:S(2)}) collective-permute-start(f32[2,128,128]{2,1,0:T(8,128)S(1)} %pad_maximum_fusion.1), channel_id=1, source_target_pairs={{0,16},{4,20},{8,24},{12,28},{16,0},{20,4},{24,8},{28,12},{1,17},{... | collective-permute-start | bytes 393224 | tf_op jit(solution)/shard_map/ppermute | solution.py:238
  84.7 1.4 %collective-permute-start.16 = (f32[2,128,128]{2,1,0:T(8,128)S(1)}, f32[2,128,128]{2,1,0:T(8,128)S(1)}, u32[]{:S(2)}, u32[]{:S(2)}) collective-permute-start(f32[2,128,128]{2,1,0:T(8,128)S(1)} %pad_maximum_fusion), channel_id=1, source_target_pairs={{0,18},{1,19},{2,16},{3,17},{4,22},{5,23},{6,20},{7,21},{8,26},{9,... | collective-permute-start | bytes 393224 | tf_op jit(solution)/shard_map/ppermute | solution.py:356
  86.2 0.0 copy-start.16
  86.2 2.2 %collective-permute-done.19 = f32[1280,128]{1,0:T(8,128)S(1)} collective-permute-done((f32[1280,128]{1,0:T(8,128)S(1)}, f32[1280,128]{1,0:T(8,128)S(1)}, u32[]{:S(2)}, u32[]{:S(2)}) %collective-permute-start.19) | collective-permute-done | bytes 655392 | tf_op jit(solution)/shard_map/ppermute | solution.py:238
  88.4 3.1 %collective-permute-done.18 = f32[2,128,128]{2,1,0:T(8,128)S(1)} collective-permute-done((f32[2,128,128]{2,1,0:T(8,128)S(1)}, f32[2,128,128]{2,1,0:T(8,128)S(1)}, u32[]{:S(2)}, u32[]{:S(2)}) %collective-permute-start.18) | collective-permute-done | bytes 131104 | tf_op jit(solution)/shard_map/ppermute | solution.py:238
  91.4 2.6 %collective-permute-done.17 = f32[2,128,128]{2,1,0:T(8,128)S(1)} collective-permute-done((f32[2,128,128]{2,1,0:T(8,128)S(1)}, f32[2,128,128]{2,1,0:T(8,128)S(1)}, u32[]{:S(2)}, u32[]{:S(2)}) %collective-permute-start.17) | collective-permute-done | bytes 131104 | tf_op jit(solution)/shard_map/ppermute | solution.py:238
  94.1 2.6 %collective-permute-done.16 = f32[2,128,128]{2,1,0:T(8,128)S(1)} collective-permute-done((f32[2,128,128]{2,1,0:T(8,128)S(1)}, f32[2,128,128]{2,1,0:T(8,128)S(1)}, u32[]{:S(2)}, u32[]{:S(2)}) %collective-permute-start.16) | collective-permute-done | bytes 131104 | tf_op jit(solution)/shard_map/ppermute | solution.py:356
  96.9 0.0 copy-start.12
  96.9 0.0 copy-start.13
  96.9 0.8 fusion.1
  97.7 0.5 copy-done.12
  98.2 0.3 copy-done.13
  (44 shorter events, 0.4 us)
Async XLA Ops:
  0.6 1.2 %copy-start.1 = (f32[4,512,128]{2,1,0:T(8,128)S(1)}, f32[4,512,128]{2,1,0:T(8,128)}, u32[]{:S(2)}) copy-start(f32[4,512,128]{2,1,0:T(8,128)} %own_ref.2) | copy-start | bytes 3145732
  1.9 13.8 %copy-start.17 = (s32[144,1]{0,1:T(1,128)S(1)}, s32[144,1]{0,1:T(1,128)}, u32[]{:S(2)}) copy-start(s32[144,1]{0,1:T(1,128)} %param.9) | copy-start | bytes 1732
  1.9 13.8 %copy-start.18 = (s32[144]{0:T(256)S(1)}, s32[144]{0:T(256)}, u32[]{:S(2)}) copy-start(s32[144]{0:T(256)} %param.10) | copy-start | bytes 1732
  1.9 13.9 %copy-start.2 = (f32[4,512,128]{2,1,0:T(8,128)S(1)}, f32[4,512,128]{2,1,0:T(8,128)}, u32[]{:S(2)}) copy-start(f32[4,512,128]{2,1,0:T(8,128)} %own_ref.2) | copy-start | bytes 3145732
  3.0 10.0 %collective-permute-start = (f32[512,128]{1,0:T(8,128)}, f32[512,128]{1,0:T(8,128)S(1)}, u32[]{:S(2)}, u32[]{:S(2)}) collective-permute-start(f32[512,128]{1,0:T(8,128)} %get-tuple-element.40), channel_id=1, source_target_pairs={{0,1},{1,0},{2,3},{3,2},{4,5},{5,4},{6,7},{7,6},{8,9},{9,8},{10,11... | collective-permute-start | bytes 786440 | tf_op jit(solution)/shard_map/ppermute | solution.py:238
  3.6 7.1 %collective-permute-start.1 = (f32[256,128]{1,0:T(8,128)}, f32[256,128]{1,0:T(8,128)S(1)}, u32[]{:S(2)}, u32[]{:S(2)}) collective-permute-start(f32[256,128]{1,0:T(8,128)} %get-tuple-element.41), channel_id=1, source_target_pairs={{0,2},{1,3},{2,0},{3,1},{4,6},{5,7},{6,4},{7,5},{8,10},{9,11},{10,... | collective-permute-start | bytes 393224 | tf_op jit(solution)/shard_map/ppermute | solution.py:238
  6.1 7.0 %collective-permute-start.2 = (f32[256,128]{1,0:T(8,128)}, f32[256,128]{1,0:T(8,128)}, u32[]{:S(2)}, u32[]{:S(2)}) collective-permute-start(f32[256,128]{1,0:T(8,128)} %get-tuple-element.42), channel_id=1, source_target_pairs={{0,3},{1,2},{2,1},{3,0},{4,7},{5,6},{6,5},{7,4},{8,11},{9,10},{10,... | collective-permute-start | bytes 393224 | tf_op jit(solution)/shard_map/ppermute | solution.py:238
  6.2 33.2 %copy-start = (f32[4,1024,128]{2,1,0:T(8,128)S(1)}, f32[4,1024,128]{2,1,0:T(8,128)}, u32[]{:S(2)}) copy-start(f32[4,1024,128]{2,1,0:T(8,128)} %own_ref.3) | copy-start | bytes 6291460
  6.2 33.2 %copy-start.5 = (s32[4]{0:T(128)S(1)}, s32[4]{0:T(128)}, u32[]{:S(2)}) copy-start(s32[4]{0:T(128)} %counts.1) | copy-start | bytes 52
  13.1 0.7 copy-start.3
  13.8 25.5 %collective-permute-start.4 = (f32[1024,128]{1,0:T(8,128)}, f32[1024,128]{1,0:T(8,128)}, u32[]{:S(2)}, u32[]{:S(2)}) collective-permute-start(f32[1024,128]{1,0:T(8,128)} %get-tuple-element.48), channel_id=1, source_target_pairs={{0,1},{1,0},{2,3},{3,2},{4,5},{5,4},{6,7},{7,6},{8,9},{9,8},{10,11... | collective-permute-start | bytes 1572872 | tf_op jit(solution)/shard_map/ppermute | solution.py:238
  13.9 25.4 %collective-permute-start.5 = (f32[1024,128]{1,0:T(8,128)}, f32[1024,128]{1,0:T(8,128)}, u32[]{:S(2)}, u32[]{:S(2)}) collective-permute-start(f32[1024,128]{1,0:T(8,128)} %get-tuple-element.49), channel_id=1, source_target_pairs={{0,2},{1,3},{2,0},{3,1},{4,6},{5,7},{6,4},{7,5},{8,10},{9,11},{10,... | collective-permute-start | bytes 1572872 | tf_op jit(solution)/shard_map/ppermute | solution.py:238
  15.6 23.7 %collective-permute-start.6 = (f32[1024,128]{1,0:T(8,128)}, f32[1024,128]{1,0:T(8,128)}, u32[]{:S(2)}, u32[]{:S(2)}) collective-permute-start(f32[1024,128]{1,0:T(8,128)} %get-tuple-element.50), channel_id=1, source_target_pairs={{0,3},{1,2},{2,1},{3,0},{4,7},{5,6},{6,5},{7,4},{8,11},{9,10},{10,... | collective-permute-start | bytes 1572872 | tf_op jit(solution)/shard_map/ppermute | solution.py:238
  15.8 1.0 copy-start.4
  36.8 0.7 copy-start.10
  37.6 8.7 %collective-permute-start.7 = (f32[512,128]{1,0:T(8,128)S(1)}, f32[512,128]{1,0:T(8,128)S(1)}, u32[]{:S(2)}, u32[]{:S(2)}) collective-permute-start(f32[512,128]{1,0:T(8,128)S(1)} %get-tuple-element.56), channel_id=1, source_target_pairs={{0,2},{1,3},{2,0},{3,1},{4,6},{5,7},{6,4},{7,5},{8,10},{9,11},{10,... | collective-permute-start | bytes 786440 | tf_op jit(solution)/shard_map/ppermute | solution.py:238
  43.9 6.0 %copy-start.6 = (f32[1280,128]{1,0:T(8,128)}, f32[1280,128]{1,0:T(8,128)S(1)}, u32[]{:S(2)}) copy-start(f32[1280,128]{1,0:T(8,128)S(1)} %get-tuple-element.68) | copy-start | bytes 1966084
  43.9 6.0 %copy-start.8 = (f32[1024,128]{1,0:T(8,128)}, f32[1024,128]{1,0:T(8,128)S(1)}, u32[]{:S(2)}) copy-start(f32[1024,128]{1,0:T(8,128)S(1)} %get-tuple-element.65) | copy-start | bytes 1572868
  46.3 8.8 %copy-start.14 = (f32[512,128]{1,0:T(8,128)}, f32[512,128]{1,0:T(8,128)S(1)}, u32[]{:S(2)}) copy-start(f32[512,128]{1,0:T(8,128)S(1)} %collective-permute-done.7) | copy-start | bytes 786436
  46.3 2.7 %collective-permute-start.8 = (f32[32,64,128]{2,1,0:T(8,128)S(1)}, f32[32,64,128]{2,1,0:T(8,128)S(1)}, u32[]{:S(2)}, u32[]{:S(2)}) collective-permute-start(f32[32,64,128]{2,1,0:T(8,128)S(1)} %get-tuple-element.59), channel_id=1, source_target_pairs={{0,1},{1,0},{2,3},{3,2},{4,5},{5,4},{6,7},{7,6},{8,9},{9,8},{10,11... | collective-permute-start | bytes 3145736 | tf_op jit(solution)/shard_map/ppermute | solution.py:238
  46.3 7.8 %collective-permute-start.10 = (f32[32,64,128]{2,1,0:T(8,128)S(1)}, f32[32,64,128]{2,1,0:T(8,128)S(1)}, u32[]{:S(2)}, u32[]{:S(2)}) collective-permute-start(f32[32,64,128]{2,1,0:T(8,128)S(1)} %get-tuple-element.63), channel_id=1, source_target_pairs={{0,1},{1,0},{2,3},{3,2},{4,5},{5,4},{6,7},{7,6},{8,9},{9,8},{10,11... | collective-permute-start | bytes 3145736 | tf_op jit(solution)/shard_map/ppermute | solution.py:238
  46.8 5.5 %collective-permute-start.9 = (f32[256,128]{1,0:T(8,128)S(1)}, f32[256,128]{1,0:T(8,128)S(1)}, u32[]{:S(2)}, u32[]{:S(2)}) collective-permute-start(f32[256,128]{1,0:T(8,128)S(1)} %get-tuple-element.60), channel_id=1, source_target_pairs={{0,3},{1,2},{2,1},{3,0},{4,7},{5,6},{6,5},{7,4},{8,11},{9,10},{10,... | collective-permute-start | bytes 393224 | tf_op jit(solution)/shard_map/ppermute | solution.py:238
  49.9 6.7 %copy-start.11 = (f32[512,128]{1,0:T(8,128)S(1)}, f32[512,128]{1,0:T(8,128)}, u32[]{:S(2)}) copy-start(f32[512,128]{1,0:T(8,128)} %copy-done.10) | copy-start | bytes 786436
  52.3 4.3 %copy-start.9 = (f32[1024,128]{1,0:T(8,128)S(1)}, f32[1024,128]{1,0:T(8,128)}, u32[]{:S(2)}) copy-start(f32[1024,128]{1,0:T(8,128)} %copy-done.8) | copy-start | bytes 1572868
  52.3 14.3 %collective-permute-start.12 = (f32[16,64,128]{2,1,0:T(8,128)}, f32[16,64,128]{2,1,0:T(8,128)}, u32[]{:S(2)}, u32[]{:S(2)}) collective-permute-start(f32[16,64,128]{2,1,0:T(8,128)} %get-tuple-element.64), channel_id=1, source_target_pairs={{0,8},{4,12},{8,0},{12,4},{16,24},{20,28},{24,16},{28,20},{1,9},{5... | collective-permute-start | bytes 1572872 | tf_op jit(solution)/shard_map/ppermute | solution.py:238
  55.1 14.0 %collective-permute-start.11 = (f32[16,64,128]{2,1,0:T(8,128)}, f32[16,64,128]{2,1,0:T(8,128)}, u32[]{:S(2)}, u32[]{:S(2)}) collective-permute-start(f32[16,64,128]{2,1,0:T(8,128)} %get-tuple-element.83), channel_id=1, source_target_pairs={{0,4},{4,0},{8,12},{12,8},{16,20},{20,16},{24,28},{28,24},{1,5},{5... | collective-permute-start | bytes 1572872 | tf_op jit(solution)/shard_map/ppermute | solution.py:238
  56.6 14.8 %collective-permute-start.3 = (f32[512,128]{1,0:T(8,128)S(1)}, f32[512,128]{1,0:T(8,128)S(1)}, u32[]{:S(2)}, u32[]{:S(2)}) collective-permute-start(f32[512,128]{1,0:T(8,128)S(1)} %copy-done.11), channel_id=1, source_target_pairs={{0,1},{1,0},{2,3},{3,2},{4,5},{5,4},{6,7},{7,6},{8,9},{9,8},{10,11... | collective-permute-start | bytes 786440 | tf_op jit(solution)/shard_map/ppermute | solution.py:238
  56.6 14.3 %collective-permute-start.13 = (f32[1024,128]{1,0:T(8,128)S(1)}, f32[1024,128]{1,0:T(8,128)S(1)}, u32[]{:S(2)}, u32[]{:S(2)}) collective-permute-start(f32[1024,128]{1,0:T(8,128)S(1)} %copy-done.9), channel_id=1, source_target_pairs={{0,2},{1,3},{2,0},{3,1},{4,6},{5,7},{6,4},{7,5},{8,10},{9,11},{10,... | collective-permute-start | bytes 1572872 | tf_op jit(solution)/shard_map/ppermute | solution.py:238
  58.4 13.1 %copy-start.7 = (f32[1280,128]{1,0:T(8,128)S(1)}, f32[1280,128]{1,0:T(8,128)}, u32[]{:S(2)}) copy-start(f32[1280,128]{1,0:T(8,128)} %copy-done.6) | copy-start | bytes 1966084
  71.0 7.9 %collective-permute-start.14 = (f32[8,64,128]{2,1,0:T(8,128)S(1)}, f32[8,64,128]{2,1,0:T(8,128)S(1)}, u32[]{:S(2)}, u32[]{:S(2)}) collective-permute-start(f32[8,64,128]{2,1,0:T(8,128)S(1)} %get-tuple-element.66), channel_id=1, source_target_pairs={{0,8},{4,12},{8,0},{12,4},{16,24},{20,28},{24,16},{28,20},{1,9},{5... | collective-permute-start | bytes 786440 | tf_op jit(solution)/shard_map/ppermute | solution.py:238
  71.4 16.9 %collective-permute-start.19 = (f32[1280,128]{1,0:T(8,128)S(1)}, f32[1280,128]{1,0:T(8,128)S(1)}, u32[]{:S(2)}, u32[]{:S(2)}) collective-permute-start(f32[1280,128]{1,0:T(8,128)S(1)} %copy-done.7), channel_id=1, source_target_pairs={{0,3},{1,2},{2,1},{3,0},{4,7},{5,6},{6,5},{7,4},{8,11},{9,10},{10,... | collective-permute-start | bytes 1966088 | tf_op jit(solution)/shard_map/ppermute | solution.py:238
  72.1 14.1 %collective-permute-start.20 = (f32[1024,128]{1,0:T(8,128)S(1)}, f32[1024,128]{1,0:T(8,128)S(1)}, u32[]{:S(2)}, u32[]{:S(2)}) collective-permute-start(f32[1024,128]{1,0:T(8,128)S(1)} %get-tuple-element.69), channel_id=1, source_target_pairs={{0,1},{1,0},{2,3},{3,2},{4,5},{5,4},{6,7},{7,6},{8,9},{9,8},{10,11... | collective-permute-start | bytes 1572872 | tf_op jit(solution)/shard_map/ppermute | solution.py:238
  73.2 8.2 %collective-permute-start.15 = (f32[8,64,128]{2,1,0:T(8,128)S(1)}, f32[8,64,128]{2,1,0:T(8,128)S(1)}, u32[]{:S(2)}, u32[]{:S(2)}) collective-permute-start(f32[8,64,128]{2,1,0:T(8,128)S(1)} %get-tuple-element.67), channel_id=1, source_target_pairs={{0,4},{4,0},{8,12},{12,8},{16,20},{20,16},{24,28},{28,24},{1,5},{5... | collective-permute-start | bytes 786440 | tf_op jit(solution)/shard_map/ppermute | solution.py:238
  74.2 11.9 %copy-start.15 = (f32[512,128]{1,0:T(8,128)S(1)}, f32[512,128]{1,0:T(8,128)}, u32[]{:S(2)}) copy-start(f32[512,128]{1,0:T(8,128)} %copy-done.14) | copy-start | bytes 786436
  81.5 9.9 %collective-permute-start.18 = (f32[2,128,128]{2,1,0:T(8,128)S(1)}, f32[2,128,128]{2,1,0:T(8,128)S(1)}, u32[]{:S(2)}, u32[]{:S(2)}) collective-permute-start(f32[2,128,128]{2,1,0:T(8,128)S(1)} %pad_maximum_fusion.2), channel_id=1, source_target_pairs={{0,2},{1,3},{2,0},{3,1},{4,6},{5,7},{6,4},{7,5},{8,10},{9,11},{10,... | collective-permute-start | bytes 393224 | tf_op jit(solution)/shard_map/ppermute | solution.py:238
  82.1 12.0 %collective-permute-start.17 = (f32[2,128,128]{2,1,0:T(8,128)S(1)}, f32[2,128,128]{2,1,0:T(8,128)S(1)}, u32[]{:S(2)}, u32[]{:S(2)}) collective-permute-start(f32[2,128,128]{2,1,0:T(8,128)S(1)} %pad_maximum_fusion.1), channel_id=1, source_target_pairs={{0,16},{4,20},{8,24},{12,28},{16,0},{20,4},{24,8},{28,12},{1,17},{... | collective-permute-start | bytes 393224 | tf_op jit(solution)/shard_map/ppermute | solution.py:238
  84.7 12.0 %collective-permute-start.16 = (f32[2,128,128]{2,1,0:T(8,128)S(1)}, f32[2,128,128]{2,1,0:T(8,128)S(1)}, u32[]{:S(2)}, u32[]{:S(2)}) collective-permute-start(f32[2,128,128]{2,1,0:T(8,128)S(1)} %pad_maximum_fusion), channel_id=1, source_target_pairs={{0,18},{1,19},{2,16},{3,17},{4,22},{5,23},{6,20},{7,21},{8,26},{9,... | collective-permute-start | bytes 393224 | tf_op jit(solution)/shard_map/ppermute | solution.py:356
  86.2 10.8 %copy-start.16 = (f32[2,128,128]{2,1,0:T(8,128)S(1)}, f32[2,128,128]{2,1,0:T(8,128)}, u32[]{:S(2)}) copy-start(f32[2,128,128]{2,1,0:T(8,128)} %param.11) | copy-start | bytes 393220
  96.9 1.4 %copy-start.12 = (f32[4,1024,128]{2,1,0:T(8,128)}, f32[4,1024,128]{2,1,0:T(8,128)S(1)}, u32[]{:S(2)}) copy-start(f32[4,1024,128]{2,1,0:T(8,128)S(1)} %bitcast_dynamic-update-slice_fusion) | copy-start | bytes 6291460
  96.9 1.7 %copy-start.13 = (f32[4,512,128]{2,1,0:T(8,128)}, f32[4,512,128]{2,1,0:T(8,128)S(1)}, u32[]{:S(2)}) copy-start(f32[4,512,128]{2,1,0:T(8,128)S(1)} %fusion) | copy-start | bytes 3145732

commit v10 on v8

--- a/solution.py
+++ b/solution.py
@@ -126,7 +126,7 @@
         c.wait()
 
 
-def factor_kernel(info, own_ref, r1, r2, r3, l0, l1, l2, l3, mt, a, l, sems):
+def factor_kernel(info, own_ref, r1, r2, r3, l0, l1, l2, l3a, l3b, mt, a, l, sems):
     me = info[0]
     side = me // 2
     far_rows = pl.ds((1 - side) * (W // 2), W // 2)
@@ -164,8 +164,10 @@
             for j in range(i + 1, k):
                 total = total + dot_nt(mt[j, pl.ds(i * B, B), :], l[j, here, :])
             mt[k, pl.ds(i * B, B), :] = dot_nt(-total, inv)
-    outs = [l0, l1, l2, l3]
-    copies = [pltpu.make_async_copy(l.at[me ^ m], outs[m], sems.at[m]) for m in range(NB)]
+    copies = [pltpu.make_async_copy(l.at[me ^ m], out, sems.at[m]) for m, out in enumerate((l0, l1, l2))]
+    for n, out in enumerate((l3a, l3b)):
+        piece = l.at[me ^ 3, pl.ds(n * (W // 2), W // 2)]
+        copies.append(pltpu.make_async_copy(piece, out, sems.at[3 + n]))
     for c in copies:
         c.start()
     for c in copies:
@@ -173,14 +175,14 @@
 
 
 def panel_kernel(
-    info, counts, tgt_a, tgt_b, own_ref, r1, r2, r3, mt, l3, x0, x1, x2, x3, keep, send, xh, xl
+    info, counts, tgt_a, tgt_b, own_ref, r1, r2, r3, mt, l3a, x0, x1, x2, x3a, x3b, keep, send, xh, xl
 ):
     me = info[0]
     count = counts[me]
     rows = P_SIZE * B
     ins = [own_ref.at[me], r1, r2, r3]
-    outs = [x0, x1, x2, x3]
-    x3[pl.ds(rows, W), :] = l3[...]
+    lead = x3a.shape[0]
+    x3b[pl.ds(rows - lead, W // 2), :] = l3a[...]
     live = lax.broadcasted_iota(jnp.int32, (rows, B), 0) < count * B
     parts = [split_bf16(jnp.where(live, ref[...], 0.0)) for ref in ins]
     left = [jnp.concatenate([part[n] for part in parts], axis=1) for n in range(2)]
@@ -190,8 +192,13 @@
             for k in range(NB)
         ]
         got = dot3(left, split_bf16(jnp.concatenate(right, axis=0)), ((1,), (0,)))
-        outs[c][pl.ds(0, rows), :] = got[:, :B]
-        outs[c + 1][pl.ds(0, rows), :] = got[:, B:]
+        if c == 0:
+            x0[...] = got[:, :B]
+            x1[...] = got[:, B:]
+        else:
+            x2[...] = got[:, :B]
+            x3a[...] = got[:lead, B:]
+            x3b[pl.ds(0, rows - lead), :] = got[lead:, B:]
         high, low = split_bf16(got)
         xh[:, pl.ds(c * B, 2 * B)] = high
         xl[:, pl.ds(c * B, 2 * B)] = low
@@ -279,35 +286,41 @@
     tgt_b = relative_index(owner, slot, wide_me, me, steps_b)
 
     slab = jax.ShapeDtypeStruct((W, B), jnp.float32)
+    low = jax.ShapeDtypeStruct((W // 2, B), jnp.float32)
     *l_parts, mt = pl.pallas_call(
         factor_kernel,
-        out_shape=[slab] * NB + [jax.ShapeDtypeStruct((NB, W, B), jnp.float32)],
+        out_shape=[slab] * (NB - 1) + [low, low, jax.ShapeDtypeStruct((NB, W, B), jnp.float32)],
         in_specs=[SMEM] + [ANY] * NB,
-        out_specs=[ANY] * NB + [VMEM],
-        scratch_shapes=[pltpu.VMEM((NB, W, B), jnp.float32)] * 2 + [pltpu.SemaphoreType.DMA((NB,))],
-        compiler_params=pltpu.CompilerParams(vmem_limit_bytes=32 * 2**20),
+        out_specs=[ANY] * (NB + 1) + [VMEM],
+        scratch_shapes=[pltpu.VMEM((NB, W, B), jnp.float32)] * 2 + [pltpu.SemaphoreType.DMA((NB + 1,))],
+        compiler_params=pltpu.CompilerParams(vmem_limit_bytes=16 * 2**20),
         cost_estimate=pl.CostEstimate(flops=2 * 10**8, bytes_accessed=4 * 10**6, transcendentals=0),
         name="factor",
     )(info, diag_block, *diag_in)
 
     rows = P_SIZE * B
     blocks = wide_count * narrow_count * T_DEV
-    slab = jax.ShapeDtypeStruct((rows, B), jnp.float32)
-    longer = jax.ShapeDtypeStruct((rows + W, B), jnp.float32)
+    lead = rows // 4
+    slab, short, longer = [
+        jax.ShapeDtypeStruct((n, B), jnp.float32) for n in (rows, lead, rows - lead + W // 2)
+    ]
     part = jax.ShapeDtypeStruct((2, blocks // 2, B // 2, B), jnp.float32)
-    *x_parts, keep, send = pl.pallas_call(
+    home, near, far_c, far_a, far_b, keep, send = pl.pallas_call(
         panel_kernel,
-        out_shape=[slab] * (NB - 1) + [longer, part, part],
+        out_shape=[slab] * 3 + [short, longer, part, part],
         in_specs=[SMEM] * 4 + [VMEM] * (NB + 2),
-        out_specs=[VMEM] * (NB + 2),
+        out_specs=[VMEM] * 7,
         scratch_shapes=[pltpu.VMEM((rows, W), jnp.bfloat16)] * 2,
-        compiler_params=pltpu.CompilerParams(vmem_limit_bytes=20 * 2**20 + 4 * blocks * B * B),
+        compiler_params=pltpu.CompilerParams(vmem_limit_bytes=16 * 2**20 + 4 * blocks * B * B),
         cost_estimate=pl.CostEstimate(flops=10**9, bytes_accessed=10 * 10**6, transcendentals=0),
         name="panel",
     )(info, panel_count, tgt_a, tgt_b, panel, *panel_in, mt, l_parts[3])
 
     l_back = [swap(l_parts[m], "narrow", m) for m in (1, 2)]
-    x_back = [swap(x_parts[m], "narrow", m) for m in masks]
+    near = swap(near, "narrow", 1)
+    far_a = swap(far_a, "narrow", 3)
+    far_b = swap(far_b, "narrow", 3)
+    far_c = swap(far_c, "narrow", 2)
 
     send, l_back[1] = lax.optimization_barrier((send, l_back[1]))
     got = swap(send, "narrow", 1)
@@ -320,9 +333,10 @@
     keep_b = lower(keep, 1) + lower(got, 1)
     for n in (1, 2):
         if n == 2:
-            send_a, send_b, x_back[1] = lax.optimization_barrier((send_a, send_b, x_back[1]))
+            send_a, send_b, far_b, late = lax.optimization_barrier((send_a, send_b, far_b, l_parts[4]))
+            l_back.append(swap(late, "narrow", 3))
         else:
-            send_a, send_b = lax.optimization_barrier((send_a, send_b))
+            send_a, send_b, far_a = lax.optimization_barrier((send_a, send_b, far_a))
         got_a = swap(send_a, *steps_a[n])
         got_b = swap(send_b, *steps_b[n])
         half = half // 2
@@ -347,19 +361,30 @@
         swap(take(2, T_DEV), *rest[0]),
         swap(take(1, T_DEV), *rest[1]),
     ]
-    got, x_back[2], x_back[0] = lax.optimization_barrier((got, x_back[2], x_back[0]))
-    l_back.append(x_back[2][rows:])
-    x_back[2] = x_back[2][:rows]
+    got, far_c, near, l_back[2] = lax.optimization_barrier((got, far_c, near, l_back[2]))
     updated = ancestor - (take(0, T_DEV) + (got[0] + (got[1] + got[2])))
 
-    def give_back(own_part, others):
-        back = [own_part] + others
-        out = jnp.zeros((NB,) + own_part.shape, jnp.float32)
-        for m in range(NB):
-            out = lax.dynamic_update_index_in_dim(out, back[m], me ^ m, 0)
+    def assemble(height, pieces):
+        out = jnp.zeros((NB, height, B), jnp.float32)
+        for m, row, piece in pieces:
+            out = lax.dynamic_update_slice(out, piece[None], (me ^ m, row, 0))
         return out
 
-    return (give_back(l_parts[0], l_back), give_back(x_parts[0], x_back), updated)
+    factor = assemble(
+        W,
+        [
+            (0, 0, l_parts[0]),
+            (1, 0, l_back[0]),
+            (2, 0, l_back[1]),
+            (3, 0, far_b[rows - lead :]),
+            (3, W // 2, l_back[2]),
+        ],
+    )
+    lower_panel = assemble(
+        rows,
+        [(0, 0, home), (1, 0, near), (2, 0, far_c), (3, 0, far_a), (3, lead, far_b[: rows - lead])],
+    )
+    return (factor, lower_panel, updated)
 
 
 def solution(mesh):

time: 94.4 us -> 95.8 us (1.015)
  waiting for transfers between devices: 41.7 us -> 37.6 us
  starting transfers between devices: 19.9 us -> 22.4 us
  local copies, waits for them, and re-layouts: 5.06 us -> 6.62 us
  other arithmetic: 6.98 us -> 8.24 us
    ppermute x18 -> x20, waiting for transfers between devices: 41.7 us -> 34.1 us  [swap(): return lax.ppermute(x, axis, xor_pairs(lax.axis_size(axis), mask))]
    ppermute x1, waiting for transfers between devices: 0.01 us -> 3.58 us  [local(): lax.ppermute(take(3, T_DEV), ('wide', 'narrow'), xor_pairs(wide_count * n...]
    ppermute x1, starting transfers between devices: 0.37 us -> 3.09 us  [local(): lax.ppermute(take(3, T_DEV), ('wide', 'narrow'), xor_pairs(wide_count * n...]
    pallas_call x1, other arithmetic: 5.38 us -> 6.42 us  [local(): pl.pallas_call(panel_kernel, out_shape=[slab] * 3 + [short, longer, part,...]
    unnamed x18 -> x22, local copies, waits for them, and re-layouts: 2.09 us -> 2.69 us
    ppermute x18 -> x20, starting transfers between devices: 19.6 us -> 19.3 us  [swap(): return lax.ppermute(x, axis, xor_pairs(lax.axis_size(axis), mask))]
  transfers between devices with their start and end apart: 19 -> 21, of which waited for: 12 -> 14; matrix products, arithmetic and copies ran while one was open for 9% -> 12% of each run, Pallas kernels for 21% -> 20%
where the time goes in v10:
time: 95.8 us; the launch traced here: 95.5 us
  waiting for transfers between devices  37.6 us (39%)
  starting transfers between devices  22.4 us (23%)
  Pallas kernels  19.7 us (21%)
  other arithmetic  8.24 us (9%)
  local copies, waits for them, and re-layouts  6.62 us (7%)
    ppermute x20, waiting for transfers between devices, swap(): return lax.ppermute(x, axis, xor_pairs(lax.axis_size(axis), mask))  34.1 us
    pallas_call x1, Pallas kernels, local(): pl.pallas_call(factor_kernel, out_shape=[slab] * (NB - 1) + [low, low, ja...  19.4 us
    ppermute x20, starting transfers between devices, swap(): return lax.ppermute(x, axis, xor_pairs(lax.axis_size(axis), mask))  19.3 us
    pallas_call x1, other arithmetic, local(): pl.pallas_call(panel_kernel, out_shape=[slab] * 3 + [short, longer, part,...  6.42 us
    ppermute x1, waiting for transfers between devices, local(): lax.ppermute(take(3, T_DEV), ('wide', 'narrow'), xor_pairs(wide_count * n...  3.58 us
    ppermute x1, starting transfers between devices, local(): lax.ppermute(take(3, T_DEV), ('wide', 'narrow'), xor_pairs(wide_count * n...  3.09 us
    unnamed x22, local copies, waits for them, and re-layouts  2.69 us
    squeeze x1, local copies, waits for them, and re-layouts, local(): own = lambda x, m: lax.dynamic_index_in_dim(x, me ^ m, 0, keepdims=False)  2.57 us
  transfers between devices with their start and end apart: 21, of which 14 were waited for; matrix products, arithmetic and copies ran while one was open for 12% of the time, Pallas kernels for 20%

profile of v10, /device:TPU:0, one launch (start us, length us, event | category | flops | bytes accessed | tf_op | source)
XLA Modules:
  0.0 95.5 jit_solution(12948276904625183846)
XLA Ops:
  0.6 1.2 %copy-done = f32[4,512,128]{2,1,0:T(8,128)S(1)} copy-done((f32[4,512,128]{2,1,0:T(8,128)S(1)}, f32[4,512,128]{2,1,0:T(8,128)}, u32[]{:S(2)}) %copy-start) | copy-done | bytes 1048600
  1.9 0.4 cut.1
  2.2 0.5 collective-permute-start
  2.8 2.6 %collective-permute-start.1 = (f32[256,128]{1,0:T(8,128)S(1)}, f32[256,128]{1,0:T(8,128)S(1)}, u32[]{:S(2)}, u32[]{:S(2)}) collective-permute-start(f32[256,128]{1,0:T(8,128)S(1)} %get-tuple-element.41), channel_id=1, source_target_pairs={{0,2},{1,3},{2,0},{3,1},{4,6},{5,7},{6,4},{7,5},{8,10},{9,11},{10,... | collective-permute-start | bytes 393224 | tf_op jit(solution)/shard_map/ppermute | solution.py:242
  5.3 0.1 collective-permute-start.2
  5.4 2.6 %dynamic-slice_bitcast_fusion = (f32[1024,128]{1,0:T(8,128)}, f32[1024,128]{1,0:T(8,128)}, f32[1024,128]{1,0:T(8,128)}) fusion(f32[4,1024,128]{2,1,0:T(8,128)} %param.7, s32[]{:T(128)S(6)} %select_n.59, s32[]{:T(128)S(6)} %select_n.58, s32[]{:T(128)S(6)} %select_n.57), kind=kLoop, calls=%fused_computation.9 | loop fusion | bytes 3145740 | tf_op jit(solution)/shard_map/jit(dynamic_index_in_dim)/squeeze | solution.py:260
  8.0 1.7 %collective-permute-done.1.r2 = f32[256,128]{1,0:T(8,128)S(1)} collective-permute-done((f32[256,128]{1,0:T(8,128)S(1)}, f32[256,128]{1,0:T(8,128)S(1)}, u32[]{:S(2)}, u32[]{:S(2)}) %collective-permute-start.1) | collective-permute-done | bytes 131104 | tf_op jit(solution)/shard_map/ppermute | solution.py:242
  9.7 2.3 %collective-permute-done.2.r3 = f32[256,128]{1,0:T(8,128)S(1)} collective-permute-done((f32[256,128]{1,0:T(8,128)S(1)}, f32[256,128]{1,0:T(8,128)S(1)}, u32[]{:S(2)}, u32[]{:S(2)}) %collective-permute-start.2) | collective-permute-done | bytes 131104 | tf_op jit(solution)/shard_map/ppermute | solution.py:242
  12.0 0.0 collective-permute-done.r1
  12.0 0.1 collective-permute-start.4
  12.1 1.7 %collective-permute-start.5 = (f32[1024,128]{1,0:T(8,128)}, f32[1024,128]{1,0:T(8,128)}, u32[]{:S(2)}, u32[]{:S(2)}) collective-permute-start(f32[1024,128]{1,0:T(8,128)} %get-tuple-element.49), channel_id=1, source_target_pairs={{0,2},{1,3},{2,0},{3,1},{4,6},{5,7},{6,4},{7,5},{8,10},{9,11},{10,... | collective-permute-start | bytes 1572872 | tf_op jit(solution)/shard_map/ppermute | solution.py:242
  13.8 0.0 collective-permute-start.6
  13.8 19.4 %factor.1 = (f32[512,128]{1,0:T(8,128)S(1)}, f32[512,128]{1,0:T(8,128)S(1)}, f32[512,128]{1,0:T(8,128)S(1)}, f32[256,128]{1,0:T(8,128)S(1)}, f32[256,128]{1,0:T(8,128)S(1)}, /*index=5*/f32[4,512,128]{2,1,0:T(8,128)S(1)}) custom-call(s32[1]{0:T(128)} %bitcast.info, f32[4,512,128]{2,1,0:T(8,128)S(1)} %copy-done.1, f32[512,128]{1,0:T(8,128)S(1)} %collective-permute-done.r1, ...), custom_call_target="tpu_custom_call" | custom-call | flops 200000000 | bytes 4000000 | tf_op jit(solution)/shard_map/factor/pallas_call | solution.py:290
  33.2 0.0 copy-start.2
  33.2 0.6 copy-done.2
  33.9 1.7 %collective-permute-start.7 = (f32[512,128]{1,0:T(8,128)S(1)}, f32[512,128]{1,0:T(8,128)}, u32[]{:S(2)}, u32[]{:S(2)}) collective-permute-start(f32[512,128]{1,0:T(8,128)S(1)} %get-tuple-element.54), channel_id=1, source_target_pairs={{0,2},{1,3},{2,0},{3,1},{4,6},{5,7},{6,4},{7,5},{8,10},{9,11},{10,... | collective-permute-start | bytes 786440 | tf_op jit(solution)/shard_map/ppermute | solution.py:242
  35.6 0.1 multiply_add_fusion
  35.7 0.0 copy-start.4
  35.7 0.1 multiply_add_fusion.1
  35.8 0.0 collective-permute-done.4
  35.8 0.0 collective-permute-done.5
  35.8 1.7 %collective-permute-done.6 = f32[1024,128]{1,0:T(8,128)} collective-permute-done((f32[1024,128]{1,0:T(8,128)}, f32[1024,128]{1,0:T(8,128)}, u32[]{:S(2)}, u32[]{:S(2)}) %collective-permute-start.6) | collective-permute-done | bytes 524320 | tf_op jit(solution)/shard_map/ppermute | solution.py:242
  37.5 0.1 broadcast_in_dim.42
  37.6 6.4 %panel.1 = (f32[4,1024,128]{2,1,0:T(8,128)S(1)}, f32[2,32,64,128]{3,2,1,0:T(8,128)S(1)}, f32[2,32,64,128]{3,2,1,0:T(8,128)S(1)}, f32[256,128]{1,0:T(8,128)S(1)},...) fusion(f32[4,1024,128]{2,1,0:T(8,128)S(1)} %broadcast_in_dim.42, s32[]{:T(128)S(6)} %select_n.60, ...), kind=kCustom, calls=%fused_computation.8 | custom fusion | flops 1000000000 | bytes 11273736 | tf_op jit(solution)/shard_map/panel/pallas_call | solution.py:308
  44.1 0.0 collective-permute-done.7
  44.1 0.1 collective-permute-start.8
  44.1 1.0 %collective-permute-start.9 = (f32[256,128]{1,0:T(8,128)S(1)}, f32[256,128]{1,0:T(8,128)S(1)}, u32[]{:S(2)}, u32[]{:S(2)}) collective-permute-start(f32[256,128]{1,0:T(8,128)S(1)} %get-tuple-element.107), channel_id=1, source_target_pairs={{0,3},{1,2},{2,1},{3,0},{4,7},{5,6},{6,5},{7,4},{8,11},{9,10},{10,... | collective-permute-start | bytes 393224 | tf_op jit(solution)/shard_map/ppermute | solution.py:242
  45.1 3.1 %collective-permute-done.8 = f32[2,32,64,128]{3,2,1,0:T(8,128)S(1)} collective-permute-done((f32[2,32,64,128]{3,2,1,0:T(8,128)S(1)}, f32[2,32,64,128]{3,2,1,0:T(8,128)S(1)}, u32[]{:S(2)}, u32[]{:S(2)}) %collective-permute-start.8) | collective-permute-done | bytes 2097184 | tf_op jit(solution)/shard_map/ppermute | solution.py:242
  48.3 0.6 slice_add_fusion
  48.9 0.6 collective-permute-done.9
  49.4 2.8 %collective-permute-start.11 = (f32[16,64,128]{2,1,0:T(8,128)S(1)}, f32[16,64,128]{2,1,0:T(8,128)S(1)}, u32[]{:S(2)}, u32[]{:S(2)}) collective-permute-start(f32[16,64,128]{2,1,0:T(8,128)S(1)} %get-tuple-element.60), channel_id=1, source_target_pairs={{0,8},{4,12},{8,0},{12,4},{16,24},{20,28},{24,16},{28,20},{1,9},{5... | collective-permute-start | bytes 1572872 | tf_op jit(solution)/shard_map/ppermute | solution.py:242
  52.2 0.0 collective-permute-start.10
  52.2 0.0 collective-permute-start.3
  52.2 1.9 %collective-permute-start.12 = (f32[1024,128]{1,0:T(8,128)S(1)}, f32[1024,128]{1,0:T(8,128)S(1)}, u32[]{:S(2)}, u32[]{:S(2)}) collective-permute-start(f32[1024,128]{1,0:T(8,128)S(1)} %get-tuple-element.109), channel_id=1, source_target_pairs={{0,3},{1,2},{2,1},{3,0},{4,7},{5,6},{6,5},{7,4},{8,11},{9,10},{10,... | collective-permute-start | bytes 1572872 | tf_op jit(solution)/shard_map/ppermute | solution.py:242
  54.1 0.1 broadcast_in_dim.36
  54.2 10.2 %collective-permute-done.11 = f32[16,64,128]{2,1,0:T(8,128)S(1)} collective-permute-done((f32[16,64,128]{2,1,0:T(8,128)S(1)}, f32[16,64,128]{2,1,0:T(8,128)S(1)}, u32[]{:S(2)}, u32[]{:S(2)}) %collective-permute-start.11) | collective-permute-done | bytes 524320 | tf_op jit(solution)/shard_map/ppermute | solution.py:242
  64.4 0.1 slice_add_fusion.4
  64.5 1.4 %collective-permute-done.10 = f32[16,64,128]{2,1,0:T(8,128)S(1)} collective-permute-done((f32[16,64,128]{2,1,0:T(8,128)S(1)}, f32[16,64,128]{2,1,0:T(8,128)S(1)}, u32[]{:S(2)}, u32[]{:S(2)}) %collective-permute-start.10) | collective-permute-done | bytes 524320 | tf_op jit(solution)/shard_map/ppermute | solution.py:242
  65.9 0.1 slice_add_fusion.5
  65.9 0.2 collective-permute-done.12
  66.1 1.5 %collective-permute-start.13 = (f32[8,64,128]{2,1,0:T(8,128)S(1)}, f32[8,64,128]{2,1,0:T(8,128)S(1)}, u32[]{:S(2)}, u32[]{:S(2)}) collective-permute-start(f32[8,64,128]{2,1,0:T(8,128)S(1)} %get-tuple-element.64), channel_id=1, source_target_pairs={{0,8},{4,12},{8,0},{12,4},{16,24},{20,28},{24,16},{28,20},{1,9},{5... | collective-permute-start | bytes 786440 | tf_op jit(solution)/shard_map/ppermute | solution.py:242
  67.6 0.0 collective-permute-done.3
  67.6 1.5 %collective-permute-start.18 = (f32[1024,128]{1,0:T(8,128)S(1)}, f32[1024,128]{1,0:T(8,128)S(1)}, u32[]{:S(2)}, u32[]{:S(2)}) collective-permute-start(f32[1024,128]{1,0:T(8,128)S(1)} %get-tuple-element.111), channel_id=1, source_target_pairs={{0,2},{1,3},{2,0},{3,1},{4,6},{5,7},{6,4},{7,5},{8,10},{9,11},{10,... | collective-permute-start | bytes 1572872 | tf_op jit(solution)/shard_map/ppermute | solution.py:242
  69.2 0.0 collective-permute-start.19
  69.2 0.2 collective-permute-start.14
  69.4 1.0 %bitcast_dynamic-update-slice_fusion.4 = f32[4,512,128]{2,1,0:T(8,128)S(1)} fusion(f32[4,512,128]{2,1,0:T(8,128)S(1)} %bitcast_dynamic-update-slice_fusion.5, s32[]{:T(128)S(6)} %select_n.58, f32[512,128]{1,0:T(8,128)} %collective-permute-done.7), kind=kLoop, calls=%fused_computation.21 | loop fusion | bytes 524292 | tf_op jit(solution)/shard_map/dynamic_update_slice | solution.py:370
  70.4 0.0 copy-done.3
  70.4 0.5 collective-permute-start.20
  70.9 3.7 %collective-permute-done.13 = f32[8,64,128]{2,1,0:T(8,128)S(1)} collective-permute-done((f32[8,64,128]{2,1,0:T(8,128)S(1)}, f32[8,64,128]{2,1,0:T(8,128)S(1)}, u32[]{:S(2)}, u32[]{:S(2)}) %collective-permute-start.13) | collective-permute-done | bytes 262176 | tf_op jit(solution)/shard_map/ppermute | solution.py:242
  74.7 3.2 %collective-permute-done.14 = f32[8,64,128]{2,1,0:T(8,128)S(1)} collective-permute-done((f32[8,64,128]{2,1,0:T(8,128)S(1)}, f32[8,64,128]{2,1,0:T(8,128)S(1)}, u32[]{:S(2)}, u32[]{:S(2)}) %collective-permute-start.14) | collective-permute-done | bytes 262176 | tf_op jit(solution)/shard_map/ppermute | solution.py:242
  78.0 0.6 collective-permute-start.17
  78.6 2.5 %collective-permute-start.16 = (f32[2,128,128]{2,1,0:T(8,128)S(1)}, f32[2,128,128]{2,1,0:T(8,128)S(1)}, u32[]{:S(2)}, u32[]{:S(2)}) collective-permute-start(f32[2,128,128]{2,1,0:T(8,128)S(1)} %pad_maximum_fusion.1), channel_id=1, source_target_pairs={{0,16},{4,20},{8,24},{12,28},{16,0},{20,4},{24,8},{28,12},{1,17},{... | collective-permute-start | bytes 393224 | tf_op jit(solution)/shard_map/ppermute | solution.py:242
  81.1 1.4 %collective-permute-done.18 = f32[1024,128]{1,0:T(8,128)S(1)} collective-permute-done((f32[1024,128]{1,0:T(8,128)S(1)}, f32[1024,128]{1,0:T(8,128)S(1)}, u32[]{:S(2)}, u32[]{:S(2)}) %collective-permute-start.18) | collective-permute-done | bytes 524320 | tf_op jit(solution)/shard_map/ppermute | solution.py:242
  82.5 3.1 %collective-permute-start.15 = (f32[2,128,128]{2,1,0:T(8,128)S(1)}, f32[2,128,128]{2,1,0:T(8,128)S(1)}, u32[]{:S(2)}, u32[]{:S(2)}) collective-permute-start(f32[2,128,128]{2,1,0:T(8,128)S(1)} %pad_maximum_fusion), channel_id=1, source_target_pairs={{0,18},{1,19},{2,16},{3,17},{4,22},{5,23},{6,20},{7,21},{8,26},{9,... | collective-permute-start | bytes 393224 | tf_op jit(solution)/shard_map/ppermute | solution.py:360
  85.6 0.0 collective-permute-done.19
  85.6 0.0 collective-permute-done.20
  85.6 1.6 %collective-permute-done.17 = f32[2,128,128]{2,1,0:T(8,128)S(1)} collective-permute-done((f32[2,128,128]{2,1,0:T(8,128)S(1)}, f32[2,128,128]{2,1,0:T(8,128)S(1)}, u32[]{:S(2)}, u32[]{:S(2)}) %collective-permute-start.17) | collective-permute-done | bytes 131104 | tf_op jit(solution)/shard_map/ppermute | solution.py:242
  87.2 2.9 %collective-permute-done.16 = f32[2,128,128]{2,1,0:T(8,128)S(1)} collective-permute-done((f32[2,128,128]{2,1,0:T(8,128)S(1)}, f32[2,128,128]{2,1,0:T(8,128)S(1)}, u32[]{:S(2)}, u32[]{:S(2)}) %collective-permute-start.16) | collective-permute-done | bytes 131104 | tf_op jit(solution)/shard_map/ppermute | solution.py:242
  90.1 3.6 %collective-permute-done.15 = f32[2,128,128]{2,1,0:T(8,128)S(1)} collective-permute-done((f32[2,128,128]{2,1,0:T(8,128)S(1)}, f32[2,128,128]{2,1,0:T(8,128)S(1)}, u32[]{:S(2)}, u32[]{:S(2)}) %collective-permute-start.15) | collective-permute-done | bytes 131104 | tf_op jit(solution)/shard_map/ppermute | solution.py:360
  93.8 0.0 copy-start.6
  93.9 0.0 copy-start.5
  93.9 0.9 fusion.2
  94.7 0.1 copy-done.6
  94.8 0.7 copy-done.5
  (25 shorter events, 0.3 us)
Async XLA Ops:
  0.6 1.2 %copy-start = (f32[4,512,128]{2,1,0:T(8,128)S(1)}, f32[4,512,128]{2,1,0:T(8,128)}, u32[]{:S(2)}) copy-start(f32[4,512,128]{2,1,0:T(8,128)} %own_ref.2) | copy-start | bytes 3145732
  1.9 12.0 %copy-start.1 = (f32[4,512,128]{2,1,0:T(8,128)S(1)}, f32[4,512,128]{2,1,0:T(8,128)}, u32[]{:S(2)}) copy-start(f32[4,512,128]{2,1,0:T(8,128)} %own_ref.2) | copy-start | bytes 3145732
  2.2 9.7 %collective-permute-start = (f32[512,128]{1,0:T(8,128)S(1)}, f32[512,128]{1,0:T(8,128)S(1)}, u32[]{:S(2)}, u32[]{:S(2)}) collective-permute-start(f32[512,128]{1,0:T(8,128)S(1)} %get-tuple-element.40), channel_id=1, source_target_pairs={{0,1},{1,0},{2,3},{3,2},{4,5},{5,4},{6,7},{7,6},{8,9},{9,8},{10,11... | collective-permute-start | bytes 786440 | tf_op jit(solution)/shard_map/ppermute | solution.py:242
  2.8 6.9 %collective-permute-start.1 = (f32[256,128]{1,0:T(8,128)S(1)}, f32[256,128]{1,0:T(8,128)S(1)}, u32[]{:S(2)}, u32[]{:S(2)}) collective-permute-start(f32[256,128]{1,0:T(8,128)S(1)} %get-tuple-element.41), channel_id=1, source_target_pairs={{0,2},{1,3},{2,0},{3,1},{4,6},{5,7},{6,4},{7,5},{8,10},{9,11},{10,... | collective-permute-start | bytes 393224 | tf_op jit(solution)/shard_map/ppermute | solution.py:242
  5.3 6.6 %collective-permute-start.2 = (f32[256,128]{1,0:T(8,128)S(1)}, f32[256,128]{1,0:T(8,128)S(1)}, u32[]{:S(2)}, u32[]{:S(2)}) collective-permute-start(f32[256,128]{1,0:T(8,128)S(1)} %get-tuple-element.42), channel_id=1, source_target_pairs={{0,3},{1,2},{2,1},{3,0},{4,7},{5,6},{6,5},{7,4},{8,11},{9,10},{10,... | collective-permute-start | bytes 393224 | tf_op jit(solution)/shard_map/ppermute | solution.py:242
  5.4 30.2 %copy-start.8 = (s32[144,1]{0,1:T(1,128)S(1)}, s32[144,1]{0,1:T(1,128)}, u32[]{:S(2)}) copy-start(s32[144,1]{0,1:T(1,128)} %param.9) | copy-start | bytes 1732
  5.4 30.2 %copy-start.9 = (s32[144]{0:T(256)S(1)}, s32[144]{0:T(256)}, u32[]{:S(2)}) copy-start(s32[144]{0:T(256)} %param.10) | copy-start | bytes 1732
  8.0 29.7 %copy-start.10 = (s32[4]{0:T(128)S(1)}, s32[4]{0:T(128)}, u32[]{:S(2)}) copy-start(s32[4]{0:T(128)} %param.8) | copy-start | bytes 52
  12.0 23.8 %collective-permute-start.4 = (f32[1024,128]{1,0:T(8,128)}, f32[1024,128]{1,0:T(8,128)}, u32[]{:S(2)}, u32[]{:S(2)}) collective-permute-start(f32[1024,128]{1,0:T(8,128)} %get-tuple-element.48), channel_id=1, source_target_pairs={{0,1},{1,0},{2,3},{3,2},{4,5},{5,4},{6,7},{7,6},{8,9},{9,8},{10,11... | collective-permute-start | bytes 1572872 | tf_op jit(solution)/shard_map/ppermute | solution.py:242
  12.1 23.7 %collective-permute-start.5 = (f32[1024,128]{1,0:T(8,128)}, f32[1024,128]{1,0:T(8,128)}, u32[]{:S(2)}, u32[]{:S(2)}) collective-permute-start(f32[1024,128]{1,0:T(8,128)} %get-tuple-element.49), channel_id=1, source_target_pairs={{0,2},{1,3},{2,0},{3,1},{4,6},{5,7},{6,4},{7,5},{8,10},{9,11},{10,... | collective-permute-start | bytes 1572872 | tf_op jit(solution)/shard_map/ppermute | solution.py:242
  13.8 23.7 %collective-permute-start.6 = (f32[1024,128]{1,0:T(8,128)}, f32[1024,128]{1,0:T(8,128)}, u32[]{:S(2)}, u32[]{:S(2)}) collective-permute-start(f32[1024,128]{1,0:T(8,128)} %get-tuple-element.50), channel_id=1, source_target_pairs={{0,3},{1,2},{2,1},{3,0},{4,7},{5,6},{6,5},{7,4},{8,11},{9,10},{10,... | collective-permute-start | bytes 1572872 | tf_op jit(solution)/shard_map/ppermute | solution.py:242
  33.2 0.7 copy-start.2
  33.9 10.2 %collective-permute-start.7 = (f32[512,128]{1,0:T(8,128)S(1)}, f32[512,128]{1,0:T(8,128)}, u32[]{:S(2)}, u32[]{:S(2)}) collective-permute-start(f32[512,128]{1,0:T(8,128)S(1)} %get-tuple-element.54), channel_id=1, source_target_pairs={{0,2},{1,3},{2,0},{3,1},{4,6},{5,7},{6,4},{7,5},{8,10},{9,11},{10,... | collective-permute-start | bytes 786440 | tf_op jit(solution)/shard_map/ppermute | solution.py:242
  35.7 2.0 %copy-start.4 = (f32[4,1024,128]{2,1,0:T(8,128)S(1)}, f32[4,1024,128]{2,1,0:T(8,128)}, u32[]{:S(2)}) copy-start(f32[4,1024,128]{2,1,0:T(8,128)} %param.7) | copy-start | bytes 6291460
  44.1 4.2 %collective-permute-start.8 = (f32[2,32,64,128]{3,2,1,0:T(8,128)S(1)}, f32[2,32,64,128]{3,2,1,0:T(8,128)S(1)}, u32[]{:S(2)}, u32[]{:S(2)}) collective-permute-start(f32[2,32,64,128]{3,2,1,0:T(8,128)S(1)} %get-tuple-element.57), channel_id=1, source_target_pairs={{0,1},{1,0},{2,3},{3,2},{4,5},{5,4},{6,7},{7,6},{8,9},{9,8},{10,11... | collective-permute-start | bytes 6291464 | tf_op jit(solution)/shard_map/ppermute | solution.py:242
  44.1 5.3 %collective-permute-start.9 = (f32[256,128]{1,0:T(8,128)S(1)}, f32[256,128]{1,0:T(8,128)S(1)}, u32[]{:S(2)}, u32[]{:S(2)}) collective-permute-start(f32[256,128]{1,0:T(8,128)S(1)} %get-tuple-element.107), channel_id=1, source_target_pairs={{0,3},{1,2},{2,1},{3,0},{4,7},{5,6},{6,5},{7,4},{8,11},{9,10},{10,... | collective-permute-start | bytes 393224 | tf_op jit(solution)/shard_map/ppermute | solution.py:242
  49.4 15.0 %collective-permute-start.11 = (f32[16,64,128]{2,1,0:T(8,128)S(1)}, f32[16,64,128]{2,1,0:T(8,128)S(1)}, u32[]{:S(2)}, u32[]{:S(2)}) collective-permute-start(f32[16,64,128]{2,1,0:T(8,128)S(1)} %get-tuple-element.60), channel_id=1, source_target_pairs={{0,8},{4,12},{8,0},{12,4},{16,24},{20,28},{24,16},{28,20},{1,9},{5... | collective-permute-start | bytes 1572872 | tf_op jit(solution)/shard_map/ppermute | solution.py:242
  52.2 13.7 %collective-permute-start.10 = (f32[16,64,128]{2,1,0:T(8,128)S(1)}, f32[16,64,128]{2,1,0:T(8,128)S(1)}, u32[]{:S(2)}, u32[]{:S(2)}) collective-permute-start(f32[16,64,128]{2,1,0:T(8,128)S(1)} %get-tuple-element.59), channel_id=1, source_target_pairs={{0,4},{4,0},{8,12},{12,8},{16,20},{20,16},{24,28},{28,24},{1,5},{5... | collective-permute-start | bytes 1572872 | tf_op jit(solution)/shard_map/ppermute | solution.py:242
  52.2 15.4 %collective-permute-start.3 = (f32[512,128]{1,0:T(8,128)S(1)}, f32[512,128]{1,0:T(8,128)S(1)}, u32[]{:S(2)}, u32[]{:S(2)}) collective-permute-start(f32[512,128]{1,0:T(8,128)S(1)} %get-tuple-element.47), channel_id=1, source_target_pairs={{0,1},{1,0},{2,3},{3,2},{4,5},{5,4},{6,7},{7,6},{8,9},{9,8},{10,11... | collective-permute-start | bytes 786440 | tf_op jit(solution)/shard_map/ppermute | solution.py:242
  52.2 13.9 %collective-permute-start.12 = (f32[1024,128]{1,0:T(8,128)S(1)}, f32[1024,128]{1,0:T(8,128)S(1)}, u32[]{:S(2)}, u32[]{:S(2)}) collective-permute-start(f32[1024,128]{1,0:T(8,128)S(1)} %get-tuple-element.109), channel_id=1, source_target_pairs={{0,3},{1,2},{2,1},{3,0},{4,7},{5,6},{6,5},{7,4},{8,11},{9,10},{10,... | collective-permute-start | bytes 1572872 | tf_op jit(solution)/shard_map/ppermute | solution.py:242
  64.4 6.0 %copy-start.3 = (f32[256,128]{1,0:T(8,128)S(1)}, f32[256,128]{1,0:T(8,128)}, u32[]{:S(2)}) copy-start(f32[256,128]{1,0:T(8,128)} %copy-done.2) | copy-start | bytes 393220
  66.1 8.5 %collective-permute-start.13 = (f32[8,64,128]{2,1,0:T(8,128)S(1)}, f32[8,64,128]{2,1,0:T(8,128)S(1)}, u32[]{:S(2)}, u32[]{:S(2)}) collective-permute-start(f32[8,64,128]{2,1,0:T(8,128)S(1)} %get-tuple-element.64), channel_id=1, source_target_pairs={{0,8},{4,12},{8,0},{12,4},{16,24},{20,28},{24,16},{28,20},{1,9},{5... | collective-permute-start | bytes 786440 | tf_op jit(solution)/shard_map/ppermute | solution.py:242
  67.6 14.8 %collective-permute-start.18 = (f32[1024,128]{1,0:T(8,128)S(1)}, f32[1024,128]{1,0:T(8,128)S(1)}, u32[]{:S(2)}, u32[]{:S(2)}) collective-permute-start(f32[1024,128]{1,0:T(8,128)S(1)} %get-tuple-element.111), channel_id=1, source_target_pairs={{0,2},{1,3},{2,0},{3,1},{4,6},{5,7},{6,4},{7,5},{8,10},{9,11},{10,... | collective-permute-start | bytes 1572872 | tf_op jit(solution)/shard_map/ppermute | solution.py:242
  69.2 16.4 %collective-permute-start.19 = (f32[1024,128]{1,0:T(8,128)S(1)}, f32[1024,128]{1,0:T(8,128)S(1)}, u32[]{:S(2)}, u32[]{:S(2)}) collective-permute-start(f32[1024,128]{1,0:T(8,128)S(1)} %get-tuple-element.113), channel_id=1, source_target_pairs={{0,1},{1,0},{2,3},{3,2},{4,5},{5,4},{6,7},{7,6},{8,9},{9,8},{10,11... | collective-permute-start | bytes 1572872 | tf_op jit(solution)/shard_map/ppermute | solution.py:242
  69.2 8.7 %collective-permute-start.14 = (f32[8,64,128]{2,1,0:T(8,128)S(1)}, f32[8,64,128]{2,1,0:T(8,128)S(1)}, u32[]{:S(2)}, u32[]{:S(2)}) collective-permute-start(f32[8,64,128]{2,1,0:T(8,128)S(1)} %get-tuple-element.65), channel_id=1, source_target_pairs={{0,4},{4,0},{8,12},{12,8},{16,20},{20,16},{24,28},{28,24},{1,5},{5... | collective-permute-start | bytes 786440 | tf_op jit(solution)/shard_map/ppermute | solution.py:242
  70.4 15.2 %collective-permute-start.20 = (f32[256,128]{1,0:T(8,128)S(1)}, f32[256,128]{1,0:T(8,128)S(1)}, u32[]{:S(2)}, u32[]{:S(2)}) collective-permute-start(f32[256,128]{1,0:T(8,128)S(1)} %copy-done.3), channel_id=1, source_target_pairs={{0,3},{1,2},{2,1},{3,0},{4,7},{5,6},{6,5},{7,4},{8,11},{9,10},{10,... | collective-permute-start | bytes 393224 | tf_op jit(solution)/shard_map/ppermute | solution.py:242
  78.0 9.2 %collective-permute-start.17 = (f32[2,128,128]{2,1,0:T(8,128)S(1)}, f32[2,128,128]{2,1,0:T(8,128)S(1)}, u32[]{:S(2)}, u32[]{:S(2)}) collective-permute-start(f32[2,128,128]{2,1,0:T(8,128)S(1)} %pad_maximum_fusion.2), channel_id=1, source_target_pairs={{0,2},{1,3},{2,0},{3,1},{4,6},{5,7},{6,4},{7,5},{8,10},{9,11},{10,... | collective-permute-start | bytes 393224 | tf_op jit(solution)/shard_map/ppermute | solution.py:242
  78.6 15.3 %copy-start.7 = (f32[2,128,128]{2,1,0:T(8,128)S(1)}, f32[2,128,128]{2,1,0:T(8,128)}, u32[]{:S(2)}) copy-start(f32[2,128,128]{2,1,0:T(8,128)} %param.11) | copy-start | bytes 393220
  78.6 11.5 %collective-permute-start.16 = (f32[2,128,128]{2,1,0:T(8,128)S(1)}, f32[2,128,128]{2,1,0:T(8,128)S(1)}, u32[]{:S(2)}, u32[]{:S(2)}) collective-permute-start(f32[2,128,128]{2,1,0:T(8,128)S(1)} %pad_maximum_fusion.1), channel_id=1, source_target_pairs={{0,16},{4,20},{8,24},{12,28},{16,0},{20,4},{24,8},{28,12},{1,17},{... | collective-permute-start | bytes 393224 | tf_op jit(solution)/shard_map/ppermute | solution.py:242
  82.5 11.2 %collective-permute-start.15 = (f32[2,128,128]{2,1,0:T(8,128)S(1)}, f32[2,128,128]{2,1,0:T(8,128)S(1)}, u32[]{:S(2)}, u32[]{:S(2)}) collective-permute-start(f32[2,128,128]{2,1,0:T(8,128)S(1)} %pad_maximum_fusion), channel_id=1, source_target_pairs={{0,18},{1,19},{2,16},{3,17},{4,22},{5,23},{6,20},{7,21},{8,26},{9,... | collective-permute-start | bytes 393224 | tf_op jit(solution)/shard_map/ppermute | solution.py:360
  93.8 1.0 %copy-start.6 = (f32[4,512,128]{2,1,0:T(8,128)}, f32[4,512,128]{2,1,0:T(8,128)S(1)}, u32[]{:S(2)}) copy-start(f32[4,512,128]{2,1,0:T(8,128)S(1)} %get-tuple-element.100) | copy-start | bytes 3145732
  93.9 1.7 %copy-start.5 = (f32[4,1024,128]{2,1,0:T(8,128)}, f32[4,1024,128]{2,1,0:T(8,128)S(1)}, u32[]{:S(2)}) copy-start(f32[4,1024,128]{2,1,0:T(8,128)S(1)} %bitcast_dynamic-update-slice_fusion.3) | copy-start | bytes 6291460

commit v11 on v8

--- a/solution.py
+++ b/solution.py
@@ -126,7 +126,7 @@
         c.wait()
 
 
-def factor_kernel(info, own_ref, r1, r2, r3, l0, l1, l2, l3, mt, a, l, sems):
+def factor_kernel(info, own_ref, r1, r2, r3, l0, l1, l2a, l2b, l3, mt, a, l, sems):
     me = info[0]
     side = me // 2
     far_rows = pl.ds((1 - side) * (W // 2), W // 2)
@@ -164,8 +164,12 @@
             for j in range(i + 1, k):
                 total = total + dot_nt(mt[j, pl.ds(i * B, B), :], l[j, here, :])
             mt[k, pl.ds(i * B, B), :] = dot_nt(-total, inv)
-    outs = [l0, l1, l2, l3]
-    copies = [pltpu.make_async_copy(l.at[me ^ m], outs[m], sems.at[m]) for m in range(NB)]
+    half = [pl.ds(n * (W // 2), W // 2) for n in range(2)]
+    pieces = [l.at[me], l.at[me ^ 1], l.at[me ^ 2, half[0]], l.at[me ^ 2, half[1]], l.at[me ^ 3]]
+    copies = [
+        pltpu.make_async_copy(piece, out, sems.at[n])
+        for n, (piece, out) in enumerate(zip(pieces, (l0, l1, l2a, l2b, l3)))
+    ]
     for c in copies:
         c.start()
     for c in copies:
@@ -173,16 +177,24 @@
 
 
 def panel_kernel(
-    info, counts, tgt_a, tgt_b, own_ref, r1, r2, r3, mt, l3, x0, x1, x2, x3, keep, send, xh, xl
+    info, counts, tgt_a, tgt_b, own_ref, r1, r2, r3, mt, l2b, x0, x1, x2, x3, keep, send, xh, xl, p, sems
 ):
     me = info[0]
     count = counts[me]
     rows = P_SIZE * B
-    ins = [own_ref.at[me], r1, r2, r3]
+    copies = [
+        pltpu.make_async_copy(ref, p.at[m], sems.at[m]) for m, ref in enumerate((own_ref.at[me], r1, r2, r3))
+    ]
+    for copy in copies:
+        copy.start()
+    keep[...] = jnp.zeros_like(keep)
+    send[...] = jnp.zeros_like(send)
     outs = [x0, x1, x2, x3]
-    x3[pl.ds(rows, W), :] = l3[...]
+    x2[pl.ds(rows, W // 2), :] = l2b[...]
+    for copy in copies:
+        copy.wait()
     live = lax.broadcasted_iota(jnp.int32, (rows, B), 0) < count * B
-    parts = [split_bf16(jnp.where(live, ref[...], 0.0)) for ref in ins]
+    parts = [split_bf16(jnp.where(live, p[m], 0.0)) for m in range(NB)]
     left = [jnp.concatenate([part[n] for part in parts], axis=1) for n in range(2)]
     for c in range(0, NB, 2):
         right = [
@@ -196,8 +208,6 @@
         xh[:, pl.ds(c * B, 2 * B)] = high
         xl[:, pl.ds(c * B, 2 * B)] = low
 
-    keep[...] = jnp.zeros_like(keep)
-    send[...] = jnp.zeros_like(send)
     half, strip = keep.shape[1:3]
     for j in range(0, P_SIZE, 2):
 
@@ -260,7 +270,7 @@
         out_specs=[VMEM] * 3,
         scratch_shapes=[pltpu.SemaphoreType.DMA((3,))],
         compiler_params=pltpu.CompilerParams(vmem_limit_bytes=8 * 2**20),
-        cost_estimate=pl.CostEstimate(flops=0, bytes_accessed=2**20, transcendentals=0),
+        cost_estimate=pl.CostEstimate(flops=0, bytes_accessed=0, transcendentals=0),
         name="cut",
     )(info, diag_block)
     diag_in = [swap(part, "narrow", m) for m, part in zip(masks, cut)]
@@ -279,37 +289,40 @@
     tgt_b = relative_index(owner, slot, wide_me, me, steps_b)
 
     slab = jax.ShapeDtypeStruct((W, B), jnp.float32)
+    low = jax.ShapeDtypeStruct((W // 2, B), jnp.float32)
     *l_parts, mt = pl.pallas_call(
         factor_kernel,
-        out_shape=[slab] * NB + [jax.ShapeDtypeStruct((NB, W, B), jnp.float32)],
+        out_shape=[slab, slab, low, low, slab, jax.ShapeDtypeStruct((NB, W, B), jnp.float32)],
         in_specs=[SMEM] + [ANY] * NB,
-        out_specs=[ANY] * NB + [VMEM],
-        scratch_shapes=[pltpu.VMEM((NB, W, B), jnp.float32)] * 2 + [pltpu.SemaphoreType.DMA((NB,))],
-        compiler_params=pltpu.CompilerParams(vmem_limit_bytes=32 * 2**20),
+        out_specs=[ANY] * (NB + 1) + [VMEM],
+        scratch_shapes=[pltpu.VMEM((NB, W, B), jnp.float32)] * 2 + [pltpu.SemaphoreType.DMA((NB + 1,))],
+        compiler_params=pltpu.CompilerParams(vmem_limit_bytes=16 * 2**20),
         cost_estimate=pl.CostEstimate(flops=2 * 10**8, bytes_accessed=4 * 10**6, transcendentals=0),
         name="factor",
     )(info, diag_block, *diag_in)
 
     rows = P_SIZE * B
     blocks = wide_count * narrow_count * T_DEV
-    slab = jax.ShapeDtypeStruct((rows, B), jnp.float32)
-    longer = jax.ShapeDtypeStruct((rows + W, B), jnp.float32)
+    slab, longer = [jax.ShapeDtypeStruct((n, B), jnp.float32) for n in (rows, rows + W // 2)]
     part = jax.ShapeDtypeStruct((2, blocks // 2, B // 2, B), jnp.float32)
-    *x_parts, keep, send = pl.pallas_call(
+    home, near, far_2, far_3, keep, send = pl.pallas_call(
         panel_kernel,
-        out_shape=[slab] * (NB - 1) + [longer, part, part],
-        in_specs=[SMEM] * 4 + [VMEM] * (NB + 2),
-        out_specs=[VMEM] * (NB + 2),
-        scratch_shapes=[pltpu.VMEM((rows, W), jnp.bfloat16)] * 2,
-        compiler_params=pltpu.CompilerParams(vmem_limit_bytes=20 * 2**20 + 4 * blocks * B * B),
+        out_shape=[slab, slab, longer, slab, part, part],
+        in_specs=[SMEM] * 4 + [ANY] * NB + [VMEM] * 2,
+        out_specs=[VMEM] * 6,
+        scratch_shapes=[pltpu.VMEM((rows, W), jnp.bfloat16)] * 2
+        + [pltpu.VMEM((NB, rows, B), jnp.float32), pltpu.SemaphoreType.DMA((NB,))],
+        compiler_params=pltpu.CompilerParams(vmem_limit_bytes=16 * 2**20 + 4 * blocks * B * B),
         cost_estimate=pl.CostEstimate(flops=10**9, bytes_accessed=10 * 10**6, transcendentals=0),
         name="panel",
     )(info, panel_count, tgt_a, tgt_b, panel, *panel_in, mt, l_parts[3])
 
-    l_back = [swap(l_parts[m], "narrow", m) for m in (1, 2)]
-    x_back = [swap(x_parts[m], "narrow", m) for m in masks]
-
-    send, l_back[1] = lax.optimization_barrier((send, l_back[1]))
+    near_l, far_l2, far_l3 = [swap(l_parts[n], "narrow", m) for n, m in ((1, 1), (2, 2), (4, 3))]
+    near = swap(near, "narrow", 1)
+    far_2 = swap(far_2, "narrow", 2)
+    far_3 = swap(far_3, "narrow", 3)
+
+    send, far_l3 = lax.optimization_barrier((send, far_l3))
     got = swap(send, "narrow", 1)
     half = blocks // 4
     upper = lambda u, n: u[n, half:]
@@ -320,9 +333,9 @@
     keep_b = lower(keep, 1) + lower(got, 1)
     for n in (1, 2):
         if n == 2:
-            send_a, send_b, x_back[1] = lax.optimization_barrier((send_a, send_b, x_back[1]))
+            send_a, send_b, far_3 = lax.optimization_barrier((send_a, send_b, far_3))
         else:
-            send_a, send_b = lax.optimization_barrier((send_a, send_b))
+            send_a, send_b, far_l2 = lax.optimization_barrier((send_a, send_b, far_l2))
         got_a = swap(send_a, *steps_a[n])
         got_b = swap(send_b, *steps_b[n])
         half = half // 2
@@ -347,19 +360,20 @@
         swap(take(2, T_DEV), *rest[0]),
         swap(take(1, T_DEV), *rest[1]),
     ]
-    got, x_back[2], x_back[0] = lax.optimization_barrier((got, x_back[2], x_back[0]))
-    l_back.append(x_back[2][rows:])
-    x_back[2] = x_back[2][:rows]
+    got, far_2, near = lax.optimization_barrier((got, far_2, near))
     updated = ancestor - (take(0, T_DEV) + (got[0] + (got[1] + got[2])))
 
-    def give_back(own_part, others):
-        back = [own_part] + others
-        out = jnp.zeros((NB,) + own_part.shape, jnp.float32)
-        for m in range(NB):
-            out = lax.dynamic_update_index_in_dim(out, back[m], me ^ m, 0)
+    def assemble(height, pieces):
+        out = jnp.zeros((NB, height, B), jnp.float32)
+        for m, row, piece in pieces:
+            out = lax.dynamic_update_slice(out, piece[None], (me ^ m, row, 0))
         return out
 
-    return (give_back(l_parts[0], l_back), give_back(x_parts[0], x_back), updated)
+    factor = assemble(
+        W, [(0, 0, l_parts[0]), (1, 0, near_l), (3, 0, far_l3), (2, 0, far_l2), (2, W // 2, far_2[rows:])]
+    )
+    lower_panel = assemble(rows, [(0, 0, home), (1, 0, near), (3, 0, far_3), (2, 0, far_2[:rows])])
+    return (factor, lower_panel, updated)
 
 
 def solution(mesh):

time: 94.4 us -> 96.2 us (1.019)
  other arithmetic: 6.98 us -> 8.09 us
    ppermute x18 -> x19, waiting for transfers between devices: 41.7 us -> 38.1 us  [swap(): return lax.ppermute(x, axis, xor_pairs(lax.axis_size(axis), mask))]
    ppermute x1, waiting for transfers between devices: 0.01 us -> 2.7 us  [local(): lax.ppermute(take(3, T_DEV), ('wide', 'narrow'), xor_pairs(wide_count * n...]
    ppermute x1, starting transfers between devices: 0.37 us -> 1.47 us  [local(): lax.ppermute(take(3, T_DEV), ('wide', 'narrow'), xor_pairs(wide_count * n...]
    unnamed x18 -> x22, local copies, waits for them, and re-layouts: 2.09 us -> 2.75 us
    ppermute x18 -> x19, starting transfers between devices: 19.6 us -> 19.1 us  [swap(): return lax.ppermute(x, axis, xor_pairs(lax.axis_size(axis), mask))]
  transfers between devices with their start and end apart: 19 -> 20, of which waited for: 12 -> 14; matrix products, arithmetic and copies ran while one was open for 9% -> 11% of each run, Pallas kernels for 21% -> 20%
where the time goes in v11:
time: 96.2 us; the launch traced here: 95.8 us
  waiting for transfers between devices  40.8 us (42%)
  starting transfers between devices  20.5 us (21%)
  Pallas kernels  19.7 us (20%)
  other arithmetic  8.09 us (8%)
  local copies, waits for them, and re-layouts  5.74 us (6%)
    ppermute x19, waiting for transfers between devices, swap(): return lax.ppermute(x, axis, xor_pairs(lax.axis_size(axis), mask))  38.1 us
    pallas_call x1, Pallas kernels, local(): pl.pallas_call(factor_kernel, out_shape=[slab, slab, low, low, slab, jax....  19.4 us
    ppermute x19, starting transfers between devices, swap(): return lax.ppermute(x, axis, xor_pairs(lax.axis_size(axis), mask))  19.1 us
    pallas_call x1, other arithmetic, local(): pl.pallas_call(panel_kernel, out_shape=[slab, slab, longer, slab, part, p...  6.31 us
    unnamed x22, local copies, waits for them, and re-layouts  2.75 us
    ppermute x1, waiting for transfers between devices, local(): lax.ppermute(take(3, T_DEV), ('wide', 'narrow'), xor_pairs(wide_count * n...  2.7 us
    squeeze x1, local copies, waits for them, and re-layouts, local(): own = lambda x, m: lax.dynamic_index_in_dim(x, me ^ m, 0, keepdims=False)  2.57 us
  transfers between devices with their start and end apart: 20, of which 14 were waited for; matrix products, arithmetic and copies ran while one was open for 11% of the time, Pallas kernels for 20%

profile of v11, /device:TPU:0, one launch (start us, length us, event | category | flops | bytes accessed | tf_op | source)
XLA Modules:
  0.0 95.8 jit_solution(5640282577884827217)
XLA Ops:
  0.6 0.0 copy-start
  0.6 1.2 %copy-done = f32[4,512,128]{2,1,0:T(8,128)S(1)} copy-done((f32[4,512,128]{2,1,0:T(8,128)S(1)}, f32[4,512,128]{2,1,0:T(8,128)}, u32[]{:S(2)}) %copy-start) | copy-done | bytes 1048600
  1.9 0.4 cut.1
  2.2 0.5 collective-permute-start
  2.8 2.6 %collective-permute-start.1 = (f32[256,128]{1,0:T(8,128)S(1)}, f32[256,128]{1,0:T(8,128)S(1)}, u32[]{:S(2)}, u32[]{:S(2)}) collective-permute-start(f32[256,128]{1,0:T(8,128)S(1)} %get-tuple-element.38), channel_id=1, source_target_pairs={{0,2},{1,3},{2,0},{3,1},{4,6},{5,7},{6,4},{7,5},{8,10},{9,11},{10,... | collective-permute-start | bytes 393224 | tf_op jit(solution)/shard_map/ppermute | solution.py:245
  5.3 0.1 collective-permute-start.2
  5.4 2.6 %dynamic-slice_bitcast_fusion = (f32[1024,128]{1,0:T(8,128)}, f32[1024,128]{1,0:T(8,128)}, f32[1024,128]{1,0:T(8,128)}) fusion(f32[4,1024,128]{2,1,0:T(8,128)} %param.7, s32[]{:T(128)S(6)} %select_n.58, s32[]{:T(128)S(6)} %select_n.57, s32[]{:T(128)S(6)} %select_n.56), kind=kLoop, calls=%fused_computation.10 | loop fusion | bytes 3145740 | tf_op jit(solution)/shard_map/jit(dynamic_index_in_dim)/squeeze | solution.py:263
  8.0 1.7 %collective-permute-done.1.r2 = f32[256,128]{1,0:T(8,128)S(1)} collective-permute-done((f32[256,128]{1,0:T(8,128)S(1)}, f32[256,128]{1,0:T(8,128)S(1)}, u32[]{:S(2)}, u32[]{:S(2)}) %collective-permute-start.1) | collective-permute-done | bytes 131104 | tf_op jit(solution)/shard_map/ppermute | solution.py:245
  9.7 2.3 %collective-permute-done.2.r3 = f32[256,128]{1,0:T(8,128)S(1)} collective-permute-done((f32[256,128]{1,0:T(8,128)S(1)}, f32[256,128]{1,0:T(8,128)S(1)}, u32[]{:S(2)}, u32[]{:S(2)}) %collective-permute-start.2) | collective-permute-done | bytes 131104 | tf_op jit(solution)/shard_map/ppermute | solution.py:245
  12.0 0.0 collective-permute-done.r1
  12.0 0.1 collective-permute-start.4
  12.1 1.7 %collective-permute-start.5 = (f32[1024,128]{1,0:T(8,128)}, f32[1024,128]{1,0:T(8,128)}, u32[]{:S(2)}, u32[]{:S(2)}) collective-permute-start(f32[1024,128]{1,0:T(8,128)} %get-tuple-element.46), channel_id=1, source_target_pairs={{0,2},{1,3},{2,0},{3,1},{4,6},{5,7},{6,4},{7,5},{8,10},{9,11},{10,... | collective-permute-start | bytes 1572872 | tf_op jit(solution)/shard_map/ppermute | solution.py:245
  13.8 0.0 collective-permute-start.6
  13.8 0.0 copy-done.1
  13.8 19.4 %factor.1 = (f32[512,128]{1,0:T(8,128)S(1)}, f32[512,128]{1,0:T(8,128)S(1)}, f32[256,128]{1,0:T(8,128)S(1)}, f32[256,128]{1,0:T(8,128)S(1)}, f32[512,128]{1,0:T(8,128)S(1)}, /*index=5*/f32[4,512,128]{2,1,0:T(8,128)S(1)}) custom-call(s32[1]{0:T(128)} %bitcast.info, f32[4,512,128]{2,1,0:T(8,128)S(1)} %copy-done.1, f32[512,128]{1,0:T(8,128)S(1)} %collective-permute-done.r1, ...), custom_call_target="tpu_custom_call" | custom-call | flops 200000000 | bytes 4000000 | tf_op jit(solution)/shard_map/factor/pallas_call | solution.py:293
  33.2 0.0 copy-start.2
  33.2 0.6 copy-done.2
  33.9 1.8 %collective-permute-start.7 = (f32[512,128]{1,0:T(8,128)S(1)}, f32[512,128]{1,0:T(8,128)S(1)}, u32[]{:S(2)}, u32[]{:S(2)}) collective-permute-start(f32[512,128]{1,0:T(8,128)S(1)} %get-tuple-element.51), channel_id=1, source_target_pairs={{0,3},{1,2},{2,1},{3,0},{4,7},{5,6},{6,5},{7,4},{8,11},{9,10},{10,... | collective-permute-start | bytes 786440 | tf_op jit(solution)/shard_map/ppermute | solution.py:245
  35.7 0.0 copy-done.8
  35.7 0.1 multiply_add_fusion
  35.8 0.0 copy-start.4
  35.8 0.1 multiply_add_fusion.1
  35.9 0.0 collective-permute-done.4
  35.9 0.0 collective-permute-done.5
  35.9 1.7 %collective-permute-done.6 = f32[1024,128]{1,0:T(8,128)} collective-permute-done((f32[1024,128]{1,0:T(8,128)}, f32[1024,128]{1,0:T(8,128)}, u32[]{:S(2)}, u32[]{:S(2)}) %collective-permute-start.6) | collective-permute-done | bytes 524320 | tf_op jit(solution)/shard_map/ppermute | solution.py:245
  37.6 0.1 broadcast_in_dim.39
  37.8 0.0 copy-start.3
  37.8 6.3 %panel.1 = (f32[4,1024,128]{2,1,0:T(8,128)S(1)}, f32[2,32,64,128]{3,2,1,0:T(8,128)S(1)}, f32[2,32,64,128]{3,2,1,0:T(8,128)S(1)}, f32[1024,128]{1,0:T(8,128)S(1)}...) fusion(f32[4,1024,128]{2,1,0:T(8,128)S(1)} %broadcast_in_dim.39, s32[]{:T(128)S(6)} %select_n.59, s32[1]{0:T(128)} %bitcast.info, ...), kind=kCustom, calls=%fused_computation.9 | custom fusion | flops 1000000000 | bytes 11273736 | tf_op jit(solution)/shard_map/panel/pallas_call | solution.py:308
  44.1 0.0 collective-permute-done.7
  44.1 1.3 %collective-permute-start.8 = (f32[2,32,64,128]{3,2,1,0:T(8,128)S(1)}, f32[2,32,64,128]{3,2,1,0:T(8,128)S(1)}, u32[]{:S(2)}, u32[]{:S(2)}) collective-permute-start(f32[2,32,64,128]{3,2,1,0:T(8,128)S(1)} %get-tuple-element.54), channel_id=1, source_target_pairs={{0,1},{1,0},{2,3},{3,2},{4,5},{5,4},{6,7},{7,6},{8,9},{9,8},{10,11... | collective-permute-start | bytes 6291464 | tf_op jit(solution)/shard_map/ppermute | solution.py:245
  45.4 1.3 %collective-permute-start.9 = (f32[256,128]{1,0:T(8,128)S(1)}, f32[256,128]{1,0:T(8,128)S(1)}, u32[]{:S(2)}, u32[]{:S(2)}) collective-permute-start(f32[256,128]{1,0:T(8,128)S(1)} %copy-done.3), channel_id=1, source_target_pairs={{0,2},{1,3},{2,0},{3,1},{4,6},{5,7},{6,4},{7,5},{8,10},{9,11},{10,... | collective-permute-start | bytes 393224 | tf_op jit(solution)/shard_map/ppermute | solution.py:245
  46.7 2.5 %collective-permute-done.8 = f32[2,32,64,128]{3,2,1,0:T(8,128)S(1)} collective-permute-done((f32[2,32,64,128]{3,2,1,0:T(8,128)S(1)}, f32[2,32,64,128]{3,2,1,0:T(8,128)S(1)}, u32[]{:S(2)}, u32[]{:S(2)}) %collective-permute-start.8) | collective-permute-done | bytes 2097184 | tf_op jit(solution)/shard_map/ppermute | solution.py:245
  49.2 0.6 slice_add_fusion
  49.7 1.1 %collective-permute-done.9 = f32[256,128]{1,0:T(8,128)S(1)} collective-permute-done((f32[256,128]{1,0:T(8,128)S(1)}, f32[256,128]{1,0:T(8,128)S(1)}, u32[]{:S(2)}, u32[]{:S(2)}) %collective-permute-start.9) | collective-permute-done | bytes 131104 | tf_op jit(solution)/shard_map/ppermute | solution.py:245
  50.9 1.4 %collective-permute-start.11 = (f32[16,64,128]{2,1,0:T(8,128)S(1)}, f32[16,64,128]{2,1,0:T(8,128)S(1)}, u32[]{:S(2)}, u32[]{:S(2)}) collective-permute-start(f32[16,64,128]{2,1,0:T(8,128)S(1)} %get-tuple-element.58), channel_id=1, source_target_pairs={{0,8},{4,12},{8,0},{12,4},{16,24},{20,28},{24,16},{28,20},{1,9},{5... | collective-permute-start | bytes 1572872 | tf_op jit(solution)/shard_map/ppermute | solution.py:245
  52.3 1.4 %collective-permute-start.10 = (f32[16,64,128]{2,1,0:T(8,128)S(1)}, f32[16,64,128]{2,1,0:T(8,128)S(1)}, u32[]{:S(2)}, u32[]{:S(2)}) collective-permute-start(f32[16,64,128]{2,1,0:T(8,128)S(1)} %get-tuple-element.57), channel_id=1, source_target_pairs={{0,4},{4,0},{8,12},{12,8},{16,20},{20,16},{24,28},{28,24},{1,5},{5... | collective-permute-start | bytes 1572872 | tf_op jit(solution)/shard_map/ppermute | solution.py:245
  53.6 0.0 collective-permute-start.3
  53.6 1.1 %collective-permute-start.12 = (f32[1024,128]{1,0:T(8,128)S(1)}, f32[1024,128]{1,0:T(8,128)S(1)}, u32[]{:S(2)}, u32[]{:S(2)}) collective-permute-start(f32[1024,128]{1,0:T(8,128)S(1)} %get-tuple-element.99), channel_id=1, source_target_pairs={{0,3},{1,2},{2,1},{3,0},{4,7},{5,6},{6,5},{7,4},{8,11},{9,10},{10,... | collective-permute-start | bytes 1572872 | tf_op jit(solution)/shard_map/ppermute | solution.py:245
  54.8 0.1 broadcast_in_dim.33
  54.9 9.1 %collective-permute-done.11 = f32[16,64,128]{2,1,0:T(8,128)S(1)} collective-permute-done((f32[16,64,128]{2,1,0:T(8,128)S(1)}, f32[16,64,128]{2,1,0:T(8,128)S(1)}, u32[]{:S(2)}, u32[]{:S(2)}) %collective-permute-start.11) | collective-permute-done | bytes 524320 | tf_op jit(solution)/shard_map/ppermute | solution.py:245
  64.0 0.1 slice_add_fusion.4
  64.1 1.0 %collective-permute-done.10 = f32[16,64,128]{2,1,0:T(8,128)S(1)} collective-permute-done((f32[16,64,128]{2,1,0:T(8,128)S(1)}, f32[16,64,128]{2,1,0:T(8,128)S(1)}, u32[]{:S(2)}, u32[]{:S(2)}) %collective-permute-start.10) | collective-permute-done | bytes 524320 | tf_op jit(solution)/shard_map/ppermute | solution.py:245
  65.1 0.1 slice_add_fusion.7
  65.2 2.0 %collective-permute-done.12 = f32[1024,128]{1,0:T(8,128)S(1)} collective-permute-done((f32[1024,128]{1,0:T(8,128)S(1)}, f32[1024,128]{1,0:T(8,128)S(1)}, u32[]{:S(2)}, u32[]{:S(2)}) %collective-permute-start.12) | collective-permute-done | bytes 524320 | tf_op jit(solution)/shard_map/ppermute | solution.py:245
  67.2 0.6 collective-permute-start.13
  67.8 0.0 collective-permute-done.3
  67.8 1.6 %collective-permute-start.18 = (f32[1280,128]{1,0:T(8,128)S(1)}, f32[1280,128]{1,0:T(8,128)S(1)}, u32[]{:S(2)}, u32[]{:S(2)}) collective-permute-start(f32[1280,128]{1,0:T(8,128)S(1)} %get-tuple-element.101), channel_id=1, source_target_pairs={{0,2},{1,3},{2,0},{3,1},{4,6},{5,7},{6,4},{7,5},{8,10},{9,11},{10,... | collective-permute-start | bytes 1966088 | tf_op jit(solution)/shard_map/ppermute | solution.py:245
  69.4 0.0 collective-permute-start.19
  69.4 0.5 collective-permute-start.14
  69.9 6.0 %collective-permute-done.13 = f32[8,64,128]{2,1,0:T(8,128)S(1)} collective-permute-done((f32[8,64,128]{2,1,0:T(8,128)S(1)}, f32[8,64,128]{2,1,0:T(8,128)S(1)}, u32[]{:S(2)}, u32[]{:S(2)}) %collective-permute-start.13) | collective-permute-done | bytes 262176 | tf_op jit(solution)/shard_map/ppermute | solution.py:245
  75.9 2.2 %collective-permute-done.14 = f32[8,64,128]{2,1,0:T(8,128)S(1)} collective-permute-done((f32[8,64,128]{2,1,0:T(8,128)S(1)}, f32[8,64,128]{2,1,0:T(8,128)S(1)}, u32[]{:S(2)}, u32[]{:S(2)}) %collective-permute-start.14) | collective-permute-done | bytes 262176 | tf_op jit(solution)/shard_map/ppermute | solution.py:245
  78.2 0.6 collective-permute-start.17
  78.8 2.5 %collective-permute-start.16 = (f32[2,128,128]{2,1,0:T(8,128)S(1)}, f32[2,128,128]{2,1,0:T(8,128)S(1)}, u32[]{:S(2)}, u32[]{:S(2)}) collective-permute-start(f32[2,128,128]{2,1,0:T(8,128)S(1)} %pad_maximum_fusion.1), channel_id=1, source_target_pairs={{0,16},{4,20},{8,24},{12,28},{16,0},{20,4},{24,8},{28,12},{1,17},{... | collective-permute-start | bytes 393224 | tf_op jit(solution)/shard_map/ppermute | solution.py:245
  81.3 1.5 %collective-permute-start.15 = (f32[2,128,128]{2,1,0:T(8,128)S(1)}, f32[2,128,128]{2,1,0:T(8,128)S(1)}, u32[]{:S(2)}, u32[]{:S(2)}) collective-permute-start(f32[2,128,128]{2,1,0:T(8,128)S(1)} %pad_maximum_fusion), channel_id=1, source_target_pairs={{0,18},{1,19},{2,16},{3,17},{4,22},{5,23},{6,20},{7,21},{8,26},{9,... | collective-permute-start | bytes 393224 | tf_op jit(solution)/shard_map/ppermute | solution.py:359
  82.8 0.0 collective-permute-done.19
  82.8 2.7 %collective-permute-done.18 = f32[1280,128]{1,0:T(8,128)S(1)} collective-permute-done((f32[1280,128]{1,0:T(8,128)S(1)}, f32[1280,128]{1,0:T(8,128)S(1)}, u32[]{:S(2)}, u32[]{:S(2)}) %collective-permute-start.18) | collective-permute-done | bytes 655392 | tf_op jit(solution)/shard_map/ppermute | solution.py:245
  85.5 1.9 %collective-permute-done.17 = f32[2,128,128]{2,1,0:T(8,128)S(1)} collective-permute-done((f32[2,128,128]{2,1,0:T(8,128)S(1)}, f32[2,128,128]{2,1,0:T(8,128)S(1)}, u32[]{:S(2)}, u32[]{:S(2)}) %collective-permute-start.17) | collective-permute-done | bytes 131104 | tf_op jit(solution)/shard_map/ppermute | solution.py:245
  87.4 3.9 %collective-permute-done.16 = f32[2,128,128]{2,1,0:T(8,128)S(1)} collective-permute-done((f32[2,128,128]{2,1,0:T(8,128)S(1)}, f32[2,128,128]{2,1,0:T(8,128)S(1)}, u32[]{:S(2)}, u32[]{:S(2)}) %collective-permute-start.16) | collective-permute-done | bytes 131104 | tf_op jit(solution)/shard_map/ppermute | solution.py:245
  91.2 2.7 %collective-permute-done.15 = f32[2,128,128]{2,1,0:T(8,128)S(1)} collective-permute-done((f32[2,128,128]{2,1,0:T(8,128)S(1)}, f32[2,128,128]{2,1,0:T(8,128)S(1)}, u32[]{:S(2)}, u32[]{:S(2)}) %collective-permute-start.15) | collective-permute-done | bytes 131104 | tf_op jit(solution)/shard_map/ppermute | solution.py:359
  94.1 0.0 copy-start.5
  94.1 0.0 copy-start.6
  94.1 0.8 fusion.2
  95.0 0.5 copy-done.5
  95.5 0.3 copy-done.6
  (23 shorter events, 0.3 us)
Async XLA Ops:
  0.6 1.2 %copy-start = (f32[4,512,128]{2,1,0:T(8,128)S(1)}, f32[4,512,128]{2,1,0:T(8,128)}, u32[]{:S(2)}) copy-start(f32[4,512,128]{2,1,0:T(8,128)} %own_ref.2) | copy-start | bytes 3145732
  1.9 12.0 %copy-start.1 = (f32[4,512,128]{2,1,0:T(8,128)S(1)}, f32[4,512,128]{2,1,0:T(8,128)}, u32[]{:S(2)}) copy-start(f32[4,512,128]{2,1,0:T(8,128)} %own_ref.2) | copy-start | bytes 3145732
  2.2 9.7 %collective-permute-start = (f32[512,128]{1,0:T(8,128)S(1)}, f32[512,128]{1,0:T(8,128)S(1)}, u32[]{:S(2)}, u32[]{:S(2)}) collective-permute-start(f32[512,128]{1,0:T(8,128)S(1)} %get-tuple-element.37), channel_id=1, source_target_pairs={{0,1},{1,0},{2,3},{3,2},{4,5},{5,4},{6,7},{7,6},{8,9},{9,8},{10,11... | collective-permute-start | bytes 786440 | tf_op jit(solution)/shard_map/ppermute | solution.py:245
  2.8 6.9 %collective-permute-start.1 = (f32[256,128]{1,0:T(8,128)S(1)}, f32[256,128]{1,0:T(8,128)S(1)}, u32[]{:S(2)}, u32[]{:S(2)}) collective-permute-start(f32[256,128]{1,0:T(8,128)S(1)} %get-tuple-element.38), channel_id=1, source_target_pairs={{0,2},{1,3},{2,0},{3,1},{4,6},{5,7},{6,4},{7,5},{8,10},{9,11},{10,... | collective-permute-start | bytes 393224 | tf_op jit(solution)/shard_map/ppermute | solution.py:245
  5.3 6.6 %collective-permute-start.2 = (f32[256,128]{1,0:T(8,128)S(1)}, f32[256,128]{1,0:T(8,128)S(1)}, u32[]{:S(2)}, u32[]{:S(2)}) collective-permute-start(f32[256,128]{1,0:T(8,128)S(1)} %get-tuple-element.39), channel_id=1, source_target_pairs={{0,3},{1,2},{2,1},{3,0},{4,7},{5,6},{6,5},{7,4},{8,11},{9,10},{10,... | collective-permute-start | bytes 393224 | tf_op jit(solution)/shard_map/ppermute | solution.py:245
  5.4 30.3 %copy-start.8 = (s32[144,1]{0,1:T(1,128)S(1)}, s32[144,1]{0,1:T(1,128)}, u32[]{:S(2)}) copy-start(s32[144,1]{0,1:T(1,128)} %param.9) | copy-start | bytes 1732
  5.4 30.3 %copy-start.9 = (s32[144]{0:T(256)S(1)}, s32[144]{0:T(256)}, u32[]{:S(2)}) copy-start(s32[144]{0:T(256)} %param.10) | copy-start | bytes 1732
  8.0 29.8 %copy-start.10 = (s32[4]{0:T(128)S(1)}, s32[4]{0:T(128)}, u32[]{:S(2)}) copy-start(s32[4]{0:T(128)} %param.8) | copy-start | bytes 52
  12.0 24.0 %collective-permute-start.4 = (f32[1024,128]{1,0:T(8,128)}, f32[1024,128]{1,0:T(8,128)}, u32[]{:S(2)}, u32[]{:S(2)}) collective-permute-start(f32[1024,128]{1,0:T(8,128)} %get-tuple-element.45), channel_id=1, source_target_pairs={{0,1},{1,0},{2,3},{3,2},{4,5},{5,4},{6,7},{7,6},{8,9},{9,8},{10,11... | collective-permute-start | bytes 1572872 | tf_op jit(solution)/shard_map/ppermute | solution.py:245
  12.1 23.9 %collective-permute-start.5 = (f32[1024,128]{1,0:T(8,128)}, f32[1024,128]{1,0:T(8,128)}, u32[]{:S(2)}, u32[]{:S(2)}) collective-permute-start(f32[1024,128]{1,0:T(8,128)} %get-tuple-element.46), channel_id=1, source_target_pairs={{0,2},{1,3},{2,0},{3,1},{4,6},{5,7},{6,4},{7,5},{8,10},{9,11},{10,... | collective-permute-start | bytes 1572872 | tf_op jit(solution)/shard_map/ppermute | solution.py:245
  13.8 23.8 %collective-permute-start.6 = (f32[1024,128]{1,0:T(8,128)}, f32[1024,128]{1,0:T(8,128)}, u32[]{:S(2)}, u32[]{:S(2)}) collective-permute-start(f32[1024,128]{1,0:T(8,128)} %get-tuple-element.47), channel_id=1, source_target_pairs={{0,3},{1,2},{2,1},{3,0},{4,7},{5,6},{6,5},{7,4},{8,11},{9,10},{10,... | collective-permute-start | bytes 1572872 | tf_op jit(solution)/shard_map/ppermute | solution.py:245
  33.2 0.7 copy-start.2
  33.9 10.3 %collective-permute-start.7 = (f32[512,128]{1,0:T(8,128)S(1)}, f32[512,128]{1,0:T(8,128)S(1)}, u32[]{:S(2)}, u32[]{:S(2)}) collective-permute-start(f32[512,128]{1,0:T(8,128)S(1)} %get-tuple-element.51), channel_id=1, source_target_pairs={{0,3},{1,2},{2,1},{3,0},{4,7},{5,6},{6,5},{7,4},{8,11},{9,10},{10,... | collective-permute-start | bytes 786440 | tf_op jit(solution)/shard_map/ppermute | solution.py:245
  35.8 2.0 %copy-start.4 = (f32[4,1024,128]{2,1,0:T(8,128)S(1)}, f32[4,1024,128]{2,1,0:T(8,128)}, u32[]{:S(2)}) copy-start(f32[4,1024,128]{2,1,0:T(8,128)} %param.7) | copy-start | bytes 6291460
  37.8 7.6 %copy-start.3 = (f32[256,128]{1,0:T(8,128)S(1)}, f32[256,128]{1,0:T(8,128)}, u32[]{:S(2)}) copy-start(f32[256,128]{1,0:T(8,128)} %copy-done.2) | copy-start | bytes 393220
  44.1 5.1 %collective-permute-start.8 = (f32[2,32,64,128]{3,2,1,0:T(8,128)S(1)}, f32[2,32,64,128]{3,2,1,0:T(8,128)S(1)}, u32[]{:S(2)}, u32[]{:S(2)}) collective-permute-start(f32[2,32,64,128]{3,2,1,0:T(8,128)S(1)} %get-tuple-element.54), channel_id=1, source_target_pairs={{0,1},{1,0},{2,3},{3,2},{4,5},{5,4},{6,7},{7,6},{8,9},{9,8},{10,11... | collective-permute-start | bytes 6291464 | tf_op jit(solution)/shard_map/ppermute | solution.py:245
  45.4 5.5 %collective-permute-start.9 = (f32[256,128]{1,0:T(8,128)S(1)}, f32[256,128]{1,0:T(8,128)S(1)}, u32[]{:S(2)}, u32[]{:S(2)}) collective-permute-start(f32[256,128]{1,0:T(8,128)S(1)} %copy-done.3), channel_id=1, source_target_pairs={{0,2},{1,3},{2,0},{3,1},{4,6},{5,7},{6,4},{7,5},{8,10},{9,11},{10,... | collective-permute-start | bytes 393224 | tf_op jit(solution)/shard_map/ppermute | solution.py:245
  50.9 13.1 %collective-permute-start.11 = (f32[16,64,128]{2,1,0:T(8,128)S(1)}, f32[16,64,128]{2,1,0:T(8,128)S(1)}, u32[]{:S(2)}, u32[]{:S(2)}) collective-permute-start(f32[16,64,128]{2,1,0:T(8,128)S(1)} %get-tuple-element.58), channel_id=1, source_target_pairs={{0,8},{4,12},{8,0},{12,4},{16,24},{20,28},{24,16},{28,20},{1,9},{5... | collective-permute-start | bytes 1572872 | tf_op jit(solution)/shard_map/ppermute | solution.py:245
  52.3 12.9 %collective-permute-start.10 = (f32[16,64,128]{2,1,0:T(8,128)S(1)}, f32[16,64,128]{2,1,0:T(8,128)S(1)}, u32[]{:S(2)}, u32[]{:S(2)}) collective-permute-start(f32[16,64,128]{2,1,0:T(8,128)S(1)} %get-tuple-element.57), channel_id=1, source_target_pairs={{0,4},{4,0},{8,12},{12,8},{16,20},{20,16},{24,28},{28,24},{1,5},{5... | collective-permute-start | bytes 1572872 | tf_op jit(solution)/shard_map/ppermute | solution.py:245
  53.6 14.2 %collective-permute-start.3 = (f32[512,128]{1,0:T(8,128)S(1)}, f32[512,128]{1,0:T(8,128)S(1)}, u32[]{:S(2)}, u32[]{:S(2)}) collective-permute-start(f32[512,128]{1,0:T(8,128)S(1)} %get-tuple-element.44), channel_id=1, source_target_pairs={{0,1},{1,0},{2,3},{3,2},{4,5},{5,4},{6,7},{7,6},{8,9},{9,8},{10,11... | collective-permute-start | bytes 786440 | tf_op jit(solution)/shard_map/ppermute | solution.py:245
  53.6 13.6 %collective-permute-start.12 = (f32[1024,128]{1,0:T(8,128)S(1)}, f32[1024,128]{1,0:T(8,128)S(1)}, u32[]{:S(2)}, u32[]{:S(2)}) collective-permute-start(f32[1024,128]{1,0:T(8,128)S(1)} %get-tuple-element.99), channel_id=1, source_target_pairs={{0,3},{1,2},{2,1},{3,0},{4,7},{5,6},{6,5},{7,4},{8,11},{9,10},{10,... | collective-permute-start | bytes 1572872 | tf_op jit(solution)/shard_map/ppermute | solution.py:245
  67.2 8.7 %collective-permute-start.13 = (f32[8,64,128]{2,1,0:T(8,128)S(1)}, f32[8,64,128]{2,1,0:T(8,128)S(1)}, u32[]{:S(2)}, u32[]{:S(2)}) collective-permute-start(f32[8,64,128]{2,1,0:T(8,128)S(1)} %get-tuple-element.60), channel_id=1, source_target_pairs={{0,8},{4,12},{8,0},{12,4},{16,24},{20,28},{24,16},{28,20},{1,9},{5... | collective-permute-start | bytes 786440 | tf_op jit(solution)/shard_map/ppermute | solution.py:245
  67.8 17.7 %collective-permute-start.18 = (f32[1280,128]{1,0:T(8,128)S(1)}, f32[1280,128]{1,0:T(8,128)S(1)}, u32[]{:S(2)}, u32[]{:S(2)}) collective-permute-start(f32[1280,128]{1,0:T(8,128)S(1)} %get-tuple-element.101), channel_id=1, source_target_pairs={{0,2},{1,3},{2,0},{3,1},{4,6},{5,7},{6,4},{7,5},{8,10},{9,11},{10,... | collective-permute-start | bytes 1966088 | tf_op jit(solution)/shard_map/ppermute | solution.py:245
  69.4 13.4 %collective-permute-start.19 = (f32[1024,128]{1,0:T(8,128)S(1)}, f32[1024,128]{1,0:T(8,128)S(1)}, u32[]{:S(2)}, u32[]{:S(2)}) collective-permute-start(f32[1024,128]{1,0:T(8,128)S(1)} %get-tuple-element.103), channel_id=1, source_target_pairs={{0,1},{1,0},{2,3},{3,2},{4,5},{5,4},{6,7},{7,6},{8,9},{9,8},{10,11... | collective-permute-start | bytes 1572872 | tf_op jit(solution)/shard_map/ppermute | solution.py:245
  69.4 8.7 %collective-permute-start.14 = (f32[8,64,128]{2,1,0:T(8,128)S(1)}, f32[8,64,128]{2,1,0:T(8,128)S(1)}, u32[]{:S(2)}, u32[]{:S(2)}) collective-permute-start(f32[8,64,128]{2,1,0:T(8,128)S(1)} %get-tuple-element.61), channel_id=1, source_target_pairs={{0,4},{4,0},{8,12},{12,8},{16,20},{20,16},{24,28},{28,24},{1,5},{5... | collective-permute-start | bytes 786440 | tf_op jit(solution)/shard_map/ppermute | solution.py:245
  78.2 9.2 %collective-permute-start.17 = (f32[2,128,128]{2,1,0:T(8,128)S(1)}, f32[2,128,128]{2,1,0:T(8,128)S(1)}, u32[]{:S(2)}, u32[]{:S(2)}) collective-permute-start(f32[2,128,128]{2,1,0:T(8,128)S(1)} %pad_maximum_fusion.2), channel_id=1, source_target_pairs={{0,2},{1,3},{2,0},{3,1},{4,6},{5,7},{6,4},{7,5},{8,10},{9,11},{10,... | collective-permute-start | bytes 393224 | tf_op jit(solution)/shard_map/ppermute | solution.py:245
  78.8 15.4 %copy-start.7 = (f32[2,128,128]{2,1,0:T(8,128)S(1)}, f32[2,128,128]{2,1,0:T(8,128)}, u32[]{:S(2)}) copy-start(f32[2,128,128]{2,1,0:T(8,128)} %param.11) | copy-start | bytes 393220
  78.8 12.5 %collective-permute-start.16 = (f32[2,128,128]{2,1,0:T(8,128)S(1)}, f32[2,128,128]{2,1,0:T(8,128)S(1)}, u32[]{:S(2)}, u32[]{:S(2)}) collective-permute-start(f32[2,128,128]{2,1,0:T(8,128)S(1)} %pad_maximum_fusion.1), channel_id=1, source_target_pairs={{0,16},{4,20},{8,24},{12,28},{16,0},{20,4},{24,8},{28,12},{1,17},{... | collective-permute-start | bytes 393224 | tf_op jit(solution)/shard_map/ppermute | solution.py:245
  81.3 12.6 %collective-permute-start.15 = (f32[2,128,128]{2,1,0:T(8,128)S(1)}, f32[2,128,128]{2,1,0:T(8,128)S(1)}, u32[]{:S(2)}, u32[]{:S(2)}) collective-permute-start(f32[2,128,128]{2,1,0:T(8,128)S(1)} %pad_maximum_fusion), channel_id=1, source_target_pairs={{0,18},{1,19},{2,16},{3,17},{4,22},{5,23},{6,20},{7,21},{8,26},{9,... | collective-permute-start | bytes 393224 | tf_op jit(solution)/shard_map/ppermute | solution.py:359
  94.1 1.4 %copy-start.5 = (f32[4,1024,128]{2,1,0:T(8,128)}, f32[4,1024,128]{2,1,0:T(8,128)S(1)}, u32[]{:S(2)}) copy-start(f32[4,1024,128]{2,1,0:T(8,128)S(1)} %bitcast_dynamic-update-slice_fusion) | copy-start | bytes 6291460
  94.1 1.7 %copy-start.6 = (f32[4,512,128]{2,1,0:T(8,128)}, f32[4,512,128]{2,1,0:T(8,128)S(1)}, u32[]{:S(2)}) copy-start(f32[4,512,128]{2,1,0:T(8,128)S(1)} %bitcast_dynamic-update-slice_fusion.7) | copy-start | bytes 3145732

commit v12 on v8

--- a/solution.py
+++ b/solution.py
@@ -172,32 +172,48 @@
         c.wait()
 
 
-def panel_kernel(
-    info, counts, tgt_a, tgt_b, own_ref, r1, r2, r3, mt, l3, x0, x1, x2, x3, keep, send, xh, xl
-):
+def masked_split(ref, count):
+    rows = ref.shape[0]
+    live = lax.broadcasted_iota(jnp.int32, (rows, B), 0) < count * B
+    return split_bf16(jnp.where(live, ref[...], 0.0))
+
+
+def inverse_rows(mt, me, blocks, c):
+    rows = [
+        jnp.concatenate([mt[me ^ m, pl.ds((me ^ k) * B, B), :] for m in (c, c + 1)], axis=1) for k in blocks
+    ]
+    return split_bf16(jnp.concatenate(rows, axis=0))
+
+
+def early_kernel(info, counts, own_ref, r1, r2, mt, acc, *sums):
+    me = info[0]
+    parts = [masked_split(ref, counts[me]) for ref in (own_ref.at[me], r1, r2)]
+    left = [jnp.concatenate([part[n] for part in parts], axis=1) for n in range(2)]
+    for c in range(0, NB, 2):
+        acc[:, pl.ds(c * B, 2 * B)] = dot3(left, inverse_rows(mt, me, range(NB - 1), c), ((1,), (0,)))
+    for ref in sums:
+        ref[...] = jnp.zeros_like(ref)
+
+
+def panel_kernel(info, counts, tgt_a, tgt_b, r3, mt, l3, acc, *rest):
+    x0, x1, x2, x3, keep, send, xh, xl = rest[-8:]
+    if len(rest) == 8:
+        keep[...] = jnp.zeros_like(keep)
+        send[...] = jnp.zeros_like(send)
     me = info[0]
     count = counts[me]
     rows = P_SIZE * B
-    ins = [own_ref.at[me], r1, r2, r3]
     outs = [x0, x1, x2, x3]
     x3[pl.ds(rows, W), :] = l3[...]
-    live = lax.broadcasted_iota(jnp.int32, (rows, B), 0) < count * B
-    parts = [split_bf16(jnp.where(live, ref[...], 0.0)) for ref in ins]
-    left = [jnp.concatenate([part[n] for part in parts], axis=1) for n in range(2)]
+    left = masked_split(r3, count)
     for c in range(0, NB, 2):
-        right = [
-            jnp.concatenate([mt[me ^ m, pl.ds((me ^ k) * B, B), :] for m in (c, c + 1)], axis=1)
-            for k in range(NB)
-        ]
-        got = dot3(left, split_bf16(jnp.concatenate(right, axis=0)), ((1,), (0,)))
+        got = acc[:, pl.ds(c * B, 2 * B)] + dot3(left, inverse_rows(mt, me, [NB - 1], c), ((1,), (0,)))
         outs[c][pl.ds(0, rows), :] = got[:, :B]
         outs[c + 1][pl.ds(0, rows), :] = got[:, B:]
         high, low = split_bf16(got)
         xh[:, pl.ds(c * B, 2 * B)] = high
         xl[:, pl.ds(c * B, 2 * B)] = low
 
-    keep[...] = jnp.zeros_like(keep)
-    send[...] = jnp.zeros_like(send)
     half, strip = keep.shape[1:3]
     for j in range(0, P_SIZE, 2):
 
@@ -295,16 +311,28 @@
     slab = jax.ShapeDtypeStruct((rows, B), jnp.float32)
     longer = jax.ShapeDtypeStruct((rows + W, B), jnp.float32)
     part = jax.ShapeDtypeStruct((2, blocks // 2, B // 2, B), jnp.float32)
+    room = pltpu.CompilerParams(vmem_limit_bytes=20 * 2**20 + 4 * blocks * B * B)
+    sums = 2 if blocks * B * B * 4 <= 8 * 2**20 else 0
+    acc, *empty = pl.pallas_call(
+        early_kernel,
+        out_shape=[jax.ShapeDtypeStruct((rows, W), jnp.float32)] + [part] * sums,
+        in_specs=[SMEM] * 2 + [VMEM] * 4,
+        out_specs=[VMEM] * (1 + sums),
+        compiler_params=room,
+        cost_estimate=pl.CostEstimate(flops=5 * 10**8, bytes_accessed=10 * 10**6, transcendentals=0),
+        name="early",
+    )(info, panel_count, panel, *panel_in[:2], mt)
     *x_parts, keep, send = pl.pallas_call(
         panel_kernel,
         out_shape=[slab] * (NB - 1) + [longer, part, part],
-        in_specs=[SMEM] * 4 + [VMEM] * (NB + 2),
+        in_specs=[SMEM] * 4 + [VMEM] * (4 + sums),
         out_specs=[VMEM] * (NB + 2),
         scratch_shapes=[pltpu.VMEM((rows, W), jnp.bfloat16)] * 2,
-        compiler_params=pltpu.CompilerParams(vmem_limit_bytes=20 * 2**20 + 4 * blocks * B * B),
+        input_output_aliases={8 + n: NB + n for n in range(sums)},
+        compiler_params=room,
         cost_estimate=pl.CostEstimate(flops=10**9, bytes_accessed=10 * 10**6, transcendentals=0),
         name="panel",
-    )(info, panel_count, tgt_a, tgt_b, panel, *panel_in, mt, l_parts[3])
+    )(info, panel_count, tgt_a, tgt_b, panel_in[2], mt, l_parts[3], acc, *empty)
 
     l_back = [swap(l_parts[m], "narrow", m) for m in (1, 2)]
     x_back = [swap(x_parts[m], "narrow", m) for m in masks]

time: 94.4 us -> 97.3 us (1.031)
  Pallas kernels: 20 us -> 28.7 us
  waiting for transfers between devices: 41.7 us -> 37.2 us
  other arithmetic: 6.98 us -> 4.71 us
  local copies, waits for them, and re-layouts: 5.06 us -> 6.89 us
  starting transfers between devices: 19.9 us -> 18.4 us
    pallas_call x0 -> x2, Pallas kernels: none -> 7.85 us  [the longest x1 4.62 us: local(): pl.pallas_call(panel_kernel, out_shape=[slab] * (NB - 1) + [longer, part,...]
    pallas_call x1 -> x0, other arithmetic: 5.38 us -> none  [local(): pl.pallas_call(panel_kernel, out_shape=[slab] * (NB - 1) + [longer, part,...]
    ppermute x18, waiting for transfers between devices: 41.7 us -> 37.2 us  [swap(): return lax.ppermute(x, axis, xor_pairs(lax.axis_size(axis), mask))]
    ppermute x18, starting transfers between devices: 19.6 us -> 17.6 us  [swap(): return lax.ppermute(x, axis, xor_pairs(lax.axis_size(axis), mask))]
    unnamed x18 -> x30, local copies, waits for them, and re-layouts: 2.09 us -> 3.75 us
    add x1, other arithmetic: 0.06 us -> 1.25 us  [local(): keep_b[:half] + got_b[:half]]
    add x1, other arithmetic: 0.06 us -> 1.09 us  [local(): keep_a[:half] + got_a[:half]]
  transfers between devices with their start and end apart: 19 -> 19, of which waited for: 12 -> 10; matrix products, arithmetic and copies ran while one was open for 9% -> 6% of each run, Pallas kernels for 21% -> 28%
where the time goes in v12:
time: 97.3 us; the launch traced here: 96.9 us
  waiting for transfers between devices  37.2 us (38%)
  Pallas kernels  28.7 us (29%)
  starting transfers between devices  18.4 us (19%)
  local copies, waits for them, and re-layouts  6.89 us (7%)
  other arithmetic  4.71 us (5%)
    ppermute x18, waiting for transfers between devices, swap(): return lax.ppermute(x, axis, xor_pairs(lax.axis_size(axis), mask))  37.2 us
    pallas_call x1, Pallas kernels, local(): pl.pallas_call(factor_kernel, out_shape=[slab] * NB + [jax.ShapeDtypeStru...  19.7 us
    ppermute x18, starting transfers between devices, swap(): return lax.ppermute(x, axis, xor_pairs(lax.axis_size(axis), mask))  17.6 us
    pallas_call x1, Pallas kernels, local(): pl.pallas_call(panel_kernel, out_shape=[slab] * (NB - 1) + [longer, part,...  4.62 us
    unnamed x30, local copies, waits for them, and re-layouts  3.75 us
    pallas_call x1, Pallas kernels, local(): pl.pallas_call(early_kernel, out_shape=[jax.ShapeDtypeStruct((rows, W), j...  3.23 us
    squeeze x1, local copies, waits for them, and re-layouts, local(): own = lambda x, m: lax.dynamic_index_in_dim(x, me ^ m, 0, keepdims=False)  2.68 us
  transfers between devices with their start and end apart: 19, of which 10 were waited for; matrix products, arithmetic and copies ran while one was open for 6% of the time, Pallas kernels for 28%

profile of v12, /device:TPU:0, one launch (start us, length us, event | category | flops | bytes accessed | tf_op | source)
XLA Modules:
  0.0 96.9 jit_solution(2220802191240016367)
XLA Ops:
  0.6 0.0 copy-start.1
  0.6 1.2 %copy-done.1 = f32[4,512,128]{2,1,0:T(8,128)S(1)} copy-done((f32[4,512,128]{2,1,0:T(8,128)S(1)}, f32[4,512,128]{2,1,0:T(8,128)}, u32[]{:S(2)}) %copy-start.1) | copy-done | bytes 1048600
  1.9 1.2 %cut.1 = (f32[512,128]{1,0:T(8,128)}, f32[256,128]{1,0:T(8,128)}, f32[256,128]{1,0:T(8,128)}) custom-call(s32[1]{0:T(128)} %bitcast.info, f32[4,512,128]{2,1,0:T(8,128)S(1)} %copy-done.1), custom_call_target="tpu_custom_call" | custom-call | bytes 1048576 | tf_op jit(solution)/shard_map/cut/pallas_call | solution.py:272
  3.0 0.5 collective-permute-start
  3.5 2.6 %collective-permute-start.1 = (f32[256,128]{1,0:T(8,128)}, f32[256,128]{1,0:T(8,128)S(1)}, u32[]{:S(2)}, u32[]{:S(2)}) collective-permute-start(f32[256,128]{1,0:T(8,128)} %get-tuple-element.39), channel_id=1, source_target_pairs={{0,2},{1,3},{2,0},{3,1},{4,6},{5,7},{6,4},{7,5},{8,10},{9,11},{10,... | collective-permute-start | bytes 393224 | tf_op jit(solution)/shard_map/ppermute | solution.py:251
  6.1 0.1 collective-permute-start.2
  6.2 2.7 %dynamic-slice_bitcast_fusion = (f32[1024,128]{1,0:T(8,128)}, f32[1024,128]{1,0:T(8,128)}, f32[1024,128]{1,0:T(8,128)}) fusion(f32[4,1024,128]{2,1,0:T(8,128)} %own_ref.3, s32[]{:T(128)S(6)} %select_n.59, s32[]{:T(128)S(6)} %select_n.58, s32[]{:T(128)S(6)} %select_n.57), kind=kLoop, calls=%fused_computation.10 | loop fusion | bytes 3145740 | tf_op jit(solution)/shard_map/jit(dynamic_index_in_dim)/squeeze | solution.py:269
  8.9 1.8 %collective-permute-done.1.r2 = f32[256,128]{1,0:T(8,128)S(1)} collective-permute-done((f32[256,128]{1,0:T(8,128)}, f32[256,128]{1,0:T(8,128)S(1)}, u32[]{:S(2)}, u32[]{:S(2)}) %collective-permute-start.1) | collective-permute-done | bytes 131104 | tf_op jit(solution)/shard_map/ppermute | solution.py:251
  10.7 2.4 %collective-permute-done.2.r3 = f32[256,128]{1,0:T(8,128)} collective-permute-done((f32[256,128]{1,0:T(8,128)}, f32[256,128]{1,0:T(8,128)}, u32[]{:S(2)}, u32[]{:S(2)}) %collective-permute-start.2) | collective-permute-done | bytes 131104 | tf_op jit(solution)/shard_map/ppermute | solution.py:251
  13.1 0.0 collective-permute-done.r1
  13.1 0.7 copy-done.3
  13.8 0.1 collective-permute-start.5
  13.9 1.7 %collective-permute-start.6 = (f32[1024,128]{1,0:T(8,128)}, f32[1024,128]{1,0:T(8,128)}, u32[]{:S(2)}, u32[]{:S(2)}) collective-permute-start(f32[1024,128]{1,0:T(8,128)} %get-tuple-element.50), channel_id=1, source_target_pairs={{0,2},{1,3},{2,0},{3,1},{4,6},{5,7},{6,4},{7,5},{8,10},{9,11},{10,... | collective-permute-start | bytes 1572872 | tf_op jit(solution)/shard_map/ppermute | solution.py:251
  15.6 0.0 collective-permute-start.4
  15.7 0.0 copy-done.13
  15.7 0.0 copy-done.14
  15.7 0.1 multiply_add_fusion
  15.8 0.9 copy-done.4
  16.7 19.7 %factor.1 = (f32[512,128]{1,0:T(8,128)S(1)}, f32[512,128]{1,0:T(8,128)S(1)}, f32[512,128]{1,0:T(8,128)S(1)}, f32[512,128]{1,0:T(8,128)S(1)}, f32[4,512,128]{2,1,0:T(8,128)S(1)}) custom-call(s32[1]{0:T(128)} %bitcast.info, f32[4,512,128]{2,1,0:T(8,128)S(1)} %copy-done.2, f32[512,128]{1,0:T(8,128)S(1)} %copy-done.4, f32[256,128]{1,0:T(8,128)S(1)} %collective-permute-done.1.r2, ...), custom_call_target="tpu_custom_call" | custom-call | flops 200000000 | bytes 4000000 | tf_op jit(solution)/shard_map/factor/pallas_call | solution.py:298
  36.4 0.0 copy-start.6
  36.4 1.7 %collective-permute-start.7 = (f32[512,128]{1,0:T(8,128)S(1)}, f32[512,128]{1,0:T(8,128)S(1)}, u32[]{:S(2)}, u32[]{:S(2)}) collective-permute-start(f32[512,128]{1,0:T(8,128)S(1)} %get-tuple-element.55), channel_id=1, source_target_pairs={{0,2},{1,3},{2,0},{3,1},{4,6},{5,7},{6,4},{7,5},{8,10},{9,11},{10,... | collective-permute-start | bytes 786440 | tf_op jit(solution)/shard_map/ppermute | solution.py:251
  38.2 0.1 multiply_add_fusion.1.tgt_a
  38.3 0.0 collective-permute-done.5.r1
  38.3 0.0 collective-permute-done.6.r2
  38.3 3.2 %early.1 = (f32[1024,512]{1,0:T(8,128)S(1)}, f32[2,32,64,128]{3,2,1,0:T(8,128)S(1)}, f32[2,32,64,128]{3,2,1,0:T(8,128)S(1)}) custom-call(s32[1]{0:T(128)} %bitcast.info, s32[4]{0:T(128)S(1)} %copy-done.5, f32[4,1024,128]{2,1,0:T(8,128)S(1)} %copy-done, f32[1024,128]{1,0:T(8,128)} %collective-permute-done.5.r1, f32[1024,128]{1,0:T(8,128)} %collective-permute-done.6.r2, ...), custom_call_target="tpu_custom_call" | custom-call | flops 500000000 | bytes 10000000 | tf_op jit(solution)/shard_map/early/pallas_call | solution.py:316
  41.6 0.0 collective-permute-done.4.r3
  41.6 4.6 %panel.1 = (f32[1024,128]{1,0:T(8,128)S(1)}, f32[1024,128]{1,0:T(8,128)S(1)}, f32[1024,128]{1,0:T(8,128)S(1)}, f32[1536,128]{1,0:T(8,128)S(1)}, f32[2,32,64,128]...) custom-call(s32[1]{0:T(128)} %bitcast.info, s32[4]{0:T(128)S(1)} %copy-done.5, ...), custom_call_target="tpu_custom_call", output_to_operand_aliasing={{4}: (8, {}), {5}: (9, {})} | custom-call | flops 1000000000 | bytes 10000000 | tf_op jit(solution)/shard_map/panel/pallas_call | solution.py:325
  46.2 0.0 collective-permute-done.7
  46.2 0.1 collective-permute-start.8
  46.3 4.1 %collective-permute-done.8 = f32[2,32,64,128]{3,2,1,0:T(8,128)S(1)} collective-permute-done((f32[2,32,64,128]{3,2,1,0:T(8,128)S(1)}, f32[2,32,64,128]{3,2,1,0:T(8,128)S(1)}, u32[]{:S(2)}, u32[]{:S(2)}) %collective-permute-start.8) | collective-permute-done | bytes 2097184 | tf_op jit(solution)/shard_map/ppermute | solution.py:251
  50.5 1.3 %slice_add_fusion = (f32[1,16,64,128]{3,2,1,0:T(8,128)}, f32[16,64,128]{2,1,0:T(8,128)}, f32[16,64,128]{2,1,0:T(8,128)}, f32[1,16,64,128]{3,2,1,0:T(8,128)S(1)}) fusion(f32[2,32,64,128]{3,2,1,0:T(8,128)S(1)} %collective-permute-done.8, f32[2,32,64,128]{3,2,1,0:T(8,128)S(1)} %get-tuple-element.57), kind=kLoop, calls=%fused_computation | loop fusion | flops 524288 | bytes 6291456 | tf_op jit(solution)/shard_map/add | solution.py:348
  51.7 1.0 collective-permute-start.10
  52.7 2.5 %collective-permute-start.9 = (f32[16,64,128]{2,1,0:T(8,128)}, f32[16,64,128]{2,1,0:T(8,128)}, u32[]{:S(2)}, u32[]{:S(2)}) collective-permute-start(f32[16,64,128]{2,1,0:T(8,128)} %get-tuple-element.59), channel_id=1, source_target_pairs={{0,4},{4,0},{8,12},{12,8},{16,20},{20,16},{24,28},{28,24},{1,5},{5... | collective-permute-start | bytes 1572872 | tf_op jit(solution)/shard_map/ppermute | solution.py:251
  55.2 0.0 collective-permute-start.3
  55.2 0.5 collective-permute-start.11
  55.7 0.1 broadcast_in_dim.32
  55.8 10.3 %collective-permute-done.10 = f32[16,64,128]{2,1,0:T(8,128)} collective-permute-done((f32[16,64,128]{2,1,0:T(8,128)}, f32[16,64,128]{2,1,0:T(8,128)}, u32[]{:S(2)}, u32[]{:S(2)}) %collective-permute-start.10) | collective-permute-done | bytes 524320 | tf_op jit(solution)/shard_map/ppermute | solution.py:251
  66.0 1.2 %slice_add_fusion.4 = (f32[8,64,128]{2,1,0:T(8,128)S(1)}, f32[8,64,128]{2,1,0:T(8,128)S(1)}) fusion(f32[16,64,128]{2,1,0:T(8,128)} %collective-permute-done.10, f32[1,16,64,128]{3,2,1,0:T(8,128)} %get-tuple-element.76), kind=kLoop, calls=%fused_computation.13 | loop fusion | flops 131072 | bytes 1572864 | tf_op jit(solution)/shard_map/add | solution.py:359
  67.3 0.4 collective-permute-done.9
  67.6 1.1 %slice_add_fusion.7 = (f32[8,64,128]{2,1,0:T(8,128)S(1)}, f32[8,64,128]{2,1,0:T(8,128)S(1)}) fusion(f32[16,64,128]{2,1,0:T(8,128)} %collective-permute-done.9, f32[1,16,64,128]{3,2,1,0:T(8,128)S(1)} %get-tuple-element.79), kind=kLoop, calls=%fused_computation.19 | loop fusion | flops 131072 | bytes 1572864 | tf_op jit(solution)/shard_map/add | solution.py:359
  68.7 0.8 collective-permute-done.11
  69.5 0.1 collective-permute-start.12
  69.6 0.0 collective-permute-done.3
  69.7 0.2 collective-permute-start.17
  69.9 1.3 %collective-permute-start.18 = (f32[1024,128]{1,0:T(8,128)S(1)}, f32[1024,128]{1,0:T(8,128)S(1)}, u32[]{:S(2)}, u32[]{:S(2)}) collective-permute-start(f32[1024,128]{1,0:T(8,128)S(1)} %get-tuple-element.65), channel_id=1, source_target_pairs={{0,1},{1,0},{2,3},{3,2},{4,5},{5,4},{6,7},{7,6},{8,9},{9,8},{10,11... | collective-permute-start | bytes 1572872 | tf_op jit(solution)/shard_map/ppermute | solution.py:251
  71.2 1.4 %collective-permute-start.13 = (f32[8,64,128]{2,1,0:T(8,128)S(1)}, f32[8,64,128]{2,1,0:T(8,128)S(1)}, u32[]{:S(2)}, u32[]{:S(2)}) collective-permute-start(f32[8,64,128]{2,1,0:T(8,128)S(1)} %get-tuple-element.63), channel_id=1, source_target_pairs={{0,4},{4,0},{8,12},{12,8},{16,20},{20,16},{24,28},{28,24},{1,5},{5... | collective-permute-start | bytes 786440 | tf_op jit(solution)/shard_map/ppermute | solution.py:251
  72.6 0.1 broadcast_in_dim.37
  72.7 0.0 copy-start.11
  72.8 4.7 %collective-permute-done.12 = f32[8,64,128]{2,1,0:T(8,128)S(1)} collective-permute-done((f32[8,64,128]{2,1,0:T(8,128)S(1)}, f32[8,64,128]{2,1,0:T(8,128)S(1)}, u32[]{:S(2)}, u32[]{:S(2)}) %collective-permute-start.12) | collective-permute-done | bytes 262176 | tf_op jit(solution)/shard_map/ppermute | solution.py:251
  77.5 1.9 %collective-permute-done.13 = f32[8,64,128]{2,1,0:T(8,128)S(1)} collective-permute-done((f32[8,64,128]{2,1,0:T(8,128)S(1)}, f32[8,64,128]{2,1,0:T(8,128)S(1)}, u32[]{:S(2)}, u32[]{:S(2)}) %collective-permute-start.13) | collective-permute-done | bytes 262176 | tf_op jit(solution)/shard_map/ppermute | solution.py:251
  79.5 1.5 %collective-permute-start.16 = (f32[2,128,128]{2,1,0:T(8,128)S(1)}, f32[2,128,128]{2,1,0:T(8,128)S(1)}, u32[]{:S(2)}, u32[]{:S(2)}) collective-permute-start(f32[2,128,128]{2,1,0:T(8,128)S(1)} %pad_maximum_fusion.2), channel_id=1, source_target_pairs={{0,2},{1,3},{2,0},{3,1},{4,6},{5,7},{6,4},{7,5},{8,10},{9,11},{10,... | collective-permute-start | bytes 393224 | tf_op jit(solution)/shard_map/ppermute | solution.py:251
  80.9 2.3 %collective-permute-start.15 = (f32[2,128,128]{2,1,0:T(8,128)S(1)}, f32[2,128,128]{2,1,0:T(8,128)S(1)}, u32[]{:S(2)}, u32[]{:S(2)}) collective-permute-start(f32[2,128,128]{2,1,0:T(8,128)S(1)} %pad_maximum_fusion.1), channel_id=1, source_target_pairs={{0,16},{4,20},{8,24},{12,28},{16,0},{20,4},{24,8},{28,12},{1,17},{... | collective-permute-start | bytes 393224 | tf_op jit(solution)/shard_map/ppermute | solution.py:251
  83.3 0.0 copy-start.12
  83.3 0.8 collective-permute-start.14
  84.1 0.0 collective-permute-done.18
  84.1 5.4 %collective-permute-done.17 = f32[1536,128]{1,0:T(8,128)S(1)} collective-permute-done((f32[1536,128]{1,0:T(8,128)S(1)}, f32[1536,128]{1,0:T(8,128)S(1)}, u32[]{:S(2)}, u32[]{:S(2)}) %collective-permute-start.17) | collective-permute-done | bytes 786464 | tf_op jit(solution)/shard_map/ppermute | solution.py:251
  89.6 5.4 %collective-permute-done.16 = f32[2,128,128]{2,1,0:T(8,128)S(1)} collective-permute-done((f32[2,128,128]{2,1,0:T(8,128)S(1)}, f32[2,128,128]{2,1,0:T(8,128)S(1)}, u32[]{:S(2)}, u32[]{:S(2)}) %collective-permute-start.16) | collective-permute-done | bytes 131104 | tf_op jit(solution)/shard_map/ppermute | solution.py:251
  95.0 0.0 collective-permute-done.15
  95.0 0.0 collective-permute-done.14
  95.2 0.0 copy-start.8
  95.2 0.0 copy-start.9
  95.2 0.8 fusion.2
  96.0 0.5 copy-done.8
  96.5 0.3 copy-done.9
  (30 shorter events, 0.4 us)
Async XLA Ops:
  0.6 1.2 %copy-start.1 = (f32[4,512,128]{2,1,0:T(8,128)S(1)}, f32[4,512,128]{2,1,0:T(8,128)}, u32[]{:S(2)}) copy-start(f32[4,512,128]{2,1,0:T(8,128)} %own_ref.2) | copy-start | bytes 3145732
  1.9 13.8 %copy-start.13 = (s32[144,1]{0,1:T(1,128)S(1)}, s32[144,1]{0,1:T(1,128)}, u32[]{:S(2)}) copy-start(s32[144,1]{0,1:T(1,128)} %param.9) | copy-start | bytes 1732
  1.9 13.8 %copy-start.14 = (s32[144]{0:T(256)S(1)}, s32[144]{0:T(256)}, u32[]{:S(2)}) copy-start(s32[144]{0:T(256)} %param.10) | copy-start | bytes 1732
  1.9 13.9 %copy-start.2 = (f32[4,512,128]{2,1,0:T(8,128)S(1)}, f32[4,512,128]{2,1,0:T(8,128)}, u32[]{:S(2)}) copy-start(f32[4,512,128]{2,1,0:T(8,128)} %own_ref.2) | copy-start | bytes 3145732
  3.0 10.0 %collective-permute-start = (f32[512,128]{1,0:T(8,128)}, f32[512,128]{1,0:T(8,128)S(1)}, u32[]{:S(2)}, u32[]{:S(2)}) collective-permute-start(f32[512,128]{1,0:T(8,128)} %get-tuple-element.38), channel_id=1, source_target_pairs={{0,1},{1,0},{2,3},{3,2},{4,5},{5,4},{6,7},{7,6},{8,9},{9,8},{10,11... | collective-permute-start | bytes 786440 | tf_op jit(solution)/shard_map/ppermute | solution.py:251
  3.5 7.1 %collective-permute-start.1 = (f32[256,128]{1,0:T(8,128)}, f32[256,128]{1,0:T(8,128)S(1)}, u32[]{:S(2)}, u32[]{:S(2)}) collective-permute-start(f32[256,128]{1,0:T(8,128)} %get-tuple-element.39), channel_id=1, source_target_pairs={{0,2},{1,3},{2,0},{3,1},{4,6},{5,7},{6,4},{7,5},{8,10},{9,11},{10,... | collective-permute-start | bytes 393224 | tf_op jit(solution)/shard_map/ppermute | solution.py:251
  6.1 7.0 %collective-permute-start.2 = (f32[256,128]{1,0:T(8,128)}, f32[256,128]{1,0:T(8,128)}, u32[]{:S(2)}, u32[]{:S(2)}) collective-permute-start(f32[256,128]{1,0:T(8,128)} %get-tuple-element.40), channel_id=1, source_target_pairs={{0,3},{1,2},{2,1},{3,0},{4,7},{5,6},{6,5},{7,4},{8,11},{9,10},{10,... | collective-permute-start | bytes 393224 | tf_op jit(solution)/shard_map/ppermute | solution.py:251
  6.2 32.1 %copy-start = (f32[4,1024,128]{2,1,0:T(8,128)S(1)}, f32[4,1024,128]{2,1,0:T(8,128)}, u32[]{:S(2)}) copy-start(f32[4,1024,128]{2,1,0:T(8,128)} %own_ref.3) | copy-start | bytes 6291460
  6.2 32.1 %copy-start.5 = (s32[4]{0:T(128)S(1)}, s32[4]{0:T(128)}, u32[]{:S(2)}) copy-start(s32[4]{0:T(128)} %counts.3) | copy-start | bytes 52
  13.1 0.7 copy-start.3
  13.8 24.5 %collective-permute-start.5 = (f32[1024,128]{1,0:T(8,128)}, f32[1024,128]{1,0:T(8,128)}, u32[]{:S(2)}, u32[]{:S(2)}) collective-permute-start(f32[1024,128]{1,0:T(8,128)} %get-tuple-element.49), channel_id=1, source_target_pairs={{0,1},{1,0},{2,3},{3,2},{4,5},{5,4},{6,7},{7,6},{8,9},{9,8},{10,11... | collective-permute-start | bytes 1572872 | tf_op jit(solution)/shard_map/ppermute | solution.py:251
  13.9 24.4 %collective-permute-start.6 = (f32[1024,128]{1,0:T(8,128)}, f32[1024,128]{1,0:T(8,128)}, u32[]{:S(2)}, u32[]{:S(2)}) collective-permute-start(f32[1024,128]{1,0:T(8,128)} %get-tuple-element.50), channel_id=1, source_target_pairs={{0,2},{1,3},{2,0},{3,1},{4,6},{5,7},{6,4},{7,5},{8,10},{9,11},{10,... | collective-permute-start | bytes 1572872 | tf_op jit(solution)/shard_map/ppermute | solution.py:251
  15.6 25.9 %collective-permute-start.4 = (f32[1024,128]{1,0:T(8,128)}, f32[1024,128]{1,0:T(8,128)}, u32[]{:S(2)}, u32[]{:S(2)}) collective-permute-start(f32[1024,128]{1,0:T(8,128)} %get-tuple-element.46), channel_id=1, source_target_pairs={{0,3},{1,2},{2,1},{3,0},{4,7},{5,6},{6,5},{7,4},{8,11},{9,10},{10,... | collective-permute-start | bytes 1572872 | tf_op jit(solution)/shard_map/ppermute | solution.py:251
  15.8 1.0 copy-start.4
  36.4 5.1 %copy-start.6 = (f32[512,128]{1,0:T(8,128)}, f32[512,128]{1,0:T(8,128)S(1)}, u32[]{:S(2)}) copy-start(f32[512,128]{1,0:T(8,128)S(1)} %get-tuple-element.45) | copy-start | bytes 786436
  36.4 9.8 %collective-permute-start.7 = (f32[512,128]{1,0:T(8,128)S(1)}, f32[512,128]{1,0:T(8,128)S(1)}, u32[]{:S(2)}, u32[]{:S(2)}) collective-permute-start(f32[512,128]{1,0:T(8,128)S(1)} %get-tuple-element.55), channel_id=1, source_target_pairs={{0,2},{1,3},{2,0},{3,1},{4,6},{5,7},{6,4},{7,5},{8,10},{9,11},{10,... | collective-permute-start | bytes 786440 | tf_op jit(solution)/shard_map/ppermute | solution.py:251
  46.2 4.2 %copy-start.10 = (f32[512,128]{1,0:T(8,128)}, f32[512,128]{1,0:T(8,128)S(1)}, u32[]{:S(2)}) copy-start(f32[512,128]{1,0:T(8,128)S(1)} %collective-permute-done.7) | copy-start | bytes 786436
  46.2 4.2 %collective-permute-start.8 = (f32[2,32,64,128]{3,2,1,0:T(8,128)S(1)}, f32[2,32,64,128]{3,2,1,0:T(8,128)S(1)}, u32[]{:S(2)}, u32[]{:S(2)}) collective-permute-start(f32[2,32,64,128]{3,2,1,0:T(8,128)S(1)} %get-tuple-element.58), channel_id=1, source_target_pairs={{0,1},{1,0},{2,3},{3,2},{4,5},{5,4},{6,7},{7,6},{8,9},{9,8},{10,11... | collective-permute-start | bytes 6291464 | tf_op jit(solution)/shard_map/ppermute | solution.py:251
  50.5 4.7 %copy-start.7 = (f32[512,128]{1,0:T(8,128)S(1)}, f32[512,128]{1,0:T(8,128)}, u32[]{:S(2)}) copy-start(f32[512,128]{1,0:T(8,128)} %copy-done.6) | copy-start | bytes 786436
  51.7 14.3 %collective-permute-start.10 = (f32[16,64,128]{2,1,0:T(8,128)}, f32[16,64,128]{2,1,0:T(8,128)}, u32[]{:S(2)}, u32[]{:S(2)}) collective-permute-start(f32[16,64,128]{2,1,0:T(8,128)} %get-tuple-element.60), channel_id=1, source_target_pairs={{0,8},{4,12},{8,0},{12,4},{16,24},{20,28},{24,16},{28,20},{1,9},{5... | collective-permute-start | bytes 1572872 | tf_op jit(solution)/shard_map/ppermute | solution.py:251
  52.7 14.9 %collective-permute-start.9 = (f32[16,64,128]{2,1,0:T(8,128)}, f32[16,64,128]{2,1,0:T(8,128)}, u32[]{:S(2)}, u32[]{:S(2)}) collective-permute-start(f32[16,64,128]{2,1,0:T(8,128)} %get-tuple-element.59), channel_id=1, source_target_pairs={{0,4},{4,0},{8,12},{12,8},{16,20},{20,16},{24,28},{28,24},{1,5},{5... | collective-permute-start | bytes 1572872 | tf_op jit(solution)/shard_map/ppermute | solution.py:251
  55.2 14.5 %collective-permute-start.3 = (f32[512,128]{1,0:T(8,128)S(1)}, f32[512,128]{1,0:T(8,128)S(1)}, u32[]{:S(2)}, u32[]{:S(2)}) collective-permute-start(f32[512,128]{1,0:T(8,128)S(1)} %copy-done.7), channel_id=1, source_target_pairs={{0,1},{1,0},{2,3},{3,2},{4,5},{5,4},{6,7},{7,6},{8,9},{9,8},{10,11... | collective-permute-start | bytes 786440 | tf_op jit(solution)/shard_map/ppermute | solution.py:251
  55.2 14.3 %collective-permute-start.11 = (f32[1024,128]{1,0:T(8,128)S(1)}, f32[1024,128]{1,0:T(8,128)S(1)}, u32[]{:S(2)}, u32[]{:S(2)}) collective-permute-start(f32[1024,128]{1,0:T(8,128)S(1)} %get-tuple-element.61), channel_id=1, source_target_pairs={{0,2},{1,3},{2,0},{3,1},{4,6},{5,7},{6,4},{7,5},{8,10},{9,11},{10,... | collective-permute-start | bytes 1572872 | tf_op jit(solution)/shard_map/ppermute | solution.py:251
  69.5 7.9 %collective-permute-start.12 = (f32[8,64,128]{2,1,0:T(8,128)S(1)}, f32[8,64,128]{2,1,0:T(8,128)S(1)}, u32[]{:S(2)}, u32[]{:S(2)}) collective-permute-start(f32[8,64,128]{2,1,0:T(8,128)S(1)} %get-tuple-element.62), channel_id=1, source_target_pairs={{0,8},{4,12},{8,0},{12,4},{16,24},{20,28},{24,16},{28,20},{1,9},{5... | collective-permute-start | bytes 786440 | tf_op jit(solution)/shard_map/ppermute | solution.py:251
  69.7 19.9 %collective-permute-start.17 = (f32[1536,128]{1,0:T(8,128)S(1)}, f32[1536,128]{1,0:T(8,128)S(1)}, u32[]{:S(2)}, u32[]{:S(2)}) collective-permute-start(f32[1536,128]{1,0:T(8,128)S(1)} %get-tuple-element.64), channel_id=1, source_target_pairs={{0,3},{1,2},{2,1},{3,0},{4,7},{5,6},{6,5},{7,4},{8,11},{9,10},{10,... | collective-permute-start | bytes 2359304 | tf_op jit(solution)/shard_map/ppermute | solution.py:251
  69.9 14.3 %collective-permute-start.18 = (f32[1024,128]{1,0:T(8,128)S(1)}, f32[1024,128]{1,0:T(8,128)S(1)}, u32[]{:S(2)}, u32[]{:S(2)}) collective-permute-start(f32[1024,128]{1,0:T(8,128)S(1)} %get-tuple-element.65), channel_id=1, source_target_pairs={{0,1},{1,0},{2,3},{3,2},{4,5},{5,4},{6,7},{7,6},{8,9},{9,8},{10,11... | collective-permute-start | bytes 1572872 | tf_op jit(solution)/shard_map/ppermute | solution.py:251
  71.2 8.2 %collective-permute-start.13 = (f32[8,64,128]{2,1,0:T(8,128)S(1)}, f32[8,64,128]{2,1,0:T(8,128)S(1)}, u32[]{:S(2)}, u32[]{:S(2)}) collective-permute-start(f32[8,64,128]{2,1,0:T(8,128)S(1)} %get-tuple-element.63), channel_id=1, source_target_pairs={{0,4},{4,0},{8,12},{12,8},{16,20},{20,16},{24,28},{28,24},{1,5},{5... | collective-permute-start | bytes 786440 | tf_op jit(solution)/shard_map/ppermute | solution.py:251
  72.7 11.4 %copy-start.11 = (f32[512,128]{1,0:T(8,128)S(1)}, f32[512,128]{1,0:T(8,128)}, u32[]{:S(2)}) copy-start(f32[512,128]{1,0:T(8,128)} %copy-done.10) | copy-start | bytes 786436
  79.5 15.5 %collective-permute-start.16 = (f32[2,128,128]{2,1,0:T(8,128)S(1)}, f32[2,128,128]{2,1,0:T(8,128)S(1)}, u32[]{:S(2)}, u32[]{:S(2)}) collective-permute-start(f32[2,128,128]{2,1,0:T(8,128)S(1)} %pad_maximum_fusion.2), channel_id=1, source_target_pairs={{0,2},{1,3},{2,0},{3,1},{4,6},{5,7},{6,4},{7,5},{8,10},{9,11},{10,... | collective-permute-start | bytes 393224 | tf_op jit(solution)/shard_map/ppermute | solution.py:251
  80.9 14.1 %collective-permute-start.15 = (f32[2,128,128]{2,1,0:T(8,128)S(1)}, f32[2,128,128]{2,1,0:T(8,128)S(1)}, u32[]{:S(2)}, u32[]{:S(2)}) collective-permute-start(f32[2,128,128]{2,1,0:T(8,128)S(1)} %pad_maximum_fusion.1), channel_id=1, source_target_pairs={{0,16},{4,20},{8,24},{12,28},{16,0},{20,4},{24,8},{28,12},{1,17},{... | collective-permute-start | bytes 393224 | tf_op jit(solution)/shard_map/ppermute | solution.py:251
  83.3 11.9 %copy-start.12 = (f32[2,128,128]{2,1,0:T(8,128)S(1)}, f32[2,128,128]{2,1,0:T(8,128)}, u32[]{:S(2)}) copy-start(f32[2,128,128]{2,1,0:T(8,128)} %param.11) | copy-start | bytes 393220
  83.3 11.7 %collective-permute-start.14 = (f32[2,128,128]{2,1,0:T(8,128)S(1)}, f32[2,128,128]{2,1,0:T(8,128)S(1)}, u32[]{:S(2)}, u32[]{:S(2)}) collective-permute-start(f32[2,128,128]{2,1,0:T(8,128)S(1)} %pad_maximum_fusion), channel_id=1, source_target_pairs={{0,18},{1,19},{2,16},{3,17},{4,22},{5,23},{6,20},{7,21},{8,26},{9,... | collective-permute-start | bytes 393224 | tf_op jit(solution)/shard_map/ppermute | solution.py:374
  95.2 1.4 %copy-start.8 = (f32[4,1024,128]{2,1,0:T(8,128)}, f32[4,1024,128]{2,1,0:T(8,128)S(1)}, u32[]{:S(2)}) copy-start(f32[4,1024,128]{2,1,0:T(8,128)S(1)} %bitcast_dynamic-update-slice_fusion) | copy-start | bytes 6291460
  95.2 1.7 %copy-start.9 = (f32[4,512,128]{2,1,0:T(8,128)}, f32[4,512,128]{2,1,0:T(8,128)S(1)}, u32[]{:S(2)}) copy-start(f32[4,512,128]{2,1,0:T(8,128)S(1)} %bitcast_dynamic-update-slice_fusion.4) | copy-start | bytes 3145732

commit v13 on v12

--- a/solution.py
+++ b/solution.py
@@ -273,9 +273,9 @@
         cut_kernel,
         out_shape=cut,
         in_specs=[SMEM, pl.BlockSpec(memory_space=pltpu.HBM)],
-        out_specs=[VMEM] * 3,
+        out_specs=[ANY] * 3,
         scratch_shapes=[pltpu.SemaphoreType.DMA((3,))],
-        compiler_params=pltpu.CompilerParams(vmem_limit_bytes=8 * 2**20),
+        compiler_params=pltpu.CompilerParams(vmem_limit_bytes=2 * 2**20),
         cost_estimate=pl.CostEstimate(flops=0, bytes_accessed=2**20, transcendentals=0),
         name="cut",
     )(info, diag_block)
@@ -301,7 +301,7 @@
         in_specs=[SMEM] + [ANY] * NB,
         out_specs=[ANY] * NB + [VMEM],
         scratch_shapes=[pltpu.VMEM((NB, W, B), jnp.float32)] * 2 + [pltpu.SemaphoreType.DMA((NB,))],
-        compiler_params=pltpu.CompilerParams(vmem_limit_bytes=32 * 2**20),
+        compiler_params=pltpu.CompilerParams(vmem_limit_bytes=12 * 2**20),
         cost_estimate=pl.CostEstimate(flops=2 * 10**8, bytes_accessed=4 * 10**6, transcendentals=0),
         name="factor",
     )(info, diag_block, *diag_in)
@@ -311,8 +311,8 @@
     slab = jax.ShapeDtypeStruct((rows, B), jnp.float32)
     longer = jax.ShapeDtypeStruct((rows + W, B), jnp.float32)
     part = jax.ShapeDtypeStruct((2, blocks // 2, B // 2, B), jnp.float32)
-    room = pltpu.CompilerParams(vmem_limit_bytes=20 * 2**20 + 4 * blocks * B * B)
-    sums = 2 if blocks * B * B * 4 <= 8 * 2**20 else 0
+    room = pltpu.CompilerParams(vmem_limit_bytes=16 * 2**20 + 4 * blocks * B * B)
+    sums = 0
     acc, *empty = pl.pallas_call(
         early_kernel,
         out_shape=[jax.ShapeDtypeStruct((rows, W), jnp.float32)] + [part] * sums,

time: 97.3 us -> 94.4 us (0.970)
  Pallas kernels: 28.7 us -> 23.6 us
  local copies, waits for them, and re-layouts: 6.89 us -> 5.18 us
  waiting for transfers between devices: 37.2 us -> 38.7 us
  other arithmetic: 4.71 us -> 6.09 us
  starting transfers between devices: 18.4 us -> 19.6 us
    pallas_call x1 -> x0, Pallas kernels: 4.62 us -> none  [local(): pl.pallas_call(panel_kernel, out_shape=[slab] * (NB - 1) + [longer, part,...]
    pallas_call x0 -> x1, other arithmetic: none -> 4.33 us  [local(): pl.pallas_call(panel_kernel, out_shape=[slab] * (NB - 1) + [longer, part,...]
    unnamed x30 -> x18, local copies, waits for them, and re-layouts: 3.75 us -> 2.09 us
    ppermute x18, waiting for transfers between devices: 37.2 us -> 38.7 us  [swap(): return lax.ppermute(x, axis, xor_pairs(lax.axis_size(axis), mask))]
    ppermute x18, starting transfers between devices: 17.6 us -> 19.1 us  [swap(): return lax.ppermute(x, axis, xor_pairs(lax.axis_size(axis), mask))]
    add x1, other arithmetic: 1.25 us -> 0.06 us  [local(): keep_b[:half] + got_b[:half]]
    add x1, other arithmetic: 1.09 us -> 0.06 us  [local(): keep_a[:half] + got_a[:half]]
  transfers between devices with their start and end apart: 19 -> 19, of which waited for: 10 -> 11; matrix products, arithmetic and copies ran while one was open for 6% -> 8% of each run, Pallas kernels for 28% -> 24%
where the time goes in v13:
time: 94.4 us; the launch traced here: 94 us
  waiting for transfers between devices  38.7 us (41%)
  Pallas kernels  23.6 us (25%)
  starting transfers between devices  19.6 us (21%)
  other arithmetic  6.09 us (6%)
  local copies, waits for them, and re-layouts  5.18 us (5%)
    ppermute x18, waiting for transfers between devices, swap(): return lax.ppermute(x, axis, xor_pairs(lax.axis_size(axis), mask))  38.7 us
    pallas_call x1, Pallas kernels, local(): pl.pallas_call(factor_kernel, out_shape=[slab] * NB + [jax.ShapeDtypeStru...  19.7 us
    ppermute x18, starting transfers between devices, swap(): return lax.ppermute(x, axis, xor_pairs(lax.axis_size(axis), mask))  19.1 us
    pallas_call x1, other arithmetic, local(): pl.pallas_call(panel_kernel, out_shape=[slab] * (NB - 1) + [longer, part,...  4.33 us
    pallas_call x1, Pallas kernels, local(): pl.pallas_call(early_kernel, out_shape=[jax.ShapeDtypeStruct((rows, W), j...  3.03 us
    squeeze x1, local copies, waits for them, and re-layouts, local(): own = lambda x, m: lax.dynamic_index_in_dim(x, me ^ m, 0, keepdims=False)  2.68 us
    unnamed x18, local copies, waits for them, and re-layouts  2.09 us
  transfers between devices with their start and end apart: 19, of which 11 were waited for; matrix products, arithmetic and copies ran while one was open for 8% of the time, Pallas kernels for 24%

profile of v13, /device:TPU:0, one launch (start us, length us, event | category | flops | bytes accessed | tf_op | source)
XLA Modules:
  0.0 94.0 jit_solution(11975203149033792916)
XLA Ops:
  0.6 0.0 copy-start.1
  0.6 1.2 %copy-done.1 = f32[4,512,128]{2,1,0:T(8,128)S(1)} copy-done((f32[4,512,128]{2,1,0:T(8,128)S(1)}, f32[4,512,128]{2,1,0:T(8,128)}, u32[]{:S(2)}) %copy-start.1) | copy-done | bytes 1048600
  1.9 0.8 cut.1
  2.7 0.5 collective-permute-start
  3.2 2.6 %collective-permute-start.1 = (f32[256,128]{1,0:T(8,128)}, f32[256,128]{1,0:T(8,128)S(1)}, u32[]{:S(2)}, u32[]{:S(2)}) collective-permute-start(f32[256,128]{1,0:T(8,128)} %get-tuple-element.36), channel_id=1, source_target_pairs={{0,2},{1,3},{2,0},{3,1},{4,6},{5,7},{6,4},{7,5},{8,10},{9,11},{10,... | collective-permute-start | bytes 393224 | tf_op jit(solution)/shard_map/ppermute | solution.py:251
  5.8 0.1 collective-permute-start.2
  5.8 2.7 %dynamic-slice_bitcast_fusion = (f32[1024,128]{1,0:T(8,128)}, f32[1024,128]{1,0:T(8,128)}, f32[1024,128]{1,0:T(8,128)}) fusion(f32[4,1024,128]{2,1,0:T(8,128)} %own_ref.3, s32[]{:T(128)S(6)} %select_n.59, s32[]{:T(128)S(6)} %select_n.58, s32[]{:T(128)S(6)} %select_n.57), kind=kLoop, calls=%fused_computation.10 | loop fusion | bytes 3145740 | tf_op jit(solution)/shard_map/jit(dynamic_index_in_dim)/squeeze | solution.py:269
  8.5 1.8 %collective-permute-done.1.r2 = f32[256,128]{1,0:T(8,128)S(1)} collective-permute-done((f32[256,128]{1,0:T(8,128)}, f32[256,128]{1,0:T(8,128)S(1)}, u32[]{:S(2)}, u32[]{:S(2)}) %collective-permute-start.1) | collective-permute-done | bytes 131104 | tf_op jit(solution)/shard_map/ppermute | solution.py:251
  10.3 2.4 %collective-permute-done.2.r3 = f32[256,128]{1,0:T(8,128)} collective-permute-done((f32[256,128]{1,0:T(8,128)}, f32[256,128]{1,0:T(8,128)}, u32[]{:S(2)}, u32[]{:S(2)}) %collective-permute-start.2) | collective-permute-done | bytes 131104 | tf_op jit(solution)/shard_map/ppermute | solution.py:251
  12.7 0.0 collective-permute-done.r1
  12.7 0.1 collective-permute-start.5
  12.8 1.7 %collective-permute-start.6 = (f32[1024,128]{1,0:T(8,128)}, f32[1024,128]{1,0:T(8,128)}, u32[]{:S(2)}, u32[]{:S(2)}) collective-permute-start(f32[1024,128]{1,0:T(8,128)} %get-tuple-element.47), channel_id=1, source_target_pairs={{0,2},{1,3},{2,0},{3,1},{4,6},{5,7},{6,4},{7,5},{8,10},{9,11},{10,... | collective-permute-start | bytes 1572872 | tf_op jit(solution)/shard_map/ppermute | solution.py:251
  14.6 0.0 collective-permute-start.4
  14.6 0.0 copy-done.7
  14.6 0.0 copy-done.8
  14.6 0.1 multiply_add_fusion
  14.7 0.0 copy-done.2
  14.7 19.7 %factor.1 = (f32[512,128]{1,0:T(8,128)S(1)}, f32[512,128]{1,0:T(8,128)S(1)}, f32[512,128]{1,0:T(8,128)S(1)}, f32[512,128]{1,0:T(8,128)S(1)}, f32[4,512,128]{2,1,0:T(8,128)S(1)}) custom-call(s32[1]{0:T(128)} %bitcast.info, f32[4,512,128]{2,1,0:T(8,128)S(1)} %copy-done.2, f32[512,128]{1,0:T(8,128)S(1)} %collective-permute-done.r1, ...), custom_call_target="tpu_custom_call" | custom-call | flops 200000000 | bytes 4000000 | tf_op jit(solution)/shard_map/factor/pallas_call | solution.py:298
  34.4 1.7 %collective-permute-start.7 = (f32[512,128]{1,0:T(8,128)S(1)}, f32[512,128]{1,0:T(8,128)S(1)}, u32[]{:S(2)}, u32[]{:S(2)}) collective-permute-start(f32[512,128]{1,0:T(8,128)S(1)} %get-tuple-element.49), channel_id=1, source_target_pairs={{0,2},{1,3},{2,0},{3,1},{4,6},{5,7},{6,4},{7,5},{8,10},{9,11},{10,... | collective-permute-start | bytes 786440 | tf_op jit(solution)/shard_map/ppermute | solution.py:251
  36.2 0.1 multiply_add_fusion.1
  36.3 0.0 collective-permute-done.5.r1
  36.3 0.0 collective-permute-done.6.r2
  36.3 0.0 copy-done
  36.3 0.0 copy-done.3
  36.3 3.0 %early.1 = f32[1024,512]{1,0:T(8,128)S(1)} custom-call(s32[1]{0:T(128)} %bitcast.info, s32[4]{0:T(128)S(1)} %copy-done.3, f32[4,1024,128]{2,1,0:T(8,128)S(1)} %copy-done, f32[1024,128]{1,0:T(8,128)} %collective-permute-done.5.r1, f32[1024,128]{1,0:T(8,128)} %collective-permute-done.6.r2, f32[4,512,128]{2,1,0:T(8,128)S(1)} %get-tuple-element.44.mt), custom_call_target="tpu_custom_call" | custom-call | flops 500000000 | bytes 10000000 | tf_op jit(solution)/shard_map/early/pallas_call | solution.py:316
  39.4 0.0 collective-permute-done.4
  39.4 0.1 broadcast_in_dim.37
  39.5 4.3 %panel.1 = (f32[4,1024,128]{2,1,0:T(8,128)S(1)}, f32[2,32,64,128]{3,2,1,0:T(8,128)S(1)}, f32[2,32,64,128]{3,2,1,0:T(8,128)S(1)}, f32[1024,128]{1,0:T(8,128)S(1)}...) fusion(f32[4,1024,128]{2,1,0:T(8,128)S(1)} %broadcast_in_dim.37, s32[]{:T(128)S(6)} %select_n.60, s32[1]{0:T(128)} %bitcast.info, ...), kind=kCustom, calls=%fused_computation.9 | custom fusion | flops 1000000000 | bytes 10487304 | tf_op jit(solution)/shard_map/panel/pallas_call | solution.py:325
  43.9 0.3 collective-permute-done.7
  44.1 1.1 %collective-permute-start.8 = (f32[2,32,64,128]{3,2,1,0:T(8,128)S(1)}, f32[2,32,64,128]{3,2,1,0:T(8,128)S(1)}, u32[]{:S(2)}, u32[]{:S(2)}) collective-permute-start(f32[2,32,64,128]{3,2,1,0:T(8,128)S(1)} %get-tuple-element.52), channel_id=1, source_target_pairs={{0,1},{1,0},{2,3},{3,2},{4,5},{5,4},{6,7},{7,6},{8,9},{9,8},{10,11... | collective-permute-start | bytes 6291464 | tf_op jit(solution)/shard_map/ppermute | solution.py:251
  45.2 3.8 %collective-permute-done.8 = f32[2,32,64,128]{3,2,1,0:T(8,128)S(1)} collective-permute-done((f32[2,32,64,128]{3,2,1,0:T(8,128)S(1)}, f32[2,32,64,128]{3,2,1,0:T(8,128)S(1)}, u32[]{:S(2)}, u32[]{:S(2)}) %collective-permute-start.8) | collective-permute-done | bytes 2097184 | tf_op jit(solution)/shard_map/ppermute | solution.py:251
  49.0 0.6 slice_add_fusion
  49.6 1.0 %collective-permute-start.10 = (f32[16,64,128]{2,1,0:T(8,128)S(1)}, f32[16,64,128]{2,1,0:T(8,128)S(1)}, u32[]{:S(2)}, u32[]{:S(2)}) collective-permute-start(f32[16,64,128]{2,1,0:T(8,128)S(1)} %get-tuple-element.54), channel_id=1, source_target_pairs={{0,8},{4,12},{8,0},{12,4},{16,24},{20,28},{24,16},{28,20},{1,9},{5... | collective-permute-start | bytes 1572872 | tf_op jit(solution)/shard_map/ppermute | solution.py:251
  50.6 1.5 %collective-permute-start.9 = (f32[16,64,128]{2,1,0:T(8,128)S(1)}, f32[16,64,128]{2,1,0:T(8,128)S(1)}, u32[]{:S(2)}, u32[]{:S(2)}) collective-permute-start(f32[16,64,128]{2,1,0:T(8,128)S(1)} %get-tuple-element.53), channel_id=1, source_target_pairs={{0,4},{4,0},{8,12},{12,8},{16,20},{20,16},{24,28},{28,24},{1,5},{5... | collective-permute-start | bytes 1572872 | tf_op jit(solution)/shard_map/ppermute | solution.py:251
  52.1 1.7 %collective-permute-start.11 = (f32[1024,128]{1,0:T(8,128)S(1)}, f32[1024,128]{1,0:T(8,128)S(1)}, u32[]{:S(2)}, u32[]{:S(2)}) collective-permute-start(f32[1024,128]{1,0:T(8,128)S(1)} %get-tuple-element.95), channel_id=1, source_target_pairs={{0,2},{1,3},{2,0},{3,1},{4,6},{5,7},{6,4},{7,5},{8,10},{9,11},{10,... | collective-permute-start | bytes 1572872 | tf_op jit(solution)/shard_map/ppermute | solution.py:251
  53.8 0.0 collective-permute-start.3
  53.8 10.0 %collective-permute-done.10 = f32[16,64,128]{2,1,0:T(8,128)S(1)} collective-permute-done((f32[16,64,128]{2,1,0:T(8,128)S(1)}, f32[16,64,128]{2,1,0:T(8,128)S(1)}, u32[]{:S(2)}, u32[]{:S(2)}) %collective-permute-start.10) | collective-permute-done | bytes 524320 | tf_op jit(solution)/shard_map/ppermute | solution.py:251
  63.8 0.1 slice_add_fusion.4
  63.9 0.4 collective-permute-done.9
  64.2 0.1 slice_add_fusion.7
  64.3 1.4 %collective-permute-done.11 = f32[1024,128]{1,0:T(8,128)S(1)} collective-permute-done((f32[1024,128]{1,0:T(8,128)S(1)}, f32[1024,128]{1,0:T(8,128)S(1)}, u32[]{:S(2)}, u32[]{:S(2)}) %collective-permute-start.11) | collective-permute-done | bytes 524320 | tf_op jit(solution)/shard_map/ppermute | solution.py:251
  65.7 1.0 %collective-permute-start.12 = (f32[8,64,128]{2,1,0:T(8,128)S(1)}, f32[8,64,128]{2,1,0:T(8,128)S(1)}, u32[]{:S(2)}, u32[]{:S(2)}) collective-permute-start(f32[8,64,128]{2,1,0:T(8,128)S(1)} %get-tuple-element.56), channel_id=1, source_target_pairs={{0,8},{4,12},{8,0},{12,4},{16,24},{20,28},{24,16},{28,20},{1,9},{5... | collective-permute-start | bytes 786440 | tf_op jit(solution)/shard_map/ppermute | solution.py:251
  66.7 0.1 broadcast_in_dim.32
  66.8 0.7 collective-permute-start.13
  67.5 0.0 collective-permute-done.3
  67.5 0.1 collective-permute-start.17
  67.6 1.1 %collective-permute-start.18 = (f32[1024,128]{1,0:T(8,128)S(1)}, f32[1024,128]{1,0:T(8,128)S(1)}, u32[]{:S(2)}, u32[]{:S(2)}) collective-permute-start(f32[1024,128]{1,0:T(8,128)S(1)} %get-tuple-element.99), channel_id=1, source_target_pairs={{0,1},{1,0},{2,3},{3,2},{4,5},{5,4},{6,7},{7,6},{8,9},{9,8},{10,11... | collective-permute-start | bytes 1572872 | tf_op jit(solution)/shard_map/ppermute | solution.py:251
  68.7 4.1 %collective-permute-done.12 = f32[8,64,128]{2,1,0:T(8,128)S(1)} collective-permute-done((f32[8,64,128]{2,1,0:T(8,128)S(1)}, f32[8,64,128]{2,1,0:T(8,128)S(1)}, u32[]{:S(2)}, u32[]{:S(2)}) %collective-permute-start.12) | collective-permute-done | bytes 262176 | tf_op jit(solution)/shard_map/ppermute | solution.py:251
  72.8 0.7 collective-permute-done.13
  73.5 1.5 %collective-permute-start.16 = (f32[2,128,128]{2,1,0:T(8,128)S(1)}, f32[2,128,128]{2,1,0:T(8,128)S(1)}, u32[]{:S(2)}, u32[]{:S(2)}) collective-permute-start(f32[2,128,128]{2,1,0:T(8,128)S(1)} %pad_maximum_fusion.2), channel_id=1, source_target_pairs={{0,2},{1,3},{2,0},{3,1},{4,6},{5,7},{6,4},{7,5},{8,10},{9,11},{10,... | collective-permute-start | bytes 393224 | tf_op jit(solution)/shard_map/ppermute | solution.py:251
  75.0 2.6 %collective-permute-start.15 = (f32[2,128,128]{2,1,0:T(8,128)S(1)}, f32[2,128,128]{2,1,0:T(8,128)S(1)}, u32[]{:S(2)}, u32[]{:S(2)}) collective-permute-start(f32[2,128,128]{2,1,0:T(8,128)S(1)} %pad_maximum_fusion.1), channel_id=1, source_target_pairs={{0,16},{4,20},{8,24},{12,28},{16,0},{20,4},{24,8},{28,12},{1,17},{... | collective-permute-start | bytes 393224 | tf_op jit(solution)/shard_map/ppermute | solution.py:251
  77.7 0.0 copy-start.6
  77.7 0.5 collective-permute-start.14
  78.2 0.0 collective-permute-done.18
  78.2 11.9 %collective-permute-done.17 = f32[1536,128]{1,0:T(8,128)S(1)} collective-permute-done((f32[1536,128]{1,0:T(8,128)S(1)}, f32[1536,128]{1,0:T(8,128)S(1)}, u32[]{:S(2)}, u32[]{:S(2)}) %collective-permute-start.17) | collective-permute-done | bytes 786464 | tf_op jit(solution)/shard_map/ppermute | solution.py:251
  90.2 2.0 %collective-permute-done.16 = f32[2,128,128]{2,1,0:T(8,128)S(1)} collective-permute-done((f32[2,128,128]{2,1,0:T(8,128)S(1)}, f32[2,128,128]{2,1,0:T(8,128)S(1)}, u32[]{:S(2)}, u32[]{:S(2)}) %collective-permute-start.16) | collective-permute-done | bytes 131104 | tf_op jit(solution)/shard_map/ppermute | solution.py:251
  92.2 0.0 collective-permute-done.15
  92.2 0.0 collective-permute-done.14
  92.3 0.0 copy-start.4
  92.4 0.0 copy-start.5
  92.4 0.0 copy-done.6
  92.4 0.8 fusion.2
  93.2 0.5 copy-done.4
  93.7 0.3 copy-done.5
  (17 shorter events, 0.3 us)
Async XLA Ops:
  0.6 1.2 %copy-start.1 = (f32[4,512,128]{2,1,0:T(8,128)S(1)}, f32[4,512,128]{2,1,0:T(8,128)}, u32[]{:S(2)}) copy-start(f32[4,512,128]{2,1,0:T(8,128)} %own_ref.2) | copy-start | bytes 3145732
  1.9 12.7 %copy-start.7 = (s32[144,1]{0,1:T(1,128)S(1)}, s32[144,1]{0,1:T(1,128)}, u32[]{:S(2)}) copy-start(s32[144,1]{0,1:T(1,128)} %param.9) | copy-start | bytes 1732
  1.9 12.7 %copy-start.8 = (s32[144]{0:T(256)S(1)}, s32[144]{0:T(256)}, u32[]{:S(2)}) copy-start(s32[144]{0:T(256)} %param.10) | copy-start | bytes 1732
  1.9 12.8 %copy-start.2 = (f32[4,512,128]{2,1,0:T(8,128)S(1)}, f32[4,512,128]{2,1,0:T(8,128)}, u32[]{:S(2)}) copy-start(f32[4,512,128]{2,1,0:T(8,128)} %own_ref.2) | copy-start | bytes 3145732
  2.7 10.0 %collective-permute-start = (f32[512,128]{1,0:T(8,128)}, f32[512,128]{1,0:T(8,128)S(1)}, u32[]{:S(2)}, u32[]{:S(2)}) collective-permute-start(f32[512,128]{1,0:T(8,128)} %get-tuple-element.35), channel_id=1, source_target_pairs={{0,1},{1,0},{2,3},{3,2},{4,5},{5,4},{6,7},{7,6},{8,9},{9,8},{10,11... | collective-permute-start | bytes 786440 | tf_op jit(solution)/shard_map/ppermute | solution.py:251
  3.2 7.1 %collective-permute-start.1 = (f32[256,128]{1,0:T(8,128)}, f32[256,128]{1,0:T(8,128)S(1)}, u32[]{:S(2)}, u32[]{:S(2)}) collective-permute-start(f32[256,128]{1,0:T(8,128)} %get-tuple-element.36), channel_id=1, source_target_pairs={{0,2},{1,3},{2,0},{3,1},{4,6},{5,7},{6,4},{7,5},{8,10},{9,11},{10,... | collective-permute-start | bytes 393224 | tf_op jit(solution)/shard_map/ppermute | solution.py:251
  5.8 7.0 %collective-permute-start.2 = (f32[256,128]{1,0:T(8,128)}, f32[256,128]{1,0:T(8,128)}, u32[]{:S(2)}, u32[]{:S(2)}) collective-permute-start(f32[256,128]{1,0:T(8,128)} %get-tuple-element.37), channel_id=1, source_target_pairs={{0,3},{1,2},{2,1},{3,0},{4,7},{5,6},{6,5},{7,4},{8,11},{9,10},{10,... | collective-permute-start | bytes 393224 | tf_op jit(solution)/shard_map/ppermute | solution.py:251
  5.8 30.5 %copy-start = (f32[4,1024,128]{2,1,0:T(8,128)S(1)}, f32[4,1024,128]{2,1,0:T(8,128)}, u32[]{:S(2)}) copy-start(f32[4,1024,128]{2,1,0:T(8,128)} %own_ref.3) | copy-start | bytes 6291460
  5.8 30.5 %copy-start.3 = (s32[4]{0:T(128)S(1)}, s32[4]{0:T(128)}, u32[]{:S(2)}) copy-start(s32[4]{0:T(128)} %counts.2) | copy-start | bytes 52
  12.7 23.6 %collective-permute-start.5 = (f32[1024,128]{1,0:T(8,128)}, f32[1024,128]{1,0:T(8,128)}, u32[]{:S(2)}, u32[]{:S(2)}) collective-permute-start(f32[1024,128]{1,0:T(8,128)} %get-tuple-element.46), channel_id=1, source_target_pairs={{0,1},{1,0},{2,3},{3,2},{4,5},{5,4},{6,7},{7,6},{8,9},{9,8},{10,11... | collective-permute-start | bytes 1572872 | tf_op jit(solution)/shard_map/ppermute | solution.py:251
  12.8 23.5 %collective-permute-start.6 = (f32[1024,128]{1,0:T(8,128)}, f32[1024,128]{1,0:T(8,128)}, u32[]{:S(2)}, u32[]{:S(2)}) collective-permute-start(f32[1024,128]{1,0:T(8,128)} %get-tuple-element.47), channel_id=1, source_target_pairs={{0,2},{1,3},{2,0},{3,1},{4,6},{5,7},{6,4},{7,5},{8,10},{9,11},{10,... | collective-permute-start | bytes 1572872 | tf_op jit(solution)/shard_map/ppermute | solution.py:251
  14.6 24.8 %collective-permute-start.4 = (f32[1024,128]{1,0:T(8,128)}, f32[1024,128]{1,0:T(8,128)}, u32[]{:S(2)}, u32[]{:S(2)}) collective-permute-start(f32[1024,128]{1,0:T(8,128)} %get-tuple-element.43), channel_id=1, source_target_pairs={{0,3},{1,2},{2,1},{3,0},{4,7},{5,6},{6,5},{7,4},{8,11},{9,10},{10,... | collective-permute-start | bytes 1572872 | tf_op jit(solution)/shard_map/ppermute | solution.py:251
  34.4 9.7 %collective-permute-start.7 = (f32[512,128]{1,0:T(8,128)S(1)}, f32[512,128]{1,0:T(8,128)S(1)}, u32[]{:S(2)}, u32[]{:S(2)}) collective-permute-start(f32[512,128]{1,0:T(8,128)S(1)} %get-tuple-element.49), channel_id=1, source_target_pairs={{0,2},{1,3},{2,0},{3,1},{4,6},{5,7},{6,4},{7,5},{8,10},{9,11},{10,... | collective-permute-start | bytes 786440 | tf_op jit(solution)/shard_map/ppermute | solution.py:251
  44.1 4.9 %collective-permute-start.8 = (f32[2,32,64,128]{3,2,1,0:T(8,128)S(1)}, f32[2,32,64,128]{3,2,1,0:T(8,128)S(1)}, u32[]{:S(2)}, u32[]{:S(2)}) collective-permute-start(f32[2,32,64,128]{3,2,1,0:T(8,128)S(1)} %get-tuple-element.52), channel_id=1, source_target_pairs={{0,1},{1,0},{2,3},{3,2},{4,5},{5,4},{6,7},{7,6},{8,9},{9,8},{10,11... | collective-permute-start | bytes 6291464 | tf_op jit(solution)/shard_map/ppermute | solution.py:251
  49.6 14.3 %collective-permute-start.10 = (f32[16,64,128]{2,1,0:T(8,128)S(1)}, f32[16,64,128]{2,1,0:T(8,128)S(1)}, u32[]{:S(2)}, u32[]{:S(2)}) collective-permute-start(f32[16,64,128]{2,1,0:T(8,128)S(1)} %get-tuple-element.54), channel_id=1, source_target_pairs={{0,8},{4,12},{8,0},{12,4},{16,24},{20,28},{24,16},{28,20},{1,9},{5... | collective-permute-start | bytes 1572872 | tf_op jit(solution)/shard_map/ppermute | solution.py:251
  50.6 13.7 %collective-permute-start.9 = (f32[16,64,128]{2,1,0:T(8,128)S(1)}, f32[16,64,128]{2,1,0:T(8,128)S(1)}, u32[]{:S(2)}, u32[]{:S(2)}) collective-permute-start(f32[16,64,128]{2,1,0:T(8,128)S(1)} %get-tuple-element.53), channel_id=1, source_target_pairs={{0,4},{4,0},{8,12},{12,8},{16,20},{20,16},{24,28},{28,24},{1,5},{5... | collective-permute-start | bytes 1572872 | tf_op jit(solution)/shard_map/ppermute | solution.py:251
  52.1 13.6 %collective-permute-start.11 = (f32[1024,128]{1,0:T(8,128)S(1)}, f32[1024,128]{1,0:T(8,128)S(1)}, u32[]{:S(2)}, u32[]{:S(2)}) collective-permute-start(f32[1024,128]{1,0:T(8,128)S(1)} %get-tuple-element.95), channel_id=1, source_target_pairs={{0,2},{1,3},{2,0},{3,1},{4,6},{5,7},{6,4},{7,5},{8,10},{9,11},{10,... | collective-permute-start | bytes 1572872 | tf_op jit(solution)/shard_map/ppermute | solution.py:251
  53.8 13.7 %collective-permute-start.3 = (f32[512,128]{1,0:T(8,128)S(1)}, f32[512,128]{1,0:T(8,128)S(1)}, u32[]{:S(2)}, u32[]{:S(2)}) collective-permute-start(f32[512,128]{1,0:T(8,128)S(1)} %get-tuple-element.42), channel_id=1, source_target_pairs={{0,1},{1,0},{2,3},{3,2},{4,5},{5,4},{6,7},{7,6},{8,9},{9,8},{10,11... | collective-permute-start | bytes 786440 | tf_op jit(solution)/shard_map/ppermute | solution.py:251
  65.7 7.1 %collective-permute-start.12 = (f32[8,64,128]{2,1,0:T(8,128)S(1)}, f32[8,64,128]{2,1,0:T(8,128)S(1)}, u32[]{:S(2)}, u32[]{:S(2)}) collective-permute-start(f32[8,64,128]{2,1,0:T(8,128)S(1)} %get-tuple-element.56), channel_id=1, source_target_pairs={{0,8},{4,12},{8,0},{12,4},{16,24},{20,28},{24,16},{28,20},{1,9},{5... | collective-permute-start | bytes 786440 | tf_op jit(solution)/shard_map/ppermute | solution.py:251
  66.8 6.7 %collective-permute-start.13 = (f32[8,64,128]{2,1,0:T(8,128)S(1)}, f32[8,64,128]{2,1,0:T(8,128)S(1)}, u32[]{:S(2)}, u32[]{:S(2)}) collective-permute-start(f32[8,64,128]{2,1,0:T(8,128)S(1)} %get-tuple-element.57), channel_id=1, source_target_pairs={{0,4},{4,0},{8,12},{12,8},{16,20},{20,16},{24,28},{28,24},{1,5},{5... | collective-permute-start | bytes 786440 | tf_op jit(solution)/shard_map/ppermute | solution.py:251
  67.5 22.6 %collective-permute-start.17 = (f32[1536,128]{1,0:T(8,128)S(1)}, f32[1536,128]{1,0:T(8,128)S(1)}, u32[]{:S(2)}, u32[]{:S(2)}) collective-permute-start(f32[1536,128]{1,0:T(8,128)S(1)} %get-tuple-element.97), channel_id=1, source_target_pairs={{0,3},{1,2},{2,1},{3,0},{4,7},{5,6},{6,5},{7,4},{8,11},{9,10},{10,... | collective-permute-start | bytes 2359304 | tf_op jit(solution)/shard_map/ppermute | solution.py:251
  67.6 10.6 %collective-permute-start.18 = (f32[1024,128]{1,0:T(8,128)S(1)}, f32[1024,128]{1,0:T(8,128)S(1)}, u32[]{:S(2)}, u32[]{:S(2)}) collective-permute-start(f32[1024,128]{1,0:T(8,128)S(1)} %get-tuple-element.99), channel_id=1, source_target_pairs={{0,1},{1,0},{2,3},{3,2},{4,5},{5,4},{6,7},{7,6},{8,9},{9,8},{10,11... | collective-permute-start | bytes 1572872 | tf_op jit(solution)/shard_map/ppermute | solution.py:251
  73.5 18.7 %collective-permute-start.16 = (f32[2,128,128]{2,1,0:T(8,128)S(1)}, f32[2,128,128]{2,1,0:T(8,128)S(1)}, u32[]{:S(2)}, u32[]{:S(2)}) collective-permute-start(f32[2,128,128]{2,1,0:T(8,128)S(1)} %pad_maximum_fusion.2), channel_id=1, source_target_pairs={{0,2},{1,3},{2,0},{3,1},{4,6},{5,7},{6,4},{7,5},{8,10},{9,11},{10,... | collective-permute-start | bytes 393224 | tf_op jit(solution)/shard_map/ppermute | solution.py:251
  75.0 17.2 %collective-permute-start.15 = (f32[2,128,128]{2,1,0:T(8,128)S(1)}, f32[2,128,128]{2,1,0:T(8,128)S(1)}, u32[]{:S(2)}, u32[]{:S(2)}) collective-permute-start(f32[2,128,128]{2,1,0:T(8,128)S(1)} %pad_maximum_fusion.1), channel_id=1, source_target_pairs={{0,16},{4,20},{8,24},{12,28},{16,0},{20,4},{24,8},{28,12},{1,17},{... | collective-permute-start | bytes 393224 | tf_op jit(solution)/shard_map/ppermute | solution.py:251
  77.7 14.7 %copy-start.6 = (f32[2,128,128]{2,1,0:T(8,128)S(1)}, f32[2,128,128]{2,1,0:T(8,128)}, u32[]{:S(2)}) copy-start(f32[2,128,128]{2,1,0:T(8,128)} %param.11) | copy-start | bytes 393220
  77.7 14.5 %collective-permute-start.14 = (f32[2,128,128]{2,1,0:T(8,128)S(1)}, f32[2,128,128]{2,1,0:T(8,128)S(1)}, u32[]{:S(2)}, u32[]{:S(2)}) collective-permute-start(f32[2,128,128]{2,1,0:T(8,128)S(1)} %pad_maximum_fusion), channel_id=1, source_target_pairs={{0,18},{1,19},{2,16},{3,17},{4,22},{5,23},{6,20},{7,21},{8,26},{9,... | collective-permute-start | bytes 393224 | tf_op jit(solution)/shard_map/ppermute | solution.py:374
  92.3 1.4 %copy-start.4 = (f32[4,1024,128]{2,1,0:T(8,128)}, f32[4,1024,128]{2,1,0:T(8,128)S(1)}, u32[]{:S(2)}) copy-start(f32[4,1024,128]{2,1,0:T(8,128)S(1)} %bitcast_dynamic-update-slice_fusion) | copy-start | bytes 6291460
  92.4 1.7 %copy-start.5 = (f32[4,512,128]{2,1,0:T(8,128)}, f32[4,512,128]{2,1,0:T(8,128)S(1)}, u32[]{:S(2)}) copy-start(f32[4,512,128]{2,1,0:T(8,128)S(1)} %bitcast_dynamic-update-slice_fusion.4) | copy-start | bytes 3145732

commit v14 on v13

--- a/solution.py
+++ b/solution.py
@@ -185,29 +185,26 @@
     return split_bf16(jnp.concatenate(rows, axis=0))
 
 
-def early_kernel(info, counts, own_ref, r1, r2, mt, acc, *sums):
+def early_kernel(info, counts, own_ref, r1, mt, acc):
     me = info[0]
-    parts = [masked_split(ref, counts[me]) for ref in (own_ref.at[me], r1, r2)]
+    parts = [masked_split(ref, counts[me]) for ref in (own_ref.at[me], r1)]
     left = [jnp.concatenate([part[n] for part in parts], axis=1) for n in range(2)]
     for c in range(0, NB, 2):
-        acc[:, pl.ds(c * B, 2 * B)] = dot3(left, inverse_rows(mt, me, range(NB - 1), c), ((1,), (0,)))
-    for ref in sums:
-        ref[...] = jnp.zeros_like(ref)
-
-
-def panel_kernel(info, counts, tgt_a, tgt_b, r3, mt, l3, acc, *rest):
-    x0, x1, x2, x3, keep, send, xh, xl = rest[-8:]
-    if len(rest) == 8:
-        keep[...] = jnp.zeros_like(keep)
-        send[...] = jnp.zeros_like(send)
+        acc[:, pl.ds(c * B, 2 * B)] = dot3(left, inverse_rows(mt, me, (0, 1), c), ((1,), (0,)))
+
+
+def panel_kernel(info, counts, tgt_a, tgt_b, r2, r3, mt, l3, acc, x0, x1, x2, x3, keep, send, xh, xl):
+    keep[...] = jnp.zeros_like(keep)
+    send[...] = jnp.zeros_like(send)
     me = info[0]
     count = counts[me]
     rows = P_SIZE * B
     outs = [x0, x1, x2, x3]
     x3[pl.ds(rows, W), :] = l3[...]
-    left = masked_split(r3, count)
+    parts = [masked_split(ref, count) for ref in (r2, r3)]
+    left = [jnp.concatenate([part[n] for part in parts], axis=1) for n in range(2)]
     for c in range(0, NB, 2):
-        got = acc[:, pl.ds(c * B, 2 * B)] + dot3(left, inverse_rows(mt, me, [NB - 1], c), ((1,), (0,)))
+        got = acc[:, pl.ds(c * B, 2 * B)] + dot3(left, inverse_rows(mt, me, (2, 3), c), ((1,), (0,)))
         outs[c][pl.ds(0, rows), :] = got[:, :B]
         outs[c + 1][pl.ds(0, rows), :] = got[:, B:]
         high, low = split_bf16(got)
@@ -312,27 +309,25 @@
     longer = jax.ShapeDtypeStruct((rows + W, B), jnp.float32)
     part = jax.ShapeDtypeStruct((2, blocks // 2, B // 2, B), jnp.float32)
     room = pltpu.CompilerParams(vmem_limit_bytes=16 * 2**20 + 4 * blocks * B * B)
-    sums = 0
-    acc, *empty = pl.pallas_call(
+    acc = pl.pallas_call(
         early_kernel,
-        out_shape=[jax.ShapeDtypeStruct((rows, W), jnp.float32)] + [part] * sums,
-        in_specs=[SMEM] * 2 + [VMEM] * 4,
-        out_specs=[VMEM] * (1 + sums),
+        out_shape=jax.ShapeDtypeStruct((rows, W), jnp.float32),
+        in_specs=[SMEM] * 2 + [VMEM] * 3,
+        out_specs=VMEM,
         compiler_params=room,
         cost_estimate=pl.CostEstimate(flops=5 * 10**8, bytes_accessed=10 * 10**6, transcendentals=0),
         name="early",
-    )(info, panel_count, panel, *panel_in[:2], mt)
+    )(info, panel_count, panel, panel_in[0], mt)
     *x_parts, keep, send = pl.pallas_call(
         panel_kernel,
         out_shape=[slab] * (NB - 1) + [longer, part, part],
-        in_specs=[SMEM] * 4 + [VMEM] * (4 + sums),
+        in_specs=[SMEM] * 4 + [VMEM] * 5,
         out_specs=[VMEM] * (NB + 2),
         scratch_shapes=[pltpu.VMEM((rows, W), jnp.bfloat16)] * 2,
-        input_output_aliases={8 + n: NB + n for n in range(sums)},
         compiler_params=room,
         cost_estimate=pl.CostEstimate(flops=10**9, bytes_accessed=10 * 10**6, transcendentals=0),
         name="panel",
-    )(info, panel_count, tgt_a, tgt_b, panel_in[2], mt, l_parts[3], acc, *empty)
+    )(info, panel_count, tgt_a, tgt_b, *panel_in[1:], mt, l_parts[3], acc)
 
     l_back = [swap(l_parts[m], "narrow", m) for m in (1, 2)]
     x_back = [swap(x_parts[m], "narrow", m) for m in masks]

time: 94.4 us -> 94.8 us (level)
  waiting for transfers between devices: 38.7 us -> 40.8 us
  Pallas kernels: 23.6 us -> 22.6 us
    ppermute x18, waiting for transfers between devices: 38.7 us -> 40.8 us  [swap(): return lax.ppermute(x, axis, xor_pairs(lax.axis_size(axis), mask))]
    pallas_call x1, Pallas kernels: 3.03 us -> 2.05 us  [local(): pl.pallas_call(early_kernel, out_shape=jax.ShapeDtypeStruct((rows, W), jn...]
  transfers between devices with their start and end apart: 19 -> 19, of which waited for: 11 -> 11; matrix products, arithmetic and copies ran while one was open for 8% -> 7% of each run, Pallas kernels for 24% -> 23%
where the time goes in v14:
time: 94.8 us; the launch traced here: 94.6 us
  waiting for transfers between devices  40.8 us (43%)
  Pallas kernels  22.6 us (24%)
  starting transfers between devices  19.6 us (21%)
  other arithmetic  5.45 us (6%)
  local copies, waits for them, and re-layouts  5.18 us (5%)
    ppermute x18, waiting for transfers between devices, swap(): return lax.ppermute(x, axis, xor_pairs(lax.axis_size(axis), mask))  40.8 us
    pallas_call x1, Pallas kernels, local(): pl.pallas_call(factor_kernel, out_shape=[slab] * NB + [jax.ShapeDtypeStru...  19.7 us
    ppermute x18, starting transfers between devices, swap(): return lax.ppermute(x, axis, xor_pairs(lax.axis_size(axis), mask))  19.6 us
    pallas_call x1, other arithmetic, local(): pl.pallas_call(panel_kernel, out_shape=[slab] * (NB - 1) + [longer, part,...  3.69 us
    squeeze x1, local copies, waits for them, and re-layouts, local(): own = lambda x, m: lax.dynamic_index_in_dim(x, me ^ m, 0, keepdims=False)  2.68 us
    unnamed x18, local copies, waits for them, and re-layouts  2.09 us
    pallas_call x1, Pallas kernels, local(): pl.pallas_call(early_kernel, out_shape=jax.ShapeDtypeStruct((rows, W), jn...  2.05 us
  transfers between devices with their start and end apart: 19, of which 11 were waited for; matrix products, arithmetic and copies ran while one was open for 7% of the time, Pallas kernels for 23%

profile of v14, /device:TPU:0, one launch (start us, length us, event | category | flops | bytes accessed | tf_op | source)
XLA Modules:
  0.0 94.6 jit_solution(1704922958042954557)
XLA Ops:
  0.6 0.0 copy-start.1
  0.6 1.2 %copy-done.1 = f32[4,512,128]{2,1,0:T(8,128)S(1)} copy-done((f32[4,512,128]{2,1,0:T(8,128)S(1)}, f32[4,512,128]{2,1,0:T(8,128)}, u32[]{:S(2)}) %copy-start.1) | copy-done | bytes 1048600
  1.9 0.8 cut.1
  2.7 0.5 collective-permute-start
  3.2 2.6 %collective-permute-start.1 = (f32[256,128]{1,0:T(8,128)}, f32[256,128]{1,0:T(8,128)S(1)}, u32[]{:S(2)}, u32[]{:S(2)}) collective-permute-start(f32[256,128]{1,0:T(8,128)} %get-tuple-element.36), channel_id=1, source_target_pairs={{0,2},{1,3},{2,0},{3,1},{4,6},{5,7},{6,4},{7,5},{8,10},{9,11},{10,... | collective-permute-start | bytes 393224 | tf_op jit(solution)/shard_map/ppermute | solution.py:248
  5.8 0.1 collective-permute-start.2
  5.8 2.7 %dynamic-slice_bitcast_fusion = (f32[1024,128]{1,0:T(8,128)}, f32[1024,128]{1,0:T(8,128)}, f32[1024,128]{1,0:T(8,128)}) fusion(f32[4,1024,128]{2,1,0:T(8,128)} %own_ref.3, s32[]{:T(128)S(6)} %select_n.59, s32[]{:T(128)S(6)} %select_n.58, s32[]{:T(128)S(6)} %select_n.57), kind=kLoop, calls=%fused_computation.10 | loop fusion | bytes 3145740 | tf_op jit(solution)/shard_map/jit(dynamic_index_in_dim)/squeeze | solution.py:266
  8.5 1.8 %collective-permute-done.1.r2 = f32[256,128]{1,0:T(8,128)S(1)} collective-permute-done((f32[256,128]{1,0:T(8,128)}, f32[256,128]{1,0:T(8,128)S(1)}, u32[]{:S(2)}, u32[]{:S(2)}) %collective-permute-start.1) | collective-permute-done | bytes 131104 | tf_op jit(solution)/shard_map/ppermute | solution.py:248
  10.3 2.4 %collective-permute-done.2.r3 = f32[256,128]{1,0:T(8,128)} collective-permute-done((f32[256,128]{1,0:T(8,128)}, f32[256,128]{1,0:T(8,128)}, u32[]{:S(2)}, u32[]{:S(2)}) %collective-permute-start.2) | collective-permute-done | bytes 131104 | tf_op jit(solution)/shard_map/ppermute | solution.py:248
  12.7 0.0 collective-permute-done.r1
  12.7 0.1 collective-permute-start.6
  12.8 1.7 %collective-permute-start.4 = (f32[1024,128]{1,0:T(8,128)}, f32[1024,128]{1,0:T(8,128)}, u32[]{:S(2)}, u32[]{:S(2)}) collective-permute-start(f32[1024,128]{1,0:T(8,128)} %get-tuple-element.43), channel_id=1, source_target_pairs={{0,2},{1,3},{2,0},{3,1},{4,6},{5,7},{6,4},{7,5},{8,10},{9,11},{10,... | collective-permute-start | bytes 1572872 | tf_op jit(solution)/shard_map/ppermute | solution.py:248
  14.6 0.0 collective-permute-start.5
  14.6 0.0 copy-done.7
  14.6 0.0 copy-done.8
  14.6 0.1 multiply_add_fusion
  14.7 0.0 copy-done.2
  14.7 19.7 %factor.1 = (f32[512,128]{1,0:T(8,128)S(1)}, f32[512,128]{1,0:T(8,128)S(1)}, f32[512,128]{1,0:T(8,128)S(1)}, f32[512,128]{1,0:T(8,128)S(1)}, f32[4,512,128]{2,1,0:T(8,128)S(1)}) custom-call(s32[1]{0:T(128)} %bitcast.info, f32[4,512,128]{2,1,0:T(8,128)S(1)} %copy-done.2, f32[512,128]{1,0:T(8,128)S(1)} %collective-permute-done.r1, ...), custom_call_target="tpu_custom_call" | custom-call | flops 200000000 | bytes 4000000 | tf_op jit(solution)/shard_map/factor/pallas_call | solution.py:295
  34.4 1.7 %collective-permute-start.7 = (f32[512,128]{1,0:T(8,128)S(1)}, f32[512,128]{1,0:T(8,128)S(1)}, u32[]{:S(2)}, u32[]{:S(2)}) collective-permute-start(f32[512,128]{1,0:T(8,128)S(1)} %get-tuple-element.49), channel_id=1, source_target_pairs={{0,2},{1,3},{2,0},{3,1},{4,6},{5,7},{6,4},{7,5},{8,10},{9,11},{10,... | collective-permute-start | bytes 786440 | tf_op jit(solution)/shard_map/ppermute | solution.py:248
  36.2 0.1 multiply_add_fusion.1
  36.3 0.0 collective-permute-done.6.r1
  36.3 0.0 copy-done
  36.3 0.0 copy-done.3
  36.3 2.0 %early.1 = f32[1024,512]{1,0:T(8,128)S(1)} custom-call(s32[1]{0:T(128)} %bitcast.info, s32[4]{0:T(128)S(1)} %copy-done.3, f32[4,1024,128]{2,1,0:T(8,128)S(1)} %copy-done, f32[1024,128]{1,0:T(8,128)} %collective-permute-done.6.r1, f32[4,512,128]{2,1,0:T(8,128)S(1)} %get-tuple-element.45.mt), custom_call_target="tpu_custom_call" | custom-call | flops 500000000 | bytes 10000000 | tf_op jit(solution)/shard_map/early/pallas_call | solution.py:312
  38.4 0.0 collective-permute-done.4
  38.4 0.0 collective-permute-done.5
  38.4 0.1 broadcast_in_dim.37
  38.5 3.7 %panel.1 = (f32[4,1024,128]{2,1,0:T(8,128)S(1)}, f32[2,32,64,128]{3,2,1,0:T(8,128)S(1)}, f32[2,32,64,128]{3,2,1,0:T(8,128)S(1)}, f32[1024,128]{1,0:T(8,128)S(1)}...) fusion(f32[4,1024,128]{2,1,0:T(8,128)S(1)} %broadcast_in_dim.37, s32[]{:T(128)S(6)} %select_n.60, s32[1]{0:T(128)} %bitcast.info, ...), kind=kCustom, calls=%fused_computation.9 | custom fusion | flops 1000000000 | bytes 11011592 | tf_op jit(solution)/shard_map/panel/pallas_call | solution.py:321
  42.2 1.9 %collective-permute-done.7 = f32[512,128]{1,0:T(8,128)S(1)} collective-permute-done((f32[512,128]{1,0:T(8,128)S(1)}, f32[512,128]{1,0:T(8,128)S(1)}, u32[]{:S(2)}, u32[]{:S(2)}) %collective-permute-start.7) | collective-permute-done | bytes 262176 | tf_op jit(solution)/shard_map/ppermute | solution.py:248
  44.1 0.0 collective-permute-start.8
  44.1 4.2 %collective-permute-done.8 = f32[2,32,64,128]{3,2,1,0:T(8,128)S(1)} collective-permute-done((f32[2,32,64,128]{3,2,1,0:T(8,128)S(1)}, f32[2,32,64,128]{3,2,1,0:T(8,128)S(1)}, u32[]{:S(2)}, u32[]{:S(2)}) %collective-permute-start.8) | collective-permute-done | bytes 2097184 | tf_op jit(solution)/shard_map/ppermute | solution.py:248
  48.3 0.6 slice_add_fusion
  48.8 2.1 %collective-permute-start.10 = (f32[16,64,128]{2,1,0:T(8,128)S(1)}, f32[16,64,128]{2,1,0:T(8,128)S(1)}, u32[]{:S(2)}, u32[]{:S(2)}) collective-permute-start(f32[16,64,128]{2,1,0:T(8,128)S(1)} %get-tuple-element.54), channel_id=1, source_target_pairs={{0,8},{4,12},{8,0},{12,4},{16,24},{20,28},{24,16},{28,20},{1,9},{5... | collective-permute-start | bytes 1572872 | tf_op jit(solution)/shard_map/ppermute | solution.py:248
  51.0 1.1 %collective-permute-start.9 = (f32[16,64,128]{2,1,0:T(8,128)S(1)}, f32[16,64,128]{2,1,0:T(8,128)S(1)}, u32[]{:S(2)}, u32[]{:S(2)}) collective-permute-start(f32[16,64,128]{2,1,0:T(8,128)S(1)} %get-tuple-element.53), channel_id=1, source_target_pairs={{0,4},{4,0},{8,12},{12,8},{16,20},{20,16},{24,28},{28,24},{1,5},{5... | collective-permute-start | bytes 1572872 | tf_op jit(solution)/shard_map/ppermute | solution.py:248
  52.1 1.5 %collective-permute-start.11 = (f32[1024,128]{1,0:T(8,128)S(1)}, f32[1024,128]{1,0:T(8,128)S(1)}, u32[]{:S(2)}, u32[]{:S(2)}) collective-permute-start(f32[1024,128]{1,0:T(8,128)S(1)} %get-tuple-element.95), channel_id=1, source_target_pairs={{0,2},{1,3},{2,0},{3,1},{4,6},{5,7},{6,4},{7,5},{8,10},{9,11},{10,... | collective-permute-start | bytes 1572872 | tf_op jit(solution)/shard_map/ppermute | solution.py:248
  53.6 0.0 collective-permute-start.3
  53.6 9.9 %collective-permute-done.10 = f32[16,64,128]{2,1,0:T(8,128)S(1)} collective-permute-done((f32[16,64,128]{2,1,0:T(8,128)S(1)}, f32[16,64,128]{2,1,0:T(8,128)S(1)}, u32[]{:S(2)}, u32[]{:S(2)}) %collective-permute-start.10) | collective-permute-done | bytes 524320 | tf_op jit(solution)/shard_map/ppermute | solution.py:248
  63.4 0.1 slice_add_fusion.4
  63.5 1.4 %collective-permute-done.9 = f32[16,64,128]{2,1,0:T(8,128)S(1)} collective-permute-done((f32[16,64,128]{2,1,0:T(8,128)S(1)}, f32[16,64,128]{2,1,0:T(8,128)S(1)}, u32[]{:S(2)}, u32[]{:S(2)}) %collective-permute-start.9) | collective-permute-done | bytes 524320 | tf_op jit(solution)/shard_map/ppermute | solution.py:248
  64.9 0.1 slice_add_fusion.7
  65.0 0.5 collective-permute-done.11
  65.5 0.4 collective-permute-start.12
  65.9 0.1 broadcast_in_dim.32
  66.0 1.1 %collective-permute-start.13 = (f32[8,64,128]{2,1,0:T(8,128)S(1)}, f32[8,64,128]{2,1,0:T(8,128)S(1)}, u32[]{:S(2)}, u32[]{:S(2)}) collective-permute-start(f32[8,64,128]{2,1,0:T(8,128)S(1)} %get-tuple-element.57), channel_id=1, source_target_pairs={{0,4},{4,0},{8,12},{12,8},{16,20},{20,16},{24,28},{28,24},{1,5},{5... | collective-permute-start | bytes 786440 | tf_op jit(solution)/shard_map/ppermute | solution.py:248
  67.2 0.0 collective-permute-done.3
  67.2 0.1 collective-permute-start.17
  67.3 1.7 %collective-permute-start.18 = (f32[1024,128]{1,0:T(8,128)S(1)}, f32[1024,128]{1,0:T(8,128)S(1)}, u32[]{:S(2)}, u32[]{:S(2)}) collective-permute-start(f32[1024,128]{1,0:T(8,128)S(1)} %get-tuple-element.99), channel_id=1, source_target_pairs={{0,1},{1,0},{2,3},{3,2},{4,5},{5,4},{6,7},{7,6},{8,9},{9,8},{10,11... | collective-permute-start | bytes 1572872 | tf_op jit(solution)/shard_map/ppermute | solution.py:248
  68.9 3.5 %collective-permute-done.12 = f32[8,64,128]{2,1,0:T(8,128)S(1)} collective-permute-done((f32[8,64,128]{2,1,0:T(8,128)S(1)}, f32[8,64,128]{2,1,0:T(8,128)S(1)}, u32[]{:S(2)}, u32[]{:S(2)}) %collective-permute-start.12) | collective-permute-done | bytes 262176 | tf_op jit(solution)/shard_map/ppermute | solution.py:248
  72.5 0.5 collective-permute-done.13
  73.1 1.7 %collective-permute-start.16 = (f32[2,128,128]{2,1,0:T(8,128)S(1)}, f32[2,128,128]{2,1,0:T(8,128)S(1)}, u32[]{:S(2)}, u32[]{:S(2)}) collective-permute-start(f32[2,128,128]{2,1,0:T(8,128)S(1)} %pad_maximum_fusion.2), channel_id=1, source_target_pairs={{0,2},{1,3},{2,0},{3,1},{4,6},{5,7},{6,4},{7,5},{8,10},{9,11},{10,... | collective-permute-start | bytes 393224 | tf_op jit(solution)/shard_map/ppermute | solution.py:248
  74.8 3.1 %collective-permute-start.15 = (f32[2,128,128]{2,1,0:T(8,128)S(1)}, f32[2,128,128]{2,1,0:T(8,128)S(1)}, u32[]{:S(2)}, u32[]{:S(2)}) collective-permute-start(f32[2,128,128]{2,1,0:T(8,128)S(1)} %pad_maximum_fusion.1), channel_id=1, source_target_pairs={{0,16},{4,20},{8,24},{12,28},{16,0},{20,4},{24,8},{28,12},{1,17},{... | collective-permute-start | bytes 393224 | tf_op jit(solution)/shard_map/ppermute | solution.py:248
  77.9 0.0 copy-start.6
  77.9 0.1 collective-permute-start.14
  78.0 0.0 collective-permute-done.18
  78.0 11.8 %collective-permute-done.17 = f32[1536,128]{1,0:T(8,128)S(1)} collective-permute-done((f32[1536,128]{1,0:T(8,128)S(1)}, f32[1536,128]{1,0:T(8,128)S(1)}, u32[]{:S(2)}, u32[]{:S(2)}) %collective-permute-start.17) | collective-permute-done | bytes 786464 | tf_op jit(solution)/shard_map/ppermute | solution.py:248
  89.8 2.9 %collective-permute-done.16 = f32[2,128,128]{2,1,0:T(8,128)S(1)} collective-permute-done((f32[2,128,128]{2,1,0:T(8,128)S(1)}, f32[2,128,128]{2,1,0:T(8,128)S(1)}, u32[]{:S(2)}, u32[]{:S(2)}) %collective-permute-start.16) | collective-permute-done | bytes 131104 | tf_op jit(solution)/shard_map/ppermute | solution.py:248
  92.7 0.0 collective-permute-done.15
  92.7 0.0 collective-permute-done.14
  92.9 0.0 copy-start.4
  92.9 0.0 copy-start.5
  92.9 0.0 copy-done.6
  92.9 0.8 fusion.2
  93.7 0.5 copy-done.4
  94.2 0.3 copy-done.5
  (17 shorter events, 0.3 us)
Async XLA Ops:
  0.6 1.2 %copy-start.1 = (f32[4,512,128]{2,1,0:T(8,128)S(1)}, f32[4,512,128]{2,1,0:T(8,128)}, u32[]{:S(2)}) copy-start(f32[4,512,128]{2,1,0:T(8,128)} %own_ref.2) | copy-start | bytes 3145732
  1.9 12.7 %copy-start.7 = (s32[144,1]{0,1:T(1,128)S(1)}, s32[144,1]{0,1:T(1,128)}, u32[]{:S(2)}) copy-start(s32[144,1]{0,1:T(1,128)} %param.9) | copy-start | bytes 1732
  1.9 12.7 %copy-start.8 = (s32[144]{0:T(256)S(1)}, s32[144]{0:T(256)}, u32[]{:S(2)}) copy-start(s32[144]{0:T(256)} %param.10) | copy-start | bytes 1732
  1.9 12.8 %copy-start.2 = (f32[4,512,128]{2,1,0:T(8,128)S(1)}, f32[4,512,128]{2,1,0:T(8,128)}, u32[]{:S(2)}) copy-start(f32[4,512,128]{2,1,0:T(8,128)} %own_ref.2) | copy-start | bytes 3145732
  2.7 10.0 %collective-permute-start = (f32[512,128]{1,0:T(8,128)}, f32[512,128]{1,0:T(8,128)S(1)}, u32[]{:S(2)}, u32[]{:S(2)}) collective-permute-start(f32[512,128]{1,0:T(8,128)} %get-tuple-element.35), channel_id=1, source_target_pairs={{0,1},{1,0},{2,3},{3,2},{4,5},{5,4},{6,7},{7,6},{8,9},{9,8},{10,11... | collective-permute-start | bytes 786440 | tf_op jit(solution)/shard_map/ppermute | solution.py:248
  3.2 7.1 %collective-permute-start.1 = (f32[256,128]{1,0:T(8,128)}, f32[256,128]{1,0:T(8,128)S(1)}, u32[]{:S(2)}, u32[]{:S(2)}) collective-permute-start(f32[256,128]{1,0:T(8,128)} %get-tuple-element.36), channel_id=1, source_target_pairs={{0,2},{1,3},{2,0},{3,1},{4,6},{5,7},{6,4},{7,5},{8,10},{9,11},{10,... | collective-permute-start | bytes 393224 | tf_op jit(solution)/shard_map/ppermute | solution.py:248
  5.8 7.0 %collective-permute-start.2 = (f32[256,128]{1,0:T(8,128)}, f32[256,128]{1,0:T(8,128)}, u32[]{:S(2)}, u32[]{:S(2)}) collective-permute-start(f32[256,128]{1,0:T(8,128)} %get-tuple-element.37), channel_id=1, source_target_pairs={{0,3},{1,2},{2,1},{3,0},{4,7},{5,6},{6,5},{7,4},{8,11},{9,10},{10,... | collective-permute-start | bytes 393224 | tf_op jit(solution)/shard_map/ppermute | solution.py:248
  5.8 30.5 %copy-start = (f32[4,1024,128]{2,1,0:T(8,128)S(1)}, f32[4,1024,128]{2,1,0:T(8,128)}, u32[]{:S(2)}) copy-start(f32[4,1024,128]{2,1,0:T(8,128)} %own_ref.3) | copy-start | bytes 6291460
  5.8 30.5 %copy-start.3 = (s32[4]{0:T(128)S(1)}, s32[4]{0:T(128)}, u32[]{:S(2)}) copy-start(s32[4]{0:T(128)} %counts.2) | copy-start | bytes 52
  12.7 23.6 %collective-permute-start.6 = (f32[1024,128]{1,0:T(8,128)}, f32[1024,128]{1,0:T(8,128)}, u32[]{:S(2)}, u32[]{:S(2)}) collective-permute-start(f32[1024,128]{1,0:T(8,128)} %get-tuple-element.47), channel_id=1, source_target_pairs={{0,1},{1,0},{2,3},{3,2},{4,5},{5,4},{6,7},{7,6},{8,9},{9,8},{10,11... | collective-permute-start | bytes 1572872 | tf_op jit(solution)/shard_map/ppermute | solution.py:248
  12.8 25.5 %collective-permute-start.4 = (f32[1024,128]{1,0:T(8,128)}, f32[1024,128]{1,0:T(8,128)}, u32[]{:S(2)}, u32[]{:S(2)}) collective-permute-start(f32[1024,128]{1,0:T(8,128)} %get-tuple-element.43), channel_id=1, source_target_pairs={{0,2},{1,3},{2,0},{3,1},{4,6},{5,7},{6,4},{7,5},{8,10},{9,11},{10,... | collective-permute-start | bytes 1572872 | tf_op jit(solution)/shard_map/ppermute | solution.py:248
  14.6 23.8 %collective-permute-start.5 = (f32[1024,128]{1,0:T(8,128)}, f32[1024,128]{1,0:T(8,128)}, u32[]{:S(2)}, u32[]{:S(2)}) collective-permute-start(f32[1024,128]{1,0:T(8,128)} %get-tuple-element.44), channel_id=1, source_target_pairs={{0,3},{1,2},{2,1},{3,0},{4,7},{5,6},{6,5},{7,4},{8,11},{9,10},{10,... | collective-permute-start | bytes 1572872 | tf_op jit(solution)/shard_map/ppermute | solution.py:248
  34.4 9.7 %collective-permute-start.7 = (f32[512,128]{1,0:T(8,128)S(1)}, f32[512,128]{1,0:T(8,128)S(1)}, u32[]{:S(2)}, u32[]{:S(2)}) collective-permute-start(f32[512,128]{1,0:T(8,128)S(1)} %get-tuple-element.49), channel_id=1, source_target_pairs={{0,2},{1,3},{2,0},{3,1},{4,6},{5,7},{6,4},{7,5},{8,10},{9,11},{10,... | collective-permute-start | bytes 786440 | tf_op jit(solution)/shard_map/ppermute | solution.py:248
  44.1 4.2 %collective-permute-start.8 = (f32[2,32,64,128]{3,2,1,0:T(8,128)S(1)}, f32[2,32,64,128]{3,2,1,0:T(8,128)S(1)}, u32[]{:S(2)}, u32[]{:S(2)}) collective-permute-start(f32[2,32,64,128]{3,2,1,0:T(8,128)S(1)} %get-tuple-element.52), channel_id=1, source_target_pairs={{0,1},{1,0},{2,3},{3,2},{4,5},{5,4},{6,7},{7,6},{8,9},{9,8},{10,11... | collective-permute-start | bytes 6291464 | tf_op jit(solution)/shard_map/ppermute | solution.py:248
  48.8 14.6 %collective-permute-start.10 = (f32[16,64,128]{2,1,0:T(8,128)S(1)}, f32[16,64,128]{2,1,0:T(8,128)S(1)}, u32[]{:S(2)}, u32[]{:S(2)}) collective-permute-start(f32[16,64,128]{2,1,0:T(8,128)S(1)} %get-tuple-element.54), channel_id=1, source_target_pairs={{0,8},{4,12},{8,0},{12,4},{16,24},{20,28},{24,16},{28,20},{1,9},{5... | collective-permute-start | bytes 1572872 | tf_op jit(solution)/shard_map/ppermute | solution.py:248
  51.0 13.9 %collective-permute-start.9 = (f32[16,64,128]{2,1,0:T(8,128)S(1)}, f32[16,64,128]{2,1,0:T(8,128)S(1)}, u32[]{:S(2)}, u32[]{:S(2)}) collective-permute-start(f32[16,64,128]{2,1,0:T(8,128)S(1)} %get-tuple-element.53), channel_id=1, source_target_pairs={{0,4},{4,0},{8,12},{12,8},{16,20},{20,16},{24,28},{28,24},{1,5},{5... | collective-permute-start | bytes 1572872 | tf_op jit(solution)/shard_map/ppermute | solution.py:248
  52.1 13.4 %collective-permute-start.11 = (f32[1024,128]{1,0:T(8,128)S(1)}, f32[1024,128]{1,0:T(8,128)S(1)}, u32[]{:S(2)}, u32[]{:S(2)}) collective-permute-start(f32[1024,128]{1,0:T(8,128)S(1)} %get-tuple-element.95), channel_id=1, source_target_pairs={{0,2},{1,3},{2,0},{3,1},{4,6},{5,7},{6,4},{7,5},{8,10},{9,11},{10,... | collective-permute-start | bytes 1572872 | tf_op jit(solution)/shard_map/ppermute | solution.py:248
  53.6 13.6 %collective-permute-start.3 = (f32[512,128]{1,0:T(8,128)S(1)}, f32[512,128]{1,0:T(8,128)S(1)}, u32[]{:S(2)}, u32[]{:S(2)}) collective-permute-start(f32[512,128]{1,0:T(8,128)S(1)} %get-tuple-element.42), channel_id=1, source_target_pairs={{0,1},{1,0},{2,3},{3,2},{4,5},{5,4},{6,7},{7,6},{8,9},{9,8},{10,11... | collective-permute-start | bytes 786440 | tf_op jit(solution)/shard_map/ppermute | solution.py:248
  65.5 7.0 %collective-permute-start.12 = (f32[8,64,128]{2,1,0:T(8,128)S(1)}, f32[8,64,128]{2,1,0:T(8,128)S(1)}, u32[]{:S(2)}, u32[]{:S(2)}) collective-permute-start(f32[8,64,128]{2,1,0:T(8,128)S(1)} %get-tuple-element.56), channel_id=1, source_target_pairs={{0,8},{4,12},{8,0},{12,4},{16,24},{20,28},{24,16},{28,20},{1,9},{5... | collective-permute-start | bytes 786440 | tf_op jit(solution)/shard_map/ppermute | solution.py:248
  66.0 7.0 %collective-permute-start.13 = (f32[8,64,128]{2,1,0:T(8,128)S(1)}, f32[8,64,128]{2,1,0:T(8,128)S(1)}, u32[]{:S(2)}, u32[]{:S(2)}) collective-permute-start(f32[8,64,128]{2,1,0:T(8,128)S(1)} %get-tuple-element.57), channel_id=1, source_target_pairs={{0,4},{4,0},{8,12},{12,8},{16,20},{20,16},{24,28},{28,24},{1,5},{5... | collective-permute-start | bytes 786440 | tf_op jit(solution)/shard_map/ppermute | solution.py:248
  67.2 22.6 %collective-permute-start.17 = (f32[1536,128]{1,0:T(8,128)S(1)}, f32[1536,128]{1,0:T(8,128)S(1)}, u32[]{:S(2)}, u32[]{:S(2)}) collective-permute-start(f32[1536,128]{1,0:T(8,128)S(1)} %get-tuple-element.97), channel_id=1, source_target_pairs={{0,3},{1,2},{2,1},{3,0},{4,7},{5,6},{6,5},{7,4},{8,11},{9,10},{10,... | collective-permute-start | bytes 2359304 | tf_op jit(solution)/shard_map/ppermute | solution.py:248
  67.3 10.7 %collective-permute-start.18 = (f32[1024,128]{1,0:T(8,128)S(1)}, f32[1024,128]{1,0:T(8,128)S(1)}, u32[]{:S(2)}, u32[]{:S(2)}) collective-permute-start(f32[1024,128]{1,0:T(8,128)S(1)} %get-tuple-element.99), channel_id=1, source_target_pairs={{0,1},{1,0},{2,3},{3,2},{4,5},{5,4},{6,7},{7,6},{8,9},{9,8},{10,11... | collective-permute-start | bytes 1572872 | tf_op jit(solution)/shard_map/ppermute | solution.py:248
  73.1 19.6 %collective-permute-start.16 = (f32[2,128,128]{2,1,0:T(8,128)S(1)}, f32[2,128,128]{2,1,0:T(8,128)S(1)}, u32[]{:S(2)}, u32[]{:S(2)}) collective-permute-start(f32[2,128,128]{2,1,0:T(8,128)S(1)} %pad_maximum_fusion.2), channel_id=1, source_target_pairs={{0,2},{1,3},{2,0},{3,1},{4,6},{5,7},{6,4},{7,5},{8,10},{9,11},{10,... | collective-permute-start | bytes 393224 | tf_op jit(solution)/shard_map/ppermute | solution.py:248
  74.8 17.9 %collective-permute-start.15 = (f32[2,128,128]{2,1,0:T(8,128)S(1)}, f32[2,128,128]{2,1,0:T(8,128)S(1)}, u32[]{:S(2)}, u32[]{:S(2)}) collective-permute-start(f32[2,128,128]{2,1,0:T(8,128)S(1)} %pad_maximum_fusion.1), channel_id=1, source_target_pairs={{0,16},{4,20},{8,24},{12,28},{16,0},{20,4},{24,8},{28,12},{1,17},{... | collective-permute-start | bytes 393224 | tf_op jit(solution)/shard_map/ppermute | solution.py:248
  77.9 15.0 %copy-start.6 = (f32[2,128,128]{2,1,0:T(8,128)S(1)}, f32[2,128,128]{2,1,0:T(8,128)}, u32[]{:S(2)}) copy-start(f32[2,128,128]{2,1,0:T(8,128)} %param.11) | copy-start | bytes 393220
  77.9 14.8 %collective-permute-start.14 = (f32[2,128,128]{2,1,0:T(8,128)S(1)}, f32[2,128,128]{2,1,0:T(8,128)S(1)}, u32[]{:S(2)}, u32[]{:S(2)}) collective-permute-start(f32[2,128,128]{2,1,0:T(8,128)S(1)} %pad_maximum_fusion), channel_id=1, source_target_pairs={{0,18},{1,19},{2,16},{3,17},{4,22},{5,23},{6,20},{7,21},{8,26},{9,... | collective-permute-start | bytes 393224 | tf_op jit(solution)/shard_map/ppermute | solution.py:369
  92.9 1.4 %copy-start.4 = (f32[4,1024,128]{2,1,0:T(8,128)}, f32[4,1024,128]{2,1,0:T(8,128)S(1)}, u32[]{:S(2)}) copy-start(f32[4,1024,128]{2,1,0:T(8,128)S(1)} %bitcast_dynamic-update-slice_fusion) | copy-start | bytes 6291460
  92.9 1.7 %copy-start.5 = (f32[4,512,128]{2,1,0:T(8,128)}, f32[4,512,128]{2,1,0:T(8,128)S(1)}, u32[]{:S(2)}) copy-start(f32[4,512,128]{2,1,0:T(8,128)S(1)} %bitcast_dynamic-update-slice_fusion.4) | copy-start | bytes 3145732
